TPU v7x, 32 devices: a whole 2x2x4 slice. The times are simulated.
32 devices in a mesh: ctx: 4 (over y, core), chan: 8 (over z, x).
Axes of the slice: x: 2, y: 2, z: 4, core: 2. Of those that a mesh axis runs over, the one named last changes fastest.
Arguments:
- features: float32 [3, 512, 8192], P(None, 'ctx', 'chan'), may hold values from -6 to 6
- saved_conv: float32 [512, 8192], P('ctx', 'chan'), may hold values from -6 to 6
- out_grad: float32 [512, 8192], P('ctx', 'chan'), may hold values from -6 to 6
- short_filter: float32 [3, 3, 8192], P(None, None, 'chan'), may hold values from -3 to 3
- residue: float32 [8192, 16], P('chan'), may hold values from -0.18 to 0.18
- rate: float32 [8192, 16], P('chan'), may hold values from 0.0001953125 to 0.0333333333
- bias: float32 [8192], P('chan'), may hold values from -1 to 1
- w_proj: bfloat16 [3, 8192, 8192], P(None, 'chan'), may hold values from -0.0625 to 0.0625
Outputs:
- grad_inputs: float32 [3, 512, 8192], P(None, 'ctx', 'chan')
- grad_x: float32 [512, 8192], P('ctx', 'chan')
- grad_residue: float32 [8192, 16], P('chan')
- grad_bias: float32 [8192], P('chan')
All inputs are finite; a program needn't handle non-finite values.
Results may differ from a plain program's by a relative error of at most 0.0029.
Values may be sent and summed in bfloat16 or wider, within the bound.
No kernel may reach another device: no remote copies, remote signals or barrier semaphores. Data moves between devices by JAX's collectives and lax.ppermute only.
A program may use at most 256 MiB of HBM per device.

v0:
```python
import jax
import jax.numpy as jnp
from jax import lax
from jax.sharding import PartitionSpec as P

STRETCH = 64


def carried_in(part, axis, combine, identity):
    count = lax.axis_size(axis)
    place = lax.axis_index(axis)
    ahead = count - 1 - place
    gathered = jax.tree.map(lambda a: lax.all_gather(a, axis), part)
    state = jax.tree.map(lambda a, e: jnp.zeros_like(a) + jnp.asarray(e, a.dtype), part, identity)

    def one(hop, state):
        source = count - 1 - hop
        return combine(
            state, jax.tree.map(lambda a: lax.dynamic_index_in_dim(a, source, 0, False), gathered)
        )

    return lax.fori_loop(0, ahead, one, state)


def from_behind(array, axis, by):
    count = lax.axis_size(axis)
    pairs = [(i, i + by) for i in range(count) if 0 <= i + by < count]
    return lax.ppermute(array, axis, pairs)


def body(features, saved_conv, out_grad, short_filter, residue, rate, bias, w_proj):
    highest = lax.Precision.HIGHEST
    gate_feat = features[0]
    key_feat = features[1]
    value_feat = features[2]
    tok_rows, channels = out_grad.shape
    blocks = tok_rows // STRETCH
    product = key_feat * value_feat
    signal = out_grad * gate_feat
    grad_gate = out_grad * (saved_conv + bias * product)
    offsets = jnp.arange(STRETCH, dtype=jnp.float32)
    powers = jnp.exp(-rate[None] * offsets[:, None, None])
    remaining = jnp.exp(-rate[None] * (STRETCH - offsets)[:, None, None])
    sig_blocks = signal.reshape(blocks, STRETCH, channels)
    prod_blocks = product.reshape(blocks, STRETCH, channels)
    summaries = jnp.einsum("kjc,jcm->kcm", sig_blocks, powers, precision=highest)
    block_index = jnp.arange(blocks, dtype=jnp.float32)
    block_decay = jnp.exp(-rate[None] * (STRETCH * block_index)[:, None, None])
    own_total = jnp.sum(summaries * block_decay, axis=0)
    span_decay = jnp.exp(-rate * tok_rows)

    def combine(earlier, later_part):
        return (later_part[0] + later_part[1] * earlier[0], later_part[1] * earlier[1])

    identity = (jnp.zeros_like(own_total), jnp.ones_like(span_decay))
    incoming, span_unused = carried_in((own_total, span_decay), "ctx", combine, identity)
    stretch_decay = jnp.exp(-rate * STRETCH)

    def back_step(state, summary):
        return (summary + stretch_decay * state, state)

    first_state, block_ends = lax.scan(back_step, incoming, summaries, reverse=True)
    far_corr = jnp.einsum("jcm,kcm->kjc", residue[None] * remaining, block_ends, precision=highest)
    far_residue = jnp.einsum(
        "kjc,jcm,kcm->cm", prod_blocks, remaining, block_ends, precision=highest
    )
    taps = jnp.einsum("lcm,cm->lc", powers, residue, precision=highest)
    padded = jnp.pad(sig_blocks, ((0, 0), (0, STRETCH), (0, 0)))

    def shift_block(offset):
        return lax.dynamic_slice_in_dim(padded, offset, STRETCH, 1)

    shifted = jax.vmap(shift_block)(jnp.arange(STRETCH, dtype=jnp.int32))
    near_corr = jnp.einsum("lkjc,lc->kjc", shifted, taps, precision=highest)
    lagged = jnp.einsum("lkjc,kjc->lc", shifted, prod_blocks, precision=highest)
    near_residue = jnp.einsum("lc,lcm->cm", lagged, powers, precision=highest)
    corr = (near_corr + far_corr).reshape(tok_rows, channels)
    grad_prod = corr + bias * signal
    grad_stream = jnp.stack([grad_gate, grad_prod * value_feat, grad_prod * key_feat])
    next_rim = from_behind(grad_stream[:, 0:2], "ctx", -1)
    extended = jnp.concatenate([grad_stream, next_rim], axis=1)
    grad_inputs = short_filter[:, 0][:, None, :] * extended[:, 0:tok_rows]
    grad_inputs = grad_inputs + short_filter[:, 1][:, None, :] * extended[:, 1 : tok_rows + 1]
    grad_inputs = grad_inputs + short_filter[:, 2][:, None, :] * extended[:, 2 : tok_rows + 2]
    scale = (tok_rows * lax.axis_size("ctx")) ** (-0.5)
    summed_residue, summed_bias = lax.psum(
        (near_residue + far_residue, jnp.sum(signal * product, axis=0)), "ctx"
    )
    grad_residue = summed_residue * scale
    grad_bias = summed_bias * scale
    rounded = grad_inputs.astype(jnp.bfloat16)
    gathered_rows = lax.all_gather(rounded, "chan", axis=2, tiled=True)
    grad_x = jnp.einsum("ptc,pdc->td", gathered_rows, w_proj, preferred_element_type=jnp.float32)
    return (grad_inputs, grad_x, grad_residue, grad_bias)


def solution(mesh):
    return jax.shard_map(
        body,
        mesh=mesh,
        in_specs=(
            P(None, "ctx", "chan"),
            P("ctx", "chan"),
            P("ctx", "chan"),
            P(None, None, "chan"),
            P("chan", None),
            P("chan", None),
            P("chan"),
            P(None, "chan", None),
        ),
        out_specs=(P(None, "ctx", "chan"), P("ctx", "chan"), P("chan", None), P("chan")),
        check_vma=False,
    )
```

profile of v0, /device:TPU:0, one launch (start us, length us, event | category | flops | bytes accessed | tf_op | source)
XLA Modules:
  0.0 418.9 jit_solution(9916396688252980656)
XLA Ops:
  8.1 2.0 multiply_reduce_fusion.2
  10.5 1.3 copy.33
  11.7 1.9 copy.39
  13.6 1.7 copy.43
  16.7 37.1 %gather_fusion = f32[64,2,64,1024]{3,1,2,0:T(2,128)} fusion(f32[2,128,1024]{2,0,1:T(2,128)S(1)} %pad.4, s32[64]{0:T(128)S(1)} %shift-left_bitcast_fusion), kind=kCustom, calls=%fused_computation | custom fusion | bytes 67109632 | tf_op jit(solution)/shard_map/vmap()/gather | solution.py:71
  53.8 61.0 %copy.46 = f32[64,2,64,1024]{2,0,1,3:T(8,128)} copy(f32[64,2,64,1024]{3,1,2,0:T(2,128)} %gather_fusion) | data formatting | bytes 67108864 | tf_op jit(solution)/shard_map/vmap()/gather | solution.py:71
  114.9 9.6 %fusion.26 = f32[64,1024,1,1]{0,2,3,1:T(1,128)} fusion(f32[1024,16,1]{1,2,0:T(1,128)S(1)} %copy-done.9, f32[1024,16]{1,0:T(8,128)S(1)} %copy.31), kind=kOutput, calls=%fused_computation.34 | convolution fusion | flops 13631488 | bytes 393216 | tf_op jit(solution)/shard_map/lcm,cm->lc/dot_general | solution.py:67
  124.4 18.7 %multiply_reduce_fusion.1 = (f32[1024,16]{1,0:T(8,128)S(1)}, f32[2,1024,16]{2,0,1:T(2,128)}) fusion(f32[1024,16]{1,0:T(8,128)S(1)} %copy.31, f32[2]{0:T(128)S(1)} %iota_multiply_fusion, f32[2,64,1024]{1,0,2:T(2,128)S(1)} %copy-done.3), kind=kOutput, calls=%fused_computation.37 | convolution fusion | flops 26296320 | bytes 786440 | tf_op jit(solution)/shard_map/kjc,jcm->kcm/dot_general | solution.py:46
  143.1 17.2 %all-gather = f32[4096,16]{1,0:T(8,128)S(1)} all-gather(f32[1024,16]{1,0:T(8,128)S(1)} %get-tuple-element.256), channel_id=2, replica_groups=mesh['ctx'=4,'chan'=8] {'ctx'}, dimensions={0}, use_global_device_ids=true | all-gather | bytes 327680 | tf_op jit(solution)/shard_map/all_gather | solution.py:13
  160.9 5.9 %all-gather.1 = f32[4096,16]{0,1:T(8,128)S(1)} all-gather(f32[1024,16]{0,1:T(8,128)S(1)} %get-tuple-element.251), channel_id=3, replica_groups=mesh['ctx'=4,'chan'=8] {'ctx'}, dimensions={0}, use_global_device_ids=true | all-gather | bytes 327680 | tf_op jit(solution)/shard_map/all_gather | solution.py:13
  167.4 1.6 copy.38
  170.4 37.0 %fusion.33 = f32[1024,1,2,64]{3,1,2,0:T(1,128)S(1)} fusion(f32[64,1024,1,1]{0,2,3,1:T(1,128)} %fusion.26, f32[64,2,64,1024]{2,0,1,3:T(8,128)} %copy.46), kind=kOutput, calls=%fused_computation.61 | convolution fusion | flops 100663296 | bytes 34340864 | tf_op jit(solution)/shard_map/lkjc,lc->kjc/dot_general | solution.py:74
  207.4 12.0 %fusion.22 = f32[2,64,1024]{1,0,2:T(2,128)} fusion(f32[1024,2,64]{2,1,0:T(2,128)S(1)} %bitcast.111, f32[2,1024,16]{2,0,1:T(2,128)S(1)} %copy-done.4, f32[64]{0:T(128)S(1)} %iota_subtract_fusion, f32[1024,16]{1,0:T(8,128)S(1)} %copy-done.8, f32[1024,16]{1,0:T(8,128)S(1)} %copy-done.6), kind=kOutput, calls=%fused_computation.32 | convolution fusion | flops 27394048 | bytes 1310976 | tf_op jit(solution)/shard_map/jcm,kcm->kjc/dot_general | solution.py:63
  219.5 2.1 copy.41
  223.6 1.3 collective-permute-start
  227.0 18.4 %fusion.27 = f32[1024,16]{1,0:T(8,128)S(1)} fusion(f32[1024,16,2]{1,2,0:T(2,128)S(1)} %copy.61, f32[2,64,1024]{1,0,2:T(2,128)} %copy.42, f32[64]{0:T(128)S(1)} %iota_subtract_fusion, f32[1024,16]{1,0:T(8,128)} %copy-done.5), kind=kOutput, calls=%fused_computation.36 | convolution fusion | flops 26263552 | bytes 786688 | tf_op jit(solution)/shard_map/kjc,jcm,kcm->cm/dot_general | solution.py:64
  246.1 21.3 %multiply_reduce_fusion = f32[1024,64]{0,1:T(8,128)S(1)} fusion(f32[64,2,64,1024]{3,1,2,0:T(2,128)} %gather_fusion, f32[1024,64,2]{0,2,1:T(2,128)S(1)} %copy.69), kind=kLoop, calls=%fused_computation.7 | loop fusion | flops 16711680 | bytes 34340864
  267.6 14.1 %fusion.5 = f32[1024,1,16]{2,1,0:T(1,128)S(1)} fusion(f32[64,1024,1]{0,2,1:T(1,128)S(1)} %bitcast.113, f32[1024,16]{1,0:T(8,128)S(1)} %copy-done.7), kind=kOutput, calls=%fused_computation.13 | convolution fusion | flops 13631488 | bytes 393216 | tf_op jit(solution)/shard_map/lc,lcm->cm/dot_general | solution.py:76
  283.0 1.9 fusion.30
  285.0 7.2 %psum.15 = f32[1024]{0:T(1024)S(1)} all-reduce(f32[1024]{0:T(1024)S(1)} %get-tuple-element.243), channel_id=1, replica_groups=mesh['ctx'=4,'chan'=8] {'ctx'}, use_global_device_ids=true, to_apply=%region_7.8 | all-reduce | flops 1024 | bytes 8192 | tf_op jit(solution)/shard_map/psum | solution.py:86
  292.8 23.5 %all-reduce.3.cloned.1.call-done = f32[1024,16]{0,1:T(8,128)} async-done(((f32[1024,16]{0,1:T(8,128)}), f32[1024,16]{0,1:T(8,128)}) %all-reduce.3.cloned.1.call-update) | async-done | bytes 65552 | tf_op jit(solution)/shard_map/psum | solution.py:86
  316.2 1.5 broadcast_multiply_fusion
  317.7 68.6 %all-gather.4.cloned.1.call-done = bf16[3,128,8192]{2,1,0:T(8,128)(2,1)} async-done(((bf16[3,128,1024]{2,1,0:T(8,128)(2,1)}), bf16[3,128,8192]{2,1,0:T(8,128)(2,1)}) %all-gather.4.cloned.1.call-update) | async-done | bytes 6291472 | tf_op jit(solution)/shard_map/all_gather | solution.py:92
  386.3 24.7 %convolution_bitcast_fusion = f32[128,1024]{1,0:T(8,128)} fusion(bf16[3,128,8192]{2,1,0:T(8,128)(2,1)} %all-gather.4.cloned.1.call-done, bf16[3,1024,8192]{2,1,0:T(8,128)(2,1)} %param.19), kind=kOutput, calls=%fused_computation.35 | convolution fusion | flops 6442450944 | bytes 57147392 | tf_op jit(solution)/shard_map/ptc,pdc->td/dot_general | solution.py:93
  (69 shorter events, 11.5 us)
Async XLA Ops:
  8.0 308.2 %all-reduce.3.cloned.1.call-start = ((), (), s32[]{:S(2)}) async-start(), calls=%async_computation.1 | async-start | bytes 131072 | tf_op jit(solution)/shard_map/psum | solution.py:86
  16.4 108.0 %copy-start.5 = (f32[1024,16]{1,0:T(8,128)}, f32[1024,16]{1,0:T(8,128)S(1)}, u32[]{:S(2)}) copy-start(f32[1024,16]{1,0:T(8,128)S(1)} %copy.31) | copy-start | bytes 196612
  53.8 61.0 %copy-start.9 = (f32[1024,16,1]{1,2,0:T(1,128)S(1)}, f32[1024,16,1]{1,2,0:T(1,128)}, u32[]{:S(2)}) copy-start(f32[1024,16,1]{1,2,0:T(1,128)} %copy.43) | copy-start | bytes 196612
  53.8 70.6 %copy-start.3 = (f32[2,64,1024]{1,0,2:T(2,128)S(1)}, f32[2,64,1024]{1,0,2:T(2,128)}, u32[]{:S(2)}) copy-start(f32[2,64,1024]{1,0,2:T(2,128)} %copy.33) | copy-start | bytes 1572868
  170.3 37.0 %copy-start.4 = (f32[2,1024,16]{2,0,1:T(2,128)S(1)}, f32[2,1024,16]{2,0,1:T(2,128)}, u32[]{:S(2)}) copy-start(f32[2,1024,16]{2,0,1:T(2,128)} %copy.40) | copy-start | bytes 393220
  170.4 37.0 %copy-start.6 = (f32[1024,16]{1,0:T(8,128)S(1)}, f32[1024,16]{1,0:T(8,128)}, u32[]{:S(2)}) copy-start(f32[1024,16]{1,0:T(8,128)} %copy-done.5) | copy-start | bytes 196612
  170.4 37.1 %copy-start.8 = (f32[1024,16]{1,0:T(8,128)S(1)}, f32[1024,16]{1,0:T(8,128)}, u32[]{:S(2)}) copy-start(f32[1024,16]{1,0:T(8,128)} %copy.39) | copy-start | bytes 196612
  207.4 14.2 %copy-start = (f32[3,128,1024]{2,1,0:T(8,128)S(1)}, f32[3,128,1024]{2,1,0:T(8,128)}, u32[]{:S(2)}) copy-start(f32[3,128,1024]{2,1,0:T(8,128)} %param.12) | copy-start | bytes 4718596
  207.4 14.2 %copy-start.11 = (f32[1024]{0:T(1024)S(1)}, f32[1024]{0:T(1024)}, u32[]{:S(2)}) copy-start(f32[1024]{0:T(1024)} %param.18) | copy-start | bytes 12292
  222.9 2.1 copy-start.1
  223.6 59.2 %collective-permute-start = (f32[3,2,1024]{2,1,0:T(2,128)}, f32[3,2,1024]{2,1,0:T(2,128)S(1)}, u32[]{:S(2)}, u32[]{:S(2)}) collective-permute-start(f32[3,2,1024]{2,1,0:T(2,128)} %slice.39), channel_id=1, source_target_pairs={{8,0},{16,8},{24,16},{9,1},{17,9},{25,17},{10,2},{18,10},{26,18},{... | collective-permute-start | bytes 73736 | tf_op jit(solution)/shard_map/ppermute | solution.py:28
  246.0 21.6 %copy-start.7 = (f32[1024,16]{1,0:T(8,128)S(1)}, f32[1024,16]{1,0:T(8,128)}, u32[]{:S(2)}) copy-start(f32[1024,16]{1,0:T(8,128)} %copy-done.5) | copy-start | bytes 196612
  267.4 15.4 %copy-start.10 = (f32[3,3,1024]{2,1,0:T(4,128)S(1)}, f32[3,3,1024]{2,1,0:T(4,128)}, u32[]{:S(2)}) copy-start(f32[3,3,1024]{2,1,0:T(4,128)} %param.15) | copy-start | bytes 110596
  267.4 15.4 %copy-start.2 = (f32[1,128,1024]{2,1,0:T(8,128)S(1)}, f32[1,128,1024]{2,1,0:T(8,128)}, u32[]{:S(2)}) copy-start(f32[1,128,1024]{2,1,0:T(8,128)} %copy-done.1) | copy-start | bytes 1572868
  282.7 103.6 %all-gather.4.cloned.1.call-start = ((), (), s32[]{:S(2)}) async-start(), calls=%async_computation | async-start | bytes 7077888 | tf_op jit(solution)/shard_map/all_gather | solution.py:92
Sparse Core Ops, SparseCore 0:
  282.8 33.3 all-reduce.2
Sparse Core Ops, SparseCore 1:
  285.4 100.9 all-gather.3
where the time goes:
time: 427 us; the launch traced here: 419 us
  matrix products  135 us (32%)
  local copies, waits for them, and re-layouts  114 us (27%)
  waiting for transfers between devices  92.1 us (22%)
  other arithmetic  30.6 us (7%)
  blocking collectives  30.3 us (7%)
  between operations  16.3 us (4%)
    gather x2, local copies, waits for them, and re-layouts, shift_block(): return lax.dynamic_slice_in_dim(padded, offset, STRETCH, 1)  98.1 us
    all_gather x1, waiting for transfers between devices, body(): gathered_rows = lax.all_gather(rounded, 'chan', axis=2, tiled=True)  68.6 us
    dot_general x1, matrix products, body(): near_corr = jnp.einsum('lkjc,lc->kjc', shifted, taps, precision=highest)  37 us
    dot_general x1, matrix products, body(): jnp.einsum('ptc,pdc->td', gathered_rows, w_proj, preferred_element_type=j...  24.7 us
    psum x1, waiting for transfers between devices, body(): lax.psum((near_residue + far_residue, jnp.sum(signal * product, axis=0)),...  23.5 us
    all_gather x2, blocking collectives, carried_in(): gathered = jax.tree.map(lambda a: lax.all_gather(a, axis), part)  23.1 us
    unnamed x1, other arithmetic  21.3 us
    dot_general x1, matrix products, body(): jnp.einsum('kjc,jcm->kcm', sig_blocks, powers, precision=highest)  18.7 us
  transfers between devices with their start and end apart: 3, of which 2 were waited for; matrix products, arithmetic and copies ran while one was open for 15% of the time, Pallas kernels for 0%

commit v1 on v0

v1 whole, which is shorter than its diff:
```python
import functools

import jax
import jax.numpy as jnp
from jax import lax
from jax.experimental import pallas as pl
from jax.experimental.pallas import tpu as pltpu
from jax.sharding import PartitionSpec as P

LANES = 128
RING = 8
VMEM = 40 * 1024 * 1024
F32 = jnp.float32
BF16 = jnp.bfloat16


def whole():
    return pl.BlockSpec(memory_space=pltpu.VMEM)


def params():
    return pltpu.CompilerParams(vmem_limit_bytes=VMEM)


def cost(flops, size):
    return pl.CostEstimate(flops=flops, bytes_accessed=size, transcendentals=0)


def by_mode(ref, out, fold, fn):
    modes = ref.shape[1]
    for j in range(fold):
        block = ref[j * LANES : (j + 1) * LANES, :]
        out[pl.ds(j, modes, stride=fold), :] = fn(block.T)


def summary_kernel(feat, og, rate, out, dec, sig):
    tokens, channels = og.shape
    modes = rate.shape[1]
    fold = channels // LANES
    by_mode(rate, dec, fold, lambda r: jnp.exp(-r))
    for j in range(fold):
        lanes = slice(j * LANES, (j + 1) * LANES)
        sig[pl.ds(j, tokens, stride=fold), :] = og[:, lanes] * feat[0, :, lanes]
    decay = [dec[m * fold : (m + 1) * fold, :] for m in range(modes)]

    def step(i, states):
        row = sig[pl.ds((tokens - 1 - i) * fold, fold), :]
        return tuple(row + d * s for d, s in zip(decay, states))

    zero = tuple(jnp.zeros((fold, LANES), F32) for _ in range(modes))
    states = lax.fori_loop(0, tokens - 2, step, zero, unroll=6)
    for m in range(modes):
        out[m * fold : (m + 1) * fold, :] = states[m]
    out[modes * fold : (modes + 2) * fold, :] = sig[0 : 2 * fold, :]


def summary(features, out_grad, rate):
    tokens, channels = out_grad.shape
    modes = rate.shape[1]
    fold = channels // LANES
    return pl.pallas_call(
        summary_kernel,
        grid=(1,),
        in_specs=[
            pl.BlockSpec((1, tokens, channels), lambda i: (0, 0, 0)),
            pl.BlockSpec((tokens, channels), lambda i: (0, 0)),
            pl.BlockSpec((channels, modes), lambda i: (0, 0)),
        ],
        out_specs=pl.BlockSpec(((modes + 2) * fold, LANES), lambda i: (0, 0)),
        out_shape=jax.ShapeDtypeStruct(((modes + 2) * fold, LANES), F32),
        scratch_shapes=[
            pltpu.VMEM((modes * fold, LANES), F32),
            pltpu.VMEM((tokens * fold, LANES), F32),
        ],
        compiler_params=params(),
        cost_estimate=cost(4 * tokens * channels * modes, 12 * tokens * channels),
        name="summary",
    )(features, out_grad, rate)


def tapped(ext, taps, lanes, tokens):
    total = taps[0][:, lanes] * ext[0:tokens, lanes]
    total = total + taps[1][:, lanes] * ext[1 : tokens + 1, lanes]
    return total + taps[2][:, lanes] * ext[2 : tokens + 2, lanes]


def gate_kernel(feat, conv, og, filt, bias, halo, out, rounded, ext):
    tokens, channels = og.shape
    taps = [filt[0, j : j + 1, :] for j in range(3)]
    ext[tokens : tokens + 2, :] = halo[8:10] * (halo[6:8] + bias[...] * (halo[2:4] * halo[4:6]))
    for j in range(channels // LANES):
        lanes = slice(j * LANES, (j + 1) * LANES)
        product = feat[1, :, lanes] * feat[2, :, lanes]
        ext[0:tokens, lanes] = og[:, lanes] * (conv[:, lanes] + bias[:, lanes] * product)
        total = tapped(ext, taps, lanes, tokens)
        out[:, lanes] = total
        rounded[:, lanes] = total.astype(BF16)


def gate_stream(features, saved_conv, out_grad, short_filter, bias_row, halo):
    tokens, channels = out_grad.shape
    return pl.pallas_call(
        gate_kernel,
        in_specs=[whole()] * 6,
        out_specs=[whole()] * 2,
        out_shape=[
            jax.ShapeDtypeStruct((tokens, channels), F32),
            jax.ShapeDtypeStruct((tokens, channels), BF16),
        ],
        scratch_shapes=[pltpu.VMEM((tokens + 8, channels), F32)],
        compiler_params=params(),
        cost_estimate=cost(12 * tokens * channels, 26 * tokens * channels),
        name="gate_stream",
    )(features, saved_conv, out_grad, short_filter, bias_row, halo)


def state_kernel(later, feat, og, filt, rate, residue, bias, bias_row, halo, *refs):
    payloads = refs[:later]
    out, rounded, sums, dec, res, far, sig, prod, gp, first, second = refs[later:]
    tokens, channels = og.shape
    modes = rate.shape[1]
    fold = channels // LANES
    by_mode(rate, dec, fold, lambda r: jnp.exp(-r))
    by_mode(rate, far, fold, lambda r: jnp.exp(-(tokens - 2) * r))
    by_mode(residue, res, fold, lambda r: r)
    for j in range(fold):
        lanes = slice(j * LANES, (j + 1) * LANES)
        s = og[:, lanes] * feat[0, :, lanes]
        p = feat[1, :, lanes] * feat[2, :, lanes]
        sig[pl.ds(j, tokens, stride=fold), :] = s
        prod[pl.ds(j, tokens, stride=fold), :] = p
        sums[modes * fold + j : modes * fold + j + 1, :] = jnp.sum(s * p, axis=0, keepdims=True)

    def rows(ref, at):
        return ref[at * fold : (at + 1) * fold, :]

    direct = bias[...]
    group = 8
    for low in range(0, modes, group):
        chosen = range(low, min(low + group, modes))
        decay = [rows(dec, m) for m in chosen]
        weight = [rows(res, m) for m in chosen]
        reach = [rows(far, m) for m in chosen]
        state = [jnp.zeros((fold, LANES), F32) for _ in chosen]
        for n, payload in enumerate(reversed(payloads)):
            block_end = [rows(payload, m) + f * s for m, f, s in zip(chosen, reach, state)]
            if n < later - 1:
                s0, s1 = rows(payload, modes), rows(payload, modes + 1)
                state = [s0 + d * (s1 + d * s) for d, s in zip(decay, block_end)]
            else:
                state = block_end

        def corr(state, weight=weight):
            terms = [w * s for w, s in zip(weight, state)]
            while len(terms) > 1:
                terms = [a + b for a, b in zip(terms[::2], terms[1::2])] + terms[len(terms) // 2 * 2 :]
            return terms[0]

        def put(at, row, state, low=low):
            here = pl.ds(at * fold, fold)
            if low == 0:
                gp[here, :] = corr(state) + direct * row
            else:
                gp[here, :] = gp[here, :] + corr(state)

        for n in (1, 0):
            row = rows(payloads[0], modes + n)
            state = [row + d * s for d, s in zip(decay, state)]
            put(tokens + n, row, state)

        def step(i, carry, decay=decay, put=put):
            state, total = carry
            at = tokens - 1 - i
            row = sig[pl.ds(at * fold, fold), :]
            other = prod[pl.ds(at * fold, fold), :]
            state = [row + d * s for d, s in zip(decay, state)]
            total = [a + other * s for a, s in zip(total, state)]
            put(at, row, state)
            return state, total

        zero = [jnp.zeros((fold, LANES), F32) for _ in chosen]
        state, total = lax.fori_loop(0, tokens, step, (state, zero), unroll=4)
        for m, a in zip(chosen, total):
            sums[m * fold : (m + 1) * fold, :] = a

    taps = [[filt[p, j : j + 1, :] for j in range(3)] for p in range(3)]
    for j in range(fold):
        lanes = slice(j * LANES, (j + 1) * LANES)
        g = gp[pl.ds(j, tokens, stride=fold), :]
        rim = gp[pl.ds(tokens * fold + j, 2, stride=fold), :]
        first[0:tokens, lanes] = g * feat[2, :, lanes]
        first[tokens : tokens + 2, lanes] = rim * halo[4:6, lanes]
        second[0:tokens, lanes] = g * feat[1, :, lanes]
        second[tokens : tokens + 2, lanes] = rim * halo[2:4, lanes]
        for p, ext in ((1, first), (2, second)):
            total = tapped(ext, taps[p], lanes, tokens)
            out[p - 1, :, lanes] = total
            rounded[p - 1, :, lanes] = total.astype(BF16)


def state_streams(features, out_grad, short_filter, rate, residue, bias, bias_row, halo, payloads):
    tokens, channels = out_grad.shape
    modes = rate.shape[1]
    fold = channels // LANES
    return pl.pallas_call(
        functools.partial(state_kernel, len(payloads)),
        in_specs=[whole()] * (8 + len(payloads)),
        out_specs=[whole()] * 3,
        out_shape=[
            jax.ShapeDtypeStruct((2, tokens, channels), F32),
            jax.ShapeDtypeStruct((2, tokens, channels), BF16),
            jax.ShapeDtypeStruct(((modes + 1) * fold, LANES), F32),
        ],
        scratch_shapes=[pltpu.VMEM((modes * fold, LANES), F32)] * 3
        + [pltpu.VMEM((tokens * fold, LANES), F32)] * 2
        + [pltpu.VMEM(((tokens + 2) * fold, LANES), F32)]
        + [pltpu.VMEM((tokens + 8, channels), F32)] * 2,
        compiler_params=params(),
        cost_estimate=cost(8 * tokens * channels * modes, 40 * tokens * channels),
        name="state_streams",
    )(features, out_grad, short_filter, rate, residue, bias, bias_row, halo, *payloads)


def product_kernel(count, heights, split, source, *refs):
    xs = refs[:count]
    w, before, out = refs[count : count + 3]
    k = pl.program_id(1)

    @pl.when(k == 0)
    def _():
        out[...] = before[...]

    def add(x, rows):
        out[rows, :] += lax.dot_general(
            x, w[0], (((1,), (1,)), ((), ())), preferred_element_type=F32
        )

    if split:
        half = xs[0].shape[1]
        for n, x in enumerate(xs):
            for h in range(heights):

                @pl.when(k == h)
                def _(n=n, x=x, h=h):
                    add(x[h], slice(n * half, (n + 1) * half))

    else:
        for n, x in enumerate(xs):
            for h in range(heights):

                @pl.when(k == n * heights + h)
                def _(x=x, h=h):
                    add(x[h], slice(None))


def add_product(total, chunks, offsets, sources, w_proj, stream, split=False):
    tokens, features = total.shape
    heights, _, channels = chunks[0].shape
    steps = heights * (1 if split else len(chunks))
    wide = min(512, features)

    def w_index(i, k, source):
        lo = source[offsets[0]]
        for n in range(1, len(offsets)):
            lo = jnp.where(k >= n * heights, source[offsets[n]], lo)
        return stream, i, lax.rem(k, heights) * RING + lo

    return pl.pallas_call(
        functools.partial(product_kernel, len(chunks), heights, split),
        grid_spec=pltpu.PrefetchScalarGridSpec(
            num_scalar_prefetch=1,
            grid=(features // wide, steps),
            in_specs=[pl.BlockSpec(c.shape, lambda i, k, s: (0, 0, 0)) for c in chunks]
            + [
                pl.BlockSpec((1, wide, channels), w_index),
                pl.BlockSpec((tokens, wide), lambda i, k, s: (0, i)),
            ],
            out_specs=pl.BlockSpec((tokens, wide), lambda i, k, s: (0, i)),
        ),
        out_shape=jax.ShapeDtypeStruct(total.shape, F32),
        input_output_aliases={len(chunks) + 2: 0},
        compiler_params=params(),
        cost_estimate=cost(
            2 * tokens * features * channels * steps, 2 * features * channels * steps + 8 * tokens * features
        ),
        name="add_product",
    )(sources, *chunks, w_proj, total)


def ring_order(size):
    return list(range(0, size, 2)) + list(range(size - 1 - size % 2, 0, -2))


def gathered_product(total, block, sources, w_proj, stream, ring, heights):
    order = ring_order(ring)
    pairs = {
        by: [
            (h * ring + order[i], h * ring + order[(i + by) % ring])
            for h in range(heights)
            for i in range(ring)
        ]
        for by in (1, -1)
    }

    def send(x, by):
        return lax.ppermute(x, "chan", pairs[by])

    if heights > 1:
        groups = [[h * ring + i for h in range(heights)] for i in range(ring)]
        block = lax.all_gather(block, "chan", axis_index_groups=groups)
    else:
        block = block[None]
    up = down = block
    for hop in range(1, ring // 2):
        up, down = send(up, 1), send(down, -1)
        chunks = [up, down]
        offsets = [ring - hop, hop]
        if hop == 1:
            chunks, offsets = [block] + chunks, [0] + offsets
        total = add_product(total, chunks, offsets, sources, w_proj, stream)
    half = block.shape[1] // 2
    last = [send(up[:, :half], 1), send(down[:, half:], -1)]
    return add_product(total, last, [ring // 2], sources, w_proj, stream, split=True)


def body(features, saved_conv, out_grad, short_filter, residue, rate, bias, w_proj):
    tokens, channels = out_grad.shape
    modes = rate.shape[1]
    fold = channels // LANES
    blocks = lax.axis_size("ctx")
    groups = lax.axis_size("chan")
    ring = min(groups, RING)
    bias_row = bias[None]

    order = ring_order(ring)
    place = [order.index(i) for i in range(ring)]
    table = jnp.array([[order[(place[i] + d) % ring] for d in range(ring)] for i in range(ring)], jnp.int32)
    sources = lax.dynamic_index_in_dim(table, lax.rem(lax.axis_index("chan"), ring), 0, False)

    def from_later(array, by):
        return lax.ppermute(array, "ctx", [(i, i - by) for i in range(by, blocks)])

    rim = jnp.concatenate([features[:, 0:2].reshape(6, channels), saved_conv[0:2], out_grad[0:2]])
    halo = from_later(rim, 1)
    own = summary(features, out_grad, rate)
    payloads = [from_later(own, by) for by in range(1, blocks)]
    gate_grad, gate_round = gate_stream(features, saved_conv, out_grad, short_filter, bias_row, halo)
    grads, rounds, sums = state_streams(
        features, out_grad, short_filter, rate, residue, bias.reshape(fold, LANES), bias_row, halo, payloads
    )
    total = jnp.zeros((tokens, w_proj.shape[1]), F32)
    for stream, block in enumerate((gate_round, rounds[0], rounds[1])):
        total = gathered_product(total, block, sources, w_proj, stream, ring, groups // ring)

    by = 1
    while by < blocks:
        sums = sums + lax.ppermute(sums, "ctx", [(i, i ^ by) for i in range(blocks)])
        by *= 2
    sums = sums * (tokens * blocks) ** (-0.5)
    grad_residue = sums[: modes * fold].reshape(modes, channels).T
    grad_bias = sums[modes * fold :].reshape(channels)
    grad_inputs = jnp.concatenate([gate_grad[None], grads])
    return (grad_inputs, total, grad_residue, grad_bias)


def solution(mesh):
    return jax.shard_map(
        body,
        mesh=mesh,
        in_specs=(
            P(None, "ctx", "chan"),
            P("ctx", "chan"),
            P("ctx", "chan"),
            P(None, None, "chan"),
            P("chan", None),
            P("chan", None),
            P("chan"),
            P(None, "chan", None),
        ),
        out_specs=(P(None, "ctx", "chan"), P("ctx", "chan"), P("chan", None), P("chan")),
        check_vma=False,
    )
```

time: 427 us -> 145 us (0.34); the launches traced: 419 us -> 144 us
  matrix products: 135 us -> 0 us
  local copies, waits for them, and re-layouts: 114 us -> 8.46 us
  Pallas kernels: 0 us -> 74 us
  waiting for transfers between devices: 92.1 us -> 24.5 us
  starting transfers between devices: 1.36 us -> 33.6 us
  blocking collectives: 30.3 us -> 0 us
  other arithmetic: 30.6 us -> 2.56 us
  between operations: 16.3 us -> 0.95 us
    dot_general x7 -> x0, matrix products: 135 us -> none  [the longest x1 37 us: body(): near_corr = jnp.einsum('lkjc,lc->kjc', shifted, taps, precision=highest)]
    gather x2 -> x0, local copies, waits for them, and re-layouts: 98.1 us -> none  [shift_block(): return lax.dynamic_slice_in_dim(padded, offset, STRETCH, 1)]
    pallas_call x0 -> x15, Pallas kernels: none -> 74 us  [the longest x12 67.6 us: add_product(): pl.pallas_call(functools.partial(product_kernel, len(chunks), heights, sp...]
    all_gather x1 -> x0, waiting for transfers between devices: 68.6 us -> none  [body(): gathered_rows = lax.all_gather(rounded, 'chan', axis=2, tiled=True)]
    ppermute x1 -> x30, starting transfers between devices: 1.28 us -> 33.6 us  [the longest x24 24.7 us: send(): return lax.ppermute(x, 'chan', pairs[by])]
    ppermute x1 -> x30, waiting for transfers between devices: 0.01 us -> 24.5 us  [the longest x24 17.9 us: send(): return lax.ppermute(x, 'chan', pairs[by])]
    psum x1 -> x0, waiting for transfers between devices: 23.5 us -> none  [body(): lax.psum((near_residue + far_residue, jnp.sum(signal * product, axis=0)),...]
    all_gather x2 -> x0, blocking collectives: 23.1 us -> none  [carried_in(): gathered = jax.tree.map(lambda a: lax.all_gather(a, axis), part)]
  transfers between devices with their start and end apart: 3 -> 30, of which waited for: 2 -> 13; matrix products, arithmetic and copies ran while one was open for 15% -> 4% of each run, Pallas kernels for 0% -> 48%
where the time goes in v1:
time: 145 us; the launch traced here: 144 us
  Pallas kernels  74 us (51%)
  starting transfers between devices  33.6 us (23%)
  waiting for transfers between devices  24.5 us (17%)
  local copies, waits for them, and re-layouts  8.46 us (6%)
  other arithmetic  2.56 us (2%)
    pallas_call x12, Pallas kernels, add_product(): pl.pallas_call(functools.partial(product_kernel, len(chunks), heights, sp...  67.6 us
    ppermute x24, starting transfers between devices, send(): return lax.ppermute(x, 'chan', pairs[by])  24.7 us
    ppermute x24, waiting for transfers between devices, send(): return lax.ppermute(x, 'chan', pairs[by])  17.9 us
    unnamed x24, local copies, waits for them, and re-layouts  5.54 us
    ppermute x4, starting transfers between devices, from_later(): return lax.ppermute(array, 'ctx', [(i, i - by) for i in range(by, blocks)])  5.16 us
    pallas_call x1, Pallas kernels, state_streams(): pl.pallas_call(functools.partial(state_kernel, len(payloads)), in_specs=[...  4.48 us
    ppermute x2, waiting for transfers between devices, body(): lax.ppermute(sums, 'ctx', [(i, i ^ by) for i in range(blocks)])  4.3 us
    ppermute x2, starting transfers between devices, body(): lax.ppermute(sums, 'ctx', [(i, i ^ by) for i in range(blocks)])  3.7 us
  transfers between devices with their start and end apart: 30, of which 13 were waited for; matrix products, arithmetic and copies ran while one was open for 4% of the time, Pallas kernels for 48%

profile of v1, /device:TPU:0, one launch (start us, length us, event | category | flops | bytes accessed | tf_op | source)
XLA Modules:
  0.0 144.0 jit_solution(17757688779423145331)
XLA Ops:
  11.2 2.3 %collective-permute-done.halo = f32[10,1024]{1,0:T(8,128)S(1)} collective-permute-done((f32[10,1024]{1,0:T(8,128)S(1)}, f32[10,1024]{1,0:T(8,128)S(1)}, u32[]{:S(2)}, u32[]{:S(2)}) %collective-permute-start) | collective-permute-done | bytes 40992 | tf_op jit(solution)/shard_map/ppermute | solution.py:341
  15.7 3.0 %collective-permute-start.20 = (bf16[1,128,1024]{2,1,0:T(8,128)(2,1)S(1)}, bf16[1,128,1024]{2,1,0:T(8,128)(2,1)}, u32[]{:S(2)}, u32[]{:S(2)}) collective-permute-start(bf16[1,128,1024]{2,1,0:T(8,128)(2,1)S(1)} %bitcast.10), channel_id=1, source_target_pairs={{0,2},{2,4},{4,6},{6,7},{7,5},{5,3},{3,1},{1,0},{8,10},{10,12},{12... | collective-permute-start | bytes 786440 | tf_op jit(solution)/shard_map/ppermute | solution.py:306
  18.8 4.5 %state_streams.1 = (f32[2,128,1024]{2,1,0:T(8,128)S(1)}, bf16[2,128,1024]{2,1,0:T(8,128)(2,1)S(1)}, f32[136,128]{1,0:T(8,128)S(1)}) custom-call(f32[3,128,1024]{2,1,0:T(8,128)S(1)} %copy-done.1, f32[128,1024]{1,0:T(8,128)S(1)} %copy-done.3, f32[3,3,1024]{2,1,0:T(4,128)S(1)} %copy-done.8, f32[1024,16]{1,0:T(8,128)S(1)} %copy.29.rate, ...), custom_call_target="tpu_custom_call" | custom-call | flops 16777216 | bytes 5242880 | tf_op jit(solution)/shard_map/state_streams/pallas_call | solution.py:205
  23.3 2.1 %collective-permute-start.12 = (bf16[1,128,1024]{2,1,0:T(8,128)(2,1)S(1)}, bf16[1,128,1024]{2,1,0:T(8,128)(2,1)S(1)}, u32[]{:S(2)}, u32[]{:S(2)}) collective-permute-start(bf16[1,128,1024]{2,1,0:T(8,128)(2,1)S(1)} %get-tuple-element.14.refs_0_), channel_id=1, source_target_pairs={{0,2},{2,4},{4,6},{6,7},{7,5},{5,3},{3,1},{1,0},{8,10},{10,12},{12... | collective-permute-start | bytes 786440 | tf_op jit(solution)/shard_map/ppermute | solution.py:306
  25.4 2.6 %collective-permute-start.28 = (f32[136,128]{1,0:T(8,128)S(1)}, f32[136,128]{1,0:T(8,128)S(1)}, u32[]{:S(2)}, u32[]{:S(2)}) collective-permute-start(f32[136,128]{1,0:T(8,128)S(1)} %get-tuple-element.13), channel_id=1, source_target_pairs={{0,8},{8,0},{16,24},{24,16},{1,9},{9,1},{17,25},{25,17},{2,10},{10... | collective-permute-start | bytes 208904 | tf_op jit(solution)/shard_map/ppermute | solution.py:357
  30.0 3.4 %collective-permute-done.29 = f32[136,128]{1,0:T(8,128)S(1)} collective-permute-done((f32[136,128]{1,0:T(8,128)S(1)}, f32[136,128]{1,0:T(8,128)S(1)}, u32[]{:S(2)}, u32[]{:S(2)}) %collective-permute-start.29) | collective-permute-done | bytes 69664 | tf_op jit(solution)/shard_map/ppermute | solution.py:357
  40.8 1.9 %collective-permute-done.4.refs_1_ = bf16[1,128,1024]{2,1,0:T(8,128)(2,1)S(1)} collective-permute-done((bf16[1,128,1024]{2,1,0:T(8,128)(2,1)S(1)}, bf16[1,128,1024]{2,1,0:T(8,128)(2,1)S(1)}, u32[]{:S(2)}, u32[]{:S(2)}) %collective-permute-start.4) | collective-permute-done | bytes 262176 | tf_op jit(solution)/shard_map/ppermute | solution.py:306
  46.4 2.0 %collective-permute-done.21.refs_0_ = bf16[1,128,1024]{2,1,0:T(8,128)(2,1)} collective-permute-done((bf16[1,128,1024]{2,1,0:T(8,128)(2,1)}, bf16[1,128,1024]{2,1,0:T(8,128)(2,1)}, u32[]{:S(2)}, u32[]{:S(2)}) %collective-permute-start.21) | collective-permute-done | bytes 262176 | tf_op jit(solution)/shard_map/ppermute | solution.py:306
  48.7 1.9 %collective-permute-done.25.refs_1_ = bf16[1,128,1024]{2,1,0:T(8,128)(2,1)} collective-permute-done((bf16[1,128,1024]{2,1,0:T(8,128)(2,1)}, bf16[1,128,1024]{2,1,0:T(8,128)(2,1)}, u32[]{:S(2)}, u32[]{:S(2)}) %collective-permute-start.25) | collective-permute-done | bytes 262176 | tf_op jit(solution)/shard_map/ppermute | solution.py:306
  52.1 2.5 %pad_maximum_fusion = f32[3,128,1024]{2,1,0:T(8,128)} fusion(f32[2,128,1024]{2,1,0:T(8,128)} %copy-done.4, f32[1,128,1024]{2,1,0:T(8,128)S(1)} %bitcast.9), kind=kLoop, calls=%fused_computation | loop fusion | flops 393216 | bytes 3145728 | tf_op jit(solution)/shard_map/concatenate | solution.py:362
  59.9 1.9 %collective-permute-done.9.refs_1_ = bf16[1,128,1024]{2,1,0:T(8,128)(2,1)} collective-permute-done((bf16[1,128,1024]{2,1,0:T(8,128)(2,1)S(1)}, bf16[1,128,1024]{2,1,0:T(8,128)(2,1)}, u32[]{:S(2)}, u32[]{:S(2)}) %collective-permute-start.9) | collective-permute-done | bytes 262176 | tf_op jit(solution)/shard_map/ppermute | solution.py:306
  61.8 3.3 %collective-permute-done.22.refs_0_ = bf16[1,128,1024]{2,1,0:T(8,128)(2,1)S(1)} collective-permute-done((bf16[1,128,1024]{2,1,0:T(8,128)(2,1)}, bf16[1,128,1024]{2,1,0:T(8,128)(2,1)S(1)}, u32[]{:S(2)}, u32[]{:S(2)}) %collective-permute-start.22) | collective-permute-done | bytes 262176 | tf_op jit(solution)/shard_map/ppermute | solution.py:306
  71.9 7.5 %add_product.12.refs_3_ = f32[128,1024]{1,0:T(8,128)} custom-call(s32[8]{0:T(128)S(1)} %dynamic-slice_bitcast_fusion.source, bf16[1,128,1024]{2,1,0:T(8,128)(2,1)S(1)} %bitcast.12, bf16[1,128,1024]{2,1,0:T(8,128)(2,1)} %collective-permute-done.20.refs_1_, bf16[1,128,1024]{2,1,0:T(8,128)(2,1)} %collective-permute-done.24.refs_2_, ...), custom_call_target="tpu_custom_call", output_to_operand_aliasing={{}: (5, {})} | custom-call | flops 805306368 | bytes 7340032 | tf_op jit(solution)/shard_map/add_product/pallas_call | solution.py:268
  79.4 5.7 %add_product.13.refs_3_ = f32[128,1024]{1,0:T(8,128)} custom-call(s32[8]{0:T(128)S(1)} %dynamic-slice_bitcast_fusion.source, bf16[1,128,1024]{2,1,0:T(8,128)(2,1)} %collective-permute-done.21.refs_0_, bf16[1,128,1024]{2,1,0:T(8,128)(2,1)} %collective-permute-done.25.refs_1_, bf16[3,1024,8192]{2,1,0:T(8,128)(2,1)} %refs_2_.17, ...), custom_call_target="tpu_custom_call", output_to_operand_aliasing={{}: (4, {})} | custom-call | flops 536870912 | bytes 5242880 | tf_op jit(solution)/shard_map/add_product/pallas_call | solution.py:268
  85.0 5.5 %add_product.14.refs_3_ = f32[128,1024]{1,0:T(8,128)} custom-call(s32[8]{0:T(128)S(1)} %dynamic-slice_bitcast_fusion.source, bf16[1,128,1024]{2,1,0:T(8,128)(2,1)S(1)} %collective-permute-done.22.refs_0_, bf16[1,128,1024]{2,1,0:T(8,128)(2,1)S(1)} %collective-permute-done.26.refs_1_, bf16[3,1024,8192]{2,1,0:T(8,128)(2,1)} %refs_2_.17, ...), custom_call_target="tpu_custom_call", output_to_operand_aliasing={{}: (4, {})} | custom-call | flops 536870912 | bytes 5242880 | tf_op jit(solution)/shard_map/add_product/pallas_call | solution.py:268
  95.0 4.1 %add_product.15.refs_4_ = f32[128,1024]{1,0:T(8,128)} custom-call(s32[8]{0:T(128)S(1)} %dynamic-slice_bitcast_fusion.source, bf16[1,64,1024]{2,1,0:T(8,128)(2,1)S(1)} %collective-permute-done.23.refs_0_, bf16[1,64,1024]{2,1,0:T(8,128)(2,1)S(1)} %collective-permute-done.27.refs_1_, bf16[3,1024,8192]{2,1,0:T(8,128)(2,1)} %refs_2_.17, ...), custom_call_target="tpu_custom_call", output_to_operand_aliasing={{}: (4, {})} | custom-call | flops 268435456 | bytes 3145728 | tf_op jit(solution)/shard_map/add_product/pallas_call | solution.py:268
  99.1 7.2 %add_product.16.refs_3_ = f32[128,1024]{1,0:T(8,128)} custom-call(s32[8]{0:T(128)S(1)} %dynamic-slice_bitcast_fusion.source, bf16[1,128,1024]{2,1,0:T(8,128)(2,1)S(1)} %get-tuple-element.14.refs_0_, bf16[1,128,1024]{2,1,0:T(8,128)(2,1)S(1)} %collective-permute-done.12.refs_1_, ...), custom_call_target="tpu_custom_call", output_to_operand_aliasing={{}: (5, {})} | custom-call | flops 805306368 | bytes 7340032 | tf_op jit(solution)/shard_map/add_product/pallas_call | solution.py:268
  106.3 5.7 %add_product.17.refs_3_ = f32[128,1024]{1,0:T(8,128)} custom-call(s32[8]{0:T(128)S(1)} %dynamic-slice_bitcast_fusion.source, bf16[1,128,1024]{2,1,0:T(8,128)(2,1)} %collective-permute-done.13.refs_0_, bf16[1,128,1024]{2,1,0:T(8,128)(2,1)} %collective-permute-done.17.refs_1_, bf16[3,1024,8192]{2,1,0:T(8,128)(2,1)} %refs_2_.17, ...), custom_call_target="tpu_custom_call", output_to_operand_aliasing={{}: (4, {})} | custom-call | flops 536870912 | bytes 5242880 | tf_op jit(solution)/shard_map/add_product/pallas_call | solution.py:268
  112.0 5.5 %add_product.18.refs_3_ = f32[128,1024]{1,0:T(8,128)} custom-call(s32[8]{0:T(128)S(1)} %dynamic-slice_bitcast_fusion.source, bf16[1,128,1024]{2,1,0:T(8,128)(2,1)S(1)} %collective-permute-done.14.refs_0_, bf16[1,128,1024]{2,1,0:T(8,128)(2,1)S(1)} %collective-permute-done.18.refs_1_, bf16[3,1024,8192]{2,1,0:T(8,128)(2,1)} %refs_2_.17, ...), custom_call_target="tpu_custom_call", output_to_operand_aliasing={{}: (4, {})} | custom-call | flops 536870912 | bytes 5242880 | tf_op jit(solution)/shard_map/add_product/pallas_call | solution.py:268
  117.5 4.1 %add_product.19.refs_4_ = f32[128,1024]{1,0:T(8,128)} custom-call(s32[8]{0:T(128)S(1)} %dynamic-slice_bitcast_fusion.source, bf16[1,64,1024]{2,1,0:T(8,128)(2,1)S(1)} %collective-permute-done.15.refs_0_, bf16[1,64,1024]{2,1,0:T(8,128)(2,1)S(1)} %collective-permute-done.19.refs_1_, bf16[3,1024,8192]{2,1,0:T(8,128)(2,1)} %refs_2_.17, ...), custom_call_target="tpu_custom_call", output_to_operand_aliasing={{}: (4, {})} | custom-call | flops 268435456 | bytes 3145728 | tf_op jit(solution)/shard_map/add_product/pallas_call | solution.py:268
  121.6 7.3 %add_product.20.refs_3_ = f32[128,1024]{1,0:T(8,128)} custom-call(s32[8]{0:T(128)S(1)} %dynamic-slice_bitcast_fusion.source, bf16[1,128,1024]{2,1,0:T(8,128)(2,1)S(1)} %get-tuple-element.15.refs_0_, bf16[1,128,1024]{2,1,0:T(8,128)(2,1)S(1)} %collective-permute-done.4.refs_1_, ...), custom_call_target="tpu_custom_call", output_to_operand_aliasing={{}: (5, {})} | custom-call | flops 805306368 | bytes 7340032 | tf_op jit(solution)/shard_map/add_product/pallas_call | solution.py:268
  128.8 5.7 %add_product.21.refs_3_ = f32[128,1024]{1,0:T(8,128)} custom-call(s32[8]{0:T(128)S(1)} %dynamic-slice_bitcast_fusion.source, bf16[1,128,1024]{2,1,0:T(8,128)(2,1)} %collective-permute-done.5.refs_0_, bf16[1,128,1024]{2,1,0:T(8,128)(2,1)} %collective-permute-done.9.refs_1_, bf16[3,1024,8192]{2,1,0:T(8,128)(2,1)} %refs_2_.17, ...), custom_call_target="tpu_custom_call", output_to_operand_aliasing={{}: (4, {})} | custom-call | flops 536870912 | bytes 5242880 | tf_op jit(solution)/shard_map/add_product/pallas_call | solution.py:268
  134.5 5.5 %add_product.22.refs_3_ = f32[128,1024]{1,0:T(8,128)} custom-call(s32[8]{0:T(128)S(1)} %dynamic-slice_bitcast_fusion.source, bf16[1,128,1024]{2,1,0:T(8,128)(2,1)S(1)} %collective-permute-done.6.refs_0_, bf16[1,128,1024]{2,1,0:T(8,128)(2,1)S(1)} %collective-permute-done.10.refs_1_, bf16[3,1024,8192]{2,1,0:T(8,128)(2,1)} %refs_2_.17, ...), custom_call_target="tpu_custom_call", output_to_operand_aliasing={{}: (4, {})} | custom-call | flops 536870912 | bytes 5242880 | tf_op jit(solution)/shard_map/add_product/pallas_call | solution.py:268
  140.0 4.1 %add_product.23 = f32[128,1024]{1,0:T(8,128)} custom-call(s32[8]{0:T(128)S(1)} %dynamic-slice_bitcast_fusion.source, bf16[1,64,1024]{2,1,0:T(8,128)(2,1)S(1)} %collective-permute-done.7.refs_0_, bf16[1,64,1024]{2,1,0:T(8,128)(2,1)S(1)} %collective-permute-done.11.refs_1_, bf16[3,1024,8192]{2,1,0:T(8,128)(2,1)} %refs_2_.17, ...), custom_call_target="tpu_custom_call", output_to_operand_aliasing={{}: (4, {})} | custom-call | flops 268435456 | bytes 3145728 | tf_op jit(solution)/shard_map/add_product/pallas_call | solution.py:268
  (97 shorter events, 44.2 us)
Async XLA Ops:
  5.7 13.1 %collective-permute-start.1 = (f32[144,128]{1,0:T(8,128)}, f32[144,128]{1,0:T(8,128)}, u32[]{:S(2)}, u32[]{:S(2)}) collective-permute-start(f32[144,128]{1,0:T(8,128)} %summary.1), channel_id=1, source_target_pairs={{8,0},{16,8},{24,16},{9,1},{17,9},{25,17},{10,2},{18,10},{26,18},{... | collective-permute-start | bytes 221192 | tf_op jit(solution)/shard_map/ppermute | solution.py:341
  7.0 11.8 %collective-permute-start.2 = (f32[144,128]{1,0:T(8,128)}, f32[144,128]{1,0:T(8,128)}, u32[]{:S(2)}, u32[]{:S(2)}) collective-permute-start(f32[144,128]{1,0:T(8,128)} %summary.1), channel_id=1, source_target_pairs={{16,0},{24,8},{17,1},{25,9},{18,2},{26,10},{19,3},{27,11},{20,4},{... | collective-permute-start | bytes 221192 | tf_op jit(solution)/shard_map/ppermute | solution.py:341
  8.3 10.5 %collective-permute-start.3 = (f32[144,128]{1,0:T(8,128)}, f32[144,128]{1,0:T(8,128)}, u32[]{:S(2)}, u32[]{:S(2)}) collective-permute-start(f32[144,128]{1,0:T(8,128)} %summary.1), channel_id=1, source_target_pairs={{24,0},{25,1},{26,2},{27,3},{28,4},{29,5},{30,6},{31,7}} | collective-permute-start | bytes 221192 | tf_op jit(solution)/shard_map/ppermute | solution.py:341
  15.7 19.3 %collective-permute-start.20 = (bf16[1,128,1024]{2,1,0:T(8,128)(2,1)S(1)}, bf16[1,128,1024]{2,1,0:T(8,128)(2,1)}, u32[]{:S(2)}, u32[]{:S(2)}) collective-permute-start(bf16[1,128,1024]{2,1,0:T(8,128)(2,1)S(1)} %bitcast.10), channel_id=1, source_target_pairs={{0,2},{2,4},{4,6},{6,7},{7,5},{5,3},{3,1},{1,0},{8,10},{10,12},{12... | collective-permute-start | bytes 786440 | tf_op jit(solution)/shard_map/ppermute | solution.py:306
  18.8 16.7 %collective-permute-start.24 = (bf16[1,128,1024]{2,1,0:T(8,128)(2,1)S(1)}, bf16[1,128,1024]{2,1,0:T(8,128)(2,1)}, u32[]{:S(2)}, u32[]{:S(2)}) collective-permute-start(bf16[1,128,1024]{2,1,0:T(8,128)(2,1)S(1)} %bitcast.11), channel_id=1, source_target_pairs={{0,1},{2,0},{4,2},{6,4},{7,6},{5,7},{3,5},{1,3},{8,9},{10,8},{12,1... | collective-permute-start | bytes 786440 | tf_op jit(solution)/shard_map/ppermute | solution.py:306
  23.3 13.7 %collective-permute-start.12 = (bf16[1,128,1024]{2,1,0:T(8,128)(2,1)S(1)}, bf16[1,128,1024]{2,1,0:T(8,128)(2,1)S(1)}, u32[]{:S(2)}, u32[]{:S(2)}) collective-permute-start(bf16[1,128,1024]{2,1,0:T(8,128)(2,1)S(1)} %get-tuple-element.14.refs_0_), channel_id=1, source_target_pairs={{0,2},{2,4},{4,6},{6,7},{7,5},{5,3},{3,1},{1,0},{8,10},{10,12},{12... | collective-permute-start | bytes 786440 | tf_op jit(solution)/shard_map/ppermute | solution.py:306
  35.5 12.9 %collective-permute-start.21 = (bf16[1,128,1024]{2,1,0:T(8,128)(2,1)}, bf16[1,128,1024]{2,1,0:T(8,128)(2,1)}, u32[]{:S(2)}, u32[]{:S(2)}) collective-permute-start(bf16[1,128,1024]{2,1,0:T(8,128)(2,1)} %collective-permute-done.20.refs_1_), channel_id=1, source_target_pairs={{0,2},{2,4},{4,6},{6,7},{7,5},{5,3},{3,1},{1,0},{8,10},{10,12},{12... | collective-permute-start | bytes 786440 | tf_op jit(solution)/shard_map/ppermute | solution.py:306
  37.0 13.5 %collective-permute-start.25 = (bf16[1,128,1024]{2,1,0:T(8,128)(2,1)}, bf16[1,128,1024]{2,1,0:T(8,128)(2,1)}, u32[]{:S(2)}, u32[]{:S(2)}) collective-permute-start(bf16[1,128,1024]{2,1,0:T(8,128)(2,1)} %collective-permute-done.24.refs_2_), channel_id=1, source_target_pairs={{0,1},{2,0},{4,2},{6,4},{7,6},{5,7},{3,5},{1,3},{8,9},{10,8},{12,1... | collective-permute-start | bytes 786440 | tf_op jit(solution)/shard_map/ppermute | solution.py:306
  39.2 15.4 %collective-permute-start.13 = (bf16[1,128,1024]{2,1,0:T(8,128)(2,1)S(1)}, bf16[1,128,1024]{2,1,0:T(8,128)(2,1)}, u32[]{:S(2)}, u32[]{:S(2)}) collective-permute-start(bf16[1,128,1024]{2,1,0:T(8,128)(2,1)S(1)} %collective-permute-done.12.refs_1_), channel_id=1, source_target_pairs={{0,2},{2,4},{4,6},{6,7},{7,5},{5,3},{3,1},{1,0},{8,10},{10,12},{12... | collective-permute-start | bytes 786440 | tf_op jit(solution)/shard_map/ppermute | solution.py:306
  42.7 13.5 %collective-permute-start.17 = (bf16[1,128,1024]{2,1,0:T(8,128)(2,1)S(1)}, bf16[1,128,1024]{2,1,0:T(8,128)(2,1)}, u32[]{:S(2)}, u32[]{:S(2)}) collective-permute-start(bf16[1,128,1024]{2,1,0:T(8,128)(2,1)S(1)} %collective-permute-done.16.refs_2_), channel_id=1, source_target_pairs={{0,1},{2,0},{4,2},{6,4},{7,6},{5,7},{3,5},{1,3},{8,9},{10,8},{12,1... | collective-permute-start | bytes 786440 | tf_op jit(solution)/shard_map/ppermute | solution.py:306
  44.8 14.8 %collective-permute-start.5 = (bf16[1,128,1024]{2,1,0:T(8,128)(2,1)S(1)}, bf16[1,128,1024]{2,1,0:T(8,128)(2,1)}, u32[]{:S(2)}, u32[]{:S(2)}) collective-permute-start(bf16[1,128,1024]{2,1,0:T(8,128)(2,1)S(1)} %collective-permute-done.4.refs_1_), channel_id=1, source_target_pairs={{0,2},{2,4},{4,6},{6,7},{7,5},{5,3},{3,1},{1,0},{8,10},{10,12},{12... | collective-permute-start | bytes 786440 | tf_op jit(solution)/shard_map/ppermute | solution.py:306
  48.4 13.4 %collective-permute-start.9 = (bf16[1,128,1024]{2,1,0:T(8,128)(2,1)S(1)}, bf16[1,128,1024]{2,1,0:T(8,128)(2,1)}, u32[]{:S(2)}, u32[]{:S(2)}) collective-permute-start(bf16[1,128,1024]{2,1,0:T(8,128)(2,1)S(1)} %collective-permute-done.8.refs_2_), channel_id=1, source_target_pairs={{0,1},{2,0},{4,2},{6,4},{7,6},{5,7},{3,5},{1,3},{8,9},{10,8},{12,1... | collective-permute-start | bytes 786440 | tf_op jit(solution)/shard_map/ppermute | solution.py:306
  50.5 14.6 %collective-permute-start.22 = (bf16[1,128,1024]{2,1,0:T(8,128)(2,1)}, bf16[1,128,1024]{2,1,0:T(8,128)(2,1)S(1)}, u32[]{:S(2)}, u32[]{:S(2)}) collective-permute-start(bf16[1,128,1024]{2,1,0:T(8,128)(2,1)} %collective-permute-done.21.refs_0_), channel_id=1, source_target_pairs={{0,2},{2,4},{4,6},{6,7},{7,5},{5,3},{3,1},{1,0},{8,10},{10,12},{12... | collective-permute-start | bytes 786440 | tf_op jit(solution)/shard_map/ppermute | solution.py:306
  54.6 13.3 %collective-permute-start.26 = (bf16[1,128,1024]{2,1,0:T(8,128)(2,1)}, bf16[1,128,1024]{2,1,0:T(8,128)(2,1)S(1)}, u32[]{:S(2)}, u32[]{:S(2)}) collective-permute-start(bf16[1,128,1024]{2,1,0:T(8,128)(2,1)} %collective-permute-done.25.refs_1_), channel_id=1, source_target_pairs={{0,1},{2,0},{4,2},{6,4},{7,6},{5,7},{3,5},{1,3},{8,9},{10,8},{12,1... | collective-permute-start | bytes 786440 | tf_op jit(solution)/shard_map/ppermute | solution.py:306
  56.2 14.6 %collective-permute-start.14 = (bf16[1,128,1024]{2,1,0:T(8,128)(2,1)}, bf16[1,128,1024]{2,1,0:T(8,128)(2,1)S(1)}, u32[]{:S(2)}, u32[]{:S(2)}) collective-permute-start(bf16[1,128,1024]{2,1,0:T(8,128)(2,1)} %collective-permute-done.13.refs_0_), channel_id=1, source_target_pairs={{0,2},{2,4},{4,6},{6,7},{7,5},{5,3},{3,1},{1,0},{8,10},{10,12},{12... | collective-permute-start | bytes 786440 | tf_op jit(solution)/shard_map/ppermute | solution.py:306
  59.6 30.9 %collective-permute-start.18 = (bf16[1,128,1024]{2,1,0:T(8,128)(2,1)}, bf16[1,128,1024]{2,1,0:T(8,128)(2,1)S(1)}, u32[]{:S(2)}, u32[]{:S(2)}) collective-permute-start(bf16[1,128,1024]{2,1,0:T(8,128)(2,1)} %collective-permute-done.17.refs_1_), channel_id=1, source_target_pairs={{0,1},{2,0},{4,2},{6,4},{7,6},{5,7},{3,5},{1,3},{8,9},{10,8},{12,1... | collective-permute-start | bytes 786440 | tf_op jit(solution)/shard_map/ppermute | solution.py:306
  61.8 30.5 %collective-permute-start.10 = (bf16[1,128,1024]{2,1,0:T(8,128)(2,1)}, bf16[1,128,1024]{2,1,0:T(8,128)(2,1)S(1)}, u32[]{:S(2)}, u32[]{:S(2)}) collective-permute-start(bf16[1,128,1024]{2,1,0:T(8,128)(2,1)} %collective-permute-done.9.refs_1_), channel_id=1, source_target_pairs={{0,1},{2,0},{4,2},{6,4},{7,6},{5,7},{3,5},{1,3},{8,9},{10,8},{12,1... | collective-permute-start | bytes 786440 | tf_op jit(solution)/shard_map/ppermute | solution.py:306
  65.1 27.6 %collective-permute-start.6 = (bf16[1,128,1024]{2,1,0:T(8,128)(2,1)}, bf16[1,128,1024]{2,1,0:T(8,128)(2,1)S(1)}, u32[]{:S(2)}, u32[]{:S(2)}) collective-permute-start(bf16[1,128,1024]{2,1,0:T(8,128)(2,1)} %collective-permute-done.5.refs_0_), channel_id=1, source_target_pairs={{0,2},{2,4},{4,6},{6,7},{7,5},{5,3},{3,1},{1,0},{8,10},{10,12},{12... | collective-permute-start | bytes 786440 | tf_op jit(solution)/shard_map/ppermute | solution.py:306
  68.0 26.4 %collective-permute-start.23 = (bf16[1,64,1024]{2,1,0:T(8,128)(2,1)S(1)}, bf16[1,64,1024]{2,1,0:T(8,128)(2,1)S(1)}, u32[]{:S(2)}, u32[]{:S(2)}) collective-permute-start(bf16[1,64,1024]{2,1,0:T(8,128)(2,1)S(1)} %slice.56), channel_id=1, source_target_pairs={{0,2},{2,4},{4,6},{6,7},{7,5},{5,3},{3,1},{1,0},{8,10},{10,12},{12... | collective-permute-start | bytes 393224 | tf_op jit(solution)/shard_map/ppermute | solution.py:306
  70.7 24.3 %collective-permute-start.27 = (bf16[1,64,1024]{2,1,0:T(8,128)(2,1)S(1)}, bf16[1,64,1024]{2,1,0:T(8,128)(2,1)S(1)}, u32[]{:S(2)}, u32[]{:S(2)}) collective-permute-start(bf16[1,64,1024]{2,1,0:T(8,128)(2,1)S(1)} %slice.57), channel_id=1, source_target_pairs={{0,1},{2,0},{4,2},{6,4},{7,6},{5,7},{3,5},{1,3},{8,9},{10,8},{12,1... | collective-permute-start | bytes 393224 | tf_op jit(solution)/shard_map/ppermute | solution.py:306
  90.5 27.0 %collective-permute-start.15 = (bf16[1,64,1024]{2,1,0:T(8,128)(2,1)S(1)}, bf16[1,64,1024]{2,1,0:T(8,128)(2,1)S(1)}, u32[]{:S(2)}, u32[]{:S(2)}) collective-permute-start(bf16[1,64,1024]{2,1,0:T(8,128)(2,1)S(1)} %slice.54), channel_id=1, source_target_pairs={{0,2},{2,4},{4,6},{6,7},{7,5},{5,3},{3,1},{1,0},{8,10},{10,12},{12... | collective-permute-start | bytes 393224 | tf_op jit(solution)/shard_map/ppermute | solution.py:306
  92.3 25.2 %collective-permute-start.19 = (bf16[1,64,1024]{2,1,0:T(8,128)(2,1)S(1)}, bf16[1,64,1024]{2,1,0:T(8,128)(2,1)S(1)}, u32[]{:S(2)}, u32[]{:S(2)}) collective-permute-start(bf16[1,64,1024]{2,1,0:T(8,128)(2,1)S(1)} %slice.55), channel_id=1, source_target_pairs={{0,1},{2,0},{4,2},{6,4},{7,6},{5,7},{3,5},{1,3},{8,9},{10,8},{12,1... | collective-permute-start | bytes 393224 | tf_op jit(solution)/shard_map/ppermute | solution.py:306
  92.7 47.3 %collective-permute-start.11 = (bf16[1,64,1024]{2,1,0:T(8,128)(2,1)S(1)}, bf16[1,64,1024]{2,1,0:T(8,128)(2,1)S(1)}, u32[]{:S(2)}, u32[]{:S(2)}) collective-permute-start(bf16[1,64,1024]{2,1,0:T(8,128)(2,1)S(1)} %slice.53), channel_id=1, source_target_pairs={{0,1},{2,0},{4,2},{6,4},{7,6},{5,7},{3,5},{1,3},{8,9},{10,8},{12,1... | collective-permute-start | bytes 393224 | tf_op jit(solution)/shard_map/ppermute | solution.py:306
  94.4 45.6 %collective-permute-start.7 = (bf16[1,64,1024]{2,1,0:T(8,128)(2,1)S(1)}, bf16[1,64,1024]{2,1,0:T(8,128)(2,1)S(1)}, u32[]{:S(2)}, u32[]{:S(2)}) collective-permute-start(bf16[1,64,1024]{2,1,0:T(8,128)(2,1)S(1)} %slice.52), channel_id=1, source_target_pairs={{0,2},{2,4},{4,6},{6,7},{7,5},{5,3},{3,1},{1,0},{8,10},{10,12},{12... | collective-permute-start | bytes 393224 | tf_op jit(solution)/shard_map/ppermute | solution.py:306
  (19 other events, 148.7 us)

commit v2 on v1

v2 whole, which is shorter than its diff:
```python
import functools

import jax
import jax.numpy as jnp
from jax import lax
from jax.experimental import pallas as pl
from jax.experimental.pallas import tpu as pltpu
from jax.sharding import PartitionSpec as P

LANES = 128
RING = 8
VMEM = 40 * 1024 * 1024
F32 = jnp.float32
BF16 = jnp.bfloat16


def whole():
    return pl.BlockSpec(memory_space=pltpu.VMEM)


def params():
    return pltpu.CompilerParams(vmem_limit_bytes=VMEM)


def cost(flops, size):
    return pl.CostEstimate(flops=flops, bytes_accessed=size, transcendentals=0)


def by_mode(values, out, fold):
    for j in range(fold):
        out[pl.ds(j, values.shape[0], stride=fold), :] = values[:, j * LANES : (j + 1) * LANES]


def summary_kernel(feat, og, rate, out, dec, sig):
    tokens, channels = og.shape
    modes = rate.shape[0]
    fold = channels // LANES
    by_mode(jnp.exp(-rate[...]), dec, fold)
    for j in range(fold):
        lanes = slice(j * LANES, (j + 1) * LANES)
        sig[pl.ds(j, tokens, stride=fold), :] = og[:, lanes] * feat[0, :, lanes]
    decay = [dec[m * fold : (m + 1) * fold, :] for m in range(modes)]

    def step(i, states):
        row = sig[pl.ds((tokens - 1 - i) * fold, fold), :]
        return tuple(row + d * s for d, s in zip(decay, states))

    zero = tuple(jnp.zeros((fold, LANES), F32) for _ in range(modes))
    states = lax.fori_loop(0, tokens - 2, step, zero, unroll=6)
    for m in range(modes):
        out[m * fold : (m + 1) * fold, :] = states[m]
    out[modes * fold : (modes + 2) * fold, :] = sig[0 : 2 * fold, :]


def summary(features, out_grad, rate):
    tokens, channels = out_grad.shape
    modes = rate.shape[0]
    fold = channels // LANES
    return pl.pallas_call(
        summary_kernel,
        in_specs=[whole()] * 3,
        out_specs=whole(),
        out_shape=jax.ShapeDtypeStruct(((modes + 2) * fold, LANES), F32),
        scratch_shapes=[
            pltpu.VMEM((modes * fold, LANES), F32),
            pltpu.VMEM((tokens * fold, LANES), F32),
        ],
        compiler_params=params(),
        cost_estimate=cost(4 * tokens * channels * modes, 12 * tokens * channels),
        name="summary",
    )(features, out_grad, rate)


def tapped(ext, taps, lanes, tokens):
    total = taps[0][:, lanes] * ext[0:tokens, lanes]
    total = total + taps[1][:, lanes] * ext[1 : tokens + 1, lanes]
    return total + taps[2][:, lanes] * ext[2 : tokens + 2, lanes]


def gate_gradient(feat, conv, og, bias, halo, ext):
    tokens, channels = og.shape
    ext[tokens : tokens + 2, :] = halo[8:10] * (halo[6:8] + bias[...] * (halo[2:4] * halo[4:6]))
    for j in range(channels // LANES):
        lanes = slice(j * LANES, (j + 1) * LANES)
        product = feat[1, :, lanes] * feat[2, :, lanes]
        ext[0:tokens, lanes] = og[:, lanes] * (conv[:, lanes] + bias[:, lanes] * product)


def gate_kernel(feat, conv, og, filt, bias, halo, rounded, ext):
    tokens, channels = og.shape
    taps = [filt[0, j : j + 1, :] for j in range(3)]
    gate_gradient(feat, conv, og, bias, halo, ext)
    for j in range(channels // LANES):
        lanes = slice(j * LANES, (j + 1) * LANES)
        rounded[0, :, lanes] = tapped(ext, taps, lanes, tokens).astype(BF16)


def gate_stream(features, saved_conv, out_grad, short_filter, bias_row, halo):
    tokens, channels = out_grad.shape
    return pl.pallas_call(
        gate_kernel,
        in_specs=[whole()] * 6,
        out_specs=whole(),
        out_shape=jax.ShapeDtypeStruct((1, tokens, channels), BF16),
        scratch_shapes=[pltpu.VMEM((tokens + 8, channels), F32)],
        compiler_params=params(),
        cost_estimate=cost(12 * tokens * channels, 26 * tokens * channels),
        name="gate_stream",
    )(features, saved_conv, out_grad, short_filter, bias_row, halo)


def state_kernel(later, feat, conv, og, filt, rate, residue, bias, bias_row, halo, *refs):
    payloads = refs[:later]
    out, rounded, sums, dec, res, far, acc, sig, prod, gp, *exts = refs[later:]
    tokens, channels = og.shape
    modes = rate.shape[0]
    fold = channels // LANES
    by_mode(jnp.exp(-rate[...]), dec, fold)
    by_mode(jnp.exp(-(tokens - 2) * rate[...]), far, fold)
    by_mode(residue[...], res, fold)
    for j in range(fold):
        lanes = slice(j * LANES, (j + 1) * LANES)
        s = og[:, lanes] * feat[0, :, lanes]
        p = feat[1, :, lanes] * feat[2, :, lanes]
        sig[pl.ds(j, tokens, stride=fold), :] = s
        prod[pl.ds(j, tokens, stride=fold), :] = p
        sums[modes : modes + 1, lanes] = jnp.sum(s * p, axis=0, keepdims=True)

    def rows(ref, at):
        return ref[at * fold : (at + 1) * fold, :]

    direct = bias[...]
    group = 8
    for low in range(0, modes, group):
        chosen = range(low, min(low + group, modes))
        decay = [rows(dec, m) for m in chosen]
        weight = [rows(res, m) for m in chosen]
        reach = [rows(far, m) for m in chosen]
        state = [jnp.zeros((fold, LANES), F32) for _ in chosen]
        for n, payload in enumerate(reversed(payloads)):
            block_end = [rows(payload, m) + f * s for m, f, s in zip(chosen, reach, state)]
            if n < later - 1:
                s0, s1 = rows(payload, modes), rows(payload, modes + 1)
                state = [s0 + d * (s1 + d * s) for d, s in zip(decay, block_end)]
            else:
                state = block_end

        def corr(state, weight=weight):
            terms = [w * s for w, s in zip(weight, state)]
            while len(terms) > 1:
                terms = [a + b for a, b in zip(terms[::2], terms[1::2])] + terms[len(terms) // 2 * 2 :]
            return terms[0]

        def put(at, row, state, low=low):
            here = pl.ds(at * fold, fold)
            if low == 0:
                gp[here, :] = corr(state) + direct * row
            else:
                gp[here, :] = gp[here, :] + corr(state)

        for n in (1, 0):
            row = rows(payloads[0], modes + n)
            state = [row + d * s for d, s in zip(decay, state)]
            put(tokens + n, row, state)

        def step(i, carry, decay=decay, put=put):
            state, total = carry
            at = tokens - 1 - i
            row = sig[pl.ds(at * fold, fold), :]
            other = prod[pl.ds(at * fold, fold), :]
            state = [row + d * s for d, s in zip(decay, state)]
            total = [a + other * s for a, s in zip(total, state)]
            put(at, row, state)
            return state, total

        zero = [jnp.zeros((fold, LANES), F32) for _ in chosen]
        state, total = lax.fori_loop(0, tokens, step, (state, zero), unroll=4)
        for m, a in zip(chosen, total):
            acc[m * fold : (m + 1) * fold, :] = a

    taps = [[filt[p, j : j + 1, :] for j in range(3)] for p in range(3)]
    gate_gradient(feat, conv, og, bias_row, halo, exts[0])
    for j in range(fold):
        lanes = slice(j * LANES, (j + 1) * LANES)
        g = gp[pl.ds(j, tokens, stride=fold), :]
        rim = gp[pl.ds(tokens * fold + j, 2, stride=fold), :]
        exts[1][0:tokens, lanes] = g * feat[2, :, lanes]
        exts[1][tokens : tokens + 2, lanes] = rim * halo[4:6, lanes]
        exts[2][0:tokens, lanes] = g * feat[1, :, lanes]
        exts[2][tokens : tokens + 2, lanes] = rim * halo[2:4, lanes]
        for p, ext in enumerate(exts):
            total = tapped(ext, taps[p], lanes, tokens)
            out[p, :, lanes] = total
            if p:
                rounded[p - 1, :, lanes] = total.astype(BF16)
        sums[0:modes, lanes] = acc[pl.ds(j, modes, stride=fold), :]


def state_streams(features, saved_conv, out_grad, short_filter, rate, residue, bias, halo, payloads):
    tokens, channels = out_grad.shape
    modes = rate.shape[0]
    fold = channels // LANES
    return pl.pallas_call(
        functools.partial(state_kernel, len(payloads)),
        in_specs=[whole()] * (9 + len(payloads)),
        out_specs=[whole()] * 3,
        out_shape=[
            jax.ShapeDtypeStruct((3, tokens, channels), F32),
            jax.ShapeDtypeStruct((2, tokens, channels), BF16),
            jax.ShapeDtypeStruct((modes + 1, channels), F32),
        ],
        scratch_shapes=[pltpu.VMEM((modes * fold, LANES), F32)] * 4
        + [pltpu.VMEM((tokens * fold, LANES), F32)] * 2
        + [pltpu.VMEM(((tokens + 2) * fold, LANES), F32)]
        + [pltpu.VMEM((tokens + 8, channels), F32)] * 3,
        compiler_params=params(),
        cost_estimate=cost(8 * tokens * channels * modes, 40 * tokens * channels),
        name="state_streams",
    )(
        features, saved_conv, out_grad, short_filter, rate, residue,
        bias.reshape(fold, LANES), bias[None], halo, *payloads,
    )


def product_kernel(plan, first, last, source, *refs):
    *xs, w = refs[: len(refs) - 1 - (not first)]
    out = refs[-1]
    before = None if first else refs[-2]
    total = None
    k = pl.program_id(1)
    for at, parts in enumerate(plan):

        @pl.when(k == at)
        def _(at=at, parts=parts):
            x = [xs[n][h, p] for n, h, p in parts]
            x = x[0] if len(x) == 1 else jnp.concatenate(x, axis=0)
            y = lax.dot_general(w[0], x, (((1,), (1,)), ((), ())), preferred_element_type=F32)
            if at == 0:
                if not first:
                    y = y + before[...]
            else:
                y = y + (out[...].T if last else out[...])
            out[...] = y.T if last else y


def add_product(total, pieces, sources, w_proj, last=False):
    features = w_proj.shape[1]
    arrays, plan, where = [], [], []
    for array, stream, offset in pieces:
        halves = array if isinstance(array, tuple) else (array,)
        heights, streams, _, channels = halves[0].shape
        for h in range(heights):
            for p in range(streams):
                plan.append([(len(arrays) + n, h, p) for n in range(len(halves))])
                where.append((stream + p, h, offset))
        arrays += halves
    tokens = sum(arrays[n].shape[2] for n, _, _ in plan[0])
    wide = min(512, features)

    def w_index(i, k, source):
        stream, height, offset = (jnp.int32(v) for v in where[0])
        for at, (s, h, o) in enumerate(where):
            stream = jnp.where(k == at, s, stream)
            height = jnp.where(k == at, h, height)
            offset = jnp.where(k == at, o, offset)
        return stream, i, height * RING + source[offset]

    def kept(array):
        return pl.BlockSpec(array.shape, lambda i, k, s: (0,) * array.ndim)

    tile = pl.BlockSpec((wide, tokens), lambda i, k, s: (i, 0))
    first = total is None
    return pl.pallas_call(
        functools.partial(product_kernel, plan, first, last),
        grid_spec=pltpu.PrefetchScalarGridSpec(
            num_scalar_prefetch=1,
            grid=(features // wide, len(plan)),
            in_specs=[kept(a) for a in arrays]
            + [pl.BlockSpec((1, wide, channels), w_index)]
            + [tile] * (not first),
            out_specs=pl.BlockSpec((tokens, wide), lambda i, k, s: (0, i)) if last else tile,
        ),
        out_shape=jax.ShapeDtypeStruct((tokens, features) if last else (features, tokens), F32),
        compiler_params=params(),
        cost_estimate=cost(
            2 * tokens * features * channels * len(plan),
            2 * features * channels * len(plan) + 8 * tokens * features,
        ),
        name="add_product",
    )(sources, *arrays, w_proj, *([] if first else [total]))


def ring_order(size):
    return list(range(0, size, 2)) + list(range(size - 1 - size % 2, 0, -2))


def after(array, *others):
    return lax.optimization_barrier((array, *others))[0]


def body(features, saved_conv, out_grad, short_filter, residue, rate, bias, w_proj):
    tokens, channels = out_grad.shape
    modes = rate.shape[1]
    blocks = lax.axis_size("ctx")
    groups = lax.axis_size("chan")
    ring = min(groups, RING)
    heights = groups // ring

    order = ring_order(ring)
    place = [order.index(i) for i in range(ring)]
    table = jnp.array([[order[(place[i] + d) % ring] for d in range(ring)] for i in range(ring)], jnp.int32)
    sources = lax.dynamic_index_in_dim(table, lax.rem(lax.axis_index("chan"), ring), 0, False)
    pairs = {
        by: [
            (h * ring + order[i], h * ring + order[(i + by) % ring])
            for h in range(heights)
            for i in range(ring)
        ]
        for by in (1, -1)
    }

    def up(x):
        return lax.ppermute(x, "chan", pairs[1])

    def down(x):
        return lax.ppermute(x, "chan", pairs[-1])

    def stacked(block):
        if heights == 1:
            return block[None]
        groups = [[h * ring + i for h in range(heights)] for i in range(ring)]
        return lax.all_gather(block, "chan", axis_index_groups=groups)

    def from_later(array, by):
        return lax.ppermute(array, "ctx", [(i, i - by) for i in range(by, blocks)])

    rim = jnp.concatenate([features[:, 0:2].reshape(6, channels), saved_conv[0:2], out_grad[0:2]])
    halo = from_later(rim, 1)
    own = summary(features, out_grad, rate.T)
    gate = gate_stream(features, saved_conv, out_grad, short_filter, bias[None], halo)
    own = after(own, gate)
    payloads = [from_later(own, by) for by in range(1, blocks)]
    a0 = stacked(gate)
    a1, z1 = up(a0), down(a0)

    grads, rounds, sums = state_streams(
        features, saved_conv, out_grad, short_filter, rate.T, residue.T, bias, halo, payloads
    )
    b0 = stacked(rounds)
    half = tokens // 2
    back = ring // 2

    a2, z2 = up(a1), down(z1)
    b1, y1 = up(b0), down(b0)
    a3, z3 = up(after(a2, b0)), down(after(z2, b0))
    total = add_product(
        None, [(a0, 0, 0), (a1, 0, ring - 1), (z1, 0, 1), (a2, 0, ring - 2), (z2, 0, 2)], sources, w_proj
    )
    by = 1
    sums = after(sums, total)
    while by < blocks:
        sums = sums + lax.ppermute(sums, "ctx", [(i, i ^ by) for i in range(blocks)])
        by *= 2
    sums = sums * (tokens * blocks) ** (-0.5)

    a3, z3, total = lax.optimization_barrier((a3, z3, total))
    tail = (up(a3[:, :, :half]), down(z3[:, :, half:]))
    total = add_product(total, [(a3, 0, ring - 3), (z3, 0, 3)], sources, w_proj)
    b1, y1, total = lax.optimization_barrier((b1, y1, total))
    b2, y2 = up(b1), down(y1)
    total = add_product(total, [(b0, 1, 0), (b1, 1, ring - 1), (y1, 1, 1)], sources, w_proj)
    tail, total = lax.optimization_barrier((tail, total))
    total = add_product(total, [(tail, 0, back)], sources, w_proj)
    b2, y2, total = lax.optimization_barrier((b2, y2, total))
    b3, y3 = up(b2), down(y2)
    total = add_product(total, [(b2, 1, ring - 2), (y2, 1, 2)], sources, w_proj)
    b3, y3, total = lax.optimization_barrier((b3, y3, total))
    b4, y4 = up(b3[:, :1]), down(y3[:, 1:])
    total = add_product(total, [(b3, 1, ring - 3), (y3, 1, 3)], sources, w_proj)
    grad_x = add_product(total, [(b4, 1, back), (y4, 2, back)], sources, w_proj, last=True)
    return (grads, grad_x, sums[:modes].T, sums[modes])


def solution(mesh):
    return jax.shard_map(
        body,
        mesh=mesh,
        in_specs=(
            P(None, "ctx", "chan"),
            P("ctx", "chan"),
            P("ctx", "chan"),
            P(None, None, "chan"),
            P("chan", None),
            P("chan", None),
            P("chan"),
            P(None, "chan", None),
        ),
        out_specs=(P(None, "ctx", "chan"), P("ctx", "chan"), P("chan", None), P("chan")),
        check_vma=False,
    )
```

time: 145 us -> 109 us (0.75)
  Pallas kernels: 74 us -> 55.8 us
  starting transfers between devices: 33.6 us -> 23.4 us
  waiting for transfers between devices: 24.5 us -> 18.2 us
  other arithmetic: 2.56 us -> 0.05 us
    pallas_call x14 -> x9, Pallas kernels: 69.5 us -> 51.2 us  [the longest x7 50 us: add_product(): pl.pallas_call(functools.partial(product_kernel, plan, first, last), grid...]
    ppermute x24 -> x16, waiting for transfers between devices: 17.9 us -> 9.53 us  [the longest x8 8.87 us: up(): return lax.ppermute(x, 'chan', pairs[1])]
    ppermute x24 -> x16, starting transfers between devices: 24.7 us -> 18.2 us  [the longest x8 13.6 us: down(): return lax.ppermute(x, 'chan', pairs[-1])]
    ppermute x2, starting transfers between devices: 3.7 us -> 0.07 us  [body(): lax.ppermute(sums, 'ctx', [(i, i ^ by) for i in range(blocks)])]
    concatenate x1 -> x0, other arithmetic: 2.52 us -> none  [body(): grad_inputs = jnp.concatenate([gate_grad[None], grads])]
    ppermute x2, waiting for transfers between devices: 4.3 us -> 6.14 us  [body(): lax.ppermute(sums, 'ctx', [(i, i ^ by) for i in range(blocks)])]
    unnamed x24 -> x18, local copies, waits for them, and re-layouts: 5.54 us -> 5 us
  transfers between devices with their start and end apart: 30 -> 22, of which waited for: 13 -> 10; matrix products, arithmetic and copies ran while one was open for 4% -> 2% of each run, Pallas kernels for 48% -> 46%
where the time goes in v2:
time: 109 us; the launch traced here: 108 us
  Pallas kernels  55.8 us (51%)
  starting transfers between devices  23.4 us (21%)
  waiting for transfers between devices  18.2 us (17%)
  local copies, waits for them, and re-layouts  9.42 us (9%)
    pallas_call x7, Pallas kernels, add_product(): pl.pallas_call(functools.partial(product_kernel, plan, first, last), grid...  50 us
    ppermute x8, starting transfers between devices, down(): return lax.ppermute(x, 'chan', pairs[-1])  13.6 us
    ppermute x8, waiting for transfers between devices, up(): return lax.ppermute(x, 'chan', pairs[1])  8.87 us
    ppermute x2, waiting for transfers between devices, body(): lax.ppermute(sums, 'ctx', [(i, i ^ by) for i in range(blocks)])  6.14 us
    ppermute x4, starting transfers between devices, from_later(): return lax.ppermute(array, 'ctx', [(i, i - by) for i in range(by, blocks)])  5.17 us
    unnamed x18, local copies, waits for them, and re-layouts  5 us
    pallas_call x1, Pallas kernels, state_streams(): pl.pallas_call(functools.partial(state_kernel, len(payloads)), in_specs=[...  4.66 us
    ppermute x8, starting transfers between devices, up(): return lax.ppermute(x, 'chan', pairs[1])  4.57 us
  transfers between devices with their start and end apart: 22, of which 10 were waited for; matrix products, arithmetic and copies ran while one was open for 2% of the time, Pallas kernels for 46%

profile of v2, /device:TPU:0, one launch (start us, length us, event | category | flops | bytes accessed | tf_op | source)
XLA Modules:
  0.0 107.8 jit_solution(17497670815562100683)
XLA Ops:
  3.1 1.3 %collective-permute-start = (f32[10,1024]{1,0:T(8,128)S(1)}, f32[10,1024]{1,0:T(8,128)S(1)}, u32[]{:S(2)}, u32[]{:S(2)}) collective-permute-start(f32[10,1024]{1,0:T(8,128)S(1)} %pad_maximum_fusion), channel_id=1, source_target_pairs={{8,0},{16,8},{24,16},{9,1},{17,9},{25,17},{10,2},{18,10},{26,18},{... | collective-permute-start | bytes 122888 | tf_op jit(solution)/shard_map/ppermute | solution.py:335
  4.4 1.8 %collective-permute-done.halo = f32[10,1024]{1,0:T(8,128)S(1)} collective-permute-done((f32[10,1024]{1,0:T(8,128)S(1)}, f32[10,1024]{1,0:T(8,128)S(1)}, u32[]{:S(2)}, u32[]{:S(2)}) %collective-permute-start) | collective-permute-done | bytes 40992 | tf_op jit(solution)/shard_map/ppermute | solution.py:335
  6.3 1.4 %copy-done = f32[3,128,1024]{2,1,0:T(8,128)S(1)} copy-done((f32[3,128,1024]{2,1,0:T(8,128)S(1)}, f32[3,128,1024]{2,1,0:T(8,128)}, u32[]{:S(2)}) %copy-start) | copy-done | bytes 1572888
  11.7 3.0 %collective-permute-start.9 = (bf16[1,1,128,1024]{3,2,1,0:T(8,128)(2,1)S(1)}, bf16[1,1,128,1024]{3,2,1,0:T(8,128)(2,1)S(1)}, u32[]{:S(2)}, u32[]{:S(2)}) collective-permute-start(bf16[1,1,128,1024]{3,2,1,0:T(8,128)(2,1)S(1)} %bitcast.11), channel_id=1, source_target_pairs={{0,1},{2,0},{4,2},{6,4},{7,6},{5,7},{3,5},{1,3},{8,9},{10,8},{12,1... | collective-permute-start | bytes 786440 | tf_op jit(solution)/shard_map/ppermute | solution.py:326
  15.6 1.3 %collective-permute-start.3 = (f32[144,128]{1,0:T(8,128)S(1)}, f32[144,128]{1,0:T(8,128)S(1)}, u32[]{:S(2)}, u32[]{:S(2)}) collective-permute-start(f32[144,128]{1,0:T(8,128)S(1)} %summary.1), channel_id=1, source_target_pairs={{24,0},{25,1},{26,2},{27,3},{28,4},{29,5},{30,6},{31,7}} | collective-permute-start | bytes 221192 | tf_op jit(solution)/shard_map/ppermute | solution.py:335
  20.0 2.4 %collective-permute-start.10 = (bf16[1,1,128,1024]{3,2,1,0:T(8,128)(2,1)S(1)}, bf16[1,1,128,1024]{3,2,1,0:T(8,128)(2,1)S(1)}, u32[]{:S(2)}, u32[]{:S(2)}) collective-permute-start(bf16[1,1,128,1024]{3,2,1,0:T(8,128)(2,1)S(1)} %collective-permute-done.9.refs_2_), channel_id=1, source_target_pairs={{0,1},{2,0},{4,2},{6,4},{7,6},{5,7},{3,5},{1,3},{8,9},{10,8},{12,1... | collective-permute-start | bytes 786440 | tf_op jit(solution)/shard_map/ppermute | solution.py:326
  23.4 4.7 %state_streams.1 = (f32[3,128,1024]{2,1,0:T(8,128)}, bf16[2,128,1024]{2,1,0:T(8,128)(2,1)S(1)}, f32[17,1024]{1,0:T(8,128)S(1)}) custom-call(f32[3,128,1024]{2,1,0:T(8,128)S(1)} %copy-done, f32[128,1024]{1,0:T(8,128)S(1)} %copy-done.3, f32[128,1024]{1,0:T(8,128)S(1)} %copy-done.1, f32[3,3,1024]{2,1,0:T(4,128)S(1)} %copy-done.5, f32[16,1024]{1,0:T(8,128)S(1)} %bitcast.18, ...), custom_call_target="tpu_custom_call" | custom-call | flops 16777216 | bytes 5242880 | tf_op jit(solution)/shard_map/state_streams/pallas_call | solution.py:203
  28.1 2.2 %collective-permute-start.5 = (bf16[1,2,128,1024]{3,2,1,0:T(8,128)(2,1)S(1)}, bf16[1,2,128,1024]{3,2,1,0:T(8,128)(2,1)S(1)}, u32[]{:S(2)}, u32[]{:S(2)}) collective-permute-start(bf16[1,2,128,1024]{3,2,1,0:T(8,128)(2,1)S(1)} %bitcast.14), channel_id=1, source_target_pairs={{0,1},{2,0},{4,2},{6,4},{7,6},{5,7},{3,5},{1,3},{8,9},{10,8},{12,1... | collective-permute-start | bytes 1572872 | tf_op jit(solution)/shard_map/ppermute | solution.py:326
  30.4 1.5 %collective-permute-done.7.refs_3_ = bf16[1,1,128,1024]{3,2,1,0:T(8,128)(2,1)S(1)} collective-permute-done((bf16[1,1,128,1024]{3,2,1,0:T(8,128)(2,1)S(1)}, bf16[1,1,128,1024]{3,2,1,0:T(8,128)(2,1)S(1)}, u32[]{:S(2)}, u32[]{:S(2)}) %collective-permute-start.7) | collective-permute-done | bytes 262176 | tf_op jit(solution)/shard_map/ppermute | solution.py:323
  32.4 1.5 %collective-permute-start.11 = (bf16[1,1,128,1024]{3,2,1,0:T(8,128)(2,1)S(1)}, bf16[1,1,128,1024]{3,2,1,0:T(8,128)(2,1)S(1)}, u32[]{:S(2)}, u32[]{:S(2)}) collective-permute-start(bf16[1,1,128,1024]{3,2,1,0:T(8,128)(2,1)S(1)} %collective-permute-done.10.refs_4_), channel_id=1, source_target_pairs={{0,1},{2,0},{4,2},{6,4},{7,6},{5,7},{3,5},{1,3},{8,9},{10,8},{12,1... | collective-permute-start | bytes 786440 | tf_op jit(solution)/shard_map/ppermute | solution.py:326
  34.6 9.8 %add_product.7.refs_3_ = f32[1024,128]{1,0:T(8,128)S(1)} custom-call(s32[8]{0:T(128)S(1)} %dynamic-slice_bitcast_fusion.source, bf16[1,1,128,1024]{3,2,1,0:T(8,128)(2,1)S(1)} %bitcast.13, bf16[1,1,128,1024]{3,2,1,0:T(8,128)(2,1)S(1)} %collective-permute-done.6.refs_1_, bf16[1,1,128,1024]{3,2,1,0:T(8,128)(2,1)S(1)} %collective-permute-done.9.refs_2_, ...), custom_call_target="tpu_custom_call" | custom-call | flops 1342177280 | bytes 11534336 | tf_op jit(solution)/shard_map/add_product/pallas_call | solution.py:273
  44.4 6.1 %collective-permute-done.8.refs_0_ = bf16[1,1,128,1024]{3,2,1,0:T(8,128)(2,1)S(1)} collective-permute-done((bf16[1,1,128,1024]{3,2,1,0:T(8,128)(2,1)S(1)}, bf16[1,1,128,1024]{3,2,1,0:T(8,128)(2,1)S(1)}, u32[]{:S(2)}, u32[]{:S(2)}) %collective-permute-start.8) | collective-permute-done | bytes 262176 | tf_op jit(solution)/shard_map/ppermute | solution.py:323
  50.4 4.5 %add_product.8.refs_4_ = f32[1024,128]{1,0:T(8,128)S(1)} custom-call(s32[8]{0:T(128)S(1)} %dynamic-slice_bitcast_fusion.source, bf16[1,1,128,1024]{3,2,1,0:T(8,128)(2,1)S(1)} %collective-permute-done.8.refs_0_, bf16[1,1,128,1024]{3,2,1,0:T(8,128)(2,1)S(1)} %collective-permute-done.11.refs_1_, bf16[3,1024,8192]{2,1,0:T(8,128)(2,1)} %refs_2_.9, ...), custom_call_target="tpu_custom_call" | custom-call | flops 536870912 | bytes 5242880 | tf_op jit(solution)/shard_map/add_product/pallas_call | solution.py:273
  55.0 2.0 %collective-permute-start.13 = (bf16[1,2,128,1024]{3,2,1,0:T(8,128)(2,1)S(1)}, bf16[1,2,128,1024]{3,2,1,0:T(8,128)(2,1)S(1)}, u32[]{:S(2)}, u32[]{:S(2)}) collective-permute-start(bf16[1,2,128,1024]{3,2,1,0:T(8,128)(2,1)S(1)} %collective-permute-done.5.refs_2_), channel_id=1, source_target_pairs={{0,1},{2,0},{4,2},{6,4},{7,6},{5,7},{3,5},{1,3},{8,9},{10,8},{12,1... | collective-permute-start | bytes 1572872 | tf_op jit(solution)/shard_map/ppermute | solution.py:326
  57.1 1.9 %collective-permute-start.15 = (bf16[1,1,64,1024]{3,2,1,0:T(8,128)(2,1)S(1)}, bf16[1,1,64,1024]{3,2,1,0:T(8,128)(2,1)S(1)}, u32[]{:S(2)}, u32[]{:S(2)}) collective-permute-start(bf16[1,1,64,1024]{3,2,1,0:T(8,128)(2,1)S(1)} %slice.31), channel_id=1, source_target_pairs={{0,1},{2,0},{4,2},{6,4},{7,6},{5,7},{3,5},{1,3},{8,9},{10,8},{12,1... | collective-permute-start | bytes 393224 | tf_op jit(solution)/shard_map/ppermute | solution.py:326
  59.1 11.6 %add_product.9.refs_3_ = f32[1024,128]{1,0:T(8,128)S(1)} custom-call(s32[8]{0:T(128)S(1)} %dynamic-slice_bitcast_fusion.source, bf16[1,2,128,1024]{3,2,1,0:T(8,128)(2,1)S(1)} %bitcast.16, bf16[1,2,128,1024]{3,2,1,0:T(8,128)(2,1)S(1)} %collective-permute-done.4.refs_1_, bf16[1,2,128,1024]{3,2,1,0:T(8,128)(2,1)S(1)} %collective-permute-done.5.refs_2_, ...), custom_call_target="tpu_custom_call" | custom-call | flops 1610612736 | bytes 13631488 | tf_op jit(solution)/shard_map/add_product/pallas_call | solution.py:273
  71.8 2.7 %add_product.10.refs_3_ = f32[1024,128]{1,0:T(8,128)S(1)} custom-call(s32[8]{0:T(128)S(1)} %dynamic-slice_bitcast_fusion.source, bf16[1,1,64,1024]{3,2,1,0:T(8,128)(2,1)S(1)} %collective-permute-done.14.refs_0_, bf16[1,1,64,1024]{3,2,1,0:T(8,128)(2,1)S(1)} %collective-permute-done.15.refs_1_, bf16[3,1024,8192]{2,1,0:T(8,128)(2,1)} %refs_2_.9, ...), custom_call_target="tpu_custom_call" | custom-call | flops 268435456 | bytes 3145728 | tf_op jit(solution)/shard_map/add_product/pallas_call | solution.py:273
  74.5 1.8 %collective-permute-start.16 = (bf16[1,2,128,1024]{3,2,1,0:T(8,128)(2,1)S(1)}, bf16[1,2,128,1024]{3,2,1,0:T(8,128)(2,1)S(1)}, u32[]{:S(2)}, u32[]{:S(2)}) collective-permute-start(bf16[1,2,128,1024]{3,2,1,0:T(8,128)(2,1)S(1)} %collective-permute-done.12.refs_0_), channel_id=1, source_target_pairs={{0,2},{2,4},{4,6},{6,7},{7,5},{5,3},{3,1},{1,0},{8,10},{10,12},{12... | collective-permute-start | bytes 1572872 | tf_op jit(solution)/shard_map/ppermute | solution.py:323
  76.6 1.3 %collective-permute-done.20 = f32[17,1024]{1,0:T(8,128)S(1)} collective-permute-done((f32[17,1024]{1,0:T(8,128)S(1)}, f32[17,1024]{1,0:T(8,128)S(1)}, u32[]{:S(2)}, u32[]{:S(2)}) %collective-permute-start.20) | collective-permute-done | bytes 69664 | tf_op jit(solution)/shard_map/ppermute | solution.py:362
  78.0 4.8 %collective-permute-done.21 = f32[17,1024]{1,0:T(8,128)S(1)} collective-permute-done((f32[17,1024]{1,0:T(8,128)S(1)}, f32[17,1024]{1,0:T(8,128)S(1)}, u32[]{:S(2)}, u32[]{:S(2)}) %collective-permute-start.21) | collective-permute-done | bytes 69664 | tf_op jit(solution)/shard_map/ppermute | solution.py:362
  83.4 8.0 %add_product.11.refs_3_ = f32[1024,128]{1,0:T(8,128)S(1)} custom-call(s32[8]{0:T(128)S(1)} %dynamic-slice_bitcast_fusion.source, bf16[1,2,128,1024]{3,2,1,0:T(8,128)(2,1)S(1)} %collective-permute-done.12.refs_0_, bf16[1,2,128,1024]{3,2,1,0:T(8,128)(2,1)S(1)} %collective-permute-done.13.refs_1_, bf16[3,1024,8192]{2,1,0:T(8,128)(2,1)} %refs_2_.9, ...), custom_call_target="tpu_custom_call" | custom-call | flops 1073741824 | bytes 9437184 | tf_op jit(solution)/shard_map/add_product/pallas_call | solution.py:273
  91.6 1.8 %collective-permute-start.18 = (bf16[1,1,128,1024]{3,2,1,0:T(8,128)(2,1)S(1)}, bf16[1,1,128,1024]{3,2,1,0:T(8,128)(2,1)S(1)}, u32[]{:S(2)}, u32[]{:S(2)}) collective-permute-start(bf16[1,1,128,1024]{3,2,1,0:T(8,128)(2,1)S(1)} %slice.32), channel_id=1, source_target_pairs={{0,2},{2,4},{4,6},{6,7},{7,5},{5,3},{3,1},{1,0},{8,10},{10,12},{12... | collective-permute-start | bytes 786440 | tf_op jit(solution)/shard_map/ppermute | solution.py:323
  94.3 8.0 %add_product.12.refs_3_ = f32[1024,128]{1,0:T(8,128)S(1)} custom-call(s32[8]{0:T(128)S(1)} %dynamic-slice_bitcast_fusion.source, bf16[1,2,128,1024]{3,2,1,0:T(8,128)(2,1)S(1)} %collective-permute-done.16.refs_0_, bf16[1,2,128,1024]{3,2,1,0:T(8,128)(2,1)S(1)} %collective-permute-done.17.refs_1_, bf16[3,1024,8192]{2,1,0:T(8,128)(2,1)} %refs_2_.9, ...), custom_call_target="tpu_custom_call" | custom-call | flops 1073741824 | bytes 9437184 | tf_op jit(solution)/shard_map/add_product/pallas_call | solution.py:273
  102.3 5.5 %add_product.13 = f32[128,1024]{1,0:T(8,128)} custom-call(s32[8]{0:T(128)S(1)} %dynamic-slice_bitcast_fusion.source, bf16[1,1,128,1024]{3,2,1,0:T(8,128)(2,1)S(1)} %collective-permute-done.18.refs_0_, bf16[1,1,128,1024]{3,2,1,0:T(8,128)(2,1)S(1)} %collective-permute-done.19.refs_1_, bf16[3,1024,8192]{2,1,0:T(8,128)(2,1)} %refs_2_.9, ...), custom_call_target="tpu_custom_call" | custom-call | flops 536870912 | bytes 5242880 | tf_op jit(solution)/shard_map/add_product/pallas_call | solution.py:273
  (62 shorter events, 16.1 us)
Async XLA Ops:
  3.1 3.1 %collective-permute-start = (f32[10,1024]{1,0:T(8,128)S(1)}, f32[10,1024]{1,0:T(8,128)S(1)}, u32[]{:S(2)}, u32[]{:S(2)}) collective-permute-start(f32[10,1024]{1,0:T(8,128)S(1)} %pad_maximum_fusion), channel_id=1, source_target_pairs={{8,0},{16,8},{24,16},{9,1},{17,9},{25,17},{10,2},{18,10},{26,18},{... | collective-permute-start | bytes 122888 | tf_op jit(solution)/shard_map/ppermute | solution.py:335
  11.6 11.8 %copy-start.3 = (f32[128,1024]{1,0:T(8,128)S(1)}, f32[128,1024]{1,0:T(8,128)}, u32[]{:S(2)}) copy-start(f32[128,1024]{1,0:T(8,128)} %conv.3) | copy-start | bytes 1572868
  11.7 11.8 %copy-start.6 = (f32[1024,16]{0,1:T(8,128)S(1)}, f32[1024,16]{0,1:T(8,128)}, u32[]{:S(2)}) copy-start(f32[1024,16]{0,1:T(8,128)} %param.13) | copy-start | bytes 196612
  11.7 8.4 %collective-permute-start.9 = (bf16[1,1,128,1024]{3,2,1,0:T(8,128)(2,1)S(1)}, bf16[1,1,128,1024]{3,2,1,0:T(8,128)(2,1)S(1)}, u32[]{:S(2)}, u32[]{:S(2)}) collective-permute-start(bf16[1,1,128,1024]{3,2,1,0:T(8,128)(2,1)S(1)} %bitcast.11), channel_id=1, source_target_pairs={{0,1},{2,0},{4,2},{6,4},{7,6},{5,7},{3,5},{1,3},{8,9},{10,8},{12,1... | collective-permute-start | bytes 786440 | tf_op jit(solution)/shard_map/ppermute | solution.py:326
  14.7 8.1 %collective-permute-start.6 = (bf16[1,1,128,1024]{3,2,1,0:T(8,128)(2,1)S(1)}, bf16[1,1,128,1024]{3,2,1,0:T(8,128)(2,1)S(1)}, u32[]{:S(2)}, u32[]{:S(2)}) collective-permute-start(bf16[1,1,128,1024]{3,2,1,0:T(8,128)(2,1)S(1)} %bitcast.12), channel_id=1, source_target_pairs={{0,2},{2,4},{4,6},{6,7},{7,5},{5,3},{3,1},{1,0},{8,10},{10,12},{12... | collective-permute-start | bytes 786440 | tf_op jit(solution)/shard_map/ppermute | solution.py:323
  15.6 7.2 %collective-permute-start.3 = (f32[144,128]{1,0:T(8,128)S(1)}, f32[144,128]{1,0:T(8,128)S(1)}, u32[]{:S(2)}, u32[]{:S(2)}) collective-permute-start(f32[144,128]{1,0:T(8,128)S(1)} %summary.1), channel_id=1, source_target_pairs={{24,0},{25,1},{26,2},{27,3},{28,4},{29,5},{30,6},{31,7}} | collective-permute-start | bytes 221192 | tf_op jit(solution)/shard_map/ppermute | solution.py:335
  16.9 6.5 %collective-permute-start.2 = (f32[144,128]{1,0:T(8,128)S(1)}, f32[144,128]{1,0:T(8,128)S(1)}, u32[]{:S(2)}, u32[]{:S(2)}) collective-permute-start(f32[144,128]{1,0:T(8,128)S(1)} %summary.1), channel_id=1, source_target_pairs={{16,0},{24,8},{17,1},{25,9},{18,2},{26,10},{19,3},{27,11},{20,4},{... | collective-permute-start | bytes 221192 | tf_op jit(solution)/shard_map/ppermute | solution.py:335
  18.2 5.2 %collective-permute-start.1 = (f32[144,128]{1,0:T(8,128)S(1)}, f32[144,128]{1,0:T(8,128)S(1)}, u32[]{:S(2)}, u32[]{:S(2)}) collective-permute-start(f32[144,128]{1,0:T(8,128)S(1)} %summary.1), channel_id=1, source_target_pairs={{8,0},{16,8},{24,16},{9,1},{17,9},{25,17},{10,2},{18,10},{26,18},{... | collective-permute-start | bytes 221192 | tf_op jit(solution)/shard_map/ppermute | solution.py:335
  20.0 10.3 %collective-permute-start.10 = (bf16[1,1,128,1024]{3,2,1,0:T(8,128)(2,1)S(1)}, bf16[1,1,128,1024]{3,2,1,0:T(8,128)(2,1)S(1)}, u32[]{:S(2)}, u32[]{:S(2)}) collective-permute-start(bf16[1,1,128,1024]{3,2,1,0:T(8,128)(2,1)S(1)} %collective-permute-done.9.refs_2_), channel_id=1, source_target_pairs={{0,1},{2,0},{4,2},{6,4},{7,6},{5,7},{3,5},{1,3},{8,9},{10,8},{12,1... | collective-permute-start | bytes 786440 | tf_op jit(solution)/shard_map/ppermute | solution.py:326
  22.8 9.1 %collective-permute-start.7 = (bf16[1,1,128,1024]{3,2,1,0:T(8,128)(2,1)S(1)}, bf16[1,1,128,1024]{3,2,1,0:T(8,128)(2,1)S(1)}, u32[]{:S(2)}, u32[]{:S(2)}) collective-permute-start(bf16[1,1,128,1024]{3,2,1,0:T(8,128)(2,1)S(1)} %collective-permute-done.6.refs_1_), channel_id=1, source_target_pairs={{0,2},{2,4},{4,6},{6,7},{7,5},{5,3},{3,1},{1,0},{8,10},{10,12},{12... | collective-permute-start | bytes 786440 | tf_op jit(solution)/shard_map/ppermute | solution.py:323
  28.1 26.8 %collective-permute-start.5 = (bf16[1,2,128,1024]{3,2,1,0:T(8,128)(2,1)S(1)}, bf16[1,2,128,1024]{3,2,1,0:T(8,128)(2,1)S(1)}, u32[]{:S(2)}, u32[]{:S(2)}) collective-permute-start(bf16[1,2,128,1024]{3,2,1,0:T(8,128)(2,1)S(1)} %bitcast.14), channel_id=1, source_target_pairs={{0,1},{2,0},{4,2},{6,4},{7,6},{5,7},{3,5},{1,3},{8,9},{10,8},{12,1... | collective-permute-start | bytes 1572872 | tf_op jit(solution)/shard_map/ppermute | solution.py:326
  30.3 24.6 %collective-permute-start.4 = (bf16[1,2,128,1024]{3,2,1,0:T(8,128)(2,1)S(1)}, bf16[1,2,128,1024]{3,2,1,0:T(8,128)(2,1)S(1)}, u32[]{:S(2)}, u32[]{:S(2)}) collective-permute-start(bf16[1,2,128,1024]{3,2,1,0:T(8,128)(2,1)S(1)} %bitcast.15), channel_id=1, source_target_pairs={{0,2},{2,4},{4,6},{6,7},{7,5},{5,3},{3,1},{1,0},{8,10},{10,12},{12... | collective-permute-start | bytes 1572872 | tf_op jit(solution)/shard_map/ppermute | solution.py:323
  31.9 18.6 %collective-permute-start.8 = (bf16[1,1,128,1024]{3,2,1,0:T(8,128)(2,1)S(1)}, bf16[1,1,128,1024]{3,2,1,0:T(8,128)(2,1)S(1)}, u32[]{:S(2)}, u32[]{:S(2)}) collective-permute-start(bf16[1,1,128,1024]{3,2,1,0:T(8,128)(2,1)S(1)} %collective-permute-done.7.refs_3_), channel_id=1, source_target_pairs={{0,2},{2,4},{4,6},{6,7},{7,5},{5,3},{3,1},{1,0},{8,10},{10,12},{12... | collective-permute-start | bytes 786440 | tf_op jit(solution)/shard_map/ppermute | solution.py:323
  32.4 18.0 %collective-permute-start.11 = (bf16[1,1,128,1024]{3,2,1,0:T(8,128)(2,1)S(1)}, bf16[1,1,128,1024]{3,2,1,0:T(8,128)(2,1)S(1)}, u32[]{:S(2)}, u32[]{:S(2)}) collective-permute-start(bf16[1,1,128,1024]{3,2,1,0:T(8,128)(2,1)S(1)} %collective-permute-done.10.refs_4_), channel_id=1, source_target_pairs={{0,1},{2,0},{4,2},{6,4},{7,6},{5,7},{3,5},{1,3},{8,9},{10,8},{12,1... | collective-permute-start | bytes 786440 | tf_op jit(solution)/shard_map/ppermute | solution.py:326
  54.9 19.6 %collective-permute-start.12 = (bf16[1,2,128,1024]{3,2,1,0:T(8,128)(2,1)S(1)}, bf16[1,2,128,1024]{3,2,1,0:T(8,128)(2,1)S(1)}, u32[]{:S(2)}, u32[]{:S(2)}) collective-permute-start(bf16[1,2,128,1024]{3,2,1,0:T(8,128)(2,1)S(1)} %collective-permute-done.4.refs_1_), channel_id=1, source_target_pairs={{0,2},{2,4},{4,6},{6,7},{7,5},{5,3},{3,1},{1,0},{8,10},{10,12},{12... | collective-permute-start | bytes 1572872 | tf_op jit(solution)/shard_map/ppermute | solution.py:323
  55.0 19.5 %collective-permute-start.13 = (bf16[1,2,128,1024]{3,2,1,0:T(8,128)(2,1)S(1)}, bf16[1,2,128,1024]{3,2,1,0:T(8,128)(2,1)S(1)}, u32[]{:S(2)}, u32[]{:S(2)}) collective-permute-start(bf16[1,2,128,1024]{3,2,1,0:T(8,128)(2,1)S(1)} %collective-permute-done.5.refs_2_), channel_id=1, source_target_pairs={{0,1},{2,0},{4,2},{6,4},{7,6},{5,7},{3,5},{1,3},{8,9},{10,8},{12,1... | collective-permute-start | bytes 1572872 | tf_op jit(solution)/shard_map/ppermute | solution.py:326
  57.0 14.7 %collective-permute-start.14 = (bf16[1,1,64,1024]{3,2,1,0:T(8,128)(2,1)S(1)}, bf16[1,1,64,1024]{3,2,1,0:T(8,128)(2,1)S(1)}, u32[]{:S(2)}, u32[]{:S(2)}) collective-permute-start(bf16[1,1,64,1024]{3,2,1,0:T(8,128)(2,1)S(1)} %slice.30), channel_id=1, source_target_pairs={{0,2},{2,4},{4,6},{6,7},{7,5},{5,3},{3,1},{1,0},{8,10},{10,12},{12... | collective-permute-start | bytes 393224 | tf_op jit(solution)/shard_map/ppermute | solution.py:323
  57.1 14.7 %collective-permute-start.15 = (bf16[1,1,64,1024]{3,2,1,0:T(8,128)(2,1)S(1)}, bf16[1,1,64,1024]{3,2,1,0:T(8,128)(2,1)S(1)}, u32[]{:S(2)}, u32[]{:S(2)}) collective-permute-start(bf16[1,1,64,1024]{3,2,1,0:T(8,128)(2,1)S(1)} %slice.31), channel_id=1, source_target_pairs={{0,1},{2,0},{4,2},{6,4},{7,6},{5,7},{3,5},{1,3},{8,9},{10,8},{12,1... | collective-permute-start | bytes 393224 | tf_op jit(solution)/shard_map/ppermute | solution.py:326
  74.5 17.0 %collective-permute-start.16 = (bf16[1,2,128,1024]{3,2,1,0:T(8,128)(2,1)S(1)}, bf16[1,2,128,1024]{3,2,1,0:T(8,128)(2,1)S(1)}, u32[]{:S(2)}, u32[]{:S(2)}) collective-permute-start(bf16[1,2,128,1024]{3,2,1,0:T(8,128)(2,1)S(1)} %collective-permute-done.12.refs_0_), channel_id=1, source_target_pairs={{0,2},{2,4},{4,6},{6,7},{7,5},{5,3},{3,1},{1,0},{8,10},{10,12},{12... | collective-permute-start | bytes 1572872 | tf_op jit(solution)/shard_map/ppermute | solution.py:323
  76.3 15.2 %collective-permute-start.17 = (bf16[1,2,128,1024]{3,2,1,0:T(8,128)(2,1)S(1)}, bf16[1,2,128,1024]{3,2,1,0:T(8,128)(2,1)S(1)}, u32[]{:S(2)}, u32[]{:S(2)}) collective-permute-start(bf16[1,2,128,1024]{3,2,1,0:T(8,128)(2,1)S(1)} %collective-permute-done.13.refs_1_), channel_id=1, source_target_pairs={{0,1},{2,0},{4,2},{6,4},{7,6},{5,7},{3,5},{1,3},{8,9},{10,8},{12,1... | collective-permute-start | bytes 1572872 | tf_op jit(solution)/shard_map/ppermute | solution.py:326
  76.6 1.3 %collective-permute-start.20 = (f32[17,1024]{1,0:T(8,128)S(1)}, f32[17,1024]{1,0:T(8,128)S(1)}, u32[]{:S(2)}, u32[]{:S(2)}) collective-permute-start(f32[17,1024]{1,0:T(8,128)S(1)} %get-tuple-element.47), channel_id=1, source_target_pairs={{0,8},{8,0},{16,24},{24,16},{1,9},{9,1},{17,25},{25,17},{2,10},{10... | collective-permute-start | bytes 208904 | tf_op jit(solution)/shard_map/ppermute | solution.py:362
  77.9 4.9 %collective-permute-start.21 = (f32[17,1024]{1,0:T(8,128)S(1)}, f32[17,1024]{1,0:T(8,128)S(1)}, u32[]{:S(2)}, u32[]{:S(2)}) collective-permute-start(f32[17,1024]{1,0:T(8,128)S(1)} %add.11), channel_id=1, source_target_pairs={{0,16},{8,24},{16,0},{24,8},{1,17},{9,25},{17,1},{25,9},{2,18},{10... | collective-permute-start | bytes 208904 | tf_op jit(solution)/shard_map/ppermute | solution.py:362
  91.6 10.7 %collective-permute-start.18 = (bf16[1,1,128,1024]{3,2,1,0:T(8,128)(2,1)S(1)}, bf16[1,1,128,1024]{3,2,1,0:T(8,128)(2,1)S(1)}, u32[]{:S(2)}, u32[]{:S(2)}) collective-permute-start(bf16[1,1,128,1024]{3,2,1,0:T(8,128)(2,1)S(1)} %slice.32), channel_id=1, source_target_pairs={{0,2},{2,4},{4,6},{6,7},{7,5},{5,3},{3,1},{1,0},{8,10},{10,12},{12... | collective-permute-start | bytes 786440 | tf_op jit(solution)/shard_map/ppermute | solution.py:323
  93.3 9.0 %collective-permute-start.19 = (bf16[1,1,128,1024]{3,2,1,0:T(8,128)(2,1)S(1)}, bf16[1,1,128,1024]{3,2,1,0:T(8,128)(2,1)S(1)}, u32[]{:S(2)}, u32[]{:S(2)}) collective-permute-start(bf16[1,1,128,1024]{3,2,1,0:T(8,128)(2,1)S(1)} %slice.33), channel_id=1, source_target_pairs={{0,1},{2,0},{4,2},{6,4},{7,6},{5,7},{3,5},{1,3},{8,9},{10,8},{12,1... | collective-permute-start | bytes 786440 | tf_op jit(solution)/shard_map/ppermute | solution.py:326
  (7 other events, 28.5 us)

commit v3 on v2

v3 whole, which is shorter than its diff:
```python
import functools

import jax
import jax.numpy as jnp
from jax import lax
from jax.experimental import pallas as pl
from jax.experimental.pallas import tpu as pltpu
from jax.sharding import PartitionSpec as P

LANES = 128
RING = 8
VMEM = 40 * 1024 * 1024
F32 = jnp.float32
BF16 = jnp.bfloat16


def whole():
    return pl.BlockSpec(memory_space=pltpu.VMEM)


def in_hbm():
    return pl.BlockSpec(memory_space=pltpu.HBM)


def params():
    return pltpu.CompilerParams(vmem_limit_bytes=VMEM)


def cost(flops, size):
    return pl.CostEstimate(flops=flops, bytes_accessed=size, transcendentals=0)


def by_row(values, out, fold, base=0):
    for j in range(fold):
        out[pl.ds(base * fold + j, values.shape[0], stride=fold), :] = values[:, j * LANES : (j + 1) * LANES]


def front_kernel(features, saved_conv, out_grad, short_filter, residue, rate, bias, *refs):
    feat, conv, og, filt, bias_in, dec, far, res, sig, own, res_in, rate_in, sems = refs
    tokens, channels = og.shape
    modes = rate_in.shape[0]
    fold = channels // LANES
    moves = [
        pltpu.make_async_copy(source, target, sems.at[n])
        for n, (source, target) in enumerate((
            (rate, rate_in),
            (out_grad, og),
            (features, feat),
            (saved_conv, conv),
            (short_filter, filt),
            (residue, res_in),
            (bias, bias_in),
        ))
    ]
    for move in moves:
        move.start()
    moves[0].wait()
    by_row(jnp.exp(-rate_in[...]), dec, fold)
    by_row(jnp.exp(-(tokens - 2) * rate_in[...]), far, fold)
    moves[1].wait()
    moves[2].wait()
    for j in range(fold):
        lanes = slice(j * LANES, (j + 1) * LANES)
        sig[pl.ds(j, tokens, stride=fold), :] = og[:, lanes] * feat[0, :, lanes]
    decay = [dec[m * fold : (m + 1) * fold, :] for m in range(modes)]

    def step(i, states):
        row = sig[pl.ds((tokens - 1 - i) * fold, fold), :]
        return tuple(row + d * s for d, s in zip(decay, states))

    zero = tuple(jnp.zeros((fold, LANES), F32) for _ in range(modes))
    states = lax.fori_loop(0, tokens - 2, step, zero, unroll=6)
    for m in range(modes):
        own[m * fold : (m + 1) * fold, :] = states[m]
    own[modes * fold : (modes + 2) * fold, :] = sig[0 : 2 * fold, :]
    for n in range(3):
        by_row(feat[n, 0:2, :], own, fold, modes + 2 + 2 * n)
    by_row(og[0:2, :], own, fold, modes + 10)
    for n in range(3, 7):
        moves[n].wait()
    by_row(conv[0:2, :], own, fold, modes + 8)
    by_row(res_in[...], res, fold)


def front(features, saved_conv, out_grad, short_filter, residue, rate, bias):
    tokens, channels = out_grad.shape
    modes = rate.shape[0]
    fold = channels // LANES
    inputs = (features, saved_conv, out_grad, short_filter, residue, rate, bias)
    by_mode = pltpu.VMEM((modes * fold, LANES), F32)
    return pl.pallas_call(
        front_kernel,
        in_specs=[in_hbm()] * 7,
        out_specs=[whole()] * 10,
        out_shape=[pltpu.VMEM(a.shape, F32) for a in (*inputs[:4], bias)]
        + [by_mode] * 3
        + [pltpu.VMEM((tokens * fold, LANES), F32), pltpu.VMEM(((modes + 12) * fold, LANES), F32)],
        scratch_shapes=[pltpu.VMEM(rate.shape, F32)] * 2 + [pltpu.SemaphoreType.DMA((7,))],
        compiler_params=params(),
        cost_estimate=cost(4 * tokens * channels * modes, 20 * tokens * channels),
        name="front",
    )(*(pltpu.with_memory_space_constraint(a, pltpu.HBM) for a in inputs))


def tapped(ext, taps, lanes, tokens):
    total = taps[0][:, lanes] * ext[0:tokens, lanes]
    total = total + taps[1][:, lanes] * ext[1 : tokens + 1, lanes]
    return total + taps[2][:, lanes] * ext[2 : tokens + 2, lanes]


def rim_rows(later, which, j, fold):
    modes = later.shape[0] // fold - 12
    return later[pl.ds((modes + 2 + 2 * which) * fold + j, 2, stride=fold), :]


def gate_gradient(feat, conv, og, bias, later, ext):
    tokens, channels = og.shape
    fold = channels // LANES
    for j in range(fold):
        lanes = slice(j * LANES, (j + 1) * LANES)
        product = feat[1, :, lanes] * feat[2, :, lanes]
        ext[0:tokens, lanes] = og[:, lanes] * (conv[:, lanes] + bias[:, lanes] * product)
        key, value, held, cotangent = (rim_rows(later, n, j, fold) for n in (1, 2, 3, 4))
        ext[tokens : tokens + 2, lanes] = cotangent * (held + bias[:, lanes] * (key * value))


def gate_kernel(feat, conv, og, filt, bias, later, rounded, ext):
    tokens, channels = og.shape
    taps = [filt[0, j : j + 1, :] for j in range(3)]
    gate_gradient(feat, conv, og, bias, later, ext)
    for j in range(channels // LANES):
        lanes = slice(j * LANES, (j + 1) * LANES)
        rounded[0, :, lanes] = tapped(ext, taps, lanes, tokens).astype(BF16)


def gate_stream(feat, conv, og, filt, bias, later):
    tokens, channels = og.shape
    return pl.pallas_call(
        gate_kernel,
        in_specs=[whole()] * 6,
        out_specs=whole(),
        out_shape=jax.ShapeDtypeStruct((1, tokens, channels), BF16),
        scratch_shapes=[pltpu.VMEM((tokens + 8, channels), F32)],
        compiler_params=params(),
        cost_estimate=cost(12 * tokens * channels, 26 * tokens * channels),
        name="gate_stream",
    )(feat, conv, og, filt, bias, later)


def product_gradients(feat, gp, later, exts):
    tokens, channels = feat.shape[1:]
    fold = channels // LANES
    for j in range(fold):
        lanes = slice(j * LANES, (j + 1) * LANES)
        g = gp[pl.ds(j, tokens, stride=fold), :]
        rim = gp[pl.ds(tokens * fold + j, 2, stride=fold), :]
        for ext, n in zip(exts, (2, 1)):
            ext[0:tokens, lanes] = g * feat[n, :, lanes]
            ext[tokens : tokens + 2, lanes] = rim * rim_rows(later, n, j, fold)


def gradients_kernel(feat, conv, og, filt, bias, later, gp, out, first, second, third, ready, sems):
    tokens, channels = og.shape
    gate_gradient(feat, conv, og, bias, later, first)
    product_gradients(feat, gp, later, (second, third))
    moves = []
    for p, ext in enumerate((first, second, third)):
        taps = [filt[p, j : j + 1, :] for j in range(3)]
        for j in range(channels // LANES):
            lanes = slice(j * LANES, (j + 1) * LANES)
            ready[p, :, lanes] = tapped(ext, taps, lanes, tokens)
        moves.append(pltpu.make_async_copy(ready.at[p], out.at[p], sems.at[p]))
        moves[-1].start()
    for move in moves:
        move.wait()


def gradients(feat, conv, og, filt, bias, later, gp):
    tokens, channels = og.shape
    return pl.pallas_call(
        gradients_kernel,
        in_specs=[whole()] * 7,
        out_specs=in_hbm(),
        out_shape=jax.ShapeDtypeStruct((3, tokens, channels), F32),
        scratch_shapes=[pltpu.VMEM((tokens + 8, channels), F32)] * 3
        + [pltpu.VMEM((3, tokens, channels), F32), pltpu.SemaphoreType.DMA((3,))],
        compiler_params=params(),
        cost_estimate=cost(30 * tokens * channels, 40 * tokens * channels),
        name="gradients",
    )(feat, conv, og, filt, bias, later, gp)


def state_kernel(later, feat, og, filt, dec, far, res, bias, sig, *refs):
    payloads = refs[:later]
    rounded, sums, gp, acc, prod, *exts = refs[later:]
    tokens, channels = og.shape
    fold = channels // LANES
    modes = dec.shape[0] // fold
    for j in range(fold):
        lanes = slice(j * LANES, (j + 1) * LANES)
        p = feat[1, :, lanes] * feat[2, :, lanes]
        prod[pl.ds(j, tokens, stride=fold), :] = p
        s = og[:, lanes] * feat[0, :, lanes]
        sums[modes : modes + 1, lanes] = jnp.sum(s * p, axis=0, keepdims=True)

    def rows(ref, at):
        return ref[at * fold : (at + 1) * fold, :]

    direct = bias[...]
    group = 8
    for low in range(0, modes, group):
        chosen = range(low, min(low + group, modes))
        decay = [rows(dec, m) for m in chosen]
        weight = [rows(res, m) for m in chosen]
        reach = [rows(far, m) for m in chosen]
        state = [jnp.zeros((fold, LANES), F32) for _ in chosen]
        for n, payload in enumerate(reversed(payloads)):
            block_end = [rows(payload, m) + f * s for m, f, s in zip(chosen, reach, state)]
            if n < later - 1:
                s0, s1 = rows(payload, modes), rows(payload, modes + 1)
                state = [s0 + d * (s1 + d * s) for d, s in zip(decay, block_end)]
            else:
                state = block_end

        def corr(state, weight=weight):
            terms = [w * s for w, s in zip(weight, state)]
            while len(terms) > 1:
                terms = [a + b for a, b in zip(terms[::2], terms[1::2])] + terms[len(terms) // 2 * 2 :]
            return terms[0]

        def put(at, row, state, low=low, corr=corr):
            here = pl.ds(at * fold, fold)
            if low == 0:
                gp[here, :] = corr(state) + direct * row
            else:
                gp[here, :] = gp[here, :] + corr(state)

        for n in (1, 0):
            row = rows(payloads[0], modes + n)
            state = [row + d * s for d, s in zip(decay, state)]
            put(tokens + n, row, state)

        def step(i, carry, decay=decay, put=put):
            state, total = carry
            at = tokens - 1 - i
            row = sig[pl.ds(at * fold, fold), :]
            other = prod[pl.ds(at * fold, fold), :]
            state = [row + d * s for d, s in zip(decay, state)]
            total = [a + other * s for a, s in zip(total, state)]
            put(at, row, state)
            return state, total

        zero = [jnp.zeros((fold, LANES), F32) for _ in chosen]
        state, total = lax.fori_loop(0, tokens, step, (state, zero), unroll=4)
        for m, a in zip(chosen, total):
            acc[m * fold : (m + 1) * fold, :] = a

    product_gradients(feat, gp, payloads[0], exts)
    for p, ext in enumerate(exts):
        taps = [filt[p + 1, j : j + 1, :] for j in range(3)]
        for j in range(fold):
            lanes = slice(j * LANES, (j + 1) * LANES)
            rounded[p, :, lanes] = tapped(ext, taps, lanes, tokens).astype(BF16)
    for j in range(fold):
        sums[0:modes, j * LANES : (j + 1) * LANES] = acc[pl.ds(j, modes, stride=fold), :]


def state_streams(feat, og, filt, dec, far, res, bias, sig, payloads):
    tokens, channels = og.shape
    fold = channels // LANES
    modes = dec.shape[0] // fold
    return pl.pallas_call(
        functools.partial(state_kernel, len(payloads)),
        in_specs=[whole()] * (8 + len(payloads)),
        out_specs=[whole()] * 3,
        out_shape=[
            jax.ShapeDtypeStruct((2, tokens, channels), BF16),
            jax.ShapeDtypeStruct((modes + 1, channels), F32),
            jax.ShapeDtypeStruct(((tokens + 2) * fold, LANES), F32),
        ],
        scratch_shapes=[pltpu.VMEM((modes * fold, LANES), F32), pltpu.VMEM((tokens * fold, LANES), F32)]
        + [pltpu.VMEM((tokens + 8, channels), F32)] * 2,
        compiler_params=params(),
        cost_estimate=cost(8 * tokens * channels * modes, 40 * tokens * channels),
        name="state_streams",
    )(feat, og, filt, dec, far, res, bias, sig, *payloads)


def product_kernel(plan, first, last, source, *refs):
    *refs, w_all, sems = refs
    *refs, out = refs
    before = None if first else refs[-1]
    w = refs[-1 - (not first)]
    features, channels = w_all.shape[1:]
    wide = min(512, features)
    moves = []
    for k, (stream, height, offset, _) in enumerate(plan):
        begin = pl.multiple_of((height * RING + source[offset]) * channels, LANES)
        for d in range(0, features, wide):
            moves.append(pltpu.make_async_copy(
                w.at[stream, pl.ds(d, wide), pl.ds(begin, channels)],
                w_all.at[k, pl.ds(d, wide)],
                sems.at[k, d // wide],
            ))
            moves[-1].start()
    totals = {}
    for k, (_, _, _, parts) in enumerate(plan):
        x = [refs[n][h, p] for n, h, p in parts]
        x = x[0] if len(x) == 1 else jnp.concatenate(x, axis=0)
        for d in range(0, features, wide):
            moves.pop(0).wait()
            rows = slice(d, d + wide)
            y = lax.dot_general(w_all[k, rows], x, (((1,), (1,)), ((), ())), preferred_element_type=F32)
            if k:
                y = y + (out[:, rows].T if last else out[rows])
            elif not first:
                y = y + before[rows]
            if last:
                out[:, rows] = y.T
            else:
                out[rows] = y


def add_product(total, pieces, sources, w_proj, last=False):
    features = w_proj.shape[1]
    arrays, plan = [], []
    for array, stream, offset in pieces:
        halves = array if isinstance(array, tuple) else (array,)
        heights, streams, _, channels = halves[0].shape
        for h in range(heights):
            for p in range(streams):
                plan.append((stream + p, h, offset, [(len(arrays) + n, h, p) for n in range(len(halves))]))
        arrays += halves
    tokens = sum(arrays[n].shape[2] for n, _, _ in plan[0][3])
    first = total is None
    return pl.pallas_call(
        functools.partial(product_kernel, plan, first, last),
        in_specs=[pl.BlockSpec(memory_space=pltpu.SMEM)]
        + [whole()] * len(arrays)
        + [in_hbm()]
        + [whole()] * (not first),
        out_specs=whole(),
        out_shape=jax.ShapeDtypeStruct((tokens, features) if last else (features, tokens), F32),
        scratch_shapes=[
            pltpu.VMEM((len(plan), features, channels), BF16),
            pltpu.SemaphoreType.DMA((len(plan), max(1, features // 512))),
        ],
        compiler_params=params(),
        cost_estimate=cost(
            2 * tokens * features * channels * len(plan),
            2 * features * channels * len(plan) + 8 * tokens * features,
        ),
        name="add_product",
    )(sources, *arrays, w_proj, *([] if first else [total]))


def ring_order(size):
    return list(range(0, size, 2)) + list(range(size - 1 - size % 2, 0, -2))


def after(array, *others):
    return lax.optimization_barrier((array, *others))[0]


def body(features, saved_conv, out_grad, short_filter, residue, rate, bias, w_proj):
    tokens, channels = out_grad.shape
    modes = rate.shape[1]
    blocks = lax.axis_size("ctx")
    groups = lax.axis_size("chan")
    ring = min(groups, RING)
    heights = groups // ring

    order = ring_order(ring)
    place = [order.index(i) for i in range(ring)]
    table = jnp.array([[order[(place[i] + d) % ring] for d in range(ring)] for i in range(ring)], jnp.int32)
    sources = lax.dynamic_index_in_dim(table, lax.rem(lax.axis_index("chan"), ring), 0, False)
    pairs = {
        by: [
            (h * ring + order[i], h * ring + order[(i + by) % ring])
            for h in range(heights)
            for i in range(ring)
        ]
        for by in (1, -1)
    }

    def up(x):
        return lax.ppermute(x, "chan", pairs[1])

    def down(x):
        return lax.ppermute(x, "chan", pairs[-1])

    def stacked(block):
        if heights == 1:
            return block[None]
        groups = [[h * ring + i for h in range(heights)] for i in range(ring)]
        return lax.all_gather(block, "chan", axis_index_groups=groups)

    def from_later(array, by):
        return lax.ppermute(array, "ctx", [(i, i - by) for i in range(by, blocks)])

    fold = channels // LANES
    feat, conv, og, filt, bias_row, dec, far, res, sig, own = front(
        features, saved_conv, out_grad, short_filter, residue.T, rate.T, bias[None]
    )
    payloads = [from_later(own, by) for by in range(1, min(3, blocks))]
    gate = gate_stream(feat, conv, og, filt, bias_row, payloads[0])
    own, gate = lax.optimization_barrier((own, gate))
    payloads += [from_later(own, by) for by in range(3, blocks)]
    a0 = stacked(gate)
    a1, z1 = up(a0), down(a0)
    rounds, sums, gp = state_streams(
        feat, og, filt, dec, far, res, bias_row.reshape(fold, LANES), sig, payloads
    )
    b0 = stacked(rounds)
    half = tokens // 2
    back = ring // 2

    b1, y1 = up(b0), down(b0)
    a1, z1, b0 = lax.optimization_barrier((a1, z1, b0))
    a2, z2 = up(a1), down(z1)
    total = add_product(
        None, [(a0, 0, 0), (b0, 1, 0), (a1, 0, ring - 1), (z1, 0, 1)], sources, w_proj
    )
    a2, z2, total = lax.optimization_barrier((a2, z2, total))
    a3, z3 = up(a2), down(z2)
    total = add_product(total, [(a2, 0, ring - 2), (z2, 0, 2)], sources, w_proj)
    gp = after(gp, total)
    grads = gradients(feat, conv, og, filt, bias_row, payloads[0], gp)
    b1, y1, total, grads = lax.optimization_barrier((b1, y1, total, grads))
    b2, y2 = up(b1), down(y1)
    total = add_product(total, [(b1, 1, ring - 1), (y1, 1, 1)], sources, w_proj)
    a3, z3, total = lax.optimization_barrier((a3, z3, total))
    tail = (up(a3[:, :, :half]), down(z3[:, :, half:]))
    total = add_product(total, [(a3, 0, ring - 3), (z3, 0, 3)], sources, w_proj)
    sums = after(sums, total)
    by = 1
    while by < blocks:
        sums = sums + lax.ppermute(sums, "ctx", [(i, i ^ by) for i in range(blocks)])
        by *= 2
    sums = sums * (tokens * blocks) ** (-0.5)
    b2, y2, total, sums = lax.optimization_barrier((b2, y2, total, sums))
    b3, y3 = up(b2), down(y2)
    total = add_product(total, [(b2, 1, ring - 2), (y2, 1, 2)], sources, w_proj)
    tail, total = lax.optimization_barrier((tail, total))
    total = add_product(total, [(tail, 0, back)], sources, w_proj)
    b3, y3, total = lax.optimization_barrier((b3, y3, total))
    b4, y4 = up(b3[:, :1]), down(y3[:, 1:])
    total = add_product(total, [(b3, 1, ring - 3), (y3, 1, 3)], sources, w_proj)
    grad_x = add_product(total, [(b4, 1, back), (y4, 2, back)], sources, w_proj, last=True)
    return (grads, grad_x, sums[:modes].T, sums[modes])


def solution(mesh):
    return jax.shard_map(
        body,
        mesh=mesh,
        in_specs=(
            P(None, "ctx", "chan"),
            P("ctx", "chan"),
            P("ctx", "chan"),
            P(None, None, "chan"),
            P("chan", None),
            P("chan", None),
            P("chan"),
            P(None, "chan", None),
        ),
        out_specs=(P(None, "ctx", "chan"), P("ctx", "chan"), P("chan", None), P("chan")),
        check_vma=False,
    )
```

time: 109 us -> 108 us (level)
  waiting for transfers between devices: 18.2 us -> 26.8 us
  local copies, waits for them, and re-layouts: 9.42 us -> 2.65 us
  starting transfers between devices: 23.4 us -> 21.5 us
    ppermute x4 -> x3, waiting for transfers between devices: 2.51 us -> 8.95 us  [from_later(): return lax.ppermute(array, 'ctx', [(i, i - by) for i in range(by, blocks)])]
    unnamed x18 -> x8, local copies, waits for them, and re-layouts: 5 us -> 0.67 us
    ppermute x8, waiting for transfers between devices: 8.87 us -> 11.4 us  [up(): return lax.ppermute(x, 'chan', pairs[1])]
    slice x3 -> x0, local copies, waits for them, and re-layouts: 2.42 us -> none  [the longest x1 0.9 us: body(): features[:, 0:2].reshape(6, channels)]
    ppermute x8, starting transfers between devices: 13.6 us -> 11.3 us  [down(): return lax.ppermute(x, 'chan', pairs[-1])]
    ppermute x8, starting transfers between devices: 4.57 us -> 6.19 us  [up(): return lax.ppermute(x, 'chan', pairs[1])]
    ppermute x4 -> x3, starting transfers between devices: 5.17 us -> 3.86 us  [from_later(): return lax.ppermute(array, 'ctx', [(i, i - by) for i in range(by, blocks)])]
    pallas_call x8 -> x10, Pallas kernels: 50.8 us -> 51.3 us  [the longest x8 47.1 us: add_product(): pl.pallas_call(functools.partial(product_kernel, plan, first, last), in_s...]
  transfers between devices with their start and end apart: 22 -> 21, of which waited for: 10 -> 8; matrix products, arithmetic and copies ran while one was open for 2% -> 2% of each run, Pallas kernels for 46% -> 44%
where the time goes in v3:
time: 108 us
  Pallas kernels  55.4 us (51%)
  waiting for transfers between devices  26.8 us (25%)
  starting transfers between devices  21.5 us (20%)
  local copies, waits for them, and re-layouts  2.65 us (2%)
  between operations  1.08 us (1%)
    pallas_call x8, Pallas kernels, add_product(): pl.pallas_call(functools.partial(product_kernel, plan, first, last), in_s...  47.1 us
    ppermute x8, waiting for transfers between devices, up(): return lax.ppermute(x, 'chan', pairs[1])  11.4 us
    ppermute x8, starting transfers between devices, down(): return lax.ppermute(x, 'chan', pairs[-1])  11.3 us
    ppermute x3, waiting for transfers between devices, from_later(): return lax.ppermute(array, 'ctx', [(i, i - by) for i in range(by, blocks)])  8.95 us
    ppermute x8, starting transfers between devices, up(): return lax.ppermute(x, 'chan', pairs[1])  6.19 us
    ppermute x2, waiting for transfers between devices, body(): lax.ppermute(sums, 'ctx', [(i, i ^ by) for i in range(blocks)])  6.13 us
    ppermute x3, starting transfers between devices, from_later(): return lax.ppermute(array, 'ctx', [(i, i - by) for i in range(by, blocks)])  3.86 us
    pallas_call x1, Pallas kernels, state_streams(): pl.pallas_call(functools.partial(state_kernel, len(payloads)), in_specs=[...  3.69 us
  transfers between devices with their start and end apart: 21, of which 8 were waited for; matrix products, arithmetic and copies ran while one was open for 2% of the time, Pallas kernels for 44%

profile of v3, /device:TPU:0, one launch (start us, length us, event | category | flops | bytes accessed | tf_op | source)
XLA Modules:
  0.0 107.5 jit_solution(10495426031059788666)
XLA Ops:
  0.6 2.5 %front.1 = (f32[3,128,1024]{2,1,0:T(8,128)S(1)}, f32[128,1024]{1,0:T(8,128)S(1)}, f32[128,1024]{1,0:T(8,128)S(1)}, f32[3,3,1024]{2,1,0:T(4,128)S(1)}, f32[1,1024...) custom-call(f32[3,128,1024]{2,1,0:T(8,128)} %features.1, ...), custom_call_target="tpu_custom_call" | custom-call | flops 8388608 | bytes 2621440 | tf_op jit(solution)/shard_map/front/pallas_call | solution.py:91
  4.4 1.9 %collective-permute-done.later.refs_0_ = f32[224,128]{1,0:T(8,128)S(1)} collective-permute-done((f32[224,128]{1,0:T(8,128)S(1)}, f32[224,128]{1,0:T(8,128)S(1)}, u32[]{:S(2)}, u32[]{:S(2)}) %collective-permute-start) | collective-permute-done | bytes 114720 | tf_op jit(solution)/shard_map/ppermute | solution.py:399
  6.7 3.0 %collective-permute-start.6 = (bf16[1,1,128,1024]{3,2,1,0:T(8,128)(2,1)S(1)}, bf16[1,1,128,1024]{3,2,1,0:T(8,128)(2,1)}, u32[]{:S(2)}, u32[]{:S(2)}) collective-permute-start(bf16[1,1,128,1024]{3,2,1,0:T(8,128)(2,1)S(1)} %bitcast.11), channel_id=1, source_target_pairs={{0,1},{2,0},{4,2},{6,4},{7,6},{5,7},{3,5},{1,3},{8,9},{10,8},{12,1... | collective-permute-start | bytes 786440 | tf_op jit(solution)/shard_map/ppermute | solution.py:390
  12.5 4.4 %collective-permute-done.1.refs_1_ = f32[224,128]{1,0:T(8,128)S(1)} collective-permute-done((f32[224,128]{1,0:T(8,128)S(1)}, f32[224,128]{1,0:T(8,128)S(1)}, u32[]{:S(2)}, u32[]{:S(2)}) %collective-permute-start.1) | collective-permute-done | bytes 114720 | tf_op jit(solution)/shard_map/ppermute | solution.py:399
  16.9 2.6 %collective-permute-done.2.refs_2_ = f32[224,128]{1,0:T(8,128)S(1)} collective-permute-done((f32[224,128]{1,0:T(8,128)S(1)}, f32[224,128]{1,0:T(8,128)S(1)}, u32[]{:S(2)}, u32[]{:S(2)}) %collective-permute-start.2) | collective-permute-done | bytes 114720 | tf_op jit(solution)/shard_map/ppermute | solution.py:399
  19.5 3.7 %state_streams.1 = (bf16[2,128,1024]{2,1,0:T(8,128)(2,1)}, f32[17,1024]{1,0:T(8,128)S(1)}, f32[1040,128]{1,0:T(8,128)S(1)}) custom-call(f32[3,128,1024]{2,1,0:T(8,128)S(1)} %get-tuple-element.44.feat, f32[128,1024]{1,0:T(8,128)S(1)} %get-tuple-element.45.og, f32[3,3,1024]{2,1,0:T(4,128)S(1)} %get-tuple-element.46.filt, ...), custom_call_target="tpu_custom_call" | custom-call | flops 16777216 | bytes 5242880 | tf_op jit(solution)/shard_map/state_streams/pallas_call | solution.py:272
  23.9 1.5 %collective-permute-start.4 = (bf16[1,2,128,1024]{3,2,1,0:T(8,128)(2,1)}, bf16[1,2,128,1024]{3,2,1,0:T(8,128)(2,1)}, u32[]{:S(2)}, u32[]{:S(2)}) collective-permute-start(bf16[1,2,128,1024]{3,2,1,0:T(8,128)(2,1)} %bitcast.4.refs_1_), channel_id=1, source_target_pairs={{0,1},{2,0},{4,2},{6,4},{7,6},{5,7},{3,5},{1,3},{8,9},{10,8},{12,1... | collective-permute-start | bytes 1572872 | tf_op jit(solution)/shard_map/ppermute | solution.py:390
  25.9 1.6 %collective-permute-start.7 = (bf16[1,1,128,1024]{3,2,1,0:T(8,128)(2,1)}, bf16[1,1,128,1024]{3,2,1,0:T(8,128)(2,1)}, u32[]{:S(2)}, u32[]{:S(2)}) collective-permute-start(bf16[1,1,128,1024]{3,2,1,0:T(8,128)(2,1)} %collective-permute-done.5.refs_2_), channel_id=1, source_target_pairs={{0,2},{2,4},{4,6},{6,7},{7,5},{5,3},{3,1},{1,0},{8,10},{10,12},{12... | collective-permute-start | bytes 786440 | tf_op jit(solution)/shard_map/ppermute | solution.py:387
  28.6 8.5 %add_product.8.refs_3_ = f32[1024,128]{1,0:T(8,128)S(1)} custom-call(s32[8]{0:T(128)S(1)} %dynamic-slice_bitcast_fusion.source, bf16[1,1,128,1024]{3,2,1,0:T(8,128)(2,1)S(1)} %bitcast.13, bf16[1,2,128,1024]{3,2,1,0:T(8,128)(2,1)} %bitcast.4.refs_1_, bf16[1,1,128,1024]{3,2,1,0:T(8,128)(2,1)} %collective-permute-done.5.refs_2_, ...), custom_call_target="tpu_custom_call" | custom-call | flops 1342177280 | bytes 11534336 | tf_op jit(solution)/shard_map/add_product/pallas_call | solution.py:336
  37.1 6.3 %collective-permute-done.7.refs_0_ = bf16[1,1,128,1024]{3,2,1,0:T(8,128)(2,1)} collective-permute-done((bf16[1,1,128,1024]{3,2,1,0:T(8,128)(2,1)}, bf16[1,1,128,1024]{3,2,1,0:T(8,128)(2,1)}, u32[]{:S(2)}, u32[]{:S(2)}) %collective-permute-start.7) | collective-permute-done | bytes 262176 | tf_op jit(solution)/shard_map/ppermute | solution.py:387
  45.4 4.8 %add_product.9.refs_3_ = f32[1024,128]{1,0:T(8,128)S(1)} custom-call(s32[8]{0:T(128)S(1)} %dynamic-slice_bitcast_fusion.source, bf16[1,1,128,1024]{3,2,1,0:T(8,128)(2,1)} %collective-permute-done.7.refs_0_, bf16[1,1,128,1024]{3,2,1,0:T(8,128)(2,1)} %collective-permute-done.8.refs_1_, bf16[3,1024,8192]{2,1,0:T(8,128)(2,1)} %refs_2_.13, ...), custom_call_target="tpu_custom_call" | custom-call | flops 536870912 | bytes 5242880 | tf_op jit(solution)/shard_map/add_product/pallas_call | solution.py:336
  50.2 1.8 %gradients.1 = f32[3,128,1024]{2,1,0:T(8,128)} custom-call(f32[3,128,1024]{2,1,0:T(8,128)S(1)} %get-tuple-element.44.feat, f32[128,1024]{1,0:T(8,128)S(1)} %get-tuple-element.53.conv, f32[128,1024]{1,0:T(8,128)S(1)} %get-tuple-element.45.og, f32[3,3,1024]{2,1,0:T(4,128)S(1)} %copy-done.1, f32[1,1024]{1,0:T(1,128)S(1)} %get-tuple-element.50.bias, ...), custom_call_target="tpu_custom_call" | custom-call | flops 3932160 | bytes 5242880 | tf_op jit(solution)/shard_map/gradients/pallas_call | solution.py:180
  52.7 1.5 %collective-permute-start.10 = (bf16[1,2,128,1024]{3,2,1,0:T(8,128)(2,1)}, bf16[1,2,128,1024]{3,2,1,0:T(8,128)(2,1)S(1)}, u32[]{:S(2)}, u32[]{:S(2)}) collective-permute-start(bf16[1,2,128,1024]{3,2,1,0:T(8,128)(2,1)} %collective-permute-done.4.refs_1_), channel_id=1, source_target_pairs={{0,1},{2,0},{4,2},{6,4},{7,6},{5,7},{3,5},{1,3},{8,9},{10,8},{12,1... | collective-permute-start | bytes 1572872 | tf_op jit(solution)/shard_map/ppermute | solution.py:390
  54.2 7.3 %add_product.10.refs_3_ = f32[1024,128]{1,0:T(8,128)S(1)} custom-call(s32[8]{0:T(128)S(1)} %dynamic-slice_bitcast_fusion.source, bf16[1,2,128,1024]{3,2,1,0:T(8,128)(2,1)} %collective-permute-done.3.refs_0_, bf16[1,2,128,1024]{3,2,1,0:T(8,128)(2,1)} %collective-permute-done.4.refs_1_, bf16[3,1024,8192]{2,1,0:T(8,128)(2,1)} %refs_2_.13, ...), custom_call_target="tpu_custom_call" | custom-call | flops 1073741824 | bytes 9437184 | tf_op jit(solution)/shard_map/add_product/pallas_call | solution.py:336
  61.5 4.3 %add_product.11.refs_3_ = f32[1024,128]{1,0:T(8,128)S(1)} custom-call(s32[8]{0:T(128)S(1)} %dynamic-slice_bitcast_fusion.source, bf16[1,1,128,1024]{3,2,1,0:T(8,128)(2,1)S(1)} %collective-permute-done.11.refs_0_, bf16[1,1,128,1024]{3,2,1,0:T(8,128)(2,1)S(1)} %collective-permute-done.12.refs_1_, bf16[3,1024,8192]{2,1,0:T(8,128)(2,1)} %refs_2_.13, ...), custom_call_target="tpu_custom_call" | custom-call | flops 536870912 | bytes 5242880 | tf_op jit(solution)/shard_map/add_product/pallas_call | solution.py:336
  67.3 4.8 %collective-permute-done.14 = f32[17,1024]{1,0:T(8,128)S(1)} collective-permute-done((f32[17,1024]{1,0:T(8,128)S(1)}, f32[17,1024]{1,0:T(8,128)S(1)}, u32[]{:S(2)}, u32[]{:S(2)}) %collective-permute-start.14) | collective-permute-done | bytes 69664 | tf_op jit(solution)/shard_map/ppermute | solution.py:438
  72.8 1.5 %collective-permute-start.16 = (bf16[1,2,128,1024]{3,2,1,0:T(8,128)(2,1)S(1)}, bf16[1,2,128,1024]{3,2,1,0:T(8,128)(2,1)S(1)}, u32[]{:S(2)}, u32[]{:S(2)}) collective-permute-start(bf16[1,2,128,1024]{3,2,1,0:T(8,128)(2,1)S(1)} %collective-permute-done.10.refs_1_), channel_id=1, source_target_pairs={{0,1},{2,0},{4,2},{6,4},{7,6},{5,7},{3,5},{1,3},{8,9},{10,8},{12,1... | collective-permute-start | bytes 1572872 | tf_op jit(solution)/shard_map/ppermute | solution.py:390
  74.9 1.5 %collective-permute-start.18 = (bf16[1,1,64,1024]{3,2,1,0:T(8,128)(2,1)S(1)}, bf16[1,1,64,1024]{3,2,1,0:T(8,128)(2,1)S(1)}, u32[]{:S(2)}, u32[]{:S(2)}) collective-permute-start(bf16[1,1,64,1024]{3,2,1,0:T(8,128)(2,1)S(1)} %slice.19), channel_id=1, source_target_pairs={{0,1},{2,0},{4,2},{6,4},{7,6},{5,7},{3,5},{1,3},{8,9},{10,8},{12,1... | collective-permute-start | bytes 393224 | tf_op jit(solution)/shard_map/ppermute | solution.py:390
  76.4 6.7 %add_product.12.refs_3_ = f32[1024,128]{1,0:T(8,128)S(1)} custom-call(s32[8]{0:T(128)S(1)} %dynamic-slice_bitcast_fusion.source, bf16[1,2,128,1024]{3,2,1,0:T(8,128)(2,1)S(1)} %collective-permute-done.9.refs_0_, bf16[1,2,128,1024]{3,2,1,0:T(8,128)(2,1)S(1)} %collective-permute-done.10.refs_1_, bf16[3,1024,8192]{2,1,0:T(8,128)(2,1)} %refs_2_.13, ...), custom_call_target="tpu_custom_call" | custom-call | flops 1073741824 | bytes 9437184 | tf_op jit(solution)/shard_map/add_product/pallas_call | solution.py:336
  83.1 5.2 %collective-permute-done.17.refs_0_ = bf16[1,1,64,1024]{3,2,1,0:T(8,128)(2,1)S(1)} collective-permute-done((bf16[1,1,64,1024]{3,2,1,0:T(8,128)(2,1)S(1)}, bf16[1,1,64,1024]{3,2,1,0:T(8,128)(2,1)S(1)}, u32[]{:S(2)}, u32[]{:S(2)}) %collective-permute-start.17) | collective-permute-done | bytes 131104 | tf_op jit(solution)/shard_map/ppermute | solution.py:387
  89.1 3.2 %add_product.13.refs_3_ = f32[1024,128]{1,0:T(8,128)S(1)} custom-call(s32[8]{0:T(128)S(1)} %dynamic-slice_bitcast_fusion.source, bf16[1,1,64,1024]{3,2,1,0:T(8,128)(2,1)S(1)} %collective-permute-done.17.refs_0_, bf16[1,1,64,1024]{3,2,1,0:T(8,128)(2,1)S(1)} %collective-permute-done.18.refs_1_, bf16[3,1024,8192]{2,1,0:T(8,128)(2,1)} %refs_2_.13, ...), custom_call_target="tpu_custom_call" | custom-call | flops 268435456 | bytes 3145728 | tf_op jit(solution)/shard_map/add_product/pallas_call | solution.py:336
  92.3 1.6 %collective-permute-start.19 = (bf16[1,1,128,1024]{3,2,1,0:T(8,128)(2,1)S(1)}, bf16[1,1,128,1024]{3,2,1,0:T(8,128)(2,1)S(1)}, u32[]{:S(2)}, u32[]{:S(2)}) collective-permute-start(bf16[1,1,128,1024]{3,2,1,0:T(8,128)(2,1)S(1)} %slice.20), channel_id=1, source_target_pairs={{0,2},{2,4},{4,6},{6,7},{7,5},{5,3},{3,1},{1,0},{8,10},{10,12},{12... | collective-permute-start | bytes 786440 | tf_op jit(solution)/shard_map/ppermute | solution.py:387
  95.0 6.7 %add_product.14.refs_3_ = f32[1024,128]{1,0:T(8,128)S(1)} custom-call(s32[8]{0:T(128)S(1)} %dynamic-slice_bitcast_fusion.source, bf16[1,2,128,1024]{3,2,1,0:T(8,128)(2,1)S(1)} %collective-permute-done.15.refs_0_, bf16[1,2,128,1024]{3,2,1,0:T(8,128)(2,1)S(1)} %collective-permute-done.16.refs_1_, bf16[3,1024,8192]{2,1,0:T(8,128)(2,1)} %refs_2_.13, ...), custom_call_target="tpu_custom_call" | custom-call | flops 1073741824 | bytes 9437184 | tf_op jit(solution)/shard_map/add_product/pallas_call | solution.py:336
  101.7 5.6 %add_product.15 = f32[128,1024]{1,0:T(8,128)} custom-call(s32[8]{0:T(128)S(1)} %dynamic-slice_bitcast_fusion.source, bf16[1,1,128,1024]{3,2,1,0:T(8,128)(2,1)S(1)} %collective-permute-done.19.refs_0_, bf16[1,1,128,1024]{3,2,1,0:T(8,128)(2,1)S(1)} %collective-permute-done.20.refs_1_, bf16[3,1024,8192]{2,1,0:T(8,128)(2,1)} %refs_2_.13, ...), custom_call_target="tpu_custom_call" | custom-call | flops 536870912 | bytes 5242880 | tf_op jit(solution)/shard_map/add_product/pallas_call | solution.py:336
  (47 shorter events, 14.0 us)
Async XLA Ops:
  3.1 20.1 %copy-start = (f32[3,3,1024]{2,1,0:T(4,128)}, f32[3,3,1024]{2,1,0:T(4,128)S(1)}, u32[]{:S(2)}) copy-start(f32[3,3,1024]{2,1,0:T(4,128)S(1)} %get-tuple-element.46.filt) | copy-start | bytes 110596
  3.1 3.2 %collective-permute-start = (f32[224,128]{1,0:T(8,128)S(1)}, f32[224,128]{1,0:T(8,128)S(1)}, u32[]{:S(2)}, u32[]{:S(2)}) collective-permute-start(f32[224,128]{1,0:T(8,128)S(1)} %get-tuple-element.54), channel_id=1, source_target_pairs={{8,0},{16,8},{24,16},{9,1},{17,9},{25,17},{10,2},{18,10},{26,18},{... | collective-permute-start | bytes 344072 | tf_op jit(solution)/shard_map/ppermute | solution.py:399
  6.7 19.1 %collective-permute-start.6 = (bf16[1,1,128,1024]{3,2,1,0:T(8,128)(2,1)S(1)}, bf16[1,1,128,1024]{3,2,1,0:T(8,128)(2,1)}, u32[]{:S(2)}, u32[]{:S(2)}) collective-permute-start(bf16[1,1,128,1024]{3,2,1,0:T(8,128)(2,1)S(1)} %bitcast.11), channel_id=1, source_target_pairs={{0,1},{2,0},{4,2},{6,4},{7,6},{5,7},{3,5},{1,3},{8,9},{10,8},{12,1... | collective-permute-start | bytes 786440 | tf_op jit(solution)/shard_map/ppermute | solution.py:390
  9.7 16.2 %collective-permute-start.5 = (bf16[1,1,128,1024]{3,2,1,0:T(8,128)(2,1)S(1)}, bf16[1,1,128,1024]{3,2,1,0:T(8,128)(2,1)}, u32[]{:S(2)}, u32[]{:S(2)}) collective-permute-start(bf16[1,1,128,1024]{3,2,1,0:T(8,128)(2,1)S(1)} %bitcast.12), channel_id=1, source_target_pairs={{0,2},{2,4},{4,6},{6,7},{7,5},{5,3},{3,1},{1,0},{8,10},{10,12},{12... | collective-permute-start | bytes 786440 | tf_op jit(solution)/shard_map/ppermute | solution.py:387
  9.9 7.0 %collective-permute-start.1 = (f32[224,128]{1,0:T(8,128)S(1)}, f32[224,128]{1,0:T(8,128)S(1)}, u32[]{:S(2)}, u32[]{:S(2)}) collective-permute-start(f32[224,128]{1,0:T(8,128)S(1)} %get-tuple-element.54), channel_id=1, source_target_pairs={{16,0},{24,8},{17,1},{25,9},{18,2},{26,10},{19,3},{27,11},{20,4},{... | collective-permute-start | bytes 344072 | tf_op jit(solution)/shard_map/ppermute | solution.py:399
  11.2 8.3 %collective-permute-start.2 = (f32[224,128]{1,0:T(8,128)S(1)}, f32[224,128]{1,0:T(8,128)S(1)}, u32[]{:S(2)}, u32[]{:S(2)}) collective-permute-start(f32[224,128]{1,0:T(8,128)S(1)} %get-tuple-element.54), channel_id=1, source_target_pairs={{24,0},{25,1},{26,2},{27,3},{28,4},{29,5},{30,6},{31,7}} | collective-permute-start | bytes 344072 | tf_op jit(solution)/shard_map/ppermute | solution.py:399
  23.9 28.2 %collective-permute-start.4 = (bf16[1,2,128,1024]{3,2,1,0:T(8,128)(2,1)}, bf16[1,2,128,1024]{3,2,1,0:T(8,128)(2,1)}, u32[]{:S(2)}, u32[]{:S(2)}) collective-permute-start(bf16[1,2,128,1024]{3,2,1,0:T(8,128)(2,1)} %bitcast.4.refs_1_), channel_id=1, source_target_pairs={{0,1},{2,0},{4,2},{6,4},{7,6},{5,7},{3,5},{1,3},{8,9},{10,8},{12,1... | collective-permute-start | bytes 1572872 | tf_op jit(solution)/shard_map/ppermute | solution.py:390
  25.3 26.7 %collective-permute-start.3 = (bf16[1,2,128,1024]{3,2,1,0:T(8,128)(2,1)}, bf16[1,2,128,1024]{3,2,1,0:T(8,128)(2,1)}, u32[]{:S(2)}, u32[]{:S(2)}) collective-permute-start(bf16[1,2,128,1024]{3,2,1,0:T(8,128)(2,1)} %bitcast.4.refs_1_), channel_id=1, source_target_pairs={{0,2},{2,4},{4,6},{6,7},{7,5},{5,3},{3,1},{1,0},{8,10},{10,12},{12... | collective-permute-start | bytes 1572872 | tf_op jit(solution)/shard_map/ppermute | solution.py:387
  25.9 17.5 %collective-permute-start.7 = (bf16[1,1,128,1024]{3,2,1,0:T(8,128)(2,1)}, bf16[1,1,128,1024]{3,2,1,0:T(8,128)(2,1)}, u32[]{:S(2)}, u32[]{:S(2)}) collective-permute-start(bf16[1,1,128,1024]{3,2,1,0:T(8,128)(2,1)} %collective-permute-done.5.refs_2_), channel_id=1, source_target_pairs={{0,2},{2,4},{4,6},{6,7},{7,5},{5,3},{3,1},{1,0},{8,10},{10,12},{12... | collective-permute-start | bytes 786440 | tf_op jit(solution)/shard_map/ppermute | solution.py:387
  27.5 15.9 %collective-permute-start.8 = (bf16[1,1,128,1024]{3,2,1,0:T(8,128)(2,1)}, bf16[1,1,128,1024]{3,2,1,0:T(8,128)(2,1)}, u32[]{:S(2)}, u32[]{:S(2)}) collective-permute-start(bf16[1,1,128,1024]{3,2,1,0:T(8,128)(2,1)} %collective-permute-done.6.refs_3_), channel_id=1, source_target_pairs={{0,1},{2,0},{4,2},{6,4},{7,6},{5,7},{3,5},{1,3},{8,9},{10,8},{12,1... | collective-permute-start | bytes 786440 | tf_op jit(solution)/shard_map/ppermute | solution.py:390
  37.1 13.1 %copy-start.1 = (f32[3,3,1024]{2,1,0:T(4,128)S(1)}, f32[3,3,1024]{2,1,0:T(4,128)}, u32[]{:S(2)}) copy-start(f32[3,3,1024]{2,1,0:T(4,128)} %copy-done) | copy-start | bytes 110596
  43.4 18.1 %collective-permute-start.11 = (bf16[1,1,128,1024]{3,2,1,0:T(8,128)(2,1)}, bf16[1,1,128,1024]{3,2,1,0:T(8,128)(2,1)S(1)}, u32[]{:S(2)}, u32[]{:S(2)}) collective-permute-start(bf16[1,1,128,1024]{3,2,1,0:T(8,128)(2,1)} %collective-permute-done.7.refs_0_), channel_id=1, source_target_pairs={{0,2},{2,4},{4,6},{6,7},{7,5},{5,3},{3,1},{1,0},{8,10},{10,12},{12... | collective-permute-start | bytes 786440 | tf_op jit(solution)/shard_map/ppermute | solution.py:387
  43.9 17.6 %collective-permute-start.12 = (bf16[1,1,128,1024]{3,2,1,0:T(8,128)(2,1)}, bf16[1,1,128,1024]{3,2,1,0:T(8,128)(2,1)S(1)}, u32[]{:S(2)}, u32[]{:S(2)}) collective-permute-start(bf16[1,1,128,1024]{3,2,1,0:T(8,128)(2,1)} %collective-permute-done.8.refs_1_), channel_id=1, source_target_pairs={{0,1},{2,0},{4,2},{6,4},{7,6},{5,7},{3,5},{1,3},{8,9},{10,8},{12,1... | collective-permute-start | bytes 786440 | tf_op jit(solution)/shard_map/ppermute | solution.py:390
  52.1 20.1 %collective-permute-start.9 = (bf16[1,2,128,1024]{3,2,1,0:T(8,128)(2,1)}, bf16[1,2,128,1024]{3,2,1,0:T(8,128)(2,1)S(1)}, u32[]{:S(2)}, u32[]{:S(2)}) collective-permute-start(bf16[1,2,128,1024]{3,2,1,0:T(8,128)(2,1)} %collective-permute-done.3.refs_0_), channel_id=1, source_target_pairs={{0,2},{2,4},{4,6},{6,7},{7,5},{5,3},{3,1},{1,0},{8,10},{10,12},{12... | collective-permute-start | bytes 1572872 | tf_op jit(solution)/shard_map/ppermute | solution.py:387
  52.7 19.5 %collective-permute-start.10 = (bf16[1,2,128,1024]{3,2,1,0:T(8,128)(2,1)}, bf16[1,2,128,1024]{3,2,1,0:T(8,128)(2,1)S(1)}, u32[]{:S(2)}, u32[]{:S(2)}) collective-permute-start(bf16[1,2,128,1024]{3,2,1,0:T(8,128)(2,1)} %collective-permute-done.4.refs_1_), channel_id=1, source_target_pairs={{0,1},{2,0},{4,2},{6,4},{7,6},{5,7},{3,5},{1,3},{8,9},{10,8},{12,1... | collective-permute-start | bytes 1572872 | tf_op jit(solution)/shard_map/ppermute | solution.py:390
  61.5 4.4 %copy-start.3 = (f32[17,1024]{1,0:T(8,128)S(1)}, f32[17,1024]{1,0:T(8,128)}, u32[]{:S(2)}) copy-start(f32[17,1024]{1,0:T(8,128)} %copy-done.2) | copy-start | bytes 208900
  65.9 1.4 %collective-permute-start.13 = (f32[17,1024]{1,0:T(8,128)S(1)}, f32[17,1024]{1,0:T(8,128)S(1)}, u32[]{:S(2)}, u32[]{:S(2)}) collective-permute-start(f32[17,1024]{1,0:T(8,128)S(1)} %copy-done.3), channel_id=1, source_target_pairs={{0,8},{8,0},{16,24},{24,16},{1,9},{9,1},{17,25},{25,17},{2,10},{10... | collective-permute-start | bytes 208904 | tf_op jit(solution)/shard_map/ppermute | solution.py:438
  67.3 4.9 %collective-permute-start.14 = (f32[17,1024]{1,0:T(8,128)S(1)}, f32[17,1024]{1,0:T(8,128)S(1)}, u32[]{:S(2)}, u32[]{:S(2)}) collective-permute-start(f32[17,1024]{1,0:T(8,128)S(1)} %add.11), channel_id=1, source_target_pairs={{0,16},{8,24},{16,0},{24,8},{1,17},{9,25},{17,1},{25,9},{2,18},{10... | collective-permute-start | bytes 208904 | tf_op jit(solution)/shard_map/ppermute | solution.py:438
  72.2 20.0 %collective-permute-start.15 = (bf16[1,2,128,1024]{3,2,1,0:T(8,128)(2,1)S(1)}, bf16[1,2,128,1024]{3,2,1,0:T(8,128)(2,1)S(1)}, u32[]{:S(2)}, u32[]{:S(2)}) collective-permute-start(bf16[1,2,128,1024]{3,2,1,0:T(8,128)(2,1)S(1)} %collective-permute-done.9.refs_0_), channel_id=1, source_target_pairs={{0,2},{2,4},{4,6},{6,7},{7,5},{5,3},{3,1},{1,0},{8,10},{10,12},{12... | collective-permute-start | bytes 1572872 | tf_op jit(solution)/shard_map/ppermute | solution.py:387
  72.8 19.5 %collective-permute-start.16 = (bf16[1,2,128,1024]{3,2,1,0:T(8,128)(2,1)S(1)}, bf16[1,2,128,1024]{3,2,1,0:T(8,128)(2,1)S(1)}, u32[]{:S(2)}, u32[]{:S(2)}) collective-permute-start(bf16[1,2,128,1024]{3,2,1,0:T(8,128)(2,1)S(1)} %collective-permute-done.10.refs_1_), channel_id=1, source_target_pairs={{0,1},{2,0},{4,2},{6,4},{7,6},{5,7},{3,5},{1,3},{8,9},{10,8},{12,1... | collective-permute-start | bytes 1572872 | tf_op jit(solution)/shard_map/ppermute | solution.py:390
  74.3 13.9 %collective-permute-start.17 = (bf16[1,1,64,1024]{3,2,1,0:T(8,128)(2,1)S(1)}, bf16[1,1,64,1024]{3,2,1,0:T(8,128)(2,1)S(1)}, u32[]{:S(2)}, u32[]{:S(2)}) collective-permute-start(bf16[1,1,64,1024]{3,2,1,0:T(8,128)(2,1)S(1)} %slice.18), channel_id=1, source_target_pairs={{0,2},{2,4},{4,6},{6,7},{7,5},{5,3},{3,1},{1,0},{8,10},{10,12},{12... | collective-permute-start | bytes 393224 | tf_op jit(solution)/shard_map/ppermute | solution.py:387
  74.9 13.6 %collective-permute-start.18 = (bf16[1,1,64,1024]{3,2,1,0:T(8,128)(2,1)S(1)}, bf16[1,1,64,1024]{3,2,1,0:T(8,128)(2,1)S(1)}, u32[]{:S(2)}, u32[]{:S(2)}) collective-permute-start(bf16[1,1,64,1024]{3,2,1,0:T(8,128)(2,1)S(1)} %slice.19), channel_id=1, source_target_pairs={{0,1},{2,0},{4,2},{6,4},{7,6},{5,7},{3,5},{1,3},{8,9},{10,8},{12,1... | collective-permute-start | bytes 393224 | tf_op jit(solution)/shard_map/ppermute | solution.py:390
  92.3 9.4 %collective-permute-start.19 = (bf16[1,1,128,1024]{3,2,1,0:T(8,128)(2,1)S(1)}, bf16[1,1,128,1024]{3,2,1,0:T(8,128)(2,1)S(1)}, u32[]{:S(2)}, u32[]{:S(2)}) collective-permute-start(bf16[1,1,128,1024]{3,2,1,0:T(8,128)(2,1)S(1)} %slice.20), channel_id=1, source_target_pairs={{0,2},{2,4},{4,6},{6,7},{7,5},{5,3},{3,1},{1,0},{8,10},{10,12},{12... | collective-permute-start | bytes 786440 | tf_op jit(solution)/shard_map/ppermute | solution.py:387
  93.9 7.8 %collective-permute-start.20 = (bf16[1,1,128,1024]{3,2,1,0:T(8,128)(2,1)S(1)}, bf16[1,1,128,1024]{3,2,1,0:T(8,128)(2,1)S(1)}, u32[]{:S(2)}, u32[]{:S(2)}) collective-permute-start(bf16[1,1,128,1024]{3,2,1,0:T(8,128)(2,1)S(1)} %slice.21), channel_id=1, source_target_pairs={{0,1},{2,0},{4,2},{6,4},{7,6},{5,7},{3,5},{1,3},{8,9},{10,8},{12,1... | collective-permute-start | bytes 786440 | tf_op jit(solution)/shard_map/ppermute | solution.py:390
  (1 other events, 0.7 us)

commit v4 on v3

--- a/solution.py
+++ b/solution.py
@@ -9,7 +9,9 @@
 
 LANES = 128
 RING = 8
-VMEM = 40 * 1024 * 1024
+LONG = 1 << 36
+SHORT = 1 << 16
+VMEM = 16 * 1024 * 1024
 F32 = jnp.float32
 BF16 = jnp.bfloat16
 
@@ -130,7 +132,7 @@
     gate_gradient(feat, conv, og, bias, later, ext)
     for j in range(channels // LANES):
         lanes = slice(j * LANES, (j + 1) * LANES)
-        rounded[0, :, lanes] = tapped(ext, taps, lanes, tokens).astype(BF16)
+        rounded[0, lanes, :] = tapped(ext, taps, lanes, tokens).T.astype(BF16)
 
 
 def gate_stream(feat, conv, og, filt, bias, later):
@@ -139,7 +141,7 @@
         gate_kernel,
         in_specs=[whole()] * 6,
         out_specs=whole(),
-        out_shape=jax.ShapeDtypeStruct((1, tokens, channels), BF16),
+        out_shape=jax.ShapeDtypeStruct((1, channels, tokens), BF16),
         scratch_shapes=[pltpu.VMEM((tokens + 8, channels), F32)],
         compiler_params=params(),
         cost_estimate=cost(12 * tokens * channels, 26 * tokens * channels),
@@ -190,9 +192,23 @@
     )(feat, conv, og, filt, bias, later, gp)
 
 
-def state_kernel(later, feat, og, filt, dec, far, res, bias, sig, *refs):
+def fetches(plan, source, w_proj, ready, sems):
+    channels = ready.shape[2]
+    moves = []
+    for k, (stream, height, offset, _) in enumerate(plan):
+        begin = pl.multiple_of((height * RING + source[offset]) * channels, LANES)
+        columns = w_proj.at[stream, :, pl.ds(begin, channels)]
+        moves.append(pltpu.make_async_copy(columns, ready.at[k], sems.at[k]))
+    return moves
+
+
+def state_kernel(later, plan, source, feat, og, filt, dec, far, res, bias, sig, *refs):
     payloads = refs[:later]
-    rounded, sums, gp, acc, prod, *exts = refs[later:]
+    w_proj, rounded, sums, gp, ready, acc, prod, first_ext, second_ext, sems = refs[later:]
+    exts = first_ext, second_ext
+    moves = fetches(plan, source, w_proj, ready, sems)
+    for move in moves:
+        move.start()
     tokens, channels = og.shape
     fold = channels // LANES
     modes = dec.shape[0] // fold
@@ -260,98 +276,100 @@
         taps = [filt[p + 1, j : j + 1, :] for j in range(3)]
         for j in range(fold):
             lanes = slice(j * LANES, (j + 1) * LANES)
-            rounded[p, :, lanes] = tapped(ext, taps, lanes, tokens).astype(BF16)
+            rounded[p, lanes, :] = tapped(ext, taps, lanes, tokens).T.astype(BF16)
     for j in range(fold):
         sums[0:modes, j * LANES : (j + 1) * LANES] = acc[pl.ds(j, modes, stride=fold), :]
-
-
-def state_streams(feat, og, filt, dec, far, res, bias, sig, payloads):
+    for move in moves:
+        move.wait()
+
+
+def state_streams(feat, og, filt, dec, far, res, bias, sig, payloads, plan, sources, w_proj):
     tokens, channels = og.shape
     fold = channels // LANES
     modes = dec.shape[0] // fold
     return pl.pallas_call(
-        functools.partial(state_kernel, len(payloads)),
-        in_specs=[whole()] * (8 + len(payloads)),
-        out_specs=[whole()] * 3,
+        functools.partial(state_kernel, len(payloads), plan),
+        in_specs=[pl.BlockSpec(memory_space=pltpu.SMEM)] + [whole()] * (8 + len(payloads)) + [in_hbm()],
+        out_specs=[whole()] * 4,
         out_shape=[
-            jax.ShapeDtypeStruct((2, tokens, channels), BF16),
-            jax.ShapeDtypeStruct((modes + 1, channels), F32),
-            jax.ShapeDtypeStruct(((tokens + 2) * fold, LANES), F32),
+            pltpu.VMEM((2, channels, tokens), BF16),
+            pltpu.VMEM((modes + 1, channels), F32),
+            pltpu.VMEM(((tokens + 2) * fold, LANES), F32),
+            pltpu.VMEM((len(plan), w_proj.shape[1], channels), BF16),
         ],
         scratch_shapes=[pltpu.VMEM((modes * fold, LANES), F32), pltpu.VMEM((tokens * fold, LANES), F32)]
-        + [pltpu.VMEM((tokens + 8, channels), F32)] * 2,
+        + [pltpu.VMEM((tokens + 8, channels), F32)] * 2
+        + [pltpu.SemaphoreType.DMA((len(plan),))],
         compiler_params=params(),
         cost_estimate=cost(8 * tokens * channels * modes, 40 * tokens * channels),
         name="state_streams",
-    )(feat, og, filt, dec, far, res, bias, sig, *payloads)
-
-
-def product_kernel(plan, first, last, source, *refs):
-    *refs, w_all, sems = refs
-    *refs, out = refs
-    before = None if first else refs[-1]
-    w = refs[-1 - (not first)]
-    features, channels = w_all.shape[1:]
+    )(sources, feat, og, filt, dec, far, res, bias, sig, *payloads, w_proj)
+
+
+def product_kernel(plan, later, first, source, w_proj, w, *refs):
+    refs = list(refs)
+    moves = []
+    if later:
+        sems = refs.pop()
+        moves = fetches(later, source, w_proj, refs.pop(), sems)
+    out = refs.pop()
+    before = None if first else refs.pop()
+    for move in moves:
+        move.start()
+    features = w.shape[1]
     wide = min(512, features)
-    moves = []
-    for k, (stream, height, offset, _) in enumerate(plan):
-        begin = pl.multiple_of((height * RING + source[offset]) * channels, LANES)
-        for d in range(0, features, wide):
-            moves.append(pltpu.make_async_copy(
-                w.at[stream, pl.ds(d, wide), pl.ds(begin, channels)],
-                w_all.at[k, pl.ds(d, wide)],
-                sems.at[k, d // wide],
-            ))
-            moves[-1].start()
-    totals = {}
-    for k, (_, _, _, parts) in enumerate(plan):
-        x = [refs[n][h, p] for n, h, p in parts]
-        x = x[0] if len(x) == 1 else jnp.concatenate(x, axis=0)
-        for d in range(0, features, wide):
-            moves.pop(0).wait()
-            rows = slice(d, d + wide)
-            y = lax.dot_general(w_all[k, rows], x, (((1,), (1,)), ((), ())), preferred_element_type=F32)
-            if k:
-                y = y + (out[:, rows].T if last else out[rows])
-            elif not first:
-                y = y + before[rows]
-            if last:
-                out[:, rows] = y.T
-            else:
-                out[rows] = y
-
-
-def add_product(total, pieces, sources, w_proj, last=False):
-    features = w_proj.shape[1]
+    for d in range(0, features, wide):
+        rows = slice(d, d + wide)
+        total = None if first else before[rows]
+        for k, (_, _, _, parts) in enumerate(plan):
+            x = [refs[n][h, p] for n, h, p in parts]
+            x = x[0] if len(x) == 1 else jnp.concatenate(x, axis=0)
+            y = jnp.dot(w[k, rows], x, preferred_element_type=F32)
+            total = y if total is None else total + y
+        if later:
+            out[rows] = total
+        else:
+            out[:, rows] = total.T
+    for move in moves:
+        move.wait()
+
+
+def steps_of(pieces):
     arrays, plan = [], []
     for array, stream, offset in pieces:
         halves = array if isinstance(array, tuple) else (array,)
-        heights, streams, _, channels = halves[0].shape
+        heights, streams = halves[0].shape[:2]
         for h in range(heights):
             for p in range(streams):
                 plan.append((stream + p, h, offset, [(len(arrays) + n, h, p) for n in range(len(halves))]))
         arrays += halves
-    tokens = sum(arrays[n].shape[2] for n, _, _ in plan[0][3])
+    return arrays, plan
+
+
+def add_product(total, ready, pieces, later, sources, w_proj, span):
+    features = w_proj.shape[1]
+    arrays, plan = steps_of(pieces)
+    channels, tokens = ready.shape[2], arrays[0].shape[3]
     first = total is None
+    out_shape = [jax.ShapeDtypeStruct((tokens, features), F32)]
+    scratch = []
+    if later:
+        out_shape = [
+            pltpu.VMEM((features, tokens), F32),
+            pltpu.VMEM((len(later), features, channels), BF16),
+        ]
+        scratch = [pltpu.SemaphoreType.DMA((len(later),))]
     return pl.pallas_call(
-        functools.partial(product_kernel, plan, first, last),
-        in_specs=[pl.BlockSpec(memory_space=pltpu.SMEM)]
-        + [whole()] * len(arrays)
-        + [in_hbm()]
-        + [whole()] * (not first),
-        out_specs=whole(),
-        out_shape=jax.ShapeDtypeStruct((tokens, features) if last else (features, tokens), F32),
-        scratch_shapes=[
-            pltpu.VMEM((len(plan), features, channels), BF16),
-            pltpu.SemaphoreType.DMA((len(plan), max(1, features // 512))),
-        ],
+        functools.partial(product_kernel, plan, later, first),
+        in_specs=[pl.BlockSpec(memory_space=pltpu.SMEM), in_hbm()]
+        + [whole()] * (1 + len(arrays) + (not first)),
+        out_specs=[whole()] * len(out_shape),
+        out_shape=out_shape,
+        scratch_shapes=scratch,
         compiler_params=params(),
-        cost_estimate=cost(
-            2 * tokens * features * channels * len(plan),
-            2 * features * channels * len(plan) + 8 * tokens * features,
-        ),
+        cost_estimate=cost(span, span // 256),
         name="add_product",
-    )(sources, *arrays, w_proj, *([] if first else [total]))
+    )(sources, w_proj, ready, *arrays, *([] if first else [total]))
 
 
 def ring_order(size):
@@ -398,55 +416,81 @@
     def from_later(array, by):
         return lax.ppermute(array, "ctx", [(i, i - by) for i in range(by, blocks)])
 
+    def exchanged(sums, by):
+        return sums + lax.ppermute(sums, "ctx", [(i, i ^ by) for i in range(blocks)])
+
     fold = channels // LANES
     feat, conv, og, filt, bias_row, dec, far, res, sig, own = front(
         features, saved_conv, out_grad, short_filter, residue.T, rate.T, bias[None]
     )
-    payloads = [from_later(own, by) for by in range(1, min(3, blocks))]
+    payloads = [from_later(own, by) for by in range(1, blocks)]
+    payloads = list(lax.optimization_barrier(tuple(payloads)))
     gate = gate_stream(feat, conv, og, filt, bias_row, payloads[0])
-    own, gate = lax.optimization_barrier((own, gate))
-    payloads += [from_later(own, by) for by in range(3, blocks)]
     a0 = stacked(gate)
     a1, z1 = up(a0), down(a0)
-    rounds, sums, gp = state_streams(
-        feat, og, filt, dec, far, res, bias_row.reshape(fold, LANES), sig, payloads
+
+    half = channels // 2
+    back = ring // 2
+
+    def plan_of(streams, *offsets):
+        shape = jax.ShapeDtypeStruct((heights, len(streams), channels, tokens), BF16)
+        return steps_of([(shape, streams[0], o) for o in offsets])[1]
+
+    start = plan_of((0,), 0) + plan_of((1, 2), 0) + plan_of((0,), ring - 1, 1)
+    payloads[0], a0 = lax.optimization_barrier((payloads[0], a0))
+    rounds, sums, gp, ready = state_streams(
+        feat, og, filt, dec, far, res, bias_row.reshape(fold, LANES), sig, payloads, start, sources, w_proj
     )
     b0 = stacked(rounds)
-    half = tokens // 2
-    back = ring // 2
 
     b1, y1 = up(b0), down(b0)
     a1, z1, b0 = lax.optimization_barrier((a1, z1, b0))
     a2, z2 = up(a1), down(z1)
-    total = add_product(
-        None, [(a0, 0, 0), (b0, 1, 0), (a1, 0, ring - 1), (z1, 0, 1)], sources, w_proj
-    )
-    a2, z2, total = lax.optimization_barrier((a2, z2, total))
-    a3, z3 = up(a2), down(z2)
-    total = add_product(total, [(a2, 0, ring - 2), (z2, 0, 2)], sources, w_proj)
-    gp = after(gp, total)
-    grads = gradients(feat, conv, og, filt, bias_row, payloads[0], gp)
+    total, ready = add_product(
+        None, ready, [(a0, 0, 0), (b0, 1, 0), (a1, 0, ring - 1), (z1, 0, 1)],
+        plan_of((1, 2), ring - 1, 1), sources, w_proj, LONG,
+    )
+    grads = gradients(feat, conv, og, filt, bias_row, payloads[0], after(gp, total))
+
     b1, y1, total, grads = lax.optimization_barrier((b1, y1, total, grads))
     b2, y2 = up(b1), down(y1)
-    total = add_product(total, [(b1, 1, ring - 1), (y1, 1, 1)], sources, w_proj)
-    a3, z3, total = lax.optimization_barrier((a3, z3, total))
-    tail = (up(a3[:, :, :half]), down(z3[:, :, half:]))
-    total = add_product(total, [(a3, 0, ring - 3), (z3, 0, 3)], sources, w_proj)
-    sums = after(sums, total)
-    by = 1
-    while by < blocks:
-        sums = sums + lax.ppermute(sums, "ctx", [(i, i ^ by) for i in range(blocks)])
-        by *= 2
-    sums = sums * (tokens * blocks) ** (-0.5)
+    total, ready = add_product(
+        total, ready, [(b1, 1, ring - 1), (y1, 1, 1)], plan_of((0,), ring - 2, 2), sources, w_proj, SHORT
+    )
+
+    a2, z2, total, sums = lax.optimization_barrier((a2, z2, total, sums))
+    a3, z3 = up(a2), down(z2)
+    distances = [1 << n for n in range((blocks - 1).bit_length())]
+    for by in distances[:-1]:
+        sums = exchanged(sums, by)
+    total, ready = add_product(
+        total, ready, [(a2, 0, ring - 2), (z2, 0, 2)], plan_of((1, 2), ring - 2, 2), sources, w_proj, LONG
+    )
+
     b2, y2, total, sums = lax.optimization_barrier((b2, y2, total, sums))
     b3, y3 = up(b2), down(y2)
-    total = add_product(total, [(b2, 1, ring - 2), (y2, 1, 2)], sources, w_proj)
-    tail, total = lax.optimization_barrier((tail, total))
-    total = add_product(total, [(tail, 0, back)], sources, w_proj)
-    b3, y3, total = lax.optimization_barrier((b3, y3, total))
+    total, ready = add_product(
+        total, ready, [(b2, 1, ring - 2), (y2, 1, 2)], plan_of((0,), ring - 3, 3), sources, w_proj, SHORT
+    )
+
+    a3, z3, total, sums = lax.optimization_barrier((a3, z3, total, sums))
+    for by in distances[-1:]:
+        sums = exchanged(sums, by)
+    sums = sums * (tokens * blocks) ** (-0.5)
+    a4 = up(a3[:, :, :half]), down(z3[:, :, half:])
+    total, ready = add_product(
+        total, ready, [(a3, 0, ring - 3), (z3, 0, 3)], plan_of((1, 2), ring - 3, 3), sources, w_proj, LONG
+    )
+
+    b3, y3, total, sums = lax.optimization_barrier((b3, y3, total, sums))
     b4, y4 = up(b3[:, :1]), down(y3[:, 1:])
-    total = add_product(total, [(b3, 1, ring - 3), (y3, 1, 3)], sources, w_proj)
-    grad_x = add_product(total, [(b4, 1, back), (y4, 2, back)], sources, w_proj, last=True)
+    total, ready = add_product(
+        total, ready, [(b3, 1, ring - 3), (y3, 1, 3)], plan_of((0,), back), sources, w_proj, 9 << 28
+    )
+
+    a4, total = lax.optimization_barrier((a4, total))
+    total, ready = add_product(total, ready, [(a4, 0, back)], plan_of((1, 2), back), sources, w_proj, 3 << 28)
+    (grad_x,) = add_product(total, ready, [(b4, 1, back), (y4, 2, back)], None, sources, w_proj, SHORT)
     return (grads, grad_x, sums[:modes].T, sums[modes])
 
 

time: 108 us -> 89.6 us (0.83)
  waiting for transfers between devices: 26.8 us -> 15.3 us
  Pallas kernels: 55.4 us -> 44.2 us
  local copies, waits for them, and re-layouts: 2.65 us -> 6.36 us
    pallas_call x9, Pallas kernels: 50.7 us -> 38.9 us  [the longest x8 34.2 us: add_product(): pl.pallas_call(functools.partial(product_kernel, plan, later, first), in_...]
    ppermute x2, waiting for transfers between devices: 6.13 us -> 0.01 us  [exchanged(): lax.ppermute(sums, 'ctx', [(i, i ^ by) for i in range(blocks)])]
    ppermute x8, waiting for transfers between devices: 11.4 us -> 7.23 us  [up(): return lax.ppermute(x, 'chan', pairs[1])]
    ppermute x3, waiting for transfers between devices: 8.95 us -> 4.79 us  [from_later(): return lax.ppermute(array, 'ctx', [(i, i - by) for i in range(by, blocks)])]
    unnamed x8 -> x12, local copies, waits for them, and re-layouts: 0.67 us -> 4.38 us
    ppermute x8, waiting for transfers between devices: 0.27 us -> 3.25 us  [down(): return lax.ppermute(x, 'chan', pairs[-1])]
    ppermute x8, starting transfers between devices: 6.19 us -> 3.22 us  [up(): return lax.ppermute(x, 'chan', pairs[1])]
    ppermute x8, starting transfers between devices: 11.3 us -> 14.2 us  [down(): return lax.ppermute(x, 'chan', pairs[-1])]
  transfers between devices with their start and end apart: 21 -> 21, of which waited for: 8 -> 8; matrix products, arithmetic and copies ran while one was open for 2% -> 2% of each run, Pallas kernels for 44% -> 43%
where the time goes in v4:
time: 89.6 us; the launch traced here: 89.2 us
  Pallas kernels  44.2 us (49%)
  starting transfers between devices  22.4 us (25%)
  waiting for transfers between devices  15.3 us (17%)
  local copies, waits for them, and re-layouts  6.36 us (7%)
    pallas_call x8, Pallas kernels, add_product(): pl.pallas_call(functools.partial(product_kernel, plan, later, first), in_...  34.2 us
    ppermute x8, starting transfers between devices, down(): return lax.ppermute(x, 'chan', pairs[-1])  14.2 us
    ppermute x8, waiting for transfers between devices, up(): return lax.ppermute(x, 'chan', pairs[1])  7.23 us
    ppermute x3, waiting for transfers between devices, from_later(): return lax.ppermute(array, 'ctx', [(i, i - by) for i in range(by, blocks)])  4.79 us
    pallas_call x1, Pallas kernels, state_streams(): pl.pallas_call(functools.partial(state_kernel, len(payloads), plan), in_s...  4.7 us
    unnamed x12, local copies, waits for them, and re-layouts  4.38 us
    ppermute x3, starting transfers between devices, from_later(): return lax.ppermute(array, 'ctx', [(i, i - by) for i in range(by, blocks)])  3.86 us
    ppermute x8, waiting for transfers between devices, down(): return lax.ppermute(x, 'chan', pairs[-1])  3.25 us
  transfers between devices with their start and end apart: 21, of which 8 were waited for; matrix products, arithmetic and copies ran while one was open for 2% of the time, Pallas kernels for 43%

profile of v4, /device:TPU:0, one launch (start us, length us, event | category | flops | bytes accessed | tf_op | source)
XLA Modules:
  0.0 89.2 jit_solution(16228150540001235680)
XLA Ops:
  0.6 2.5 %front.1 = (f32[3,128,1024]{2,1,0:T(8,128)S(1)}, f32[128,1024]{1,0:T(8,128)S(1)}, f32[128,1024]{1,0:T(8,128)S(1)}, f32[3,3,1024]{2,1,0:T(4,128)S(1)}, f32[1,1024...) custom-call(f32[3,128,1024]{2,1,0:T(8,128)} %features.1, ...), custom_call_target="tpu_custom_call" | custom-call | flops 8388608 | bytes 2621440 | tf_op jit(solution)/shard_map/front/pallas_call | solution.py:93
  8.9 2.3 %collective-permute-done.2.refs_2_ = f32[224,128]{1,0:T(8,128)S(1)} collective-permute-done((f32[224,128]{1,0:T(8,128)S(1)}, f32[224,128]{1,0:T(8,128)S(1)}, u32[]{:S(2)}, u32[]{:S(2)}) %collective-permute-start.2) | collective-permute-done | bytes 114720 | tf_op jit(solution)/shard_map/ppermute | solution.py:417
  11.1 2.5 %collective-permute-done.1.refs_1_ = f32[224,128]{1,0:T(8,128)S(1)} collective-permute-done((f32[224,128]{1,0:T(8,128)S(1)}, f32[224,128]{1,0:T(8,128)S(1)}, u32[]{:S(2)}, u32[]{:S(2)}) %collective-permute-start.1) | collective-permute-done | bytes 114720 | tf_op jit(solution)/shard_map/ppermute | solution.py:417
  14.7 2.9 %collective-permute-start.6 = (bf16[1,1,1024,128]{3,2,1,0:T(8,128)(2,1)}, bf16[1,1,1024,128]{3,2,1,0:T(8,128)(2,1)}, u32[]{:S(2)}, u32[]{:S(2)}) collective-permute-start(bf16[1,1,1024,128]{3,2,1,0:T(8,128)(2,1)} %bitcast.5.refs_0_), channel_id=1, source_target_pairs={{0,1},{2,0},{4,2},{6,4},{7,6},{5,7},{3,5},{1,3},{8,9},{10,8},{12,1... | collective-permute-start | bytes 786440 | tf_op jit(solution)/shard_map/ppermute | solution.py:408
  20.9 4.7 %state_streams.1 = (bf16[2,1024,128]{2,1,0:T(8,128)(2,1)S(1)}, f32[17,1024]{1,0:T(8,128)S(1)}, f32[1040,128]{1,0:T(8,128)S(1)}, bf16[5,1024,1024]{2,1,0:T(8,128)(2,1)S(1)}) custom-call(s32[8]{0:T(128)S(1)} %dynamic-slice_bitcast_fusion.source, f32[3,128,1024]{2,1,0:T(8,128)S(1)} %get-tuple-element.64.feat, f32[128,1024]{1,0:T(8,128)S(1)} %get-tuple-element.65.og, ...), custom_call_target="tpu_custom_call" | custom-call | flops 16777216 | bytes 5242880 | tf_op jit(solution)/shard_map/state_streams/pallas_call | solution.py:290
  25.6 2.0 %collective-permute-start.4 = (bf16[1,2,1024,128]{3,2,1,0:T(8,128)(2,1)S(1)}, bf16[1,2,1024,128]{3,2,1,0:T(8,128)(2,1)S(1)}, u32[]{:S(2)}, u32[]{:S(2)}) collective-permute-start(bf16[1,2,1024,128]{3,2,1,0:T(8,128)(2,1)S(1)} %bitcast.12), channel_id=1, source_target_pairs={{0,1},{2,0},{4,2},{6,4},{7,6},{5,7},{3,5},{1,3},{8,9},{10,8},{12,1... | collective-permute-start | bytes 1572872 | tf_op jit(solution)/shard_map/ppermute | solution.py:408
  27.7 2.0 %collective-permute-start.7 = (bf16[1,1,1024,128]{3,2,1,0:T(8,128)(2,1)}, bf16[1,1,1024,128]{3,2,1,0:T(8,128)(2,1)S(1)}, u32[]{:S(2)}, u32[]{:S(2)}) collective-permute-start(bf16[1,1,1024,128]{3,2,1,0:T(8,128)(2,1)} %collective-permute-done.5.refs_2_), channel_id=1, source_target_pairs={{0,2},{2,4},{4,6},{6,7},{7,5},{5,3},{3,1},{1,0},{8,10},{10,12},{12... | collective-permute-start | bytes 786440 | tf_op jit(solution)/shard_map/ppermute | solution.py:405
  29.8 6.1 %add_product.8 = (f32[1024,128]{1,0:T(8,128)S(1)}, bf16[4,1024,1024]{2,1,0:T(8,128)(2,1)S(1)}) custom-call(s32[8]{0:T(128)S(1)} %dynamic-slice_bitcast_fusion.source, bf16[3,1024,8192]{2,1,0:T(8,128)(2,1)} %w_proj.15, bf16[5,1024,1024]{2,1,0:T(8,128)(2,1)S(1)} %get-tuple-element.79.w, bf16[1,1,1024,128]{3,2,1,0:T(8,128)(2,1)} %bitcast.5.refs_0_, ...), custom_call_target="tpu_custom_call" | custom-call | flops 68719476736 | bytes 268435456 | tf_op jit(solution)/shard_map/add_product/pallas_call | solution.py:362
  35.9 1.8 %gradients.1 = f32[3,128,1024]{2,1,0:T(8,128)} custom-call(f32[3,128,1024]{2,1,0:T(8,128)S(1)} %get-tuple-element.64.feat, f32[128,1024]{1,0:T(8,128)S(1)} %get-tuple-element.74.conv, f32[128,1024]{1,0:T(8,128)S(1)} %get-tuple-element.65.og, f32[3,3,1024]{2,1,0:T(4,128)S(1)} %get-tuple-element.66.filt, f32[1,1024]{1,0:T(1,128)S(1)} %get-tuple-element.70.bias, ...), custom_call_target="tpu_custom_call" | custom-call | flops 3932160 | bytes 5242880 | tf_op jit(solution)/shard_map/gradients/pallas_call | solution.py:182
  37.7 2.8 %collective-permute-done.4.refs_1_ = bf16[1,2,1024,128]{3,2,1,0:T(8,128)(2,1)S(1)} collective-permute-done((bf16[1,2,1024,128]{3,2,1,0:T(8,128)(2,1)S(1)}, bf16[1,2,1024,128]{3,2,1,0:T(8,128)(2,1)S(1)}, u32[]{:S(2)}, u32[]{:S(2)}) %collective-permute-start.4) | collective-permute-done | bytes 524320 | tf_op jit(solution)/shard_map/ppermute | solution.py:408
  40.5 1.9 %collective-permute-done.3.refs_0_ = bf16[1,2,1024,128]{3,2,1,0:T(8,128)(2,1)S(1)} collective-permute-done((bf16[1,2,1024,128]{3,2,1,0:T(8,128)(2,1)S(1)}, bf16[1,2,1024,128]{3,2,1,0:T(8,128)(2,1)S(1)}, u32[]{:S(2)}, u32[]{:S(2)}) %collective-permute-start.3) | collective-permute-done | bytes 524320 | tf_op jit(solution)/shard_map/ppermute | solution.py:405
  42.5 1.9 %collective-permute-start.10 = (bf16[1,2,1024,128]{3,2,1,0:T(8,128)(2,1)S(1)}, bf16[1,2,1024,128]{3,2,1,0:T(8,128)(2,1)S(1)}, u32[]{:S(2)}, u32[]{:S(2)}) collective-permute-start(bf16[1,2,1024,128]{3,2,1,0:T(8,128)(2,1)S(1)} %collective-permute-done.4.refs_1_), channel_id=1, source_target_pairs={{0,1},{2,0},{4,2},{6,4},{7,6},{5,7},{3,5},{1,3},{8,9},{10,8},{12,1... | collective-permute-start | bytes 1572872 | tf_op jit(solution)/shard_map/ppermute | solution.py:408
  44.4 4.8 %add_product.9 = (f32[1024,128]{1,0:T(8,128)S(1)}, bf16[2,1024,1024]{2,1,0:T(8,128)(2,1)S(1)}) custom-call(s32[8]{0:T(128)S(1)} %dynamic-slice_bitcast_fusion.source, bf16[3,1024,8192]{2,1,0:T(8,128)(2,1)} %w_proj.15, bf16[4,1024,1024]{2,1,0:T(8,128)(2,1)S(1)} %get-tuple-element.88.w, bf16[1,2,1024,128]{3,2,1,0:T(8,128)(2,1)S(1)} %collective-permute-done.3.refs_0_, ...), custom_call_target="tpu_custom_call" | custom-call | flops 65536 | bytes 256 | tf_op jit(solution)/shard_map/add_product/pallas_call | solution.py:362
  49.4 1.9 %collective-permute-start.13 = (bf16[1,1,1024,128]{3,2,1,0:T(8,128)(2,1)S(1)}, bf16[1,1,1024,128]{3,2,1,0:T(8,128)(2,1)S(1)}, u32[]{:S(2)}, u32[]{:S(2)}) collective-permute-start(bf16[1,1,1024,128]{3,2,1,0:T(8,128)(2,1)S(1)} %collective-permute-done.8.refs_1_), channel_id=1, source_target_pairs={{0,1},{2,0},{4,2},{6,4},{7,6},{5,7},{3,5},{1,3},{8,9},{10,8},{12,1... | collective-permute-start | bytes 786440 | tf_op jit(solution)/shard_map/ppermute | solution.py:408
  51.3 5.0 %add_product.10 = (f32[1024,128]{1,0:T(8,128)S(1)}, bf16[4,1024,1024]{2,1,0:T(8,128)(2,1)S(1)}) custom-call(s32[8]{0:T(128)S(1)} %dynamic-slice_bitcast_fusion.source, bf16[3,1024,8192]{2,1,0:T(8,128)(2,1)} %w_proj.15, bf16[2,1024,1024]{2,1,0:T(8,128)(2,1)S(1)} %get-tuple-element.92.w, bf16[1,1,1024,128]{3,2,1,0:T(8,128)(2,1)S(1)} %collective-permute-done.7.refs_0_, ...), custom_call_target="tpu_custom_call" | custom-call | flops 68719476736 | bytes 268435456 | tf_op jit(solution)/shard_map/add_product/pallas_call | solution.py:362
  56.4 2.8 %collective-permute-done.9.refs_0_ = bf16[1,2,1024,128]{3,2,1,0:T(8,128)(2,1)S(1)} collective-permute-done((bf16[1,2,1024,128]{3,2,1,0:T(8,128)(2,1)S(1)}, bf16[1,2,1024,128]{3,2,1,0:T(8,128)(2,1)S(1)}, u32[]{:S(2)}, u32[]{:S(2)}) %collective-permute-start.9) | collective-permute-done | bytes 524320 | tf_op jit(solution)/shard_map/ppermute | solution.py:405
  59.3 1.9 %collective-permute-start.15 = (bf16[1,2,1024,128]{3,2,1,0:T(8,128)(2,1)S(1)}, bf16[1,2,1024,128]{3,2,1,0:T(8,128)(2,1)S(1)}, u32[]{:S(2)}, u32[]{:S(2)}) collective-permute-start(bf16[1,2,1024,128]{3,2,1,0:T(8,128)(2,1)S(1)} %collective-permute-done.10.refs_1_), channel_id=1, source_target_pairs={{0,1},{2,0},{4,2},{6,4},{7,6},{5,7},{3,5},{1,3},{8,9},{10,8},{12,1... | collective-permute-start | bytes 1572872 | tf_op jit(solution)/shard_map/ppermute | solution.py:408
  61.2 4.8 %add_product.11 = (f32[1024,128]{1,0:T(8,128)S(1)}, bf16[2,1024,1024]{2,1,0:T(8,128)(2,1)S(1)}) custom-call(s32[8]{0:T(128)S(1)} %dynamic-slice_bitcast_fusion.source, bf16[3,1024,8192]{2,1,0:T(8,128)(2,1)} %w_proj.15, bf16[4,1024,1024]{2,1,0:T(8,128)(2,1)S(1)} %get-tuple-element.98.w, bf16[1,2,1024,128]{3,2,1,0:T(8,128)(2,1)S(1)} %collective-permute-done.9.refs_0_, ...), custom_call_target="tpu_custom_call" | custom-call | flops 65536 | bytes 256 | tf_op jit(solution)/shard_map/add_product/pallas_call | solution.py:362
  69.2 5.0 %add_product.12 = (f32[1024,128]{1,0:T(8,128)S(1)}, bf16[4,1024,1024]{2,1,0:T(8,128)(2,1)S(1)}) custom-call(s32[8]{0:T(128)S(1)} %dynamic-slice_bitcast_fusion.source, bf16[3,1024,8192]{2,1,0:T(8,128)(2,1)} %w_proj.15, bf16[2,1024,1024]{2,1,0:T(8,128)(2,1)S(1)} %get-tuple-element.104.w, bf16[1,1,1024,128]{3,2,1,0:T(8,128)(2,1)S(1)} %collective-permute-done.12.refs_0_, ...), custom_call_target="tpu_custom_call" | custom-call | flops 68719476736 | bytes 268435456 | tf_op jit(solution)/shard_map/add_product/pallas_call | solution.py:362
  74.2 1.8 %collective-permute-done.14.refs_0_ = bf16[1,2,1024,128]{3,2,1,0:T(8,128)(2,1)S(1)} collective-permute-done((bf16[1,2,1024,128]{3,2,1,0:T(8,128)(2,1)S(1)}, bf16[1,2,1024,128]{3,2,1,0:T(8,128)(2,1)S(1)}, u32[]{:S(2)}, u32[]{:S(2)}) %collective-permute-start.14) | collective-permute-done | bytes 524320 | tf_op jit(solution)/shard_map/ppermute | solution.py:405
  76.1 2.9 %add_product.13 = (f32[1024,128]{1,0:T(8,128)S(1)}, bf16[1,1024,1024]{2,1,0:T(8,128)(2,1)S(1)}) custom-call(s32[8]{0:T(128)S(1)} %dynamic-slice_bitcast_fusion.source, bf16[3,1024,8192]{2,1,0:T(8,128)(2,1)} %w_proj.15, bf16[4,1024,1024]{2,1,0:T(8,128)(2,1)S(1)} %get-tuple-element.110.w, bf16[1,2,1024,128]{3,2,1,0:T(8,128)(2,1)S(1)} %collective-permute-done.14.refs_0_, ...), custom_call_target="tpu_custom_call" | custom-call | flops 2415919104 | bytes 9437184 | tf_op jit(solution)/shard_map/add_product/pallas_call | solution.py:362
  79.2 1.9 %collective-permute-start.20 = (bf16[1,1,1024,128]{3,2,1,0:T(8,128)(2,1)S(1)}, bf16[1,1,1024,128]{3,2,1,0:T(8,128)(2,1)S(1)}, u32[]{:S(2)}, u32[]{:S(2)}) collective-permute-start(bf16[1,1,1024,128]{3,2,1,0:T(8,128)(2,1)S(1)} %slice.21), channel_id=1, source_target_pairs={{0,1},{2,0},{4,2},{6,4},{7,6},{5,7},{3,5},{1,3},{8,9},{10,8},{12,1... | collective-permute-start | bytes 786440 | tf_op jit(solution)/shard_map/ppermute | solution.py:408
  81.1 3.0 %add_product.14 = (f32[1024,128]{1,0:T(8,128)S(1)}, bf16[2,1024,1024]{2,1,0:T(8,128)(2,1)S(1)}) custom-call(s32[8]{0:T(128)S(1)} %dynamic-slice_bitcast_fusion.source, bf16[3,1024,8192]{2,1,0:T(8,128)(2,1)} %w_proj.15, bf16[1,1024,1024]{2,1,0:T(8,128)(2,1)S(1)} %get-tuple-element.116.w, bf16[1,1,512,128]{3,2,1,0:T(8,128)(2,1)S(1)} %collective-permute-done.17.refs_0_, ...), custom_call_target="tpu_custom_call" | custom-call | flops 805306368 | bytes 3145728 | tf_op jit(solution)/shard_map/add_product/pallas_call | solution.py:362
  86.5 2.7 %add_product.15 = f32[128,1024]{1,0:T(8,128)} custom-call(s32[8]{0:T(128)S(1)} %dynamic-slice_bitcast_fusion.source, bf16[3,1024,8192]{2,1,0:T(8,128)(2,1)} %w_proj.15, bf16[2,1024,1024]{2,1,0:T(8,128)(2,1)S(1)} %get-tuple-element.121.w, bf16[1,1,1024,128]{3,2,1,0:T(8,128)(2,1)S(1)} %collective-permute-done.19.refs_0_, ...), custom_call_target="tpu_custom_call" | custom-call | flops 65536 | bytes 256 | tf_op jit(solution)/shard_map/add_product/pallas_call | solution.py:362
  (51 shorter events, 16.5 us)
Async XLA Ops:
  5.0 6.1 %collective-permute-start.2 = (f32[224,128]{1,0:T(8,128)S(1)}, f32[224,128]{1,0:T(8,128)S(1)}, u32[]{:S(2)}, u32[]{:S(2)}) collective-permute-start(f32[224,128]{1,0:T(8,128)S(1)} %get-tuple-element.72), channel_id=1, source_target_pairs={{24,0},{25,1},{26,2},{27,3},{28,4},{29,5},{30,6},{31,7}} | collective-permute-start | bytes 344072 | tf_op jit(solution)/shard_map/ppermute | solution.py:417
  6.3 7.4 %collective-permute-start.1 = (f32[224,128]{1,0:T(8,128)S(1)}, f32[224,128]{1,0:T(8,128)S(1)}, u32[]{:S(2)}, u32[]{:S(2)}) collective-permute-start(f32[224,128]{1,0:T(8,128)S(1)} %get-tuple-element.72), channel_id=1, source_target_pairs={{16,0},{24,8},{17,1},{25,9},{18,2},{26,10},{19,3},{27,11},{20,4},{... | collective-permute-start | bytes 344072 | tf_op jit(solution)/shard_map/ppermute | solution.py:417
  7.6 6.1 %collective-permute-start = (f32[224,128]{1,0:T(8,128)S(1)}, f32[224,128]{1,0:T(8,128)S(1)}, u32[]{:S(2)}, u32[]{:S(2)}) collective-permute-start(f32[224,128]{1,0:T(8,128)S(1)} %get-tuple-element.72), channel_id=1, source_target_pairs={{8,0},{16,8},{24,16},{9,1},{17,9},{25,17},{10,2},{18,10},{26,18},{... | collective-permute-start | bytes 344072 | tf_op jit(solution)/shard_map/ppermute | solution.py:417
  14.7 13.0 %collective-permute-start.6 = (bf16[1,1,1024,128]{3,2,1,0:T(8,128)(2,1)}, bf16[1,1,1024,128]{3,2,1,0:T(8,128)(2,1)}, u32[]{:S(2)}, u32[]{:S(2)}) collective-permute-start(bf16[1,1,1024,128]{3,2,1,0:T(8,128)(2,1)} %bitcast.5.refs_0_), channel_id=1, source_target_pairs={{0,1},{2,0},{4,2},{6,4},{7,6},{5,7},{3,5},{1,3},{8,9},{10,8},{12,1... | collective-permute-start | bytes 786440 | tf_op jit(solution)/shard_map/ppermute | solution.py:408
  17.6 10.2 %collective-permute-start.5 = (bf16[1,1,1024,128]{3,2,1,0:T(8,128)(2,1)}, bf16[1,1,1024,128]{3,2,1,0:T(8,128)(2,1)}, u32[]{:S(2)}, u32[]{:S(2)}) collective-permute-start(bf16[1,1,1024,128]{3,2,1,0:T(8,128)(2,1)} %bitcast.5.refs_0_), channel_id=1, source_target_pairs={{0,2},{2,4},{4,6},{6,7},{7,5},{5,3},{3,1},{1,0},{8,10},{10,12},{12... | collective-permute-start | bytes 786440 | tf_op jit(solution)/shard_map/ppermute | solution.py:405
  18.4 0.8 copy-start.1
  19.2 0.8 copy-start.3
  20.1 0.8 copy-start.5
  25.6 14.9 %collective-permute-start.4 = (bf16[1,2,1024,128]{3,2,1,0:T(8,128)(2,1)S(1)}, bf16[1,2,1024,128]{3,2,1,0:T(8,128)(2,1)S(1)}, u32[]{:S(2)}, u32[]{:S(2)}) collective-permute-start(bf16[1,2,1024,128]{3,2,1,0:T(8,128)(2,1)S(1)} %bitcast.12), channel_id=1, source_target_pairs={{0,1},{2,0},{4,2},{6,4},{7,6},{5,7},{3,5},{1,3},{8,9},{10,8},{12,1... | collective-permute-start | bytes 1572872 | tf_op jit(solution)/shard_map/ppermute | solution.py:408
  27.6 14.8 %collective-permute-start.3 = (bf16[1,2,1024,128]{3,2,1,0:T(8,128)(2,1)S(1)}, bf16[1,2,1024,128]{3,2,1,0:T(8,128)(2,1)S(1)}, u32[]{:S(2)}, u32[]{:S(2)}) collective-permute-start(bf16[1,2,1024,128]{3,2,1,0:T(8,128)(2,1)S(1)} %bitcast.13), channel_id=1, source_target_pairs={{0,2},{2,4},{4,6},{6,7},{7,5},{5,3},{3,1},{1,0},{8,10},{10,12},{12... | collective-permute-start | bytes 1572872 | tf_op jit(solution)/shard_map/ppermute | solution.py:405
  27.7 21.4 %collective-permute-start.7 = (bf16[1,1,1024,128]{3,2,1,0:T(8,128)(2,1)}, bf16[1,1,1024,128]{3,2,1,0:T(8,128)(2,1)S(1)}, u32[]{:S(2)}, u32[]{:S(2)}) collective-permute-start(bf16[1,1,1024,128]{3,2,1,0:T(8,128)(2,1)} %collective-permute-done.5.refs_2_), channel_id=1, source_target_pairs={{0,2},{2,4},{4,6},{6,7},{7,5},{5,3},{3,1},{1,0},{8,10},{10,12},{12... | collective-permute-start | bytes 786440 | tf_op jit(solution)/shard_map/ppermute | solution.py:405
  29.7 19.4 %collective-permute-start.8 = (bf16[1,1,1024,128]{3,2,1,0:T(8,128)(2,1)}, bf16[1,1,1024,128]{3,2,1,0:T(8,128)(2,1)S(1)}, u32[]{:S(2)}, u32[]{:S(2)}) collective-permute-start(bf16[1,1,1024,128]{3,2,1,0:T(8,128)(2,1)} %collective-permute-done.6.refs_3_), channel_id=1, source_target_pairs={{0,1},{2,0},{4,2},{6,4},{7,6},{5,7},{3,5},{1,3},{8,9},{10,8},{12,1... | collective-permute-start | bytes 786440 | tf_op jit(solution)/shard_map/ppermute | solution.py:408
  42.3 16.9 %collective-permute-start.9 = (bf16[1,2,1024,128]{3,2,1,0:T(8,128)(2,1)S(1)}, bf16[1,2,1024,128]{3,2,1,0:T(8,128)(2,1)S(1)}, u32[]{:S(2)}, u32[]{:S(2)}) collective-permute-start(bf16[1,2,1024,128]{3,2,1,0:T(8,128)(2,1)S(1)} %collective-permute-done.3.refs_0_), channel_id=1, source_target_pairs={{0,2},{2,4},{4,6},{6,7},{7,5},{5,3},{3,1},{1,0},{8,10},{10,12},{12... | collective-permute-start | bytes 1572872 | tf_op jit(solution)/shard_map/ppermute | solution.py:405
  42.5 16.7 %collective-permute-start.10 = (bf16[1,2,1024,128]{3,2,1,0:T(8,128)(2,1)S(1)}, bf16[1,2,1024,128]{3,2,1,0:T(8,128)(2,1)S(1)}, u32[]{:S(2)}, u32[]{:S(2)}) collective-permute-start(bf16[1,2,1024,128]{3,2,1,0:T(8,128)(2,1)S(1)} %collective-permute-done.4.refs_1_), channel_id=1, source_target_pairs={{0,1},{2,0},{4,2},{6,4},{7,6},{5,7},{3,5},{1,3},{8,9},{10,8},{12,1... | collective-permute-start | bytes 1572872 | tf_op jit(solution)/shard_map/ppermute | solution.py:408
  49.2 7.2 %collective-permute-start.11 = (f32[17,1024]{1,0:T(8,128)S(1)}, f32[17,1024]{1,0:T(8,128)S(1)}, u32[]{:S(2)}, u32[]{:S(2)}) collective-permute-start(f32[17,1024]{1,0:T(8,128)S(1)} %get-tuple-element.100), channel_id=1, source_target_pairs={{0,8},{8,0},{16,24},{24,16},{1,9},{9,1},{17,25},{25,17},{2,10},{10... | collective-permute-start | bytes 208904 | tf_op jit(solution)/shard_map/ppermute | solution.py:420
  49.2 16.8 %collective-permute-start.12 = (bf16[1,1,1024,128]{3,2,1,0:T(8,128)(2,1)S(1)}, bf16[1,1,1024,128]{3,2,1,0:T(8,128)(2,1)S(1)}, u32[]{:S(2)}, u32[]{:S(2)}) collective-permute-start(bf16[1,1,1024,128]{3,2,1,0:T(8,128)(2,1)S(1)} %collective-permute-done.7.refs_0_), channel_id=1, source_target_pairs={{0,2},{2,4},{4,6},{6,7},{7,5},{5,3},{3,1},{1,0},{8,10},{10,12},{12... | collective-permute-start | bytes 786440 | tf_op jit(solution)/shard_map/ppermute | solution.py:405
  49.4 16.6 %collective-permute-start.13 = (bf16[1,1,1024,128]{3,2,1,0:T(8,128)(2,1)S(1)}, bf16[1,1,1024,128]{3,2,1,0:T(8,128)(2,1)S(1)}, u32[]{:S(2)}, u32[]{:S(2)}) collective-permute-start(bf16[1,1,1024,128]{3,2,1,0:T(8,128)(2,1)S(1)} %collective-permute-done.8.refs_1_), channel_id=1, source_target_pairs={{0,1},{2,0},{4,2},{6,4},{7,6},{5,7},{3,5},{1,3},{8,9},{10,8},{12,1... | collective-permute-start | bytes 786440 | tf_op jit(solution)/shard_map/ppermute | solution.py:408
  59.2 16.8 %collective-permute-start.14 = (bf16[1,2,1024,128]{3,2,1,0:T(8,128)(2,1)S(1)}, bf16[1,2,1024,128]{3,2,1,0:T(8,128)(2,1)S(1)}, u32[]{:S(2)}, u32[]{:S(2)}) collective-permute-start(bf16[1,2,1024,128]{3,2,1,0:T(8,128)(2,1)S(1)} %collective-permute-done.9.refs_0_), channel_id=1, source_target_pairs={{0,2},{2,4},{4,6},{6,7},{7,5},{5,3},{3,1},{1,0},{8,10},{10,12},{12... | collective-permute-start | bytes 1572872 | tf_op jit(solution)/shard_map/ppermute | solution.py:405
  59.3 16.7 %collective-permute-start.15 = (bf16[1,2,1024,128]{3,2,1,0:T(8,128)(2,1)S(1)}, bf16[1,2,1024,128]{3,2,1,0:T(8,128)(2,1)S(1)}, u32[]{:S(2)}, u32[]{:S(2)}) collective-permute-start(bf16[1,2,1024,128]{3,2,1,0:T(8,128)(2,1)S(1)} %collective-permute-done.10.refs_1_), channel_id=1, source_target_pairs={{0,1},{2,0},{4,2},{6,4},{7,6},{5,7},{3,5},{1,3},{8,9},{10,8},{12,1... | collective-permute-start | bytes 1572872 | tf_op jit(solution)/shard_map/ppermute | solution.py:408
  66.0 8.2 %collective-permute-start.16 = (f32[17,1024]{1,0:T(8,128)S(1)}, f32[17,1024]{1,0:T(8,128)S(1)}, u32[]{:S(2)}, u32[]{:S(2)}) collective-permute-start(f32[17,1024]{1,0:T(8,128)S(1)} %add.11), channel_id=1, source_target_pairs={{0,16},{8,24},{16,0},{24,8},{1,17},{9,25},{17,1},{25,9},{2,18},{10... | collective-permute-start | bytes 208904 | tf_op jit(solution)/shard_map/ppermute | solution.py:420
  67.1 11.9 %collective-permute-start.18 = (bf16[1,1,512,128]{3,2,1,0:T(8,128)(2,1)S(1)}, bf16[1,1,512,128]{3,2,1,0:T(8,128)(2,1)S(1)}, u32[]{:S(2)}, u32[]{:S(2)}) collective-permute-start(bf16[1,1,512,128]{3,2,1,0:T(8,128)(2,1)S(1)} %slice.19), channel_id=1, source_target_pairs={{0,1},{2,0},{4,2},{6,4},{7,6},{5,7},{3,5},{1,3},{8,9},{10,8},{12,1... | collective-permute-start | bytes 393224 | tf_op jit(solution)/shard_map/ppermute | solution.py:408
  68.7 10.3 %collective-permute-start.17 = (bf16[1,1,512,128]{3,2,1,0:T(8,128)(2,1)S(1)}, bf16[1,1,512,128]{3,2,1,0:T(8,128)(2,1)S(1)}, u32[]{:S(2)}, u32[]{:S(2)}) collective-permute-start(bf16[1,1,512,128]{3,2,1,0:T(8,128)(2,1)S(1)} %slice.18), channel_id=1, source_target_pairs={{0,2},{2,4},{4,6},{6,7},{7,5},{5,3},{3,1},{1,0},{8,10},{10,12},{12... | collective-permute-start | bytes 393224 | tf_op jit(solution)/shard_map/ppermute | solution.py:405
  79.0 7.0 %collective-permute-start.19 = (bf16[1,1,1024,128]{3,2,1,0:T(8,128)(2,1)S(1)}, bf16[1,1,1024,128]{3,2,1,0:T(8,128)(2,1)S(1)}, u32[]{:S(2)}, u32[]{:S(2)}) collective-permute-start(bf16[1,1,1024,128]{3,2,1,0:T(8,128)(2,1)S(1)} %slice.20), channel_id=1, source_target_pairs={{0,2},{2,4},{4,6},{6,7},{7,5},{5,3},{3,1},{1,0},{8,10},{10,12},{12... | collective-permute-start | bytes 786440 | tf_op jit(solution)/shard_map/ppermute | solution.py:405
  79.2 7.3 %collective-permute-start.20 = (bf16[1,1,1024,128]{3,2,1,0:T(8,128)(2,1)S(1)}, bf16[1,1,1024,128]{3,2,1,0:T(8,128)(2,1)S(1)}, u32[]{:S(2)}, u32[]{:S(2)}) collective-permute-start(bf16[1,1,1024,128]{3,2,1,0:T(8,128)(2,1)S(1)} %slice.21), channel_id=1, source_target_pairs={{0,1},{2,0},{4,2},{6,4},{7,6},{5,7},{3,5},{1,3},{8,9},{10,8},{12,1... | collective-permute-start | bytes 786440 | tf_op jit(solution)/shard_map/ppermute | solution.py:408
  (3 other events, 1.9 us)

commit v5 on v4

--- a/solution.py
+++ b/solution.py
@@ -9,9 +9,11 @@
 
 LANES = 128
 RING = 8
-LONG = 1 << 36
-SHORT = 1 << 16
-VMEM = 16 * 1024 * 1024
+LONG = 1 << 36, 1 << 28
+SHORT = 1 << 16, 1 << 8
+MIDDLE = 1 << 30, 9 << 20
+SMALL = 1 << 28, 3 << 20
+VMEM = 8 * 1024 * 1024
 F32 = jnp.float32
 BF16 = jnp.bfloat16
 
@@ -38,7 +40,7 @@
 
 
 def front_kernel(features, saved_conv, out_grad, short_filter, residue, rate, bias, *refs):
-    feat, conv, og, filt, bias_in, dec, far, res, sig, own, res_in, rate_in, sems = refs
+    feat, conv, og, filt, bias_in, tables, own, brief, res_in, rate_in, sems = refs
     tokens, channels = og.shape
     modes = rate_in.shape[0]
     fold = channels // LANES
@@ -47,7 +49,8 @@
         for n, (source, target) in enumerate((
             (rate, rate_in),
             (out_grad, og),
-            (features, feat),
+            (features.at[0], feat.at[0]),
+            (features.at[pl.ds(1, 2)], feat.at[pl.ds(1, 2)]),
             (saved_conv, conv),
             (short_filter, filt),
             (residue, res_in),
@@ -57,31 +60,32 @@
     for move in moves:
         move.start()
     moves[0].wait()
-    by_row(jnp.exp(-rate_in[...]), dec, fold)
-    by_row(jnp.exp(-(tokens - 2) * rate_in[...]), far, fold)
+    by_row(jnp.exp(-rate_in[...]), tables, fold, tokens)
+    by_row(jnp.exp(-(tokens - 2) * rate_in[...]), tables, fold, tokens + modes)
     moves[1].wait()
     moves[2].wait()
     for j in range(fold):
         lanes = slice(j * LANES, (j + 1) * LANES)
-        sig[pl.ds(j, tokens, stride=fold), :] = og[:, lanes] * feat[0, :, lanes]
-    decay = [dec[m * fold : (m + 1) * fold, :] for m in range(modes)]
+        tables[pl.ds(j, tokens, stride=fold), :] = og[:, lanes] * feat[0, :, lanes]
+    decay = [tables[(tokens + m) * fold : (tokens + m + 1) * fold, :] for m in range(modes)]
 
     def step(i, states):
-        row = sig[pl.ds((tokens - 1 - i) * fold, fold), :]
+        row = tables[pl.ds((tokens - 1 - i) * fold, fold), :]
         return tuple(row + d * s for d, s in zip(decay, states))
 
     zero = tuple(jnp.zeros((fold, LANES), F32) for _ in range(modes))
     states = lax.fori_loop(0, tokens - 2, step, zero, unroll=6)
-    for m in range(modes):
-        own[m * fold : (m + 1) * fold, :] = states[m]
-    own[modes * fold : (modes + 2) * fold, :] = sig[0 : 2 * fold, :]
+    for target in (own, brief):
+        for m in range(modes):
+            target[m * fold : (m + 1) * fold, :] = states[m]
+        target[modes * fold : (modes + 2) * fold, :] = tables[0 : 2 * fold, :]
+    for n in range(3, 8):
+        moves[n].wait()
     for n in range(3):
         by_row(feat[n, 0:2, :], own, fold, modes + 2 + 2 * n)
+    by_row(conv[0:2, :], own, fold, modes + 8)
     by_row(og[0:2, :], own, fold, modes + 10)
-    for n in range(3, 7):
-        moves[n].wait()
-    by_row(conv[0:2, :], own, fold, modes + 8)
-    by_row(res_in[...], res, fold)
+    by_row(res_in[...], tables, fold, tokens + 2 * modes)
 
 
 def front(features, saved_conv, out_grad, short_filter, residue, rate, bias):
@@ -89,15 +93,13 @@
     modes = rate.shape[0]
     fold = channels // LANES
     inputs = (features, saved_conv, out_grad, short_filter, residue, rate, bias)
-    by_mode = pltpu.VMEM((modes * fold, LANES), F32)
     return pl.pallas_call(
         front_kernel,
         in_specs=[in_hbm()] * 7,
-        out_specs=[whole()] * 10,
+        out_specs=[whole()] * 8,
         out_shape=[pltpu.VMEM(a.shape, F32) for a in (*inputs[:4], bias)]
-        + [by_mode] * 3
-        + [pltpu.VMEM((tokens * fold, LANES), F32), pltpu.VMEM(((modes + 12) * fold, LANES), F32)],
-        scratch_shapes=[pltpu.VMEM(rate.shape, F32)] * 2 + [pltpu.SemaphoreType.DMA((7,))],
+        + [pltpu.VMEM((n * fold, LANES), F32) for n in (tokens + 3 * modes, modes + 12, modes + 2)],
+        scratch_shapes=[pltpu.VMEM(rate.shape, F32)] * 2 + [pltpu.SemaphoreType.DMA((8,))],
         compiler_params=params(),
         cost_estimate=cost(4 * tokens * channels * modes, 20 * tokens * channels),
         name="front",
@@ -132,7 +134,7 @@
     gate_gradient(feat, conv, og, bias, later, ext)
     for j in range(channels // LANES):
         lanes = slice(j * LANES, (j + 1) * LANES)
-        rounded[0, lanes, :] = tapped(ext, taps, lanes, tokens).T.astype(BF16)
+        rounded[0, lanes, :] = tapped(ext, taps, lanes, tokens).astype(BF16).T
 
 
 def gate_stream(feat, conv, og, filt, bias, later):
@@ -141,10 +143,10 @@
         gate_kernel,
         in_specs=[whole()] * 6,
         out_specs=whole(),
-        out_shape=jax.ShapeDtypeStruct((1, channels, tokens), BF16),
+        out_shape=pltpu.VMEM((1, channels, tokens), BF16),
         scratch_shapes=[pltpu.VMEM((tokens + 8, channels), F32)],
         compiler_params=params(),
-        cost_estimate=cost(12 * tokens * channels, 26 * tokens * channels),
+        cost_estimate=cost(*LONG),
         name="gate_stream",
     )(feat, conv, og, filt, bias, later)
 
@@ -193,16 +195,16 @@
 
 
 def fetches(plan, source, w_proj, ready, sems):
-    channels = ready.shape[2]
+    channels = ready.shape[1] // len(plan)
     moves = []
     for k, (stream, height, offset, _) in enumerate(plan):
         begin = pl.multiple_of((height * RING + source[offset]) * channels, LANES)
         columns = w_proj.at[stream, :, pl.ds(begin, channels)]
-        moves.append(pltpu.make_async_copy(columns, ready.at[k], sems.at[k]))
+        moves.append(pltpu.make_async_copy(columns, ready.at[:, pl.ds(k * channels, channels)], sems.at[k]))
     return moves
 
 
-def state_kernel(later, plan, source, feat, og, filt, dec, far, res, bias, sig, *refs):
+def state_kernel(later, plan, source, feat, og, filt, bias, tables, *refs):
     payloads = refs[:later]
     w_proj, rounded, sums, gp, ready, acc, prod, first_ext, second_ext, sems = refs[later:]
     exts = first_ext, second_ext
@@ -211,7 +213,8 @@
         move.start()
     tokens, channels = og.shape
     fold = channels // LANES
-    modes = dec.shape[0] // fold
+    modes = (tables.shape[0] // fold - tokens) // 3
+    dec, far, res = (tokens + n * modes for n in range(3))
     for j in range(fold):
         lanes = slice(j * LANES, (j + 1) * LANES)
         p = feat[1, :, lanes] * feat[2, :, lanes]
@@ -226,9 +229,7 @@
     group = 8
     for low in range(0, modes, group):
         chosen = range(low, min(low + group, modes))
-        decay = [rows(dec, m) for m in chosen]
-        weight = [rows(res, m) for m in chosen]
-        reach = [rows(far, m) for m in chosen]
+        decay, weight, reach = ([rows(tables, at + m) for m in chosen] for at in (dec, res, far))
         state = [jnp.zeros((fold, LANES), F32) for _ in chosen]
         for n, payload in enumerate(reversed(payloads)):
             block_end = [rows(payload, m) + f * s for m, f, s in zip(chosen, reach, state)]
@@ -259,7 +260,7 @@
         def step(i, carry, decay=decay, put=put):
             state, total = carry
             at = tokens - 1 - i
-            row = sig[pl.ds(at * fold, fold), :]
+            row = tables[pl.ds(at * fold, fold), :]
             other = prod[pl.ds(at * fold, fold), :]
             state = [row + d * s for d, s in zip(decay, state)]
             total = [a + other * s for a, s in zip(total, state)]
@@ -276,26 +277,26 @@
         taps = [filt[p + 1, j : j + 1, :] for j in range(3)]
         for j in range(fold):
             lanes = slice(j * LANES, (j + 1) * LANES)
-            rounded[p, lanes, :] = tapped(ext, taps, lanes, tokens).T.astype(BF16)
+            rounded[p, lanes, :] = tapped(ext, taps, lanes, tokens).astype(BF16).T
     for j in range(fold):
         sums[0:modes, j * LANES : (j + 1) * LANES] = acc[pl.ds(j, modes, stride=fold), :]
     for move in moves:
         move.wait()
 
 
-def state_streams(feat, og, filt, dec, far, res, bias, sig, payloads, plan, sources, w_proj):
-    tokens, channels = og.shape
-    fold = channels // LANES
-    modes = dec.shape[0] // fold
+def state_streams(feat, og, filt, bias, tables, payloads, plan, sources, w_proj):
+    tokens, channels = og.shape
+    fold = channels // LANES
+    modes = (tables.shape[0] // fold - tokens) // 3
     return pl.pallas_call(
         functools.partial(state_kernel, len(payloads), plan),
-        in_specs=[pl.BlockSpec(memory_space=pltpu.SMEM)] + [whole()] * (8 + len(payloads)) + [in_hbm()],
+        in_specs=[pl.BlockSpec(memory_space=pltpu.SMEM)] + [whole()] * (5 + len(payloads)) + [in_hbm()],
         out_specs=[whole()] * 4,
         out_shape=[
             pltpu.VMEM((2, channels, tokens), BF16),
             pltpu.VMEM((modes + 1, channels), F32),
             pltpu.VMEM(((tokens + 2) * fold, LANES), F32),
-            pltpu.VMEM((len(plan), w_proj.shape[1], channels), BF16),
+            pltpu.VMEM((w_proj.shape[1], len(plan) * channels), BF16),
         ],
         scratch_shapes=[pltpu.VMEM((modes * fold, LANES), F32), pltpu.VMEM((tokens * fold, LANES), F32)]
         + [pltpu.VMEM((tokens + 8, channels), F32)] * 2
@@ -303,71 +304,79 @@
         compiler_params=params(),
         cost_estimate=cost(8 * tokens * channels * modes, 40 * tokens * channels),
         name="state_streams",
-    )(sources, feat, og, filt, dec, far, res, bias, sig, *payloads, w_proj)
-
-
-def product_kernel(plan, later, first, source, w_proj, w, *refs):
+    )(sources, feat, og, filt, bias, tables, *payloads, w_proj)
+
+
+def product_kernel(plan, base, later, first, last, source, w_proj, w, *refs):
     refs = list(refs)
     moves = []
     if later:
         sems = refs.pop()
         moves = fetches(later, source, w_proj, refs.pop(), sems)
+    elif last:
+        sems = refs.pop()
+        turned = refs.pop()
     out = refs.pop()
     before = None if first else refs.pop()
     for move in moves:
         move.start()
-    features = w.shape[1]
+    x = jnp.concatenate([refs[n][h, p] for *_, parts in plan for n, h, p in parts], axis=0)
+    columns = slice(base * (x.shape[0] // len(plan)), (base + len(plan)) * (x.shape[0] // len(plan)))
+    features = w.shape[0]
     wide = min(512, features)
     for d in range(0, features, wide):
         rows = slice(d, d + wide)
-        total = None if first else before[rows]
-        for k, (_, _, _, parts) in enumerate(plan):
-            x = [refs[n][h, p] for n, h, p in parts]
-            x = x[0] if len(x) == 1 else jnp.concatenate(x, axis=0)
-            y = jnp.dot(w[k, rows], x, preferred_element_type=F32)
-            total = y if total is None else total + y
-        if later:
-            out[rows] = total
+        y = jnp.dot(w[rows, columns], x, preferred_element_type=F32)
+        if not first:
+            y = y + before[rows]
+        if last:
+            turned[:, rows] = y.T
+            moves.append(pltpu.make_async_copy(
+                turned.at[:, pl.ds(d, wide)], out.at[:, pl.ds(d, wide)], sems.at[d // wide]
+            ))
+            moves[-1].start()
         else:
-            out[:, rows] = total.T
+            out[rows] = y
     for move in moves:
         move.wait()
 
 
 def steps_of(pieces):
     arrays, plan = [], []
-    for array, stream, offset in pieces:
+    for array, places, stream, offset in pieces:
         halves = array if isinstance(array, tuple) else (array,)
-        heights, streams = halves[0].shape[:2]
-        for h in range(heights):
-            for p in range(streams):
+        for h in range(halves[0].shape[0]):
+            for p in places:
                 plan.append((stream + p, h, offset, [(len(arrays) + n, h, p) for n in range(len(halves))]))
         arrays += halves
     return arrays, plan
 
 
-def add_product(total, ready, pieces, later, sources, w_proj, span):
+def add_product(total, ready, base, pieces, later, last, sources, w_proj, span):
     features = w_proj.shape[1]
     arrays, plan = steps_of(pieces)
-    channels, tokens = ready.shape[2], arrays[0].shape[3]
+    channels, tokens = w_proj.shape[2] // lax.axis_size("chan"), arrays[0].shape[3]
     first = total is None
-    out_shape = [jax.ShapeDtypeStruct((tokens, features), F32)]
+    out_specs = [whole()]
+    out_shape = [pltpu.VMEM((features, tokens), F32)]
     scratch = []
-    if later:
-        out_shape = [
-            pltpu.VMEM((features, tokens), F32),
-            pltpu.VMEM((len(later), features, channels), BF16),
-        ]
+    if last:
+        out_specs = [in_hbm()]
+        out_shape = [jax.ShapeDtypeStruct((tokens, features), F32)]
+        scratch = [pltpu.VMEM((tokens, features), F32), pltpu.SemaphoreType.DMA((max(1, features // 512),))]
+    elif later:
+        out_specs += [whole()]
+        out_shape += [pltpu.VMEM((features, len(later) * channels), BF16)]
         scratch = [pltpu.SemaphoreType.DMA((len(later),))]
     return pl.pallas_call(
-        functools.partial(product_kernel, plan, later, first),
+        functools.partial(product_kernel, plan, base, later, first, last),
         in_specs=[pl.BlockSpec(memory_space=pltpu.SMEM), in_hbm()]
         + [whole()] * (1 + len(arrays) + (not first)),
-        out_specs=[whole()] * len(out_shape),
+        out_specs=out_specs,
         out_shape=out_shape,
         scratch_shapes=scratch,
         compiler_params=params(),
-        cost_estimate=cost(span, span // 256),
+        cost_estimate=cost(*span),
         name="add_product",
     )(sources, w_proj, ready, *arrays, *([] if first else [total]))
 
@@ -420,11 +429,10 @@
         return sums + lax.ppermute(sums, "ctx", [(i, i ^ by) for i in range(blocks)])
 
     fold = channels // LANES
-    feat, conv, og, filt, bias_row, dec, far, res, sig, own = front(
+    feat, conv, og, filt, bias_row, tables, own, brief = front(
         features, saved_conv, out_grad, short_filter, residue.T, rate.T, bias[None]
     )
-    payloads = [from_later(own, by) for by in range(1, blocks)]
-    payloads = list(lax.optimization_barrier(tuple(payloads)))
+    payloads = [from_later(own, 1)] + [from_later(brief, by) for by in range(2, blocks)]
     gate = gate_stream(feat, conv, og, filt, bias_row, payloads[0])
     a0 = stacked(gate)
     a1, z1 = up(a0), down(a0)
@@ -432,65 +440,72 @@
     half = channels // 2
     back = ring // 2
 
-    def plan_of(streams, *offsets):
-        shape = jax.ShapeDtypeStruct((heights, len(streams), channels, tokens), BF16)
-        return steps_of([(shape, streams[0], o) for o in offsets])[1]
-
-    start = plan_of((0,), 0) + plan_of((1, 2), 0) + plan_of((0,), ring - 1, 1)
+    a, b = (0,), (0, 1)
+    sets = [
+        [("a0", a, 0, 0), ("b0", b, 1, 0)],
+        [("a1", a, 0, ring - 1), ("z1", a, 0, 1)],
+        [("b1", b, 1, ring - 1), ("y1", (0,), 1, 1)],
+        [("y1", (1,), 1, 1), ("a2", a, 0, ring - 2), ("z2", a, 0, 2)],
+        [("b2", b, 1, ring - 2), ("y2", (0,), 1, 2)],
+        [("y2", (1,), 1, 2), ("a3", a, 0, ring - 3), ("z3", a, 0, 3)],
+        [("b3", b, 1, ring - 3), ("y3", (0,), 1, 3)],
+        [("y3", (1,), 1, 3), ("a4", a, 0, back)],
+        [("b4", a, 1, back), ("y4", a, 2, back)],
+    ]
+    spans = [LONG, LONG, SHORT, LONG, SHORT, LONG, MIDDLE, SMALL, SHORT]
+    hollow = jax.ShapeDtypeStruct((heights, 2, channels, tokens), BF16)
+
+    def plan_of(n):
+        return steps_of([(hollow, *piece[1:]) for piece in sets[n]])[1]
+
+    def times(n, total, ready, **arrays):
+        pieces = [(arrays[name], *rest) for name, *rest in sets[n]]
+        later = plan_of(n + 1) if n < 6 else plan_of(7) + plan_of(8) if n == 6 else None
+        base = len(plan_of(7)) if n == 8 else 0
+        return add_product(total, ready, base, pieces, later, n == 8, sources, w_proj, spans[n])
+
     payloads[0], a0 = lax.optimization_barrier((payloads[0], a0))
     rounds, sums, gp, ready = state_streams(
-        feat, og, filt, dec, far, res, bias_row.reshape(fold, LANES), sig, payloads, start, sources, w_proj
+        feat, og, filt, bias_row.reshape(fold, LANES), tables, payloads, plan_of(0), sources, w_proj
     )
     b0 = stacked(rounds)
 
     b1, y1 = up(b0), down(b0)
     a1, z1, b0 = lax.optimization_barrier((a1, z1, b0))
     a2, z2 = up(a1), down(z1)
-    total, ready = add_product(
-        None, ready, [(a0, 0, 0), (b0, 1, 0), (a1, 0, ring - 1), (z1, 0, 1)],
-        plan_of((1, 2), ring - 1, 1), sources, w_proj, LONG,
-    )
-    grads = gradients(feat, conv, og, filt, bias_row, payloads[0], after(gp, total))
+    total, ready = times(0, None, ready, a0=a0, b0=b0)
+    total, ready = times(1, total, ready, a1=a1, z1=z1)
+    grads = gradients(feat, saved_conv, og, filt, bias_row, payloads[0], after(gp, total))
 
     b1, y1, total, grads = lax.optimization_barrier((b1, y1, total, grads))
     b2, y2 = up(b1), down(y1)
-    total, ready = add_product(
-        total, ready, [(b1, 1, ring - 1), (y1, 1, 1)], plan_of((0,), ring - 2, 2), sources, w_proj, SHORT
-    )
+    total, ready = times(2, total, ready, b1=b1, y1=y1)
 
     a2, z2, total, sums = lax.optimization_barrier((a2, z2, total, sums))
     a3, z3 = up(a2), down(z2)
     distances = [1 << n for n in range((blocks - 1).bit_length())]
     for by in distances[:-1]:
         sums = exchanged(sums, by)
-    total, ready = add_product(
-        total, ready, [(a2, 0, ring - 2), (z2, 0, 2)], plan_of((1, 2), ring - 2, 2), sources, w_proj, LONG
-    )
+    total, ready = times(3, total, ready, y1=y1, a2=a2, z2=z2)
 
     b2, y2, total, sums = lax.optimization_barrier((b2, y2, total, sums))
     b3, y3 = up(b2), down(y2)
-    total, ready = add_product(
-        total, ready, [(b2, 1, ring - 2), (y2, 1, 2)], plan_of((0,), ring - 3, 3), sources, w_proj, SHORT
-    )
+    total, ready = times(4, total, ready, b2=b2, y2=y2)
 
     a3, z3, total, sums = lax.optimization_barrier((a3, z3, total, sums))
     for by in distances[-1:]:
         sums = exchanged(sums, by)
     sums = sums * (tokens * blocks) ** (-0.5)
     a4 = up(a3[:, :, :half]), down(z3[:, :, half:])
-    total, ready = add_product(
-        total, ready, [(a3, 0, ring - 3), (z3, 0, 3)], plan_of((1, 2), ring - 3, 3), sources, w_proj, LONG
-    )
+    total, ready = times(5, total, ready, y2=y2, a3=a3, z3=z3)
 
     b3, y3, total, sums = lax.optimization_barrier((b3, y3, total, sums))
     b4, y4 = up(b3[:, :1]), down(y3[:, 1:])
-    total, ready = add_product(
-        total, ready, [(b3, 1, ring - 3), (y3, 1, 3)], plan_of((0,), back), sources, w_proj, 9 << 28
-    )
+    total, ready = times(6, total, ready, b3=b3, y3=y3)
 
     a4, total = lax.optimization_barrier((a4, total))
-    total, ready = add_product(total, ready, [(a4, 0, back)], plan_of((1, 2), back), sources, w_proj, 3 << 28)
-    (grad_x,) = add_product(total, ready, [(b4, 1, back), (y4, 2, back)], None, sources, w_proj, SHORT)
+    (total,) = times(7, total, ready, y3=y3, a4=a4)
+    (grad_x,) = times(8, total, ready, b4=b4, y4=y4)
     return (grads, grad_x, sums[:modes].T, sums[modes])
 
 

time: 89.6 us -> 85 us (0.949)
  local copies, waits for them, and re-layouts: 6.36 us -> 1.99 us
  Pallas kernels: 44.2 us -> 45.8 us
  waiting for transfers between devices: 15.3 us -> 14.1 us
    ppermute x8, starting transfers between devices: 3.22 us -> 14.3 us  [up(): return lax.ppermute(x, 'chan', pairs[1])]
    ppermute x8, starting transfers between devices: 14.2 us -> 3.43 us  [down(): return lax.ppermute(x, 'chan', pairs[-1])]
    ppermute x8, waiting for transfers between devices: 7.23 us -> 1.76 us  [up(): return lax.ppermute(x, 'chan', pairs[1])]
    unnamed x12 -> x2, local copies, waits for them, and re-layouts: 4.38 us -> 0.01 us
    pallas_call x8 -> x9, Pallas kernels: 34.2 us -> 38 us  [add_product(): pl.pallas_call(functools.partial(product_kernel, plan, base, later, first...]
    ppermute x3, waiting for transfers between devices: 4.79 us -> 7.87 us  [from_later(): return lax.ppermute(array, 'ctx', [(i, i - by) for i in range(by, blocks)])]
    pallas_call x1, Pallas kernels: 4.7 us -> 3.46 us  [state_streams(): pl.pallas_call(functools.partial(state_kernel, len(payloads), plan), in_s...]
    ppermute x8, waiting for transfers between devices: 3.25 us -> 4.46 us  [down(): return lax.ppermute(x, 'chan', pairs[-1])]
  transfers between devices with their start and end apart: 21 -> 21, of which waited for: 8 -> 9; matrix products, arithmetic and copies ran while one was open for 2% -> 2% of each run, Pallas kernels for 43% -> 48%
where the time goes in v5:
time: 85 us; the launch traced here: 84.7 us
  Pallas kernels  45.8 us (54%)
  starting transfers between devices  21.8 us (26%)
  waiting for transfers between devices  14.1 us (17%)
  local copies, waits for them, and re-layouts  1.99 us (2%)
  between operations  1.05 us (1%)
    pallas_call x9, Pallas kernels, add_product(): pl.pallas_call(functools.partial(product_kernel, plan, base, later, first...  38 us
    ppermute x8, starting transfers between devices, up(): return lax.ppermute(x, 'chan', pairs[1])  14.3 us
    ppermute x3, waiting for transfers between devices, from_later(): return lax.ppermute(array, 'ctx', [(i, i - by) for i in range(by, blocks)])  7.87 us
    ppermute x8, waiting for transfers between devices, down(): return lax.ppermute(x, 'chan', pairs[-1])  4.46 us
    ppermute x3, starting transfers between devices, from_later(): return lax.ppermute(array, 'ctx', [(i, i - by) for i in range(by, blocks)])  3.86 us
    pallas_call x1, Pallas kernels, state_streams(): pl.pallas_call(functools.partial(state_kernel, len(payloads), plan), in_s...  3.46 us
    ppermute x8, starting transfers between devices, down(): return lax.ppermute(x, 'chan', pairs[-1])  3.43 us
    pallas_call x1, Pallas kernels, front(): pl.pallas_call(front_kernel, in_specs=[in_hbm()] * 7, out_specs=[whole()]...  2.11 us
  transfers between devices with their start and end apart: 21, of which 9 were waited for; matrix products, arithmetic and copies ran while one was open for 2% of the time, Pallas kernels for 48%

profile of v5, /device:TPU:0, one launch (start us, length us, event | category | flops | bytes accessed | tf_op | source)
XLA Modules:
  0.0 84.7 jit_solution(884024854557965977)
XLA Ops:
  0.6 2.1 %front.1 = (f32[3,128,1024]{2,1,0:T(8,128)S(1)}, f32[128,1024]{1,0:T(8,128)S(1)}, f32[128,1024]{1,0:T(8,128)S(1)}, f32[3,3,1024]{2,1,0:T(4,128)S(1)}, f32[1,1024...) custom-call(f32[3,128,1024]{2,1,0:T(8,128)} %features.1, ...), custom_call_target="tpu_custom_call" | custom-call | flops 8388608 | bytes 2621440 | tf_op jit(solution)/shard_map/front/pallas_call | solution.py:96
  4.1 1.9 %collective-permute-done.later.refs_0_ = f32[224,128]{1,0:T(8,128)S(1)} collective-permute-done((f32[224,128]{1,0:T(8,128)S(1)}, f32[224,128]{1,0:T(8,128)S(1)}, u32[]{:S(2)}, u32[]{:S(2)}) %collective-permute-start) | collective-permute-done | bytes 114720 | tf_op jit(solution)/shard_map/ppermute | solution.py:426
  6.3 3.1 %collective-permute-start.5 = (bf16[1,1,1024,128]{3,2,1,0:T(8,128)(2,1)S(1)}, bf16[1,1,1024,128]{3,2,1,0:T(8,128)(2,1)}, u32[]{:S(2)}, u32[]{:S(2)}) collective-permute-start(bf16[1,1,1024,128]{3,2,1,0:T(8,128)(2,1)S(1)} %bitcast.15), channel_id=1, source_target_pairs={{0,2},{2,4},{4,6},{6,7},{7,5},{5,3},{3,1},{1,0},{8,10},{10,12},{12... | collective-permute-start | bytes 786440 | tf_op jit(solution)/shard_map/ppermute | solution.py:414
  12.7 3.3 %collective-permute-done.1.refs_1_ = f32[144,128]{1,0:T(8,128)S(1)} collective-permute-done((f32[144,128]{1,0:T(8,128)S(1)}, f32[144,128]{1,0:T(8,128)S(1)}, u32[]{:S(2)}, u32[]{:S(2)}) %collective-permute-start.1) | collective-permute-done | bytes 73760 | tf_op jit(solution)/shard_map/ppermute | solution.py:426
  16.0 2.6 %collective-permute-done.2.refs_2_ = f32[144,128]{1,0:T(8,128)S(1)} collective-permute-done((f32[144,128]{1,0:T(8,128)S(1)}, f32[144,128]{1,0:T(8,128)S(1)}, u32[]{:S(2)}, u32[]{:S(2)}) %collective-permute-start.2) | collective-permute-done | bytes 73760 | tf_op jit(solution)/shard_map/ppermute | solution.py:426
  18.6 3.5 %state_streams.1 = (bf16[2,1024,128]{2,1,0:T(8,128)(2,1)S(1)}, f32[17,1024]{1,0:T(8,128)S(1)}, f32[1040,128]{1,0:T(8,128)S(1)}, bf16[1024,3072]{1,0:T(8,128)(2,1)S(1)}) custom-call(s32[8]{0:T(128)S(1)} %dynamic-slice_bitcast_fusion.source, f32[3,128,1024]{2,1,0:T(8,128)S(1)} %get-tuple-element.59.feat, f32[128,1024]{1,0:T(8,128)S(1)} %get-tuple-element.60.og, ...), custom_call_target="tpu_custom_call" | custom-call | flops 16777216 | bytes 5242880 | tf_op jit(solution)/shard_map/state_streams/pallas_call | solution.py:291
  22.1 1.6 %collective-permute-start.3 = (bf16[1,2,1024,128]{3,2,1,0:T(8,128)(2,1)S(1)}, bf16[1,2,1024,128]{3,2,1,0:T(8,128)(2,1)S(1)}, u32[]{:S(2)}, u32[]{:S(2)}) collective-permute-start(bf16[1,2,1024,128]{3,2,1,0:T(8,128)(2,1)S(1)} %bitcast.12), channel_id=1, source_target_pairs={{0,2},{2,4},{4,6},{6,7},{7,5},{5,3},{3,1},{1,0},{8,10},{10,12},{12... | collective-permute-start | bytes 1572872 | tf_op jit(solution)/shard_map/ppermute | solution.py:414
  24.2 1.6 %collective-permute-start.7 = (bf16[1,1,1024,128]{3,2,1,0:T(8,128)(2,1)}, bf16[1,1,1024,128]{3,2,1,0:T(8,128)(2,1)}, u32[]{:S(2)}, u32[]{:S(2)}) collective-permute-start(bf16[1,1,1024,128]{3,2,1,0:T(8,128)(2,1)} %collective-permute-done.5.refs_0_), channel_id=1, source_target_pairs={{0,2},{2,4},{4,6},{6,7},{7,5},{5,3},{3,1},{1,0},{8,10},{10,12},{12... | collective-permute-start | bytes 786440 | tf_op jit(solution)/shard_map/ppermute | solution.py:414
  26.2 3.7 %add_product.9 = (f32[1024,128]{1,0:T(8,128)S(1)}, bf16[1024,2048]{1,0:T(8,128)(2,1)S(1)}) custom-call(s32[8]{0:T(128)S(1)} %dynamic-slice_bitcast_fusion.source, bf16[3,1024,8192]{2,1,0:T(8,128)(2,1)} %w_proj.17, bf16[1024,3072]{1,0:T(8,128)(2,1)S(1)} %get-tuple-element.69.w, bf16[1,1,1024,128]{3,2,1,0:T(8,128)(2,1)S(1)} %bitcast.17, ...), custom_call_target="tpu_custom_call" | custom-call | flops 68719476736 | bytes 268435456 | tf_op jit(solution)/shard_map/add_product/pallas_call | solution.py:371
  29.9 5.1 %add_product.10 = (f32[1024,128]{1,0:T(8,128)S(1)}, bf16[1024,3072]{1,0:T(8,128)(2,1)S(1)}) custom-call(s32[8]{0:T(128)S(1)} %dynamic-slice_bitcast_fusion.source, bf16[3,1024,8192]{2,1,0:T(8,128)(2,1)} %w_proj.17, bf16[1024,2048]{1,0:T(8,128)(2,1)S(1)} %get-tuple-element.72.w, bf16[1,1,1024,128]{3,2,1,0:T(8,128)(2,1)} %collective-permute-done.5.refs_0_, ...), custom_call_target="tpu_custom_call" | custom-call | flops 68719476736 | bytes 268435456 | tf_op jit(solution)/shard_map/add_product/pallas_call | solution.py:371
  35.1 1.8 %gradients.1 = f32[3,128,1024]{2,1,0:T(8,128)} custom-call(f32[3,128,1024]{2,1,0:T(8,128)S(1)} %get-tuple-element.59.feat, f32[128,1024]{1,0:T(8,128)S(1)} %copy-done, f32[128,1024]{1,0:T(8,128)S(1)} %get-tuple-element.60.og, f32[3,3,1024]{2,1,0:T(4,128)S(1)} %get-tuple-element.61.filt, f32[1,1024]{1,0:T(1,128)S(1)} %get-tuple-element.62.bias, ...), custom_call_target="tpu_custom_call" | custom-call | flops 3932160 | bytes 5242880 | tf_op jit(solution)/shard_map/gradients/pallas_call | solution.py:184
  37.0 1.6 %collective-permute-done.4.refs_1_.refs_0_ = bf16[1,2,1024,128]{3,2,1,0:T(8,128)(2,1)S(1)} collective-permute-done((bf16[1,2,1024,128]{3,2,1,0:T(8,128)(2,1)S(1)}, bf16[1,2,1024,128]{3,2,1,0:T(8,128)(2,1)S(1)}, u32[]{:S(2)}, u32[]{:S(2)}) %collective-permute-start.4) | collective-permute-done | bytes 524320 | tf_op jit(solution)/shard_map/ppermute | solution.py:417
  38.6 1.6 %collective-permute-start.9 = (bf16[1,2,1024,128]{3,2,1,0:T(8,128)(2,1)S(1)}, bf16[1,2,1024,128]{3,2,1,0:T(8,128)(2,1)S(1)}, u32[]{:S(2)}, u32[]{:S(2)}) collective-permute-start(bf16[1,2,1024,128]{3,2,1,0:T(8,128)(2,1)S(1)} %collective-permute-done.3.refs_0_), channel_id=1, source_target_pairs={{0,2},{2,4},{4,6},{6,7},{7,5},{5,3},{3,1},{1,0},{8,10},{10,12},{12... | collective-permute-start | bytes 1572872 | tf_op jit(solution)/shard_map/ppermute | solution.py:414
  40.6 4.3 %add_product.11 = (f32[1024,128]{1,0:T(8,128)S(1)}, bf16[1024,3072]{1,0:T(8,128)(2,1)S(1)}) custom-call(s32[8]{0:T(128)S(1)} %dynamic-slice_bitcast_fusion.source, bf16[3,1024,8192]{2,1,0:T(8,128)(2,1)} %w_proj.17, bf16[1024,3072]{1,0:T(8,128)(2,1)S(1)} %get-tuple-element.80.w, bf16[1,2,1024,128]{3,2,1,0:T(8,128)(2,1)S(1)} %collective-permute-done.3.refs_0_, ...), custom_call_target="tpu_custom_call" | custom-call | flops 65536 | bytes 256 | tf_op jit(solution)/shard_map/add_product/pallas_call | solution.py:371
  45.0 1.6 %collective-permute-start.12 = (bf16[1,1,1024,128]{3,2,1,0:T(8,128)(2,1)}, bf16[1,1,1024,128]{3,2,1,0:T(8,128)(2,1)S(1)}, u32[]{:S(2)}, u32[]{:S(2)}) collective-permute-start(bf16[1,1,1024,128]{3,2,1,0:T(8,128)(2,1)} %collective-permute-done.7.refs_1_), channel_id=1, source_target_pairs={{0,2},{2,4},{4,6},{6,7},{7,5},{5,3},{3,1},{1,0},{8,10},{10,12},{12... | collective-permute-start | bytes 786440 | tf_op jit(solution)/shard_map/ppermute | solution.py:414
  47.1 5.6 %add_product.12 = (f32[1024,128]{1,0:T(8,128)S(1)}, bf16[1024,3072]{1,0:T(8,128)(2,1)S(1)}) custom-call(s32[8]{0:T(128)S(1)} %dynamic-slice_bitcast_fusion.source, bf16[3,1024,8192]{2,1,0:T(8,128)(2,1)} %w_proj.17, bf16[1024,3072]{1,0:T(8,128)(2,1)S(1)} %get-tuple-element.84.w, bf16[1,2,1024,128]{3,2,1,0:T(8,128)(2,1)S(1)} %collective-permute-done.4.refs_1_.refs_0_, ...), custom_call_target="tpu_custom_call" | custom-call | flops 68719476736 | bytes 268435456 | tf_op jit(solution)/shard_map/add_product/pallas_call | solution.py:371
  55.4 1.6 %collective-permute-start.14 = (bf16[1,2,1024,128]{3,2,1,0:T(8,128)(2,1)S(1)}, bf16[1,2,1024,128]{3,2,1,0:T(8,128)(2,1)S(1)}, u32[]{:S(2)}, u32[]{:S(2)}) collective-permute-start(bf16[1,2,1024,128]{3,2,1,0:T(8,128)(2,1)S(1)} %collective-permute-done.9.refs_0_), channel_id=1, source_target_pairs={{0,2},{2,4},{4,6},{6,7},{7,5},{5,3},{3,1},{1,0},{8,10},{10,12},{12... | collective-permute-start | bytes 1572872 | tf_op jit(solution)/shard_map/ppermute | solution.py:414
  57.5 4.3 %add_product.13 = (f32[1024,128]{1,0:T(8,128)S(1)}, bf16[1024,3072]{1,0:T(8,128)(2,1)S(1)}) custom-call(s32[8]{0:T(128)S(1)} %dynamic-slice_bitcast_fusion.source, bf16[3,1024,8192]{2,1,0:T(8,128)(2,1)} %w_proj.17, bf16[1024,3072]{1,0:T(8,128)(2,1)S(1)} %get-tuple-element.90.w, bf16[1,2,1024,128]{3,2,1,0:T(8,128)(2,1)S(1)} %collective-permute-done.9.refs_0_, ...), custom_call_target="tpu_custom_call" | custom-call | flops 65536 | bytes 256 | tf_op jit(solution)/shard_map/add_product/pallas_call | solution.py:371
  61.9 1.6 %collective-permute-start.19 = (bf16[1,1,512,128]{3,2,1,0:T(8,128)(2,1)S(1)}, bf16[1,1,512,128]{3,2,1,0:T(8,128)(2,1)S(1)}, u32[]{:S(2)}, u32[]{:S(2)}) collective-permute-start(bf16[1,1,512,128]{3,2,1,0:T(8,128)(2,1)S(1)} %slice.20), channel_id=1, source_target_pairs={{0,2},{2,4},{4,6},{6,7},{7,5},{5,3},{3,1},{1,0},{8,10},{10,12},{12... | collective-permute-start | bytes 393224 | tf_op jit(solution)/shard_map/ppermute | solution.py:414
  64.0 5.1 %add_product.14 = (f32[1024,128]{1,0:T(8,128)S(1)}, bf16[1024,3072]{1,0:T(8,128)(2,1)S(1)}) custom-call(s32[8]{0:T(128)S(1)} %dynamic-slice_bitcast_fusion.source, bf16[3,1024,8192]{2,1,0:T(8,128)(2,1)} %w_proj.17, bf16[1024,3072]{1,0:T(8,128)(2,1)S(1)} %get-tuple-element.96.w, bf16[1,2,1024,128]{3,2,1,0:T(8,128)(2,1)S(1)} %collective-permute-done.10.refs_1_.refs_0_, ...), custom_call_target="tpu_custom_call" | custom-call | flops 68719476736 | bytes 268435456 | tf_op jit(solution)/shard_map/add_product/pallas_call | solution.py:371
  70.9 1.6 %collective-permute-start.17 = (bf16[1,1,1024,128]{3,2,1,0:T(8,128)(2,1)S(1)}, bf16[1,1,1024,128]{3,2,1,0:T(8,128)(2,1)S(1)}, u32[]{:S(2)}, u32[]{:S(2)}) collective-permute-start(bf16[1,1,1024,128]{3,2,1,0:T(8,128)(2,1)S(1)} %slice.18), channel_id=1, source_target_pairs={{0,2},{2,4},{4,6},{6,7},{7,5},{5,3},{3,1},{1,0},{8,10},{10,12},{12... | collective-permute-start | bytes 786440 | tf_op jit(solution)/shard_map/ppermute | solution.py:414
  73.3 5.5 %add_product.15 = (f32[1024,128]{1,0:T(8,128)S(1)}, bf16[1024,4096]{1,0:T(8,128)(2,1)S(1)}) custom-call(s32[8]{0:T(128)S(1)} %dynamic-slice_bitcast_fusion.source, bf16[3,1024,8192]{2,1,0:T(8,128)(2,1)} %w_proj.17, bf16[1024,3072]{1,0:T(8,128)(2,1)S(1)} %get-tuple-element.102.w, bf16[1,2,1024,128]{3,2,1,0:T(8,128)(2,1)S(1)} %collective-permute-done.14.refs_0_, ...), custom_call_target="tpu_custom_call" | custom-call | flops 1073741824 | bytes 9437184 | tf_op jit(solution)/shard_map/add_product/pallas_call | solution.py:371
  79.5 1.8 %add_product.16.refs_2_ = f32[1024,128]{1,0:T(8,128)S(1)} custom-call(s32[8]{0:T(128)S(1)} %dynamic-slice_bitcast_fusion.source, bf16[3,1024,8192]{2,1,0:T(8,128)(2,1)} %w_proj.17, bf16[1024,4096]{1,0:T(8,128)(2,1)S(1)} %get-tuple-element.108.w, bf16[1,2,1024,128]{3,2,1,0:T(8,128)(2,1)S(1)} %collective-permute-done.15.refs_1_.refs_0_, ...), custom_call_target="tpu_custom_call" | custom-call | flops 268435456 | bytes 3145728 | tf_op jit(solution)/shard_map/add_product/pallas_call | solution.py:371
  81.9 2.7 %add_product.17 = f32[128,1024]{1,0:T(8,128)} custom-call(s32[8]{0:T(128)S(1)} %dynamic-slice_bitcast_fusion.source, bf16[3,1024,8192]{2,1,0:T(8,128)(2,1)} %w_proj.17, bf16[1024,4096]{1,0:T(8,128)(2,1)S(1)} %get-tuple-element.108.w, bf16[1,1,1024,128]{3,2,1,0:T(8,128)(2,1)S(1)} %collective-permute-done.17.refs_0_, ...), custom_call_target="tpu_custom_call" | custom-call | flops 65536 | bytes 256 | tf_op jit(solution)/shard_map/add_product/pallas_call | solution.py:371
  (42 shorter events, 14.4 us)
Async XLA Ops:
  2.8 3.2 %collective-permute-start = (f32[224,128]{1,0:T(8,128)S(1)}, f32[224,128]{1,0:T(8,128)S(1)}, u32[]{:S(2)}, u32[]{:S(2)}) collective-permute-start(f32[224,128]{1,0:T(8,128)S(1)} %get-tuple-element.64), channel_id=1, source_target_pairs={{8,0},{16,8},{24,16},{9,1},{17,9},{25,17},{10,2},{18,10},{26,18},{... | collective-permute-start | bytes 344072 | tf_op jit(solution)/shard_map/ppermute | solution.py:426
  6.3 17.9 %collective-permute-start.5 = (bf16[1,1,1024,128]{3,2,1,0:T(8,128)(2,1)S(1)}, bf16[1,1,1024,128]{3,2,1,0:T(8,128)(2,1)}, u32[]{:S(2)}, u32[]{:S(2)}) collective-permute-start(bf16[1,1,1024,128]{3,2,1,0:T(8,128)(2,1)S(1)} %bitcast.15), channel_id=1, source_target_pairs={{0,2},{2,4},{4,6},{6,7},{7,5},{5,3},{3,1},{1,0},{8,10},{10,12},{12... | collective-permute-start | bytes 786440 | tf_op jit(solution)/shard_map/ppermute | solution.py:414
  9.4 14.8 %collective-permute-start.6 = (bf16[1,1,1024,128]{3,2,1,0:T(8,128)(2,1)S(1)}, bf16[1,1,1024,128]{3,2,1,0:T(8,128)(2,1)}, u32[]{:S(2)}, u32[]{:S(2)}) collective-permute-start(bf16[1,1,1024,128]{3,2,1,0:T(8,128)(2,1)S(1)} %bitcast.16), channel_id=1, source_target_pairs={{0,1},{2,0},{4,2},{6,4},{7,6},{5,7},{3,5},{1,3},{8,9},{10,8},{12,1... | collective-permute-start | bytes 786440 | tf_op jit(solution)/shard_map/ppermute | solution.py:417
  9.4 6.6 %collective-permute-start.1 = (f32[144,128]{1,0:T(8,128)S(1)}, f32[144,128]{1,0:T(8,128)S(1)}, u32[]{:S(2)}, u32[]{:S(2)}) collective-permute-start(f32[144,128]{1,0:T(8,128)S(1)} %get-tuple-element.67), channel_id=1, source_target_pairs={{16,0},{24,8},{17,1},{25,9},{18,2},{26,10},{19,3},{27,11},{20,4},{... | collective-permute-start | bytes 221192 | tf_op jit(solution)/shard_map/ppermute | solution.py:426
  10.7 8.0 %collective-permute-start.2 = (f32[144,128]{1,0:T(8,128)S(1)}, f32[144,128]{1,0:T(8,128)S(1)}, u32[]{:S(2)}, u32[]{:S(2)}) collective-permute-start(f32[144,128]{1,0:T(8,128)S(1)} %get-tuple-element.67), channel_id=1, source_target_pairs={{24,0},{25,1},{26,2},{27,3},{28,4},{29,5},{30,6},{31,7}} | collective-permute-start | bytes 221192 | tf_op jit(solution)/shard_map/ppermute | solution.py:426
  22.1 14.9 %collective-permute-start.3 = (bf16[1,2,1024,128]{3,2,1,0:T(8,128)(2,1)S(1)}, bf16[1,2,1024,128]{3,2,1,0:T(8,128)(2,1)S(1)}, u32[]{:S(2)}, u32[]{:S(2)}) collective-permute-start(bf16[1,2,1024,128]{3,2,1,0:T(8,128)(2,1)S(1)} %bitcast.12), channel_id=1, source_target_pairs={{0,2},{2,4},{4,6},{6,7},{7,5},{5,3},{3,1},{1,0},{8,10},{10,12},{12... | collective-permute-start | bytes 1572872 | tf_op jit(solution)/shard_map/ppermute | solution.py:414
  23.7 14.9 %collective-permute-start.4 = (bf16[1,2,1024,128]{3,2,1,0:T(8,128)(2,1)S(1)}, bf16[1,2,1024,128]{3,2,1,0:T(8,128)(2,1)S(1)}, u32[]{:S(2)}, u32[]{:S(2)}) collective-permute-start(bf16[1,2,1024,128]{3,2,1,0:T(8,128)(2,1)S(1)} %bitcast.13), channel_id=1, source_target_pairs={{0,1},{2,0},{4,2},{6,4},{7,6},{5,7},{3,5},{1,3},{8,9},{10,8},{12,1... | collective-permute-start | bytes 1572872 | tf_op jit(solution)/shard_map/ppermute | solution.py:417
  24.2 20.7 %collective-permute-start.7 = (bf16[1,1,1024,128]{3,2,1,0:T(8,128)(2,1)}, bf16[1,1,1024,128]{3,2,1,0:T(8,128)(2,1)}, u32[]{:S(2)}, u32[]{:S(2)}) collective-permute-start(bf16[1,1,1024,128]{3,2,1,0:T(8,128)(2,1)} %collective-permute-done.5.refs_0_), channel_id=1, source_target_pairs={{0,2},{2,4},{4,6},{6,7},{7,5},{5,3},{3,1},{1,0},{8,10},{10,12},{12... | collective-permute-start | bytes 786440 | tf_op jit(solution)/shard_map/ppermute | solution.py:414
  25.8 19.1 %collective-permute-start.8 = (bf16[1,1,1024,128]{3,2,1,0:T(8,128)(2,1)}, bf16[1,1,1024,128]{3,2,1,0:T(8,128)(2,1)}, u32[]{:S(2)}, u32[]{:S(2)}) collective-permute-start(bf16[1,1,1024,128]{3,2,1,0:T(8,128)(2,1)} %collective-permute-done.6.refs_1_), channel_id=1, source_target_pairs={{0,1},{2,0},{4,2},{6,4},{7,6},{5,7},{3,5},{1,3},{8,9},{10,8},{12,1... | collective-permute-start | bytes 786440 | tf_op jit(solution)/shard_map/ppermute | solution.py:417
  29.9 5.1 %copy-start = (f32[128,1024]{1,0:T(8,128)S(1)}, f32[128,1024]{1,0:T(8,128)}, u32[]{:S(2)}) copy-start(f32[128,1024]{1,0:T(8,128)} %conv.1) | copy-start | bytes 1572868
  38.6 15.3 %collective-permute-start.9 = (bf16[1,2,1024,128]{3,2,1,0:T(8,128)(2,1)S(1)}, bf16[1,2,1024,128]{3,2,1,0:T(8,128)(2,1)S(1)}, u32[]{:S(2)}, u32[]{:S(2)}) collective-permute-start(bf16[1,2,1024,128]{3,2,1,0:T(8,128)(2,1)S(1)} %collective-permute-done.3.refs_0_), channel_id=1, source_target_pairs={{0,2},{2,4},{4,6},{6,7},{7,5},{5,3},{3,1},{1,0},{8,10},{10,12},{12... | collective-permute-start | bytes 1572872 | tf_op jit(solution)/shard_map/ppermute | solution.py:414
  40.2 15.3 %collective-permute-start.10 = (bf16[1,2,1024,128]{3,2,1,0:T(8,128)(2,1)S(1)}, bf16[1,2,1024,128]{3,2,1,0:T(8,128)(2,1)S(1)}, u32[]{:S(2)}, u32[]{:S(2)}) collective-permute-start(bf16[1,2,1024,128]{3,2,1,0:T(8,128)(2,1)S(1)} %collective-permute-done.4.refs_1_.refs_0_), channel_id=1, source_target_pairs={{0,1},{2,0},{4,2},{6,4},{7,6},{5,7},{3,5},{1,3},{8,9},{10,8},{12,1... | collective-permute-start | bytes 1572872 | tf_op jit(solution)/shard_map/ppermute | solution.py:417
  44.9 7.8 %collective-permute-start.11 = (f32[17,1024]{1,0:T(8,128)S(1)}, f32[17,1024]{1,0:T(8,128)S(1)}, u32[]{:S(2)}, u32[]{:S(2)}) collective-permute-start(f32[17,1024]{1,0:T(8,128)S(1)} %get-tuple-element.92), channel_id=1, source_target_pairs={{0,8},{8,0},{16,24},{24,16},{1,9},{9,1},{17,25},{25,17},{2,10},{10... | collective-permute-start | bytes 208904 | tf_op jit(solution)/shard_map/ppermute | solution.py:429
  45.0 16.8 %collective-permute-start.12 = (bf16[1,1,1024,128]{3,2,1,0:T(8,128)(2,1)}, bf16[1,1,1024,128]{3,2,1,0:T(8,128)(2,1)S(1)}, u32[]{:S(2)}, u32[]{:S(2)}) collective-permute-start(bf16[1,1,1024,128]{3,2,1,0:T(8,128)(2,1)} %collective-permute-done.7.refs_1_), channel_id=1, source_target_pairs={{0,2},{2,4},{4,6},{6,7},{7,5},{5,3},{3,1},{1,0},{8,10},{10,12},{12... | collective-permute-start | bytes 786440 | tf_op jit(solution)/shard_map/ppermute | solution.py:414
  46.6 15.1 %collective-permute-start.13 = (bf16[1,1,1024,128]{3,2,1,0:T(8,128)(2,1)}, bf16[1,1,1024,128]{3,2,1,0:T(8,128)(2,1)S(1)}, u32[]{:S(2)}, u32[]{:S(2)}) collective-permute-start(bf16[1,1,1024,128]{3,2,1,0:T(8,128)(2,1)} %collective-permute-done.8.refs_2_), channel_id=1, source_target_pairs={{0,1},{2,0},{4,2},{6,4},{7,6},{5,7},{3,5},{1,3},{8,9},{10,8},{12,1... | collective-permute-start | bytes 786440 | tf_op jit(solution)/shard_map/ppermute | solution.py:417
  55.4 14.2 %collective-permute-start.14 = (bf16[1,2,1024,128]{3,2,1,0:T(8,128)(2,1)S(1)}, bf16[1,2,1024,128]{3,2,1,0:T(8,128)(2,1)S(1)}, u32[]{:S(2)}, u32[]{:S(2)}) collective-permute-start(bf16[1,2,1024,128]{3,2,1,0:T(8,128)(2,1)S(1)} %collective-permute-done.9.refs_0_), channel_id=1, source_target_pairs={{0,2},{2,4},{4,6},{6,7},{7,5},{5,3},{3,1},{1,0},{8,10},{10,12},{12... | collective-permute-start | bytes 1572872 | tf_op jit(solution)/shard_map/ppermute | solution.py:414
  57.0 13.9 %collective-permute-start.15 = (bf16[1,2,1024,128]{3,2,1,0:T(8,128)(2,1)S(1)}, bf16[1,2,1024,128]{3,2,1,0:T(8,128)(2,1)S(1)}, u32[]{:S(2)}, u32[]{:S(2)}) collective-permute-start(bf16[1,2,1024,128]{3,2,1,0:T(8,128)(2,1)S(1)} %collective-permute-done.10.refs_1_.refs_0_), channel_id=1, source_target_pairs={{0,1},{2,0},{4,2},{6,4},{7,6},{5,7},{3,5},{1,3},{8,9},{10,8},{12,1... | collective-permute-start | bytes 1572872 | tf_op jit(solution)/shard_map/ppermute | solution.py:417
  61.8 7.3 %collective-permute-start.16 = (f32[17,1024]{1,0:T(8,128)S(1)}, f32[17,1024]{1,0:T(8,128)S(1)}, u32[]{:S(2)}, u32[]{:S(2)}) collective-permute-start(f32[17,1024]{1,0:T(8,128)S(1)} %add.11), channel_id=1, source_target_pairs={{0,16},{8,24},{16,0},{24,8},{1,17},{9,25},{17,1},{25,9},{2,18},{10... | collective-permute-start | bytes 208904 | tf_op jit(solution)/shard_map/ppermute | solution.py:429
  61.9 17.0 %collective-permute-start.19 = (bf16[1,1,512,128]{3,2,1,0:T(8,128)(2,1)S(1)}, bf16[1,1,512,128]{3,2,1,0:T(8,128)(2,1)S(1)}, u32[]{:S(2)}, u32[]{:S(2)}) collective-permute-start(bf16[1,1,512,128]{3,2,1,0:T(8,128)(2,1)S(1)} %slice.20), channel_id=1, source_target_pairs={{0,2},{2,4},{4,6},{6,7},{7,5},{5,3},{3,1},{1,0},{8,10},{10,12},{12... | collective-permute-start | bytes 393224 | tf_op jit(solution)/shard_map/ppermute | solution.py:414
  63.5 15.3 %collective-permute-start.20 = (bf16[1,1,512,128]{3,2,1,0:T(8,128)(2,1)S(1)}, bf16[1,1,512,128]{3,2,1,0:T(8,128)(2,1)S(1)}, u32[]{:S(2)}, u32[]{:S(2)}) collective-permute-start(bf16[1,1,512,128]{3,2,1,0:T(8,128)(2,1)S(1)} %slice.21), channel_id=1, source_target_pairs={{0,1},{2,0},{4,2},{6,4},{7,6},{5,7},{3,5},{1,3},{8,9},{10,8},{12,1... | collective-permute-start | bytes 393224 | tf_op jit(solution)/shard_map/ppermute | solution.py:417
  70.9 10.9 %collective-permute-start.17 = (bf16[1,1,1024,128]{3,2,1,0:T(8,128)(2,1)S(1)}, bf16[1,1,1024,128]{3,2,1,0:T(8,128)(2,1)S(1)}, u32[]{:S(2)}, u32[]{:S(2)}) collective-permute-start(bf16[1,1,1024,128]{3,2,1,0:T(8,128)(2,1)S(1)} %slice.18), channel_id=1, source_target_pairs={{0,2},{2,4},{4,6},{6,7},{7,5},{5,3},{3,1},{1,0},{8,10},{10,12},{12... | collective-permute-start | bytes 786440 | tf_op jit(solution)/shard_map/ppermute | solution.py:414
  72.6 9.3 %collective-permute-start.18 = (bf16[1,1,1024,128]{3,2,1,0:T(8,128)(2,1)S(1)}, bf16[1,1,1024,128]{3,2,1,0:T(8,128)(2,1)S(1)}, u32[]{:S(2)}, u32[]{:S(2)}) collective-permute-start(bf16[1,1,1024,128]{3,2,1,0:T(8,128)(2,1)S(1)} %slice.19), channel_id=1, source_target_pairs={{0,1},{2,0},{4,2},{6,4},{7,6},{5,7},{3,5},{1,3},{8,9},{10,8},{12,1... | collective-permute-start | bytes 786440 | tf_op jit(solution)/shard_map/ppermute | solution.py:417

commit v6 on v5

--- a/solution.py
+++ b/solution.py
@@ -12,7 +12,7 @@
 LONG = 1 << 36, 1 << 28
 SHORT = 1 << 16, 1 << 8
 MIDDLE = 1 << 30, 9 << 20
-SMALL = 1 << 28, 3 << 20
+TAIL = 7 << 28, 13 << 20
 VMEM = 8 * 1024 * 1024
 F32 = jnp.float32
 BF16 = jnp.bfloat16
@@ -40,7 +40,7 @@
 
 
 def front_kernel(features, saved_conv, out_grad, short_filter, residue, rate, bias, *refs):
-    feat, conv, og, filt, bias_in, tables, own, brief, res_in, rate_in, sems = refs
+    feat, conv, og, filt, bias_in, tables, own, res_in, rate_in, sems = refs
     tokens, channels = og.shape
     modes = rate_in.shape[0]
     fold = channels // LANES
@@ -61,7 +61,7 @@
         move.start()
     moves[0].wait()
     by_row(jnp.exp(-rate_in[...]), tables, fold, tokens)
-    by_row(jnp.exp(-(tokens - 2) * rate_in[...]), tables, fold, tokens + modes)
+    by_row(rate_in[...], tables, fold, tokens + modes)
     moves[1].wait()
     moves[2].wait()
     for j in range(fold):
@@ -75,10 +75,9 @@
 
     zero = tuple(jnp.zeros((fold, LANES), F32) for _ in range(modes))
     states = lax.fori_loop(0, tokens - 2, step, zero, unroll=6)
-    for target in (own, brief):
-        for m in range(modes):
-            target[m * fold : (m + 1) * fold, :] = states[m]
-        target[modes * fold : (modes + 2) * fold, :] = tables[0 : 2 * fold, :]
+    for m in range(modes):
+        own[m * fold : (m + 1) * fold, :] = states[m]
+    own[modes * fold : (modes + 2) * fold, :] = tables[0 : 2 * fold, :]
     for n in range(3, 8):
         moves[n].wait()
     for n in range(3):
@@ -96,9 +95,9 @@
     return pl.pallas_call(
         front_kernel,
         in_specs=[in_hbm()] * 7,
-        out_specs=[whole()] * 8,
+        out_specs=[whole()] * 7,
         out_shape=[pltpu.VMEM(a.shape, F32) for a in (*inputs[:4], bias)]
-        + [pltpu.VMEM((n * fold, LANES), F32) for n in (tokens + 3 * modes, modes + 12, modes + 2)],
+        + [pltpu.VMEM((n * fold, LANES), F32) for n in (tokens + 3 * modes, modes + 12)],
         scratch_shapes=[pltpu.VMEM(rate.shape, F32)] * 2 + [pltpu.SemaphoreType.DMA((8,))],
         compiler_params=params(),
         cost_estimate=cost(4 * tokens * channels * modes, 20 * tokens * channels),
@@ -128,8 +127,40 @@
         ext[tokens : tokens + 2, lanes] = cotangent * (held + bias[:, lanes] * (key * value))
 
 
-def gate_kernel(feat, conv, og, filt, bias, later, rounded, ext):
-    tokens, channels = og.shape
+def carried(own, m, later, state, decay, rate, span, fold):
+    modes = later.shape[0] // fold - 2
+    s0, s1 = (later[(modes + n) * fold : (modes + n + 1) * fold, :] for n in (0, 1))
+    return own[m * fold : (m + 1) * fold, :] + jnp.exp(-(span - 2) * rate) * (s0 + decay * (s1 + decay * state))
+
+
+def joined(own, later, tables, span, modes, tokens, out):
+    fold = out.shape[0] // (modes + 2)
+    brief = later.at[pl.ds(0, (modes + 2) * fold)]
+    for m in range(modes):
+        here = slice(m * fold, (m + 1) * fold)
+        decay, rate = (tables[(tokens + n * modes + m) * fold : (tokens + n * modes + m + 1) * fold, :] for n in (0, 1))
+        out[here, :] = carried(own, m, brief, later[here, :], decay, rate, span, fold)
+    out[modes * fold : (modes + 2) * fold, :] = own[modes * fold : (modes + 2) * fold, :]
+
+
+def join(own, later, tables, span, modes, tokens):
+    def kernel(own, later, tables, out):
+        joined(own, later, tables, span, modes, tokens, out)
+
+    return pl.pallas_call(
+        kernel,
+        in_specs=[whole()] * 3,
+        out_specs=whole(),
+        out_shape=pltpu.VMEM(own.shape, F32),
+        compiler_params=params(),
+        name="join",
+    )(own, later, tables)
+
+
+def gate_kernel(feat, conv, og, filt, bias, later, own, tables, rounded, joint, ext):
+    tokens, channels = og.shape
+    fold = channels // LANES
+    joined(own, later, tables, tokens, joint.shape[0] // fold - 2, tokens, joint)
     taps = [filt[0, j : j + 1, :] for j in range(3)]
     gate_gradient(feat, conv, og, bias, later, ext)
     for j in range(channels // LANES):
@@ -137,18 +168,19 @@
         rounded[0, lanes, :] = tapped(ext, taps, lanes, tokens).astype(BF16).T
 
 
-def gate_stream(feat, conv, og, filt, bias, later):
-    tokens, channels = og.shape
+def gate_stream(feat, conv, og, filt, bias, later, own, tables):
+    tokens, channels = og.shape
+    fold = channels // LANES
     return pl.pallas_call(
         gate_kernel,
-        in_specs=[whole()] * 6,
-        out_specs=whole(),
-        out_shape=pltpu.VMEM((1, channels, tokens), BF16),
+        in_specs=[whole()] * 8,
+        out_specs=[whole()] * 2,
+        out_shape=[pltpu.VMEM((1, channels, tokens), BF16), pltpu.VMEM((own.shape[0] - 10 * fold, LANES), F32)],
         scratch_shapes=[pltpu.VMEM((tokens + 8, channels), F32)],
         compiler_params=params(),
         cost_estimate=cost(*LONG),
         name="gate_stream",
-    )(feat, conv, og, filt, bias, later)
+    )(feat, conv, og, filt, bias, later, own, tables)
 
 
 def product_gradients(feat, gp, later, exts):
@@ -194,27 +226,34 @@
     )(feat, conv, og, filt, bias, later, gp)
 
 
-def fetches(plan, source, w_proj, ready, sems):
+def on_ring(offset, ring):
+    own = lax.rem(lax.axis_index("chan"), ring)
+    place = jnp.where(lax.rem(own, 2) == 0, own // 2, ring - 1 - own // 2)
+    place = lax.rem(place + offset, ring)
+    return jnp.where(place < (ring + 1) // 2, 2 * place, 2 * (ring - 1 - place) + 1)
+
+
+def fetches(plan, ring, w_proj, ready, sems):
     channels = ready.shape[1] // len(plan)
     moves = []
     for k, (stream, height, offset, _) in enumerate(plan):
-        begin = pl.multiple_of((height * RING + source[offset]) * channels, LANES)
+        begin = pl.multiple_of((height * ring + on_ring(offset, ring)) * channels, LANES)
         columns = w_proj.at[stream, :, pl.ds(begin, channels)]
         moves.append(pltpu.make_async_copy(columns, ready.at[:, pl.ds(k * channels, channels)], sems.at[k]))
     return moves
 
 
-def state_kernel(later, plan, source, feat, og, filt, bias, tables, *refs):
+def state_kernel(later, plan, ring, feat, og, filt, bias, tables, *refs):
     payloads = refs[:later]
     w_proj, rounded, sums, gp, ready, acc, prod, first_ext, second_ext, sems = refs[later:]
     exts = first_ext, second_ext
-    moves = fetches(plan, source, w_proj, ready, sems)
+    moves = fetches(plan, ring, w_proj, ready, sems)
     for move in moves:
         move.start()
     tokens, channels = og.shape
     fold = channels // LANES
     modes = (tables.shape[0] // fold - tokens) // 3
-    dec, far, res = (tokens + n * modes for n in range(3))
+    dec, raw, res = (tokens + n * modes for n in range(3))
     for j in range(fold):
         lanes = slice(j * LANES, (j + 1) * LANES)
         p = feat[1, :, lanes] * feat[2, :, lanes]
@@ -229,15 +268,14 @@
     group = 8
     for low in range(0, modes, group):
         chosen = range(low, min(low + group, modes))
-        decay, weight, reach = ([rows(tables, at + m) for m in chosen] for at in (dec, res, far))
-        state = [jnp.zeros((fold, LANES), F32) for _ in chosen]
-        for n, payload in enumerate(reversed(payloads)):
-            block_end = [rows(payload, m) + f * s for m, f, s in zip(chosen, reach, state)]
-            if n < later - 1:
-                s0, s1 = rows(payload, modes), rows(payload, modes + 1)
-                state = [s0 + d * (s1 + d * s) for d, s in zip(decay, block_end)]
-            else:
-                state = block_end
+        decay, weight, rate = ([rows(tables, at + m) for m in chosen] for at in (dec, res, raw))
+        state = [rows(payloads[-1], m) for m in chosen]
+        for n in reversed(range(later - 1)):
+            brief = payloads[n + 1].at[pl.ds(0, (modes + 2) * fold)]
+            state = [
+                carried(payloads[n], m, brief, s, d, r, tokens << n, fold)
+                for m, s, d, r in zip(chosen, state, decay, rate)
+            ]
 
         def corr(state, weight=weight):
             terms = [w * s for w, s in zip(weight, state)]
@@ -284,13 +322,13 @@
         move.wait()
 
 
-def state_streams(feat, og, filt, bias, tables, payloads, plan, sources, w_proj):
+def state_streams(feat, og, filt, bias, tables, payloads, plan, ring, w_proj):
     tokens, channels = og.shape
     fold = channels // LANES
     modes = (tables.shape[0] // fold - tokens) // 3
     return pl.pallas_call(
-        functools.partial(state_kernel, len(payloads), plan),
-        in_specs=[pl.BlockSpec(memory_space=pltpu.SMEM)] + [whole()] * (5 + len(payloads)) + [in_hbm()],
+        functools.partial(state_kernel, len(payloads), plan, ring),
+        in_specs=[whole()] * (5 + len(payloads)) + [in_hbm()],
         out_specs=[whole()] * 4,
         out_shape=[
             pltpu.VMEM((2, channels, tokens), BF16),
@@ -304,15 +342,15 @@
         compiler_params=params(),
         cost_estimate=cost(8 * tokens * channels * modes, 40 * tokens * channels),
         name="state_streams",
-    )(sources, feat, og, filt, bias, tables, *payloads, w_proj)
-
-
-def product_kernel(plan, base, later, first, last, source, w_proj, w, *refs):
+    )(feat, og, filt, bias, tables, *payloads, w_proj)
+
+
+def product_kernel(plan, base, later, first, last, ring, w_proj, w, *refs):
     refs = list(refs)
     moves = []
     if later:
         sems = refs.pop()
-        moves = fetches(later, source, w_proj, refs.pop(), sems)
+        moves = fetches(later, ring, w_proj, refs.pop(), sems)
     elif last:
         sems = refs.pop()
         turned = refs.pop()
@@ -352,7 +390,7 @@
     return arrays, plan
 
 
-def add_product(total, ready, base, pieces, later, last, sources, w_proj, span):
+def add_product(total, ready, base, pieces, later, last, ring, w_proj, span):
     features = w_proj.shape[1]
     arrays, plan = steps_of(pieces)
     channels, tokens = w_proj.shape[2] // lax.axis_size("chan"), arrays[0].shape[3]
@@ -369,8 +407,8 @@
         out_shape += [pltpu.VMEM((features, len(later) * channels), BF16)]
         scratch = [pltpu.SemaphoreType.DMA((len(later),))]
     return pl.pallas_call(
-        functools.partial(product_kernel, plan, base, later, first, last),
-        in_specs=[pl.BlockSpec(memory_space=pltpu.SMEM), in_hbm()]
+        functools.partial(product_kernel, plan, base, later, first, last, ring),
+        in_specs=[in_hbm()]
         + [whole()] * (1 + len(arrays) + (not first)),
         out_specs=out_specs,
         out_shape=out_shape,
@@ -378,7 +416,7 @@
         compiler_params=params(),
         cost_estimate=cost(*span),
         name="add_product",
-    )(sources, w_proj, ready, *arrays, *([] if first else [total]))
+    )(w_proj, ready, *arrays, *([] if first else [total]))
 
 
 def ring_order(size):
@@ -398,9 +436,6 @@
     heights = groups // ring
 
     order = ring_order(ring)
-    place = [order.index(i) for i in range(ring)]
-    table = jnp.array([[order[(place[i] + d) % ring] for d in range(ring)] for i in range(ring)], jnp.int32)
-    sources = lax.dynamic_index_in_dim(table, lax.rem(lax.axis_index("chan"), ring), 0, False)
     pairs = {
         by: [
             (h * ring + order[i], h * ring + order[(i + by) % ring])
@@ -429,11 +464,17 @@
         return sums + lax.ppermute(sums, "ctx", [(i, i ^ by) for i in range(blocks)])
 
     fold = channels // LANES
-    feat, conv, og, filt, bias_row, tables, own, brief = front(
+    feat, conv, og, filt, bias_row, tables, own = front(
         features, saved_conv, out_grad, short_filter, residue.T, rate.T, bias[None]
     )
-    payloads = [from_later(own, 1)] + [from_later(brief, by) for by in range(2, blocks)]
-    gate = gate_stream(feat, conv, og, filt, bias_row, payloads[0])
+    payloads = [from_later(own, 1)]
+    gate, joint = gate_stream(feat, conv, og, filt, bias_row, payloads[0], own, tables)
+    by = 2
+    while by < blocks:
+        payloads.append(from_later(joint, by))
+        if 2 * by < blocks:
+            joint = join(joint, payloads[-1], tables, by * tokens, modes, tokens)
+        by *= 2
     a0 = stacked(gate)
     a1, z1 = up(a0), down(a0)
 
@@ -448,11 +489,11 @@
         [("y1", (1,), 1, 1), ("a2", a, 0, ring - 2), ("z2", a, 0, 2)],
         [("b2", b, 1, ring - 2), ("y2", (0,), 1, 2)],
         [("y2", (1,), 1, 2), ("a3", a, 0, ring - 3), ("z3", a, 0, 3)],
-        [("b3", b, 1, ring - 3), ("y3", (0,), 1, 3)],
-        [("y3", (1,), 1, 3), ("a4", a, 0, back)],
+        [("b3", b, 1, ring - 3), ("y3", b, 1, 3)],
+        [("a4", a, 0, back)],
         [("b4", a, 1, back), ("y4", a, 2, back)],
     ]
-    spans = [LONG, LONG, SHORT, LONG, SHORT, LONG, MIDDLE, SMALL, SHORT]
+    spans = [LONG, LONG, SHORT, LONG, SHORT, LONG, MIDDLE, TAIL, SHORT]
     hollow = jax.ShapeDtypeStruct((heights, 2, channels, tokens), BF16)
 
     def plan_of(n):
@@ -462,11 +503,11 @@
         pieces = [(arrays[name], *rest) for name, *rest in sets[n]]
         later = plan_of(n + 1) if n < 6 else plan_of(7) + plan_of(8) if n == 6 else None
         base = len(plan_of(7)) if n == 8 else 0
-        return add_product(total, ready, base, pieces, later, n == 8, sources, w_proj, spans[n])
+        return add_product(total, ready, base, pieces, later, n == 8, ring, w_proj, spans[n])
 
     payloads[0], a0 = lax.optimization_barrier((payloads[0], a0))
     rounds, sums, gp, ready = state_streams(
-        feat, og, filt, bias_row.reshape(fold, LANES), tables, payloads, plan_of(0), sources, w_proj
+        feat, og, filt, bias_row.reshape(fold, LANES), tables, payloads, plan_of(0), ring, w_proj
     )
     b0 = stacked(rounds)
 
@@ -499,14 +540,15 @@
     a4 = up(a3[:, :, :half]), down(z3[:, :, half:])
     total, ready = times(5, total, ready, y2=y2, a3=a3, z3=z3)
 
-    b3, y3, total, sums = lax.optimization_barrier((b3, y3, total, sums))
+    grad_residue, grad_bias = sums[:modes].T, sums[modes]
+    b3, y3, total, grad_residue, grad_bias = lax.optimization_barrier((b3, y3, total, grad_residue, grad_bias))
     b4, y4 = up(b3[:, :1]), down(y3[:, 1:])
     total, ready = times(6, total, ready, b3=b3, y3=y3)
 
     a4, total = lax.optimization_barrier((a4, total))
-    (total,) = times(7, total, ready, y3=y3, a4=a4)
+    (total,) = times(7, total, ready, a4=a4)
     (grad_x,) = times(8, total, ready, b4=b4, y4=y4)
-    return (grads, grad_x, sums[:modes].T, sums[modes])
+    return (grads, grad_x, grad_residue, grad_bias)
 
 
 def solution(mesh):

time: 85 us -> 81.3 us (0.956)
  Pallas kernels: 45.8 us -> 40 us
  waiting for transfers between devices: 14.1 us -> 18.3 us
  starting transfers between devices: 21.8 us -> 20.5 us
    pallas_call x9, Pallas kernels: 38 us -> 32.7 us  [add_product(): pl.pallas_call(functools.partial(product_kernel, plan, base, later, first...]
    ppermute x8, waiting for transfers between devices: 4.46 us -> 6.98 us  [down(): return lax.ppermute(x, 'chan', pairs[-1])]
    ppermute x8, waiting for transfers between devices: 1.76 us -> 4.03 us  [up(): return lax.ppermute(x, 'chan', pairs[1])]
    ppermute x3 -> x2, starting transfers between devices: 3.86 us -> 2.57 us  [from_later(): return lax.ppermute(array, 'ctx', [(i, i - by) for i in range(by, blocks)])]
    ppermute x3 -> x2, waiting for transfers between devices: 7.87 us -> 7.25 us  [from_later(): return lax.ppermute(array, 'ctx', [(i, i - by) for i in range(by, blocks)])]
  transfers between devices with their start and end apart: 21 -> 20, of which waited for: 9 -> 9; matrix products, arithmetic and copies ran while one was open for 2% -> 2% of each run, Pallas kernels for 48% -> 44%
where the time goes in v6:
time: 81.3 us; the launch traced here: 81.1 us
  Pallas kernels  40 us (49%)
  starting transfers between devices  20.5 us (25%)
  waiting for transfers between devices  18.3 us (23%)
  local copies, waits for them, and re-layouts  1.29 us (2%)
  between operations  1.04 us (1%)
    pallas_call x9, Pallas kernels, add_product(): pl.pallas_call(functools.partial(product_kernel, plan, base, later, first...  32.7 us
    ppermute x8, starting transfers between devices, up(): return lax.ppermute(x, 'chan', pairs[1])  14.5 us
    ppermute x2, waiting for transfers between devices, from_later(): return lax.ppermute(array, 'ctx', [(i, i - by) for i in range(by, blocks)])  7.25 us
    ppermute x8, waiting for transfers between devices, down(): return lax.ppermute(x, 'chan', pairs[-1])  6.98 us
    ppermute x8, waiting for transfers between devices, up(): return lax.ppermute(x, 'chan', pairs[1])  4.03 us
    ppermute x8, starting transfers between devices, down(): return lax.ppermute(x, 'chan', pairs[-1])  3.3 us
    pallas_call x1, Pallas kernels, state_streams(): pl.pallas_call(functools.partial(state_kernel, len(payloads), plan, ring)...  2.96 us
    ppermute x2, starting transfers between devices, from_later(): return lax.ppermute(array, 'ctx', [(i, i - by) for i in range(by, blocks)])  2.57 us
  transfers between devices with their start and end apart: 20, of which 9 were waited for; matrix products, arithmetic and copies ran while one was open for 2% of the time, Pallas kernels for 44%

profile of v6, /device:TPU:0, one launch (start us, length us, event | category | flops | bytes accessed | tf_op | source)
XLA Modules:
  0.0 81.1 jit_solution(12295504780307765594)
XLA Ops:
  0.6 2.1 %front.1 = (f32[3,128,1024]{2,1,0:T(8,128)S(1)}, f32[128,1024]{1,0:T(8,128)S(1)}, f32[128,1024]{1,0:T(8,128)S(1)}, f32[3,3,1024]{2,1,0:T(4,128)S(1)}, f32[1,1024...) custom-call(f32[3,128,1024]{2,1,0:T(8,128)} %features.1, f32[128,1024]{1,0:T(8,128)} %conv.1, ...), custom_call_target="tpu_custom_call" | custom-call | flops 8388608 | bytes 2621440 | tf_op jit(solution)/shard_map/front/pallas_call | solution.py:95
  4.0 1.9 %collective-permute-done.later.refs_0_ = f32[224,128]{1,0:T(8,128)S(1)} collective-permute-done((f32[224,128]{1,0:T(8,128)S(1)}, f32[224,128]{1,0:T(8,128)S(1)}, u32[]{:S(2)}, u32[]{:S(2)}) %collective-permute-start) | collective-permute-done | bytes 114720 | tf_op jit(solution)/shard_map/ppermute | solution.py:461
  6.3 3.1 %collective-permute-start.4 = (bf16[1,1,1024,128]{3,2,1,0:T(8,128)(2,1)S(1)}, bf16[1,1,1024,128]{3,2,1,0:T(8,128)(2,1)}, u32[]{:S(2)}, u32[]{:S(2)}) collective-permute-start(bf16[1,1,1024,128]{3,2,1,0:T(8,128)(2,1)S(1)} %bitcast.13), channel_id=1, source_target_pairs={{0,2},{2,4},{4,6},{6,7},{7,5},{5,3},{3,1},{1,0},{8,10},{10,12},{12... | collective-permute-start | bytes 786440 | tf_op jit(solution)/shard_map/ppermute | solution.py:449
  10.7 5.3 %collective-permute-done.1.refs_1_ = f32[144,128]{1,0:T(8,128)S(1)} collective-permute-done((f32[144,128]{1,0:T(8,128)S(1)}, f32[144,128]{1,0:T(8,128)S(1)}, u32[]{:S(2)}, u32[]{:S(2)}) %collective-permute-start.1) | collective-permute-done | bytes 73760 | tf_op jit(solution)/shard_map/ppermute | solution.py:461
  16.0 3.0 %state_streams.1 = (bf16[2,1024,128]{2,1,0:T(8,128)(2,1)S(1)}, f32[17,1024]{1,0:T(8,128)S(1)}, f32[1040,128]{1,0:T(8,128)S(1)}, bf16[1024,3072]{1,0:T(8,128)(2,1)S(1)}) custom-call(f32[3,128,1024]{2,1,0:T(8,128)S(1)} %get-tuple-element.61.feat, f32[128,1024]{1,0:T(8,128)S(1)} %get-tuple-element.62.og, f32[3,3,1024]{2,1,0:T(4,128)S(1)} %get-tuple-element.63.filt, ...), custom_call_target="tpu_custom_call" | custom-call | flops 16777216 | bytes 5242880 | tf_op jit(solution)/shard_map/state_streams/pallas_call | solution.py:329
  19.0 1.7 %collective-permute-start.2 = (bf16[1,2,1024,128]{3,2,1,0:T(8,128)(2,1)S(1)}, bf16[1,2,1024,128]{3,2,1,0:T(8,128)(2,1)S(1)}, u32[]{:S(2)}, u32[]{:S(2)}) collective-permute-start(bf16[1,2,1024,128]{3,2,1,0:T(8,128)(2,1)S(1)} %bitcast.10), channel_id=1, source_target_pairs={{0,2},{2,4},{4,6},{6,7},{7,5},{5,3},{3,1},{1,0},{8,10},{10,12},{12... | collective-permute-start | bytes 1572872 | tf_op jit(solution)/shard_map/ppermute | solution.py:449
  21.1 1.6 %collective-permute-start.6 = (bf16[1,1,1024,128]{3,2,1,0:T(8,128)(2,1)}, bf16[1,1,1024,128]{3,2,1,0:T(8,128)(2,1)}, u32[]{:S(2)}, u32[]{:S(2)}) collective-permute-start(bf16[1,1,1024,128]{3,2,1,0:T(8,128)(2,1)} %collective-permute-done.4.refs_0_), channel_id=1, source_target_pairs={{0,2},{2,4},{4,6},{6,7},{7,5},{5,3},{3,1},{1,0},{8,10},{10,12},{12... | collective-permute-start | bytes 786440 | tf_op jit(solution)/shard_map/ppermute | solution.py:449
  23.1 3.9 %add_product.9 = (f32[1024,128]{1,0:T(8,128)S(1)}, bf16[1024,2048]{1,0:T(8,128)(2,1)S(1)}) custom-call(bf16[3,1024,8192]{2,1,0:T(8,128)(2,1)} %w_proj.17, bf16[1024,3072]{1,0:T(8,128)(2,1)S(1)} %get-tuple-element.72.w, bf16[1,1,1024,128]{3,2,1,0:T(8,128)(2,1)S(1)} %bitcast.15, bf16[1,2,1024,128]{3,2,1,0:T(8,128)(2,1)S(1)} %bitcast.12), custom_call_target="tpu_custom_call" | custom-call | flops 68719476736 | bytes 268435456 | tf_op jit(solution)/shard_map/add_product/pallas_call | solution.py:409
  27.0 4.0 %add_product.10 = (f32[1024,128]{1,0:T(8,128)S(1)}, bf16[1024,3072]{1,0:T(8,128)(2,1)S(1)}) custom-call(bf16[3,1024,8192]{2,1,0:T(8,128)(2,1)} %w_proj.17, bf16[1024,2048]{1,0:T(8,128)(2,1)S(1)} %get-tuple-element.75.w, bf16[1,1,1024,128]{3,2,1,0:T(8,128)(2,1)} %collective-permute-done.4.refs_0_, bf16[1,1,1024,128]{3,2,1,0:T(8,128)(2,1)} %collective-permute-done.5.refs_1_, ...), custom_call_target="tpu_custom_call" | custom-call | flops 68719476736 | bytes 268435456 | tf_op jit(solution)/shard_map/add_product/pallas_call | solution.py:409
  31.0 1.9 %gradients.1 = f32[3,128,1024]{2,1,0:T(8,128)} custom-call(f32[3,128,1024]{2,1,0:T(8,128)S(1)} %get-tuple-element.61.feat, f32[128,1024]{1,0:T(8,128)S(1)} %copy-done, f32[128,1024]{1,0:T(8,128)S(1)} %get-tuple-element.62.og, f32[3,3,1024]{2,1,0:T(4,128)S(1)} %get-tuple-element.63.filt, f32[1,1024]{1,0:T(1,128)S(1)} %get-tuple-element.64.bias, ...), custom_call_target="tpu_custom_call" | custom-call | flops 3932160 | bytes 5242880 | tf_op jit(solution)/shard_map/gradients/pallas_call | solution.py:216
  33.6 1.8 %collective-permute-done.3.refs_1_.refs_0_ = bf16[1,2,1024,128]{3,2,1,0:T(8,128)(2,1)S(1)} collective-permute-done((bf16[1,2,1024,128]{3,2,1,0:T(8,128)(2,1)S(1)}, bf16[1,2,1024,128]{3,2,1,0:T(8,128)(2,1)S(1)}, u32[]{:S(2)}, u32[]{:S(2)}) %collective-permute-start.3) | collective-permute-done | bytes 524320 | tf_op jit(solution)/shard_map/ppermute | solution.py:452
  35.5 1.6 %collective-permute-start.8 = (bf16[1,2,1024,128]{3,2,1,0:T(8,128)(2,1)S(1)}, bf16[1,2,1024,128]{3,2,1,0:T(8,128)(2,1)S(1)}, u32[]{:S(2)}, u32[]{:S(2)}) collective-permute-start(bf16[1,2,1024,128]{3,2,1,0:T(8,128)(2,1)S(1)} %collective-permute-done.2.refs_0_), channel_id=1, source_target_pairs={{0,2},{2,4},{4,6},{6,7},{7,5},{5,3},{3,1},{1,0},{8,10},{10,12},{12... | collective-permute-start | bytes 1572872 | tf_op jit(solution)/shard_map/ppermute | solution.py:449
  37.5 4.4 %add_product.11 = (f32[1024,128]{1,0:T(8,128)S(1)}, bf16[1024,3072]{1,0:T(8,128)(2,1)S(1)}) custom-call(bf16[3,1024,8192]{2,1,0:T(8,128)(2,1)} %w_proj.17, bf16[1024,3072]{1,0:T(8,128)(2,1)S(1)} %get-tuple-element.83.w, bf16[1,2,1024,128]{3,2,1,0:T(8,128)(2,1)S(1)} %collective-permute-done.2.refs_0_, ...), custom_call_target="tpu_custom_call" | custom-call | flops 65536 | bytes 256 | tf_op jit(solution)/shard_map/add_product/pallas_call | solution.py:409
  42.0 1.6 %collective-permute-start.11 = (bf16[1,1,1024,128]{3,2,1,0:T(8,128)(2,1)}, bf16[1,1,1024,128]{3,2,1,0:T(8,128)(2,1)S(1)}, u32[]{:S(2)}, u32[]{:S(2)}) collective-permute-start(bf16[1,1,1024,128]{3,2,1,0:T(8,128)(2,1)} %collective-permute-done.6.refs_1_), channel_id=1, source_target_pairs={{0,2},{2,4},{4,6},{6,7},{7,5},{5,3},{3,1},{1,0},{8,10},{10,12},{12... | collective-permute-start | bytes 786440 | tf_op jit(solution)/shard_map/ppermute | solution.py:449
  44.0 4.3 %add_product.12 = (f32[1024,128]{1,0:T(8,128)S(1)}, bf16[1024,3072]{1,0:T(8,128)(2,1)S(1)}) custom-call(bf16[3,1024,8192]{2,1,0:T(8,128)(2,1)} %w_proj.17, bf16[1024,3072]{1,0:T(8,128)(2,1)S(1)} %get-tuple-element.87.w, bf16[1,2,1024,128]{3,2,1,0:T(8,128)(2,1)S(1)} %collective-permute-done.3.refs_1_.refs_0_, ...), custom_call_target="tpu_custom_call" | custom-call | flops 68719476736 | bytes 268435456 | tf_op jit(solution)/shard_map/add_product/pallas_call | solution.py:409
  48.4 2.1 %collective-permute-done.8.refs_0_ = bf16[1,2,1024,128]{3,2,1,0:T(8,128)(2,1)S(1)} collective-permute-done((bf16[1,2,1024,128]{3,2,1,0:T(8,128)(2,1)S(1)}, bf16[1,2,1024,128]{3,2,1,0:T(8,128)(2,1)S(1)}, u32[]{:S(2)}, u32[]{:S(2)}) %collective-permute-start.8) | collective-permute-done | bytes 524320 | tf_op jit(solution)/shard_map/ppermute | solution.py:449
  50.5 1.8 %collective-permute-done.9.refs_1_.refs_0_ = bf16[1,2,1024,128]{3,2,1,0:T(8,128)(2,1)S(1)} collective-permute-done((bf16[1,2,1024,128]{3,2,1,0:T(8,128)(2,1)S(1)}, bf16[1,2,1024,128]{3,2,1,0:T(8,128)(2,1)S(1)}, u32[]{:S(2)}, u32[]{:S(2)}) %collective-permute-start.9) | collective-permute-done | bytes 524320 | tf_op jit(solution)/shard_map/ppermute | solution.py:452
  54.4 4.4 %add_product.13 = (f32[1024,128]{1,0:T(8,128)S(1)}, bf16[1024,3072]{1,0:T(8,128)(2,1)S(1)}) custom-call(bf16[3,1024,8192]{2,1,0:T(8,128)(2,1)} %w_proj.17, bf16[1024,3072]{1,0:T(8,128)(2,1)S(1)} %get-tuple-element.93.w, bf16[1,2,1024,128]{3,2,1,0:T(8,128)(2,1)S(1)} %collective-permute-done.8.refs_0_, ...), custom_call_target="tpu_custom_call" | custom-call | flops 65536 | bytes 256 | tf_op jit(solution)/shard_map/add_product/pallas_call | solution.py:409
  58.8 1.6 %collective-permute-start.18 = (bf16[1,1,512,128]{3,2,1,0:T(8,128)(2,1)S(1)}, bf16[1,1,512,128]{3,2,1,0:T(8,128)(2,1)S(1)}, u32[]{:S(2)}, u32[]{:S(2)}) collective-permute-start(bf16[1,1,512,128]{3,2,1,0:T(8,128)(2,1)S(1)} %slice.22), channel_id=1, source_target_pairs={{0,2},{2,4},{4,6},{6,7},{7,5},{5,3},{3,1},{1,0},{8,10},{10,12},{12... | collective-permute-start | bytes 393224 | tf_op jit(solution)/shard_map/ppermute | solution.py:449
  61.0 5.2 %add_product.14 = (f32[1024,128]{1,0:T(8,128)S(1)}, bf16[1024,4096]{1,0:T(8,128)(2,1)S(1)}) custom-call(bf16[3,1024,8192]{2,1,0:T(8,128)(2,1)} %w_proj.17, bf16[1024,3072]{1,0:T(8,128)(2,1)S(1)} %get-tuple-element.99.w, bf16[1,2,1024,128]{3,2,1,0:T(8,128)(2,1)S(1)} %collective-permute-done.9.refs_1_.refs_0_, ...), custom_call_target="tpu_custom_call" | custom-call | flops 68719476736 | bytes 268435456 | tf_op jit(solution)/shard_map/add_product/pallas_call | solution.py:409
  67.4 1.7 %collective-permute-done.14.refs_1_ = bf16[1,2,1024,128]{3,2,1,0:T(8,128)(2,1)S(1)} collective-permute-done((bf16[1,2,1024,128]{3,2,1,0:T(8,128)(2,1)S(1)}, bf16[1,2,1024,128]{3,2,1,0:T(8,128)(2,1)S(1)}, u32[]{:S(2)}, u32[]{:S(2)}) %collective-permute-start.14) | collective-permute-done | bytes 524320 | tf_op jit(solution)/shard_map/ppermute | solution.py:452
  69.2 1.6 %collective-permute-start.16 = (bf16[1,1,1024,128]{3,2,1,0:T(8,128)(2,1)S(1)}, bf16[1,1,1024,128]{3,2,1,0:T(8,128)(2,1)S(1)}, u32[]{:S(2)}, u32[]{:S(2)}) collective-permute-start(bf16[1,1,1024,128]{3,2,1,0:T(8,128)(2,1)S(1)} %slice.20), channel_id=1, source_target_pairs={{0,2},{2,4},{4,6},{6,7},{7,5},{5,3},{3,1},{1,0},{8,10},{10,12},{12... | collective-permute-start | bytes 786440 | tf_op jit(solution)/shard_map/ppermute | solution.py:449
  71.5 3.8 %add_product.15 = (f32[1024,128]{1,0:T(8,128)S(1)}, bf16[1024,3072]{1,0:T(8,128)(2,1)S(1)}) custom-call(bf16[3,1024,8192]{2,1,0:T(8,128)(2,1)} %w_proj.17, bf16[1024,4096]{1,0:T(8,128)(2,1)S(1)} %get-tuple-element.105.w, bf16[1,2,1024,128]{3,2,1,0:T(8,128)(2,1)S(1)} %collective-permute-done.13.refs_0_, ...), custom_call_target="tpu_custom_call" | custom-call | flops 1073741824 | bytes 9437184 | tf_op jit(solution)/shard_map/add_product/pallas_call | solution.py:409
  78.8 2.1 %add_product.17 = f32[128,1024]{1,0:T(8,128)} custom-call(bf16[3,1024,8192]{2,1,0:T(8,128)(2,1)} %w_proj.17, bf16[1024,3072]{1,0:T(8,128)(2,1)S(1)} %get-tuple-element.111.w, bf16[1,1,1024,128]{3,2,1,0:T(8,128)(2,1)S(1)} %collective-permute-done.16.refs_0_, bf16[1,1,1024,128]{3,2,1,0:T(8,128)(2,1)S(1)} %collective-permute-done.17.refs_1_, ...), custom_call_target="tpu_custom_call" | custom-call | flops 65536 | bytes 256 | tf_op jit(solution)/shard_map/add_product/pallas_call | solution.py:409
  (39 shorter events, 13.5 us)
Async XLA Ops:
  2.7 3.2 %collective-permute-start = (f32[224,128]{1,0:T(8,128)S(1)}, f32[224,128]{1,0:T(8,128)S(1)}, u32[]{:S(2)}, u32[]{:S(2)}) collective-permute-start(f32[224,128]{1,0:T(8,128)S(1)} %get-tuple-element.66.own), channel_id=1, source_target_pairs={{8,0},{16,8},{24,16},{9,1},{17,9},{25,17},{10,2},{18,10},{26,18},{... | collective-permute-start | bytes 344072 | tf_op jit(solution)/shard_map/ppermute | solution.py:461
  6.3 14.7 %collective-permute-start.4 = (bf16[1,1,1024,128]{3,2,1,0:T(8,128)(2,1)S(1)}, bf16[1,1,1024,128]{3,2,1,0:T(8,128)(2,1)}, u32[]{:S(2)}, u32[]{:S(2)}) collective-permute-start(bf16[1,1,1024,128]{3,2,1,0:T(8,128)(2,1)S(1)} %bitcast.13), channel_id=1, source_target_pairs={{0,2},{2,4},{4,6},{6,7},{7,5},{5,3},{3,1},{1,0},{8,10},{10,12},{12... | collective-permute-start | bytes 786440 | tf_op jit(solution)/shard_map/ppermute | solution.py:449
  9.4 11.7 %collective-permute-start.5 = (bf16[1,1,1024,128]{3,2,1,0:T(8,128)(2,1)S(1)}, bf16[1,1,1024,128]{3,2,1,0:T(8,128)(2,1)}, u32[]{:S(2)}, u32[]{:S(2)}) collective-permute-start(bf16[1,1,1024,128]{3,2,1,0:T(8,128)(2,1)S(1)} %bitcast.14), channel_id=1, source_target_pairs={{0,1},{2,0},{4,2},{6,4},{7,6},{5,7},{3,5},{1,3},{8,9},{10,8},{12,1... | collective-permute-start | bytes 786440 | tf_op jit(solution)/shard_map/ppermute | solution.py:452
  9.4 6.6 %collective-permute-start.1 = (f32[144,128]{1,0:T(8,128)S(1)}, f32[144,128]{1,0:T(8,128)S(1)}, u32[]{:S(2)}, u32[]{:S(2)}) collective-permute-start(f32[144,128]{1,0:T(8,128)S(1)} %get-tuple-element.70), channel_id=1, source_target_pairs={{16,0},{24,8},{17,1},{25,9},{18,2},{26,10},{19,3},{27,11},{20,4},{... | collective-permute-start | bytes 221192 | tf_op jit(solution)/shard_map/ppermute | solution.py:461
  19.0 14.6 %collective-permute-start.2 = (bf16[1,2,1024,128]{3,2,1,0:T(8,128)(2,1)S(1)}, bf16[1,2,1024,128]{3,2,1,0:T(8,128)(2,1)S(1)}, u32[]{:S(2)}, u32[]{:S(2)}) collective-permute-start(bf16[1,2,1024,128]{3,2,1,0:T(8,128)(2,1)S(1)} %bitcast.10), channel_id=1, source_target_pairs={{0,2},{2,4},{4,6},{6,7},{7,5},{5,3},{3,1},{1,0},{8,10},{10,12},{12... | collective-permute-start | bytes 1572872 | tf_op jit(solution)/shard_map/ppermute | solution.py:449
  20.7 14.8 %collective-permute-start.3 = (bf16[1,2,1024,128]{3,2,1,0:T(8,128)(2,1)S(1)}, bf16[1,2,1024,128]{3,2,1,0:T(8,128)(2,1)S(1)}, u32[]{:S(2)}, u32[]{:S(2)}) collective-permute-start(bf16[1,2,1024,128]{3,2,1,0:T(8,128)(2,1)S(1)} %bitcast.11), channel_id=1, source_target_pairs={{0,1},{2,0},{4,2},{6,4},{7,6},{5,7},{3,5},{1,3},{8,9},{10,8},{12,1... | collective-permute-start | bytes 1572872 | tf_op jit(solution)/shard_map/ppermute | solution.py:452
  21.1 20.8 %collective-permute-start.6 = (bf16[1,1,1024,128]{3,2,1,0:T(8,128)(2,1)}, bf16[1,1,1024,128]{3,2,1,0:T(8,128)(2,1)}, u32[]{:S(2)}, u32[]{:S(2)}) collective-permute-start(bf16[1,1,1024,128]{3,2,1,0:T(8,128)(2,1)} %collective-permute-done.4.refs_0_), channel_id=1, source_target_pairs={{0,2},{2,4},{4,6},{6,7},{7,5},{5,3},{3,1},{1,0},{8,10},{10,12},{12... | collective-permute-start | bytes 786440 | tf_op jit(solution)/shard_map/ppermute | solution.py:449
  22.7 19.2 %collective-permute-start.7 = (bf16[1,1,1024,128]{3,2,1,0:T(8,128)(2,1)}, bf16[1,1,1024,128]{3,2,1,0:T(8,128)(2,1)}, u32[]{:S(2)}, u32[]{:S(2)}) collective-permute-start(bf16[1,1,1024,128]{3,2,1,0:T(8,128)(2,1)} %collective-permute-done.5.refs_1_), channel_id=1, source_target_pairs={{0,1},{2,0},{4,2},{6,4},{7,6},{5,7},{3,5},{1,3},{8,9},{10,8},{12,1... | collective-permute-start | bytes 786440 | tf_op jit(solution)/shard_map/ppermute | solution.py:452
  27.0 4.0 %copy-start = (f32[128,1024]{1,0:T(8,128)S(1)}, f32[128,1024]{1,0:T(8,128)}, u32[]{:S(2)}) copy-start(f32[128,1024]{1,0:T(8,128)} %conv.1) | copy-start | bytes 1572868
  35.5 15.0 %collective-permute-start.8 = (bf16[1,2,1024,128]{3,2,1,0:T(8,128)(2,1)S(1)}, bf16[1,2,1024,128]{3,2,1,0:T(8,128)(2,1)S(1)}, u32[]{:S(2)}, u32[]{:S(2)}) collective-permute-start(bf16[1,2,1024,128]{3,2,1,0:T(8,128)(2,1)S(1)} %collective-permute-done.2.refs_0_), channel_id=1, source_target_pairs={{0,2},{2,4},{4,6},{6,7},{7,5},{5,3},{3,1},{1,0},{8,10},{10,12},{12... | collective-permute-start | bytes 1572872 | tf_op jit(solution)/shard_map/ppermute | solution.py:449
  37.0 15.3 %collective-permute-start.9 = (bf16[1,2,1024,128]{3,2,1,0:T(8,128)(2,1)S(1)}, bf16[1,2,1024,128]{3,2,1,0:T(8,128)(2,1)S(1)}, u32[]{:S(2)}, u32[]{:S(2)}) collective-permute-start(bf16[1,2,1024,128]{3,2,1,0:T(8,128)(2,1)S(1)} %collective-permute-done.3.refs_1_.refs_0_), channel_id=1, source_target_pairs={{0,1},{2,0},{4,2},{6,4},{7,6},{5,7},{3,5},{1,3},{8,9},{10,8},{12,1... | collective-permute-start | bytes 1572872 | tf_op jit(solution)/shard_map/ppermute | solution.py:452
  41.9 6.5 %collective-permute-start.10 = (f32[17,1024]{1,0:T(8,128)S(1)}, f32[17,1024]{1,0:T(8,128)S(1)}, u32[]{:S(2)}, u32[]{:S(2)}) collective-permute-start(f32[17,1024]{1,0:T(8,128)S(1)} %get-tuple-element.95), channel_id=1, source_target_pairs={{0,8},{8,0},{16,24},{24,16},{1,9},{9,1},{17,25},{25,17},{2,10},{10... | collective-permute-start | bytes 208904 | tf_op jit(solution)/shard_map/ppermute | solution.py:464
  42.0 16.8 %collective-permute-start.11 = (bf16[1,1,1024,128]{3,2,1,0:T(8,128)(2,1)}, bf16[1,1,1024,128]{3,2,1,0:T(8,128)(2,1)S(1)}, u32[]{:S(2)}, u32[]{:S(2)}) collective-permute-start(bf16[1,1,1024,128]{3,2,1,0:T(8,128)(2,1)} %collective-permute-done.6.refs_1_), channel_id=1, source_target_pairs={{0,2},{2,4},{4,6},{6,7},{7,5},{5,3},{3,1},{1,0},{8,10},{10,12},{12... | collective-permute-start | bytes 786440 | tf_op jit(solution)/shard_map/ppermute | solution.py:449
  43.6 15.1 %collective-permute-start.12 = (bf16[1,1,1024,128]{3,2,1,0:T(8,128)(2,1)}, bf16[1,1,1024,128]{3,2,1,0:T(8,128)(2,1)S(1)}, u32[]{:S(2)}, u32[]{:S(2)}) collective-permute-start(bf16[1,1,1024,128]{3,2,1,0:T(8,128)(2,1)} %collective-permute-done.7.refs_2_), channel_id=1, source_target_pairs={{0,1},{2,0},{4,2},{6,4},{7,6},{5,7},{3,5},{1,3},{8,9},{10,8},{12,1... | collective-permute-start | bytes 786440 | tf_op jit(solution)/shard_map/ppermute | solution.py:452
  52.3 15.1 %collective-permute-start.13 = (bf16[1,2,1024,128]{3,2,1,0:T(8,128)(2,1)S(1)}, bf16[1,2,1024,128]{3,2,1,0:T(8,128)(2,1)S(1)}, u32[]{:S(2)}, u32[]{:S(2)}) collective-permute-start(bf16[1,2,1024,128]{3,2,1,0:T(8,128)(2,1)S(1)} %collective-permute-done.8.refs_0_), channel_id=1, source_target_pairs={{0,2},{2,4},{4,6},{6,7},{7,5},{5,3},{3,1},{1,0},{8,10},{10,12},{12... | collective-permute-start | bytes 1572872 | tf_op jit(solution)/shard_map/ppermute | solution.py:449
  53.9 15.3 %collective-permute-start.14 = (bf16[1,2,1024,128]{3,2,1,0:T(8,128)(2,1)S(1)}, bf16[1,2,1024,128]{3,2,1,0:T(8,128)(2,1)S(1)}, u32[]{:S(2)}, u32[]{:S(2)}) collective-permute-start(bf16[1,2,1024,128]{3,2,1,0:T(8,128)(2,1)S(1)} %collective-permute-done.9.refs_1_.refs_0_), channel_id=1, source_target_pairs={{0,1},{2,0},{4,2},{6,4},{7,6},{5,7},{3,5},{1,3},{8,9},{10,8},{12,1... | collective-permute-start | bytes 1572872 | tf_op jit(solution)/shard_map/ppermute | solution.py:452
  58.7 7.4 %collective-permute-start.15 = (f32[17,1024]{1,0:T(8,128)S(1)}, f32[17,1024]{1,0:T(8,128)S(1)}, u32[]{:S(2)}, u32[]{:S(2)}) collective-permute-start(f32[17,1024]{1,0:T(8,128)S(1)} %add.6), channel_id=1, source_target_pairs={{0,16},{8,24},{16,0},{24,8},{1,17},{9,25},{17,1},{25,9},{2,18},{10... | collective-permute-start | bytes 208904 | tf_op jit(solution)/shard_map/ppermute | solution.py:464
  58.8 16.5 %collective-permute-start.18 = (bf16[1,1,512,128]{3,2,1,0:T(8,128)(2,1)S(1)}, bf16[1,1,512,128]{3,2,1,0:T(8,128)(2,1)S(1)}, u32[]{:S(2)}, u32[]{:S(2)}) collective-permute-start(bf16[1,1,512,128]{3,2,1,0:T(8,128)(2,1)S(1)} %slice.22), channel_id=1, source_target_pairs={{0,2},{2,4},{4,6},{6,7},{7,5},{5,3},{3,1},{1,0},{8,10},{10,12},{12... | collective-permute-start | bytes 393224 | tf_op jit(solution)/shard_map/ppermute | solution.py:449
  60.5 14.9 %collective-permute-start.19 = (bf16[1,1,512,128]{3,2,1,0:T(8,128)(2,1)S(1)}, bf16[1,1,512,128]{3,2,1,0:T(8,128)(2,1)S(1)}, u32[]{:S(2)}, u32[]{:S(2)}) collective-permute-start(bf16[1,1,512,128]{3,2,1,0:T(8,128)(2,1)S(1)} %slice.23), channel_id=1, source_target_pairs={{0,1},{2,0},{4,2},{6,4},{7,6},{5,7},{3,5},{1,3},{8,9},{10,8},{12,1... | collective-permute-start | bytes 393224 | tf_op jit(solution)/shard_map/ppermute | solution.py:452
  69.2 8.1 %collective-permute-start.16 = (bf16[1,1,1024,128]{3,2,1,0:T(8,128)(2,1)S(1)}, bf16[1,1,1024,128]{3,2,1,0:T(8,128)(2,1)S(1)}, u32[]{:S(2)}, u32[]{:S(2)}) collective-permute-start(bf16[1,1,1024,128]{3,2,1,0:T(8,128)(2,1)S(1)} %slice.20), channel_id=1, source_target_pairs={{0,2},{2,4},{4,6},{6,7},{7,5},{5,3},{3,1},{1,0},{8,10},{10,12},{12... | collective-permute-start | bytes 786440 | tf_op jit(solution)/shard_map/ppermute | solution.py:449
  70.8 8.0 %collective-permute-start.17 = (bf16[1,1,1024,128]{3,2,1,0:T(8,128)(2,1)S(1)}, bf16[1,1,1024,128]{3,2,1,0:T(8,128)(2,1)S(1)}, u32[]{:S(2)}, u32[]{:S(2)}) collective-permute-start(bf16[1,1,1024,128]{3,2,1,0:T(8,128)(2,1)S(1)} %slice.21), channel_id=1, source_target_pairs={{0,1},{2,0},{4,2},{6,4},{7,6},{5,7},{3,5},{1,3},{8,9},{10,8},{12,1... | collective-permute-start | bytes 786440 | tf_op jit(solution)/shard_map/ppermute | solution.py:452

commit v7 on v6

--- a/solution.py
+++ b/solution.py
@@ -340,7 +340,7 @@
         + [pltpu.VMEM((tokens + 8, channels), F32)] * 2
         + [pltpu.SemaphoreType.DMA((len(plan),))],
         compiler_params=params(),
-        cost_estimate=cost(8 * tokens * channels * modes, 40 * tokens * channels),
+        cost_estimate=cost(4 << 30, 16 << 20),
         name="state_streams",
     )(feat, og, filt, bias, tables, *payloads, w_proj)
 
@@ -491,9 +491,10 @@
         [("y2", (1,), 1, 2), ("a3", a, 0, ring - 3), ("z3", a, 0, 3)],
         [("b3", b, 1, ring - 3), ("y3", b, 1, 3)],
         [("a4", a, 0, back)],
-        [("b4", a, 1, back), ("y4", a, 2, back)],
+        [("b4", a, 1, back)],
+        [("y4", a, 2, back)],
     ]
-    spans = [LONG, LONG, SHORT, LONG, SHORT, LONG, MIDDLE, TAIL, SHORT]
+    spans = [LONG, LONG, SHORT, LONG, SHORT, LONG, MIDDLE, TAIL, SHORT, SHORT]
     hollow = jax.ShapeDtypeStruct((heights, 2, channels, tokens), BF16)
 
     def plan_of(n):
@@ -501,9 +502,10 @@
 
     def times(n, total, ready, **arrays):
         pieces = [(arrays[name], *rest) for name, *rest in sets[n]]
-        later = plan_of(n + 1) if n < 6 else plan_of(7) + plan_of(8) if n == 6 else None
-        base = len(plan_of(7)) if n == 8 else 0
-        return add_product(total, ready, base, pieces, later, n == 8, ring, w_proj, spans[n])
+        after_next = [plan_of(k) for k in range(7, len(sets))]
+        later = plan_of(n + 1) if n < 6 else sum(after_next, []) if n == 6 else None
+        base = sum(len(plan) for plan in after_next[: max(0, n - 7)])
+        return add_product(total, ready, base, pieces, later, n == len(sets) - 1, ring, w_proj, spans[n])
 
     payloads[0], a0 = lax.optimization_barrier((payloads[0], a0))
     rounds, sums, gp, ready = state_streams(
@@ -547,7 +549,8 @@
 
     a4, total = lax.optimization_barrier((a4, total))
     (total,) = times(7, total, ready, a4=a4)
-    (grad_x,) = times(8, total, ready, b4=b4, y4=y4)
+    (total,) = times(8, total, ready, b4=b4)
+    (grad_x,) = times(9, total, ready, y4=y4)
     return (grads, grad_x, grad_residue, grad_bias)
 
 

time: 81.3 us -> 79.1 us (0.973)
  waiting for transfers between devices: 18.3 us -> 14.1 us
  starting transfers between devices: 20.5 us -> 22.2 us
    ppermute x2, waiting for transfers between devices: 7.25 us -> 5.17 us  [from_later(): return lax.ppermute(array, 'ctx', [(i, i - by) for i in range(by, blocks)])]
    ppermute x2, starting transfers between devices: 0.14 us -> 1.91 us  [exchanged(): lax.ppermute(sums, 'ctx', [(i, i ^ by) for i in range(blocks)])]
    ppermute x8, waiting for transfers between devices: 4.03 us -> 2.55 us  [up(): return lax.ppermute(x, 'chan', pairs[1])]
    pallas_call x9 -> x10, Pallas kernels: 32.7 us -> 32.9 us  [add_product(): pl.pallas_call(functools.partial(product_kernel, plan, base, later, first...]
  transfers between devices with their start and end apart: 20 -> 20, of which waited for: 9 -> 8; matrix products, arithmetic and copies ran while one was open for 2% -> 2% of each run, Pallas kernels for 44% -> 46%
where the time goes in v7:
time: 79.1 us; the launch traced here: 78.9 us
  Pallas kernels  40.2 us (51%)
  starting transfers between devices  22.2 us (28%)
  waiting for transfers between devices  14.1 us (18%)
  local copies, waits for them, and re-layouts  1.29 us (2%)
  between operations  1.03 us (1%)
    pallas_call x10, Pallas kernels, add_product(): pl.pallas_call(functools.partial(product_kernel, plan, base, later, first...  32.9 us
    ppermute x8, starting transfers between devices, up(): return lax.ppermute(x, 'chan', pairs[1])  14.4 us
    ppermute x8, waiting for transfers between devices, down(): return lax.ppermute(x, 'chan', pairs[-1])  6.41 us
    ppermute x2, waiting for transfers between devices, from_later(): return lax.ppermute(array, 'ctx', [(i, i - by) for i in range(by, blocks)])  5.17 us
    ppermute x8, starting transfers between devices, down(): return lax.ppermute(x, 'chan', pairs[-1])  3.3 us
    pallas_call x1, Pallas kernels, state_streams(): pl.pallas_call(functools.partial(state_kernel, len(payloads), plan, ring)...  2.96 us
    ppermute x2, starting transfers between devices, from_later(): return lax.ppermute(array, 'ctx', [(i, i - by) for i in range(by, blocks)])  2.58 us
    ppermute x8, waiting for transfers between devices, up(): return lax.ppermute(x, 'chan', pairs[1])  2.55 us
  transfers between devices with their start and end apart: 20, of which 8 were waited for; matrix products, arithmetic and copies ran while one was open for 2% of the time, Pallas kernels for 46%

profile of v7, /device:TPU:0, one launch (start us, length us, event | category | flops | bytes accessed | tf_op | source)
XLA Modules:
  0.0 78.9 jit_solution(229333943381673188)
XLA Ops:
  0.6 2.1 %front.1 = (f32[3,128,1024]{2,1,0:T(8,128)S(1)}, f32[128,1024]{1,0:T(8,128)S(1)}, f32[128,1024]{1,0:T(8,128)S(1)}, f32[3,3,1024]{2,1,0:T(4,128)S(1)}, f32[1,1024...) custom-call(f32[3,128,1024]{2,1,0:T(8,128)} %features.1, f32[128,1024]{1,0:T(8,128)} %conv.1, ...), custom_call_target="tpu_custom_call" | custom-call | flops 8388608 | bytes 2621440 | tf_op jit(solution)/shard_map/front/pallas_call | solution.py:95
  4.0 1.9 %collective-permute-done.later.refs_0_ = f32[224,128]{1,0:T(8,128)S(1)} collective-permute-done((f32[224,128]{1,0:T(8,128)S(1)}, f32[224,128]{1,0:T(8,128)S(1)}, u32[]{:S(2)}, u32[]{:S(2)}) %collective-permute-start) | collective-permute-done | bytes 114720 | tf_op jit(solution)/shard_map/ppermute | solution.py:461
  7.6 3.1 %collective-permute-start.4 = (bf16[1,1,1024,128]{3,2,1,0:T(8,128)(2,1)S(1)}, bf16[1,1,1024,128]{3,2,1,0:T(8,128)(2,1)}, u32[]{:S(2)}, u32[]{:S(2)}) collective-permute-start(bf16[1,1,1024,128]{3,2,1,0:T(8,128)(2,1)S(1)} %bitcast.13), channel_id=1, source_target_pairs={{0,2},{2,4},{4,6},{6,7},{7,5},{5,3},{3,1},{1,0},{8,10},{10,12},{12... | collective-permute-start | bytes 786440 | tf_op jit(solution)/shard_map/ppermute | solution.py:449
  10.7 3.2 %collective-permute-done.1.refs_1_ = f32[144,128]{1,0:T(8,128)S(1)} collective-permute-done((f32[144,128]{1,0:T(8,128)S(1)}, f32[144,128]{1,0:T(8,128)S(1)}, u32[]{:S(2)}, u32[]{:S(2)}) %collective-permute-start.1) | collective-permute-done | bytes 73760 | tf_op jit(solution)/shard_map/ppermute | solution.py:461
  13.9 3.0 %state_streams.1 = (bf16[2,1024,128]{2,1,0:T(8,128)(2,1)S(1)}, f32[17,1024]{1,0:T(8,128)S(1)}, f32[1040,128]{1,0:T(8,128)S(1)}, bf16[1024,3072]{1,0:T(8,128)(2,1)S(1)}) custom-call(f32[3,128,1024]{2,1,0:T(8,128)S(1)} %get-tuple-element.61.feat, f32[128,1024]{1,0:T(8,128)S(1)} %get-tuple-element.62.og, f32[3,3,1024]{2,1,0:T(4,128)S(1)} %get-tuple-element.63.filt, ...), custom_call_target="tpu_custom_call" | custom-call | flops 4294967296 | bytes 16777216 | tf_op jit(solution)/shard_map/state_streams/pallas_call | solution.py:329
  16.9 1.7 %collective-permute-start.2 = (bf16[1,2,1024,128]{3,2,1,0:T(8,128)(2,1)S(1)}, bf16[1,2,1024,128]{3,2,1,0:T(8,128)(2,1)S(1)}, u32[]{:S(2)}, u32[]{:S(2)}) collective-permute-start(bf16[1,2,1024,128]{3,2,1,0:T(8,128)(2,1)S(1)} %bitcast.10), channel_id=1, source_target_pairs={{0,2},{2,4},{4,6},{6,7},{7,5},{5,3},{3,1},{1,0},{8,10},{10,12},{12... | collective-permute-start | bytes 1572872 | tf_op jit(solution)/shard_map/ppermute | solution.py:449
  19.0 1.6 %collective-permute-start.6 = (bf16[1,1,1024,128]{3,2,1,0:T(8,128)(2,1)}, bf16[1,1,1024,128]{3,2,1,0:T(8,128)(2,1)}, u32[]{:S(2)}, u32[]{:S(2)}) collective-permute-start(bf16[1,1,1024,128]{3,2,1,0:T(8,128)(2,1)} %collective-permute-done.4.refs_0_), channel_id=1, source_target_pairs={{0,2},{2,4},{4,6},{6,7},{7,5},{5,3},{3,1},{1,0},{8,10},{10,12},{12... | collective-permute-start | bytes 786440 | tf_op jit(solution)/shard_map/ppermute | solution.py:449
  21.0 3.9 %add_product.10 = (f32[1024,128]{1,0:T(8,128)S(1)}, bf16[1024,2048]{1,0:T(8,128)(2,1)S(1)}) custom-call(bf16[3,1024,8192]{2,1,0:T(8,128)(2,1)} %w_proj.19, bf16[1024,3072]{1,0:T(8,128)(2,1)S(1)} %get-tuple-element.72.w, bf16[1,1,1024,128]{3,2,1,0:T(8,128)(2,1)S(1)} %bitcast.15, bf16[1,2,1024,128]{3,2,1,0:T(8,128)(2,1)S(1)} %bitcast.12), custom_call_target="tpu_custom_call" | custom-call | flops 68719476736 | bytes 268435456 | tf_op jit(solution)/shard_map/add_product/pallas_call | solution.py:409
  24.9 4.0 %add_product.11 = (f32[1024,128]{1,0:T(8,128)S(1)}, bf16[1024,3072]{1,0:T(8,128)(2,1)S(1)}) custom-call(bf16[3,1024,8192]{2,1,0:T(8,128)(2,1)} %w_proj.19, bf16[1024,2048]{1,0:T(8,128)(2,1)S(1)} %get-tuple-element.75.w, bf16[1,1,1024,128]{3,2,1,0:T(8,128)(2,1)} %collective-permute-done.4.refs_0_, bf16[1,1,1024,128]{3,2,1,0:T(8,128)(2,1)} %collective-permute-done.5.refs_1_, ...), custom_call_target="tpu_custom_call" | custom-call | flops 68719476736 | bytes 268435456 | tf_op jit(solution)/shard_map/add_product/pallas_call | solution.py:409
  29.0 1.9 %gradients.1 = f32[3,128,1024]{2,1,0:T(8,128)} custom-call(f32[3,128,1024]{2,1,0:T(8,128)S(1)} %get-tuple-element.61.feat, f32[128,1024]{1,0:T(8,128)S(1)} %copy-done, f32[128,1024]{1,0:T(8,128)S(1)} %get-tuple-element.62.og, f32[3,3,1024]{2,1,0:T(4,128)S(1)} %get-tuple-element.63.filt, f32[1,1024]{1,0:T(1,128)S(1)} %get-tuple-element.64.bias, ...), custom_call_target="tpu_custom_call" | custom-call | flops 3932160 | bytes 5242880 | tf_op jit(solution)/shard_map/gradients/pallas_call | solution.py:216
  30.9 1.8 %collective-permute-done.3.refs_1_.refs_0_ = bf16[1,2,1024,128]{3,2,1,0:T(8,128)(2,1)S(1)} collective-permute-done((bf16[1,2,1024,128]{3,2,1,0:T(8,128)(2,1)S(1)}, bf16[1,2,1024,128]{3,2,1,0:T(8,128)(2,1)S(1)}, u32[]{:S(2)}, u32[]{:S(2)}) %collective-permute-start.3) | collective-permute-done | bytes 524320 | tf_op jit(solution)/shard_map/ppermute | solution.py:452
  32.6 1.6 %collective-permute-start.8 = (bf16[1,2,1024,128]{3,2,1,0:T(8,128)(2,1)S(1)}, bf16[1,2,1024,128]{3,2,1,0:T(8,128)(2,1)S(1)}, u32[]{:S(2)}, u32[]{:S(2)}) collective-permute-start(bf16[1,2,1024,128]{3,2,1,0:T(8,128)(2,1)S(1)} %collective-permute-done.2.refs_0_), channel_id=1, source_target_pairs={{0,2},{2,4},{4,6},{6,7},{7,5},{5,3},{3,1},{1,0},{8,10},{10,12},{12... | collective-permute-start | bytes 1572872 | tf_op jit(solution)/shard_map/ppermute | solution.py:449
  34.7 4.4 %add_product.12 = (f32[1024,128]{1,0:T(8,128)S(1)}, bf16[1024,3072]{1,0:T(8,128)(2,1)S(1)}) custom-call(bf16[3,1024,8192]{2,1,0:T(8,128)(2,1)} %w_proj.19, bf16[1024,3072]{1,0:T(8,128)(2,1)S(1)} %get-tuple-element.83.w, bf16[1,2,1024,128]{3,2,1,0:T(8,128)(2,1)S(1)} %collective-permute-done.2.refs_0_, ...), custom_call_target="tpu_custom_call" | custom-call | flops 65536 | bytes 256 | tf_op jit(solution)/shard_map/add_product/pallas_call | solution.py:409
  40.3 1.6 %collective-permute-start.11 = (bf16[1,1,1024,128]{3,2,1,0:T(8,128)(2,1)}, bf16[1,1,1024,128]{3,2,1,0:T(8,128)(2,1)S(1)}, u32[]{:S(2)}, u32[]{:S(2)}) collective-permute-start(bf16[1,1,1024,128]{3,2,1,0:T(8,128)(2,1)} %collective-permute-done.6.refs_1_), channel_id=1, source_target_pairs={{0,2},{2,4},{4,6},{6,7},{7,5},{5,3},{3,1},{1,0},{8,10},{10,12},{12... | collective-permute-start | bytes 786440 | tf_op jit(solution)/shard_map/ppermute | solution.py:449
  42.3 4.3 %add_product.13 = (f32[1024,128]{1,0:T(8,128)S(1)}, bf16[1024,3072]{1,0:T(8,128)(2,1)S(1)}) custom-call(bf16[3,1024,8192]{2,1,0:T(8,128)(2,1)} %w_proj.19, bf16[1024,3072]{1,0:T(8,128)(2,1)S(1)} %get-tuple-element.87.w, bf16[1,2,1024,128]{3,2,1,0:T(8,128)(2,1)S(1)} %collective-permute-done.3.refs_1_.refs_0_, ...), custom_call_target="tpu_custom_call" | custom-call | flops 68719476736 | bytes 268435456 | tf_op jit(solution)/shard_map/add_product/pallas_call | solution.py:409
  47.5 2.0 %collective-permute-done.9.refs_1_.refs_0_ = bf16[1,2,1024,128]{3,2,1,0:T(8,128)(2,1)S(1)} collective-permute-done((bf16[1,2,1024,128]{3,2,1,0:T(8,128)(2,1)S(1)}, bf16[1,2,1024,128]{3,2,1,0:T(8,128)(2,1)S(1)}, u32[]{:S(2)}, u32[]{:S(2)}) %collective-permute-start.9) | collective-permute-done | bytes 524320 | tf_op jit(solution)/shard_map/ppermute | solution.py:452
  49.5 1.6 %collective-permute-start.13 = (bf16[1,2,1024,128]{3,2,1,0:T(8,128)(2,1)S(1)}, bf16[1,2,1024,128]{3,2,1,0:T(8,128)(2,1)S(1)}, u32[]{:S(2)}, u32[]{:S(2)}) collective-permute-start(bf16[1,2,1024,128]{3,2,1,0:T(8,128)(2,1)S(1)} %collective-permute-done.8.refs_0_), channel_id=1, source_target_pairs={{0,2},{2,4},{4,6},{6,7},{7,5},{5,3},{3,1},{1,0},{8,10},{10,12},{12... | collective-permute-start | bytes 1572872 | tf_op jit(solution)/shard_map/ppermute | solution.py:449
  51.5 4.4 %add_product.14 = (f32[1024,128]{1,0:T(8,128)S(1)}, bf16[1024,3072]{1,0:T(8,128)(2,1)S(1)}) custom-call(bf16[3,1024,8192]{2,1,0:T(8,128)(2,1)} %w_proj.19, bf16[1024,3072]{1,0:T(8,128)(2,1)S(1)} %get-tuple-element.93.w, bf16[1,2,1024,128]{3,2,1,0:T(8,128)(2,1)S(1)} %collective-permute-done.8.refs_0_, ...), custom_call_target="tpu_custom_call" | custom-call | flops 65536 | bytes 256 | tf_op jit(solution)/shard_map/add_product/pallas_call | solution.py:409
  56.6 1.6 %collective-permute-start.18 = (bf16[1,1,512,128]{3,2,1,0:T(8,128)(2,1)S(1)}, bf16[1,1,512,128]{3,2,1,0:T(8,128)(2,1)S(1)}, u32[]{:S(2)}, u32[]{:S(2)}) collective-permute-start(bf16[1,1,512,128]{3,2,1,0:T(8,128)(2,1)S(1)} %slice.22), channel_id=1, source_target_pairs={{0,2},{2,4},{4,6},{6,7},{7,5},{5,3},{3,1},{1,0},{8,10},{10,12},{12... | collective-permute-start | bytes 393224 | tf_op jit(solution)/shard_map/ppermute | solution.py:449
  58.7 5.2 %add_product.15 = (f32[1024,128]{1,0:T(8,128)S(1)}, bf16[1024,4096]{1,0:T(8,128)(2,1)S(1)}) custom-call(bf16[3,1024,8192]{2,1,0:T(8,128)(2,1)} %w_proj.19, bf16[1024,3072]{1,0:T(8,128)(2,1)S(1)} %get-tuple-element.99.w, bf16[1,2,1024,128]{3,2,1,0:T(8,128)(2,1)S(1)} %collective-permute-done.9.refs_1_.refs_0_, ...), custom_call_target="tpu_custom_call" | custom-call | flops 68719476736 | bytes 268435456 | tf_op jit(solution)/shard_map/add_product/pallas_call | solution.py:409
  66.4 1.6 %collective-permute-start.17 = (bf16[1,1,1024,128]{3,2,1,0:T(8,128)(2,1)S(1)}, bf16[1,1,1024,128]{3,2,1,0:T(8,128)(2,1)S(1)}, u32[]{:S(2)}, u32[]{:S(2)}) collective-permute-start(bf16[1,1,1024,128]{3,2,1,0:T(8,128)(2,1)S(1)} %slice.21), channel_id=1, source_target_pairs={{0,2},{2,4},{4,6},{6,7},{7,5},{5,3},{3,1},{1,0},{8,10},{10,12},{12... | collective-permute-start | bytes 786440 | tf_op jit(solution)/shard_map/ppermute | solution.py:449
  68.7 3.8 %add_product.16 = (f32[1024,128]{1,0:T(8,128)S(1)}, bf16[1024,3072]{1,0:T(8,128)(2,1)S(1)}) custom-call(bf16[3,1024,8192]{2,1,0:T(8,128)(2,1)} %w_proj.19, bf16[1024,4096]{1,0:T(8,128)(2,1)S(1)} %get-tuple-element.105.w, bf16[1,2,1024,128]{3,2,1,0:T(8,128)(2,1)S(1)} %collective-permute-done.13.refs_0_, ...), custom_call_target="tpu_custom_call" | custom-call | flops 1073741824 | bytes 9437184 | tf_op jit(solution)/shard_map/add_product/pallas_call | solution.py:409
  73.2 1.7 %collective-permute-done.17.refs_0_ = bf16[1,1,1024,128]{3,2,1,0:T(8,128)(2,1)S(1)} collective-permute-done((bf16[1,1,1024,128]{3,2,1,0:T(8,128)(2,1)S(1)}, bf16[1,1,1024,128]{3,2,1,0:T(8,128)(2,1)S(1)}, u32[]{:S(2)}, u32[]{:S(2)}) %collective-permute-start.17) | collective-permute-done | bytes 262176 | tf_op jit(solution)/shard_map/ppermute | solution.py:449
  77.1 1.6 %add_product.19 = f32[128,1024]{1,0:T(8,128)} custom-call(bf16[3,1024,8192]{2,1,0:T(8,128)(2,1)} %w_proj.19, bf16[1024,3072]{1,0:T(8,128)(2,1)S(1)} %get-tuple-element.111.w, bf16[1,1,1024,128]{3,2,1,0:T(8,128)(2,1)S(1)} %collective-permute-done.16.refs_0_, f32[1024,128]{1,0:T(8,128)S(1)} %add_product.18.refs_1_), custom_call_target="tpu_custom_call" | custom-call | flops 65536 | bytes 256 | tf_op jit(solution)/shard_map/add_product/pallas_call | solution.py:409
  (40 shorter events, 14.3 us)
Async XLA Ops:
  2.7 3.2 %collective-permute-start = (f32[224,128]{1,0:T(8,128)S(1)}, f32[224,128]{1,0:T(8,128)S(1)}, u32[]{:S(2)}, u32[]{:S(2)}) collective-permute-start(f32[224,128]{1,0:T(8,128)S(1)} %get-tuple-element.66.own), channel_id=1, source_target_pairs={{8,0},{16,8},{24,16},{9,1},{17,9},{25,17},{10,2},{18,10},{26,18},{... | collective-permute-start | bytes 344072 | tf_op jit(solution)/shard_map/ppermute | solution.py:461
  6.3 7.6 %collective-permute-start.1 = (f32[144,128]{1,0:T(8,128)S(1)}, f32[144,128]{1,0:T(8,128)S(1)}, u32[]{:S(2)}, u32[]{:S(2)}) collective-permute-start(f32[144,128]{1,0:T(8,128)S(1)} %get-tuple-element.70), channel_id=1, source_target_pairs={{16,0},{24,8},{17,1},{25,9},{18,2},{26,10},{19,3},{27,11},{20,4},{... | collective-permute-start | bytes 221192 | tf_op jit(solution)/shard_map/ppermute | solution.py:461
  7.6 11.4 %collective-permute-start.4 = (bf16[1,1,1024,128]{3,2,1,0:T(8,128)(2,1)S(1)}, bf16[1,1,1024,128]{3,2,1,0:T(8,128)(2,1)}, u32[]{:S(2)}, u32[]{:S(2)}) collective-permute-start(bf16[1,1,1024,128]{3,2,1,0:T(8,128)(2,1)S(1)} %bitcast.13), channel_id=1, source_target_pairs={{0,2},{2,4},{4,6},{6,7},{7,5},{5,3},{3,1},{1,0},{8,10},{10,12},{12... | collective-permute-start | bytes 786440 | tf_op jit(solution)/shard_map/ppermute | solution.py:449
  10.7 8.3 %collective-permute-start.5 = (bf16[1,1,1024,128]{3,2,1,0:T(8,128)(2,1)S(1)}, bf16[1,1,1024,128]{3,2,1,0:T(8,128)(2,1)}, u32[]{:S(2)}, u32[]{:S(2)}) collective-permute-start(bf16[1,1,1024,128]{3,2,1,0:T(8,128)(2,1)S(1)} %bitcast.14), channel_id=1, source_target_pairs={{0,1},{2,0},{4,2},{6,4},{7,6},{5,7},{3,5},{1,3},{8,9},{10,8},{12,1... | collective-permute-start | bytes 786440 | tf_op jit(solution)/shard_map/ppermute | solution.py:452
  16.9 13.9 %collective-permute-start.2 = (bf16[1,2,1024,128]{3,2,1,0:T(8,128)(2,1)S(1)}, bf16[1,2,1024,128]{3,2,1,0:T(8,128)(2,1)S(1)}, u32[]{:S(2)}, u32[]{:S(2)}) collective-permute-start(bf16[1,2,1024,128]{3,2,1,0:T(8,128)(2,1)S(1)} %bitcast.10), channel_id=1, source_target_pairs={{0,2},{2,4},{4,6},{6,7},{7,5},{5,3},{3,1},{1,0},{8,10},{10,12},{12... | collective-permute-start | bytes 1572872 | tf_op jit(solution)/shard_map/ppermute | solution.py:449
  18.6 14.0 %collective-permute-start.3 = (bf16[1,2,1024,128]{3,2,1,0:T(8,128)(2,1)S(1)}, bf16[1,2,1024,128]{3,2,1,0:T(8,128)(2,1)S(1)}, u32[]{:S(2)}, u32[]{:S(2)}) collective-permute-start(bf16[1,2,1024,128]{3,2,1,0:T(8,128)(2,1)S(1)} %bitcast.11), channel_id=1, source_target_pairs={{0,1},{2,0},{4,2},{6,4},{7,6},{5,7},{3,5},{1,3},{8,9},{10,8},{12,1... | collective-permute-start | bytes 1572872 | tf_op jit(solution)/shard_map/ppermute | solution.py:452
  19.0 20.0 %collective-permute-start.6 = (bf16[1,1,1024,128]{3,2,1,0:T(8,128)(2,1)}, bf16[1,1,1024,128]{3,2,1,0:T(8,128)(2,1)}, u32[]{:S(2)}, u32[]{:S(2)}) collective-permute-start(bf16[1,1,1024,128]{3,2,1,0:T(8,128)(2,1)} %collective-permute-done.4.refs_0_), channel_id=1, source_target_pairs={{0,2},{2,4},{4,6},{6,7},{7,5},{5,3},{3,1},{1,0},{8,10},{10,12},{12... | collective-permute-start | bytes 786440 | tf_op jit(solution)/shard_map/ppermute | solution.py:449
  20.6 18.4 %collective-permute-start.7 = (bf16[1,1,1024,128]{3,2,1,0:T(8,128)(2,1)}, bf16[1,1,1024,128]{3,2,1,0:T(8,128)(2,1)}, u32[]{:S(2)}, u32[]{:S(2)}) collective-permute-start(bf16[1,1,1024,128]{3,2,1,0:T(8,128)(2,1)} %collective-permute-done.5.refs_1_), channel_id=1, source_target_pairs={{0,1},{2,0},{4,2},{6,4},{7,6},{5,7},{3,5},{1,3},{8,9},{10,8},{12,1... | collective-permute-start | bytes 786440 | tf_op jit(solution)/shard_map/ppermute | solution.py:452
  24.9 4.0 %copy-start = (f32[128,1024]{1,0:T(8,128)S(1)}, f32[128,1024]{1,0:T(8,128)}, u32[]{:S(2)}) copy-start(f32[128,1024]{1,0:T(8,128)} %conv.1) | copy-start | bytes 1572868
  32.6 14.8 %collective-permute-start.8 = (bf16[1,2,1024,128]{3,2,1,0:T(8,128)(2,1)S(1)}, bf16[1,2,1024,128]{3,2,1,0:T(8,128)(2,1)S(1)}, u32[]{:S(2)}, u32[]{:S(2)}) collective-permute-start(bf16[1,2,1024,128]{3,2,1,0:T(8,128)(2,1)S(1)} %collective-permute-done.2.refs_0_), channel_id=1, source_target_pairs={{0,2},{2,4},{4,6},{6,7},{7,5},{5,3},{3,1},{1,0},{8,10},{10,12},{12... | collective-permute-start | bytes 1572872 | tf_op jit(solution)/shard_map/ppermute | solution.py:449
  34.2 15.3 %collective-permute-start.9 = (bf16[1,2,1024,128]{3,2,1,0:T(8,128)(2,1)S(1)}, bf16[1,2,1024,128]{3,2,1,0:T(8,128)(2,1)S(1)}, u32[]{:S(2)}, u32[]{:S(2)}) collective-permute-start(bf16[1,2,1024,128]{3,2,1,0:T(8,128)(2,1)S(1)} %collective-permute-done.3.refs_1_.refs_0_), channel_id=1, source_target_pairs={{0,1},{2,0},{4,2},{6,4},{7,6},{5,7},{3,5},{1,3},{8,9},{10,8},{12,1... | collective-permute-start | bytes 1572872 | tf_op jit(solution)/shard_map/ppermute | solution.py:452
  39.1 7.6 %collective-permute-start.10 = (f32[17,1024]{1,0:T(8,128)S(1)}, f32[17,1024]{1,0:T(8,128)S(1)}, u32[]{:S(2)}, u32[]{:S(2)}) collective-permute-start(f32[17,1024]{1,0:T(8,128)S(1)} %get-tuple-element.95), channel_id=1, source_target_pairs={{0,8},{8,0},{16,24},{24,16},{1,9},{9,1},{17,25},{25,17},{2,10},{10... | collective-permute-start | bytes 208904 | tf_op jit(solution)/shard_map/ppermute | solution.py:464
  40.3 15.6 %collective-permute-start.11 = (bf16[1,1,1024,128]{3,2,1,0:T(8,128)(2,1)}, bf16[1,1,1024,128]{3,2,1,0:T(8,128)(2,1)S(1)}, u32[]{:S(2)}, u32[]{:S(2)}) collective-permute-start(bf16[1,1,1024,128]{3,2,1,0:T(8,128)(2,1)} %collective-permute-done.6.refs_1_), channel_id=1, source_target_pairs={{0,2},{2,4},{4,6},{6,7},{7,5},{5,3},{3,1},{1,0},{8,10},{10,12},{12... | collective-permute-start | bytes 786440 | tf_op jit(solution)/shard_map/ppermute | solution.py:449
  41.9 14.0 %collective-permute-start.12 = (bf16[1,1,1024,128]{3,2,1,0:T(8,128)(2,1)}, bf16[1,1,1024,128]{3,2,1,0:T(8,128)(2,1)S(1)}, u32[]{:S(2)}, u32[]{:S(2)}) collective-permute-start(bf16[1,1,1024,128]{3,2,1,0:T(8,128)(2,1)} %collective-permute-done.7.refs_2_), channel_id=1, source_target_pairs={{0,1},{2,0},{4,2},{6,4},{7,6},{5,7},{3,5},{1,3},{8,9},{10,8},{12,1... | collective-permute-start | bytes 786440 | tf_op jit(solution)/shard_map/ppermute | solution.py:452
  49.5 15.7 %collective-permute-start.13 = (bf16[1,2,1024,128]{3,2,1,0:T(8,128)(2,1)S(1)}, bf16[1,2,1024,128]{3,2,1,0:T(8,128)(2,1)S(1)}, u32[]{:S(2)}, u32[]{:S(2)}) collective-permute-start(bf16[1,2,1024,128]{3,2,1,0:T(8,128)(2,1)S(1)} %collective-permute-done.8.refs_0_), channel_id=1, source_target_pairs={{0,2},{2,4},{4,6},{6,7},{7,5},{5,3},{3,1},{1,0},{8,10},{10,12},{12... | collective-permute-start | bytes 1572872 | tf_op jit(solution)/shard_map/ppermute | solution.py:449
  51.1 15.3 %collective-permute-start.14 = (bf16[1,2,1024,128]{3,2,1,0:T(8,128)(2,1)S(1)}, bf16[1,2,1024,128]{3,2,1,0:T(8,128)(2,1)S(1)}, u32[]{:S(2)}, u32[]{:S(2)}) collective-permute-start(bf16[1,2,1024,128]{3,2,1,0:T(8,128)(2,1)S(1)} %collective-permute-done.9.refs_1_.refs_0_), channel_id=1, source_target_pairs={{0,1},{2,0},{4,2},{6,4},{7,6},{5,7},{3,5},{1,3},{8,9},{10,8},{12,1... | collective-permute-start | bytes 1572872 | tf_op jit(solution)/shard_map/ppermute | solution.py:452
  55.9 8.0 %collective-permute-start.15 = (f32[17,1024]{1,0:T(8,128)S(1)}, f32[17,1024]{1,0:T(8,128)S(1)}, u32[]{:S(2)}, u32[]{:S(2)}) collective-permute-start(f32[17,1024]{1,0:T(8,128)S(1)} %add.6), channel_id=1, source_target_pairs={{0,16},{8,24},{16,0},{24,8},{1,17},{9,25},{17,1},{25,9},{2,18},{10... | collective-permute-start | bytes 208904 | tf_op jit(solution)/shard_map/ppermute | solution.py:464
  56.6 15.9 %collective-permute-start.18 = (bf16[1,1,512,128]{3,2,1,0:T(8,128)(2,1)S(1)}, bf16[1,1,512,128]{3,2,1,0:T(8,128)(2,1)S(1)}, u32[]{:S(2)}, u32[]{:S(2)}) collective-permute-start(bf16[1,1,512,128]{3,2,1,0:T(8,128)(2,1)S(1)} %slice.22), channel_id=1, source_target_pairs={{0,2},{2,4},{4,6},{6,7},{7,5},{5,3},{3,1},{1,0},{8,10},{10,12},{12... | collective-permute-start | bytes 393224 | tf_op jit(solution)/shard_map/ppermute | solution.py:449
  58.2 14.3 %collective-permute-start.19 = (bf16[1,1,512,128]{3,2,1,0:T(8,128)(2,1)S(1)}, bf16[1,1,512,128]{3,2,1,0:T(8,128)(2,1)S(1)}, u32[]{:S(2)}, u32[]{:S(2)}) collective-permute-start(bf16[1,1,512,128]{3,2,1,0:T(8,128)(2,1)S(1)} %slice.23), channel_id=1, source_target_pairs={{0,1},{2,0},{4,2},{6,4},{7,6},{5,7},{3,5},{1,3},{8,9},{10,8},{12,1... | collective-permute-start | bytes 393224 | tf_op jit(solution)/shard_map/ppermute | solution.py:452
  66.4 8.6 %collective-permute-start.17 = (bf16[1,1,1024,128]{3,2,1,0:T(8,128)(2,1)S(1)}, bf16[1,1,1024,128]{3,2,1,0:T(8,128)(2,1)S(1)}, u32[]{:S(2)}, u32[]{:S(2)}) collective-permute-start(bf16[1,1,1024,128]{3,2,1,0:T(8,128)(2,1)S(1)} %slice.21), channel_id=1, source_target_pairs={{0,2},{2,4},{4,6},{6,7},{7,5},{5,3},{3,1},{1,0},{8,10},{10,12},{12... | collective-permute-start | bytes 786440 | tf_op jit(solution)/shard_map/ppermute | solution.py:449
  68.0 9.1 %collective-permute-start.16 = (bf16[1,1,1024,128]{3,2,1,0:T(8,128)(2,1)S(1)}, bf16[1,1,1024,128]{3,2,1,0:T(8,128)(2,1)S(1)}, u32[]{:S(2)}, u32[]{:S(2)}) collective-permute-start(bf16[1,1,1024,128]{3,2,1,0:T(8,128)(2,1)S(1)} %slice.20), channel_id=1, source_target_pairs={{0,1},{2,0},{4,2},{6,4},{7,6},{5,7},{3,5},{1,3},{8,9},{10,8},{12,1... | collective-permute-start | bytes 786440 | tf_op jit(solution)/shard_map/ppermute | solution.py:452

commit v8 on v7

--- a/solution.py
+++ b/solution.py
@@ -40,7 +40,7 @@
 
 
 def front_kernel(features, saved_conv, out_grad, short_filter, residue, rate, bias, *refs):
-    feat, conv, og, filt, bias_in, tables, own, res_in, rate_in, sems = refs
+    feat, conv, og, filt, bias_in, tables, own, brief, res_in, rate_in, sems = refs
     tokens, channels = og.shape
     modes = rate_in.shape[0]
     fold = channels // LANES
@@ -75,9 +75,10 @@
 
     zero = tuple(jnp.zeros((fold, LANES), F32) for _ in range(modes))
     states = lax.fori_loop(0, tokens - 2, step, zero, unroll=6)
-    for m in range(modes):
-        own[m * fold : (m + 1) * fold, :] = states[m]
-    own[modes * fold : (modes + 2) * fold, :] = tables[0 : 2 * fold, :]
+    for target in (own, brief):
+        for m in range(modes):
+            target[m * fold : (m + 1) * fold, :] = states[m]
+        target[modes * fold : (modes + 2) * fold, :] = tables[0 : 2 * fold, :]
     for n in range(3, 8):
         moves[n].wait()
     for n in range(3):
@@ -95,9 +96,9 @@
     return pl.pallas_call(
         front_kernel,
         in_specs=[in_hbm()] * 7,
-        out_specs=[whole()] * 7,
+        out_specs=[whole()] * 8,
         out_shape=[pltpu.VMEM(a.shape, F32) for a in (*inputs[:4], bias)]
-        + [pltpu.VMEM((n * fold, LANES), F32) for n in (tokens + 3 * modes, modes + 12)],
+        + [pltpu.VMEM((n * fold, LANES), F32) for n in (tokens + 3 * modes, modes + 12, modes + 2)],
         scratch_shapes=[pltpu.VMEM(rate.shape, F32)] * 2 + [pltpu.SemaphoreType.DMA((8,))],
         compiler_params=params(),
         cost_estimate=cost(4 * tokens * channels * modes, 20 * tokens * channels),
@@ -128,39 +129,40 @@
 
 
 def carried(own, m, later, state, decay, rate, span, fold):
-    modes = later.shape[0] // fold - 2
+    modes = own.shape[0] // fold - 2
     s0, s1 = (later[(modes + n) * fold : (modes + n + 1) * fold, :] for n in (0, 1))
     return own[m * fold : (m + 1) * fold, :] + jnp.exp(-(span - 2) * rate) * (s0 + decay * (s1 + decay * state))
 
 
-def joined(own, later, tables, span, modes, tokens, out):
-    fold = out.shape[0] // (modes + 2)
-    brief = later.at[pl.ds(0, (modes + 2) * fold)]
-    for m in range(modes):
-        here = slice(m * fold, (m + 1) * fold)
-        decay, rate = (tables[(tokens + n * modes + m) * fold : (tokens + n * modes + m + 1) * fold, :] for n in (0, 1))
-        out[here, :] = carried(own, m, brief, later[here, :], decay, rate, span, fold)
-    out[modes * fold : (modes + 2) * fold, :] = own[modes * fold : (modes + 2) * fold, :]
-
-
-def join(own, later, tables, span, modes, tokens):
-    def kernel(own, later, tables, out):
-        joined(own, later, tables, span, modes, tokens, out)
+def all_carried(summaries, spans, m, tables, tokens, fold):
+    modes = summaries[0].shape[0] // fold - 2
+    decay, rate = (tables[(tokens + n * modes + m) * fold : (tokens + n * modes + m + 1) * fold, :] for n in (0, 1))
+    state = summaries[-1][m * fold : (m + 1) * fold, :]
+    for own, later, span in reversed(list(zip(summaries, summaries[1:], spans))):
+        state = carried(own, m, later, state, decay, rate, span, fold)
+    return state
+
+
+def join(summaries, span, tables, tokens, fold):
+    def kernel(tables, *refs):
+        *refs, out = refs
+        modes = out.shape[0] // fold - 2
+        for m in range(modes):
+            out[m * fold : (m + 1) * fold, :] = all_carried(refs, [span] * (len(refs) - 1), m, tables, tokens, fold)
+        out[modes * fold : (modes + 2) * fold, :] = refs[0][modes * fold : (modes + 2) * fold, :]
 
     return pl.pallas_call(
         kernel,
-        in_specs=[whole()] * 3,
+        in_specs=[whole()] * (1 + len(summaries)),
         out_specs=whole(),
-        out_shape=pltpu.VMEM(own.shape, F32),
+        out_shape=pltpu.VMEM(summaries[0].shape, F32),
         compiler_params=params(),
         name="join",
-    )(own, later, tables)
-
-
-def gate_kernel(feat, conv, og, filt, bias, later, own, tables, rounded, joint, ext):
-    tokens, channels = og.shape
-    fold = channels // LANES
-    joined(own, later, tables, tokens, joint.shape[0] // fold - 2, tokens, joint)
+    )(tables, *summaries)
+
+
+def gate_kernel(feat, conv, og, filt, bias, later, rounded, ext):
+    tokens, channels = og.shape
     taps = [filt[0, j : j + 1, :] for j in range(3)]
     gate_gradient(feat, conv, og, bias, later, ext)
     for j in range(channels // LANES):
@@ -168,19 +170,18 @@
         rounded[0, lanes, :] = tapped(ext, taps, lanes, tokens).astype(BF16).T
 
 
-def gate_stream(feat, conv, og, filt, bias, later, own, tables):
-    tokens, channels = og.shape
-    fold = channels // LANES
+def gate_stream(feat, conv, og, filt, bias, later):
+    tokens, channels = og.shape
     return pl.pallas_call(
         gate_kernel,
-        in_specs=[whole()] * 8,
-        out_specs=[whole()] * 2,
-        out_shape=[pltpu.VMEM((1, channels, tokens), BF16), pltpu.VMEM((own.shape[0] - 10 * fold, LANES), F32)],
+        in_specs=[whole()] * 6,
+        out_specs=whole(),
+        out_shape=pltpu.VMEM((1, channels, tokens), BF16),
         scratch_shapes=[pltpu.VMEM((tokens + 8, channels), F32)],
         compiler_params=params(),
         cost_estimate=cost(*LONG),
         name="gate_stream",
-    )(feat, conv, og, filt, bias, later, own, tables)
+    )(feat, conv, og, filt, bias, later)
 
 
 def product_gradients(feat, gp, later, exts):
@@ -243,7 +244,8 @@
     return moves
 
 
-def state_kernel(later, plan, ring, feat, og, filt, bias, tables, *refs):
+def state_kernel(spans, plan, ring, feat, og, filt, bias, tables, *refs):
+    later = len(spans)
     payloads = refs[:later]
     w_proj, rounded, sums, gp, ready, acc, prod, first_ext, second_ext, sems = refs[later:]
     exts = first_ext, second_ext
@@ -253,7 +255,8 @@
     tokens, channels = og.shape
     fold = channels // LANES
     modes = (tables.shape[0] // fold - tokens) // 3
-    dec, raw, res = (tokens + n * modes for n in range(3))
+    dec, res = tokens, tokens + 2 * modes
+    briefs = [payloads[0].at[pl.ds(0, (modes + 2) * fold)], *payloads[1:]]
     for j in range(fold):
         lanes = slice(j * LANES, (j + 1) * LANES)
         p = feat[1, :, lanes] * feat[2, :, lanes]
@@ -268,14 +271,8 @@
     group = 8
     for low in range(0, modes, group):
         chosen = range(low, min(low + group, modes))
-        decay, weight, rate = ([rows(tables, at + m) for m in chosen] for at in (dec, res, raw))
-        state = [rows(payloads[-1], m) for m in chosen]
-        for n in reversed(range(later - 1)):
-            brief = payloads[n + 1].at[pl.ds(0, (modes + 2) * fold)]
-            state = [
-                carried(payloads[n], m, brief, s, d, r, tokens << n, fold)
-                for m, s, d, r in zip(chosen, state, decay, rate)
-            ]
+        decay, weight = ([rows(tables, at + m) for m in chosen] for at in (dec, res))
+        state = [all_carried(briefs, spans, m, tables, tokens, fold) for m in chosen]
 
         def corr(state, weight=weight):
             terms = [w * s for w, s in zip(weight, state)]
@@ -322,12 +319,12 @@
         move.wait()
 
 
-def state_streams(feat, og, filt, bias, tables, payloads, plan, ring, w_proj):
+def state_streams(feat, og, filt, bias, tables, payloads, spans, plan, ring, w_proj):
     tokens, channels = og.shape
     fold = channels // LANES
     modes = (tables.shape[0] // fold - tokens) // 3
     return pl.pallas_call(
-        functools.partial(state_kernel, len(payloads), plan, ring),
+        functools.partial(state_kernel, spans, plan, ring),
         in_specs=[whole()] * (5 + len(payloads)) + [in_hbm()],
         out_specs=[whole()] * 4,
         out_shape=[
@@ -464,17 +461,22 @@
         return sums + lax.ppermute(sums, "ctx", [(i, i ^ by) for i in range(blocks)])
 
     fold = channels // LANES
-    feat, conv, og, filt, bias_row, tables, own = front(
+    feat, conv, og, filt, bias_row, tables, own, brief = front(
         features, saved_conv, out_grad, short_filter, residue.T, rate.T, bias[None]
     )
-    payloads = [from_later(own, 1)]
-    gate, joint = gate_stream(feat, conv, og, filt, bias_row, payloads[0], own, tables)
-    by = 2
-    while by < blocks:
-        payloads.append(from_later(joint, by))
-        if 2 * by < blocks:
-            joint = join(joint, payloads[-1], tables, by * tokens, modes, tokens)
-        by *= 2
+    payloads, spans = [from_later(own, 1)], [tokens]
+    unit, window = 1, brief
+    while unit < blocks:
+        for by in range(len(payloads) % 3 + 1, 4):
+            if by * unit < blocks:
+                payloads.append(from_later(window, by * unit))
+                spans.append(unit * tokens)
+        unit *= 4
+        if unit < blocks:
+            near = [window, *payloads[-3:]]
+            near[1] = near[1][: window.shape[0]]
+            window = join(near, unit // 4 * tokens, tables, tokens, fold)
+    gate = gate_stream(feat, conv, og, filt, bias_row, payloads[0])
     a0 = stacked(gate)
     a1, z1 = up(a0), down(a0)
 
@@ -494,7 +496,7 @@
         [("b4", a, 1, back)],
         [("y4", a, 2, back)],
     ]
-    spans = [LONG, LONG, SHORT, LONG, SHORT, LONG, MIDDLE, TAIL, SHORT, SHORT]
+    costs = [LONG, LONG, SHORT, LONG, SHORT, LONG, MIDDLE, TAIL, SHORT, SHORT]
     hollow = jax.ShapeDtypeStruct((heights, 2, channels, tokens), BF16)
 
     def plan_of(n):
@@ -505,11 +507,11 @@
         after_next = [plan_of(k) for k in range(7, len(sets))]
         later = plan_of(n + 1) if n < 6 else sum(after_next, []) if n == 6 else None
         base = sum(len(plan) for plan in after_next[: max(0, n - 7)])
-        return add_product(total, ready, base, pieces, later, n == len(sets) - 1, ring, w_proj, spans[n])
+        return add_product(total, ready, base, pieces, later, n == len(sets) - 1, ring, w_proj, costs[n])
 
     payloads[0], a0 = lax.optimization_barrier((payloads[0], a0))
     rounds, sums, gp, ready = state_streams(
-        feat, og, filt, bias_row.reshape(fold, LANES), tables, payloads, plan_of(0), ring, w_proj
+        feat, og, filt, bias_row.reshape(fold, LANES), tables, payloads, spans, plan_of(0), ring, w_proj
     )
     b0 = stacked(rounds)
 

time: 79.1 us -> 76.3 us (0.965)
  waiting for transfers between devices: 14.1 us -> 11.6 us
    ppermute x2 -> x3, waiting for transfers between devices: 5.17 us -> 2.68 us  [from_later(): return lax.ppermute(array, 'ctx', [(i, i - by) for i in range(by, blocks)])]
    ppermute x8, waiting for transfers between devices: 2.55 us -> 0.26 us  [up(): return lax.ppermute(x, 'chan', pairs[1])]
    ppermute x8, waiting for transfers between devices: 6.41 us -> 8.61 us  [down(): return lax.ppermute(x, 'chan', pairs[-1])]
    ppermute x2, starting transfers between devices: 1.91 us -> 0.14 us  [exchanged(): lax.ppermute(sums, 'ctx', [(i, i ^ by) for i in range(blocks)])]
    ppermute x2 -> x3, starting transfers between devices: 2.58 us -> 3.88 us  [from_later(): return lax.ppermute(array, 'ctx', [(i, i - by) for i in range(by, blocks)])]
    ppermute x8, starting transfers between devices: 14.4 us -> 15.3 us  [up(): return lax.ppermute(x, 'chan', pairs[1])]
  transfers between devices with their start and end apart: 20 -> 21, of which waited for: 8 -> 8; matrix products, arithmetic and copies ran while one was open for 2% -> 2% of each run, Pallas kernels for 46% -> 48%
where the time goes in v8:
time: 76.3 us; the launch traced here: 76 us
  Pallas kernels  40.2 us (53%)
  starting transfers between devices  21.9 us (29%)
  waiting for transfers between devices  11.6 us (15%)
  local copies, waits for them, and re-layouts  1.29 us (2%)
  between operations  1.06 us (1%)
    pallas_call x10, Pallas kernels, add_product(): pl.pallas_call(functools.partial(product_kernel, plan, base, later, first...  32.9 us
    ppermute x8, starting transfers between devices, up(): return lax.ppermute(x, 'chan', pairs[1])  15.3 us
    ppermute x8, waiting for transfers between devices, down(): return lax.ppermute(x, 'chan', pairs[-1])  8.61 us
    ppermute x3, starting transfers between devices, from_later(): return lax.ppermute(array, 'ctx', [(i, i - by) for i in range(by, blocks)])  3.88 us
    pallas_call x1, Pallas kernels, state_streams(): pl.pallas_call(functools.partial(state_kernel, spans, plan, ring), in_spe...  2.96 us
    ppermute x3, waiting for transfers between devices, from_later(): return lax.ppermute(array, 'ctx', [(i, i - by) for i in range(by, blocks)])  2.68 us
    ppermute x8, starting transfers between devices, down(): return lax.ppermute(x, 'chan', pairs[-1])  2.55 us
    pallas_call x1, Pallas kernels, front(): pl.pallas_call(front_kernel, in_specs=[in_hbm()] * 7, out_specs=[whole()]...  2.11 us
  transfers between devices with their start and end apart: 21, of which 8 were waited for; matrix products, arithmetic and copies ran while one was open for 2% of the time, Pallas kernels for 48%

profile of v8, /device:TPU:0, one launch (start us, length us, event | category | flops | bytes accessed | tf_op | source)
XLA Modules:
  0.0 76.0 jit_solution(6843584942626572453)
XLA Ops:
  0.6 2.1 %front.1 = (f32[3,128,1024]{2,1,0:T(8,128)S(1)}, f32[128,1024]{1,0:T(8,128)S(1)}, f32[128,1024]{1,0:T(8,128)S(1)}, f32[3,3,1024]{2,1,0:T(4,128)S(1)}, f32[1,1024...) custom-call(f32[3,128,1024]{2,1,0:T(8,128)} %features.1, ...), custom_call_target="tpu_custom_call" | custom-call | flops 8388608 | bytes 2621440 | tf_op jit(solution)/shard_map/front/pallas_call | solution.py:96
  2.8 1.3 %collective-permute-start = (f32[224,128]{1,0:T(8,128)S(1)}, f32[224,128]{1,0:T(8,128)S(1)}, u32[]{:S(2)}, u32[]{:S(2)}) collective-permute-start(f32[224,128]{1,0:T(8,128)S(1)} %get-tuple-element.65), channel_id=1, source_target_pairs={{8,0},{16,8},{24,16},{9,1},{17,9},{25,17},{10,2},{18,10},{26,18},{... | collective-permute-start | bytes 344072 | tf_op jit(solution)/shard_map/ppermute | solution.py:458
  4.1 1.3 %collective-permute-start.1 = (f32[144,128]{1,0:T(8,128)S(1)}, f32[144,128]{1,0:T(8,128)S(1)}, u32[]{:S(2)}, u32[]{:S(2)}) collective-permute-start(f32[144,128]{1,0:T(8,128)S(1)} %get-tuple-element.68), channel_id=1, source_target_pairs={{16,0},{24,8},{17,1},{25,9},{18,2},{26,10},{19,3},{27,11},{20,4},{... | collective-permute-start | bytes 221192 | tf_op jit(solution)/shard_map/ppermute | solution.py:458
  7.0 3.1 %collective-permute-start.5 = (bf16[1,1,1024,128]{3,2,1,0:T(8,128)(2,1)S(1)}, bf16[1,1,1024,128]{3,2,1,0:T(8,128)(2,1)}, u32[]{:S(2)}, u32[]{:S(2)}) collective-permute-start(bf16[1,1,1024,128]{3,2,1,0:T(8,128)(2,1)S(1)} %bitcast.13), channel_id=1, source_target_pairs={{0,2},{2,4},{4,6},{6,7},{7,5},{5,3},{3,1},{1,0},{8,10},{10,12},{12... | collective-permute-start | bytes 786440 | tf_op jit(solution)/shard_map/ppermute | solution.py:446
  10.1 2.0 %collective-permute-done.1.refs_1_ = f32[144,128]{1,0:T(8,128)S(1)} collective-permute-done((f32[144,128]{1,0:T(8,128)S(1)}, f32[144,128]{1,0:T(8,128)S(1)}, u32[]{:S(2)}, u32[]{:S(2)}) %collective-permute-start.1) | collective-permute-done | bytes 73760 | tf_op jit(solution)/shard_map/ppermute | solution.py:458
  12.8 3.0 %state_streams.1 = (bf16[2,1024,128]{2,1,0:T(8,128)(2,1)S(1)}, f32[17,1024]{1,0:T(8,128)S(1)}, f32[1040,128]{1,0:T(8,128)S(1)}, bf16[1024,3072]{1,0:T(8,128)(2,1)S(1)}) custom-call(f32[3,128,1024]{2,1,0:T(8,128)S(1)} %get-tuple-element.60.feat, f32[128,1024]{1,0:T(8,128)S(1)} %get-tuple-element.61.og, f32[3,3,1024]{2,1,0:T(4,128)S(1)} %get-tuple-element.62.filt, ...), custom_call_target="tpu_custom_call" | custom-call | flops 4294967296 | bytes 16777216 | tf_op jit(solution)/shard_map/state_streams/pallas_call | solution.py:326
  15.7 2.2 %collective-permute-start.3 = (bf16[1,2,1024,128]{3,2,1,0:T(8,128)(2,1)S(1)}, bf16[1,2,1024,128]{3,2,1,0:T(8,128)(2,1)S(1)}, u32[]{:S(2)}, u32[]{:S(2)}) collective-permute-start(bf16[1,2,1024,128]{3,2,1,0:T(8,128)(2,1)S(1)} %bitcast.10), channel_id=1, source_target_pairs={{0,2},{2,4},{4,6},{6,7},{7,5},{5,3},{3,1},{1,0},{8,10},{10,12},{12... | collective-permute-start | bytes 1572872 | tf_op jit(solution)/shard_map/ppermute | solution.py:446
  18.5 1.6 %collective-permute-start.7 = (bf16[1,1,1024,128]{3,2,1,0:T(8,128)(2,1)}, bf16[1,1,1024,128]{3,2,1,0:T(8,128)(2,1)}, u32[]{:S(2)}, u32[]{:S(2)}) collective-permute-start(bf16[1,1,1024,128]{3,2,1,0:T(8,128)(2,1)} %collective-permute-done.5.refs_0_), channel_id=1, source_target_pairs={{0,2},{2,4},{4,6},{6,7},{7,5},{5,3},{3,1},{1,0},{8,10},{10,12},{12... | collective-permute-start | bytes 786440 | tf_op jit(solution)/shard_map/ppermute | solution.py:446
  20.6 3.9 %add_product.10 = (f32[1024,128]{1,0:T(8,128)S(1)}, bf16[1024,2048]{1,0:T(8,128)(2,1)S(1)}) custom-call(bf16[3,1024,8192]{2,1,0:T(8,128)(2,1)} %w_proj.19, bf16[1024,3072]{1,0:T(8,128)(2,1)S(1)} %get-tuple-element.70.w, bf16[1,1,1024,128]{3,2,1,0:T(8,128)(2,1)S(1)} %bitcast.15, bf16[1,2,1024,128]{3,2,1,0:T(8,128)(2,1)S(1)} %bitcast.12), custom_call_target="tpu_custom_call" | custom-call | flops 68719476736 | bytes 268435456 | tf_op jit(solution)/shard_map/add_product/pallas_call | solution.py:406
  24.5 4.0 %add_product.11 = (f32[1024,128]{1,0:T(8,128)S(1)}, bf16[1024,3072]{1,0:T(8,128)(2,1)S(1)}) custom-call(bf16[3,1024,8192]{2,1,0:T(8,128)(2,1)} %w_proj.19, bf16[1024,2048]{1,0:T(8,128)(2,1)S(1)} %get-tuple-element.73.w, bf16[1,1,1024,128]{3,2,1,0:T(8,128)(2,1)} %collective-permute-done.5.refs_0_, bf16[1,1,1024,128]{3,2,1,0:T(8,128)(2,1)} %collective-permute-done.6.refs_1_, ...), custom_call_target="tpu_custom_call" | custom-call | flops 68719476736 | bytes 268435456 | tf_op jit(solution)/shard_map/add_product/pallas_call | solution.py:406
  28.5 1.9 %gradients.1 = f32[3,128,1024]{2,1,0:T(8,128)} custom-call(f32[3,128,1024]{2,1,0:T(8,128)S(1)} %get-tuple-element.60.feat, f32[128,1024]{1,0:T(8,128)S(1)} %copy-done, f32[128,1024]{1,0:T(8,128)S(1)} %get-tuple-element.61.og, f32[3,3,1024]{2,1,0:T(4,128)S(1)} %get-tuple-element.62.filt, f32[1,1024]{1,0:T(1,128)S(1)} %get-tuple-element.63.bias, ...), custom_call_target="tpu_custom_call" | custom-call | flops 3932160 | bytes 5242880 | tf_op jit(solution)/shard_map/gradients/pallas_call | solution.py:217
  30.6 2.1 %collective-permute-done.4.refs_1_.refs_0_ = bf16[1,2,1024,128]{3,2,1,0:T(8,128)(2,1)S(1)} collective-permute-done((bf16[1,2,1024,128]{3,2,1,0:T(8,128)(2,1)S(1)}, bf16[1,2,1024,128]{3,2,1,0:T(8,128)(2,1)S(1)}, u32[]{:S(2)}, u32[]{:S(2)}) %collective-permute-start.4) | collective-permute-done | bytes 524320 | tf_op jit(solution)/shard_map/ppermute | solution.py:449
  32.8 2.0 %collective-permute-start.9 = (bf16[1,2,1024,128]{3,2,1,0:T(8,128)(2,1)S(1)}, bf16[1,2,1024,128]{3,2,1,0:T(8,128)(2,1)S(1)}, u32[]{:S(2)}, u32[]{:S(2)}) collective-permute-start(bf16[1,2,1024,128]{3,2,1,0:T(8,128)(2,1)S(1)} %collective-permute-done.3.refs_0_), channel_id=1, source_target_pairs={{0,2},{2,4},{4,6},{6,7},{7,5},{5,3},{3,1},{1,0},{8,10},{10,12},{12... | collective-permute-start | bytes 1572872 | tf_op jit(solution)/shard_map/ppermute | solution.py:446
  34.8 4.4 %add_product.12 = (f32[1024,128]{1,0:T(8,128)S(1)}, bf16[1024,3072]{1,0:T(8,128)(2,1)S(1)}) custom-call(bf16[3,1024,8192]{2,1,0:T(8,128)(2,1)} %w_proj.19, bf16[1024,3072]{1,0:T(8,128)(2,1)S(1)} %get-tuple-element.81.w, bf16[1,2,1024,128]{3,2,1,0:T(8,128)(2,1)S(1)} %collective-permute-done.3.refs_0_, ...), custom_call_target="tpu_custom_call" | custom-call | flops 65536 | bytes 256 | tf_op jit(solution)/shard_map/add_product/pallas_call | solution.py:406
  39.3 1.6 %collective-permute-start.12 = (bf16[1,1,1024,128]{3,2,1,0:T(8,128)(2,1)}, bf16[1,1,1024,128]{3,2,1,0:T(8,128)(2,1)S(1)}, u32[]{:S(2)}, u32[]{:S(2)}) collective-permute-start(bf16[1,1,1024,128]{3,2,1,0:T(8,128)(2,1)} %collective-permute-done.7.refs_1_), channel_id=1, source_target_pairs={{0,2},{2,4},{4,6},{6,7},{7,5},{5,3},{3,1},{1,0},{8,10},{10,12},{12... | collective-permute-start | bytes 786440 | tf_op jit(solution)/shard_map/ppermute | solution.py:446
  41.4 4.3 %add_product.13 = (f32[1024,128]{1,0:T(8,128)S(1)}, bf16[1024,3072]{1,0:T(8,128)(2,1)S(1)}) custom-call(bf16[3,1024,8192]{2,1,0:T(8,128)(2,1)} %w_proj.19, bf16[1024,3072]{1,0:T(8,128)(2,1)S(1)} %get-tuple-element.85.w, bf16[1,2,1024,128]{3,2,1,0:T(8,128)(2,1)S(1)} %collective-permute-done.4.refs_1_.refs_0_, ...), custom_call_target="tpu_custom_call" | custom-call | flops 68719476736 | bytes 268435456 | tf_op jit(solution)/shard_map/add_product/pallas_call | solution.py:406
  45.7 3.9 %collective-permute-done.10.refs_1_.refs_0_ = bf16[1,2,1024,128]{3,2,1,0:T(8,128)(2,1)S(1)} collective-permute-done((bf16[1,2,1024,128]{3,2,1,0:T(8,128)(2,1)S(1)}, bf16[1,2,1024,128]{3,2,1,0:T(8,128)(2,1)S(1)}, u32[]{:S(2)}, u32[]{:S(2)}) %collective-permute-start.10) | collective-permute-done | bytes 524320 | tf_op jit(solution)/shard_map/ppermute | solution.py:449
  49.6 1.6 %collective-permute-start.14 = (bf16[1,2,1024,128]{3,2,1,0:T(8,128)(2,1)S(1)}, bf16[1,2,1024,128]{3,2,1,0:T(8,128)(2,1)S(1)}, u32[]{:S(2)}, u32[]{:S(2)}) collective-permute-start(bf16[1,2,1024,128]{3,2,1,0:T(8,128)(2,1)S(1)} %collective-permute-done.9.refs_0_), channel_id=1, source_target_pairs={{0,2},{2,4},{4,6},{6,7},{7,5},{5,3},{3,1},{1,0},{8,10},{10,12},{12... | collective-permute-start | bytes 1572872 | tf_op jit(solution)/shard_map/ppermute | solution.py:446
  51.7 4.4 %add_product.14 = (f32[1024,128]{1,0:T(8,128)S(1)}, bf16[1024,3072]{1,0:T(8,128)(2,1)S(1)}) custom-call(bf16[3,1024,8192]{2,1,0:T(8,128)(2,1)} %w_proj.19, bf16[1024,3072]{1,0:T(8,128)(2,1)S(1)} %get-tuple-element.91.w, bf16[1,2,1024,128]{3,2,1,0:T(8,128)(2,1)S(1)} %collective-permute-done.9.refs_0_, ...), custom_call_target="tpu_custom_call" | custom-call | flops 65536 | bytes 256 | tf_op jit(solution)/shard_map/add_product/pallas_call | solution.py:406
  56.1 1.6 %collective-permute-start.19 = (bf16[1,1,512,128]{3,2,1,0:T(8,128)(2,1)S(1)}, bf16[1,1,512,128]{3,2,1,0:T(8,128)(2,1)S(1)}, u32[]{:S(2)}, u32[]{:S(2)}) collective-permute-start(bf16[1,1,512,128]{3,2,1,0:T(8,128)(2,1)S(1)} %slice.22), channel_id=1, source_target_pairs={{0,2},{2,4},{4,6},{6,7},{7,5},{5,3},{3,1},{1,0},{8,10},{10,12},{12... | collective-permute-start | bytes 393224 | tf_op jit(solution)/shard_map/ppermute | solution.py:446
  58.3 5.2 %add_product.15 = (f32[1024,128]{1,0:T(8,128)S(1)}, bf16[1024,4096]{1,0:T(8,128)(2,1)S(1)}) custom-call(bf16[3,1024,8192]{2,1,0:T(8,128)(2,1)} %w_proj.19, bf16[1024,3072]{1,0:T(8,128)(2,1)S(1)} %get-tuple-element.97.w, bf16[1,2,1024,128]{3,2,1,0:T(8,128)(2,1)S(1)} %collective-permute-done.10.refs_1_.refs_0_, ...), custom_call_target="tpu_custom_call" | custom-call | flops 68719476736 | bytes 268435456 | tf_op jit(solution)/shard_map/add_product/pallas_call | solution.py:406
  66.0 1.6 %collective-permute-start.18 = (bf16[1,1,1024,128]{3,2,1,0:T(8,128)(2,1)S(1)}, bf16[1,1,1024,128]{3,2,1,0:T(8,128)(2,1)S(1)}, u32[]{:S(2)}, u32[]{:S(2)}) collective-permute-start(bf16[1,1,1024,128]{3,2,1,0:T(8,128)(2,1)S(1)} %slice.21), channel_id=1, source_target_pairs={{0,2},{2,4},{4,6},{6,7},{7,5},{5,3},{3,1},{1,0},{8,10},{10,12},{12... | collective-permute-start | bytes 786440 | tf_op jit(solution)/shard_map/ppermute | solution.py:446
  68.4 3.8 %add_product.16 = (f32[1024,128]{1,0:T(8,128)S(1)}, bf16[1024,3072]{1,0:T(8,128)(2,1)S(1)}) custom-call(bf16[3,1024,8192]{2,1,0:T(8,128)(2,1)} %w_proj.19, bf16[1024,4096]{1,0:T(8,128)(2,1)S(1)} %get-tuple-element.103.w, bf16[1,2,1024,128]{3,2,1,0:T(8,128)(2,1)S(1)} %collective-permute-done.14.refs_0_, ...), custom_call_target="tpu_custom_call" | custom-call | flops 1073741824 | bytes 9437184 | tf_op jit(solution)/shard_map/add_product/pallas_call | solution.py:406
  74.3 1.6 %add_product.19 = f32[128,1024]{1,0:T(8,128)} custom-call(bf16[3,1024,8192]{2,1,0:T(8,128)(2,1)} %w_proj.19, bf16[1024,3072]{1,0:T(8,128)(2,1)S(1)} %get-tuple-element.109.w, bf16[1,1,1024,128]{3,2,1,0:T(8,128)(2,1)S(1)} %collective-permute-done.17.refs_0_, f32[1024,128]{1,0:T(8,128)S(1)} %add_product.18.refs_1_), custom_call_target="tpu_custom_call" | custom-call | flops 65536 | bytes 256 | tf_op jit(solution)/shard_map/add_product/pallas_call | solution.py:406
  (42 shorter events, 10.5 us)
Async XLA Ops:
  2.8 3.9 %collective-permute-start = (f32[224,128]{1,0:T(8,128)S(1)}, f32[224,128]{1,0:T(8,128)S(1)}, u32[]{:S(2)}, u32[]{:S(2)}) collective-permute-start(f32[224,128]{1,0:T(8,128)S(1)} %get-tuple-element.65), channel_id=1, source_target_pairs={{8,0},{16,8},{24,16},{9,1},{17,9},{25,17},{10,2},{18,10},{26,18},{... | collective-permute-start | bytes 344072 | tf_op jit(solution)/shard_map/ppermute | solution.py:458
  4.1 8.0 %collective-permute-start.1 = (f32[144,128]{1,0:T(8,128)S(1)}, f32[144,128]{1,0:T(8,128)S(1)}, u32[]{:S(2)}, u32[]{:S(2)}) collective-permute-start(f32[144,128]{1,0:T(8,128)S(1)} %get-tuple-element.68), channel_id=1, source_target_pairs={{16,0},{24,8},{17,1},{25,9},{18,2},{26,10},{19,3},{27,11},{20,4},{... | collective-permute-start | bytes 221192 | tf_op jit(solution)/shard_map/ppermute | solution.py:458
  5.4 7.4 %collective-permute-start.2 = (f32[144,128]{1,0:T(8,128)S(1)}, f32[144,128]{1,0:T(8,128)S(1)}, u32[]{:S(2)}, u32[]{:S(2)}) collective-permute-start(f32[144,128]{1,0:T(8,128)S(1)} %get-tuple-element.68), channel_id=1, source_target_pairs={{24,0},{25,1},{26,2},{27,3},{28,4},{29,5},{30,6},{31,7}} | collective-permute-start | bytes 221192 | tf_op jit(solution)/shard_map/ppermute | solution.py:458
  7.0 10.9 %collective-permute-start.5 = (bf16[1,1,1024,128]{3,2,1,0:T(8,128)(2,1)S(1)}, bf16[1,1,1024,128]{3,2,1,0:T(8,128)(2,1)}, u32[]{:S(2)}, u32[]{:S(2)}) collective-permute-start(bf16[1,1,1024,128]{3,2,1,0:T(8,128)(2,1)S(1)} %bitcast.13), channel_id=1, source_target_pairs={{0,2},{2,4},{4,6},{6,7},{7,5},{5,3},{3,1},{1,0},{8,10},{10,12},{12... | collective-permute-start | bytes 786440 | tf_op jit(solution)/shard_map/ppermute | solution.py:446
  10.1 8.5 %collective-permute-start.6 = (bf16[1,1,1024,128]{3,2,1,0:T(8,128)(2,1)S(1)}, bf16[1,1,1024,128]{3,2,1,0:T(8,128)(2,1)}, u32[]{:S(2)}, u32[]{:S(2)}) collective-permute-start(bf16[1,1,1024,128]{3,2,1,0:T(8,128)(2,1)S(1)} %bitcast.14), channel_id=1, source_target_pairs={{0,1},{2,0},{4,2},{6,4},{7,6},{5,7},{3,5},{1,3},{8,9},{10,8},{12,1... | collective-permute-start | bytes 786440 | tf_op jit(solution)/shard_map/ppermute | solution.py:449
  15.7 14.9 %collective-permute-start.3 = (bf16[1,2,1024,128]{3,2,1,0:T(8,128)(2,1)S(1)}, bf16[1,2,1024,128]{3,2,1,0:T(8,128)(2,1)S(1)}, u32[]{:S(2)}, u32[]{:S(2)}) collective-permute-start(bf16[1,2,1024,128]{3,2,1,0:T(8,128)(2,1)S(1)} %bitcast.10), channel_id=1, source_target_pairs={{0,2},{2,4},{4,6},{6,7},{7,5},{5,3},{3,1},{1,0},{8,10},{10,12},{12... | collective-permute-start | bytes 1572872 | tf_op jit(solution)/shard_map/ppermute | solution.py:446
  17.9 14.9 %collective-permute-start.4 = (bf16[1,2,1024,128]{3,2,1,0:T(8,128)(2,1)S(1)}, bf16[1,2,1024,128]{3,2,1,0:T(8,128)(2,1)S(1)}, u32[]{:S(2)}, u32[]{:S(2)}) collective-permute-start(bf16[1,2,1024,128]{3,2,1,0:T(8,128)(2,1)S(1)} %bitcast.11), channel_id=1, source_target_pairs={{0,1},{2,0},{4,2},{6,4},{7,6},{5,7},{3,5},{1,3},{8,9},{10,8},{12,1... | collective-permute-start | bytes 1572872 | tf_op jit(solution)/shard_map/ppermute | solution.py:449
  18.5 20.6 %collective-permute-start.7 = (bf16[1,1,1024,128]{3,2,1,0:T(8,128)(2,1)}, bf16[1,1,1024,128]{3,2,1,0:T(8,128)(2,1)}, u32[]{:S(2)}, u32[]{:S(2)}) collective-permute-start(bf16[1,1,1024,128]{3,2,1,0:T(8,128)(2,1)} %collective-permute-done.5.refs_0_), channel_id=1, source_target_pairs={{0,2},{2,4},{4,6},{6,7},{7,5},{5,3},{3,1},{1,0},{8,10},{10,12},{12... | collective-permute-start | bytes 786440 | tf_op jit(solution)/shard_map/ppermute | solution.py:446
  20.1 19.1 %collective-permute-start.8 = (bf16[1,1,1024,128]{3,2,1,0:T(8,128)(2,1)}, bf16[1,1,1024,128]{3,2,1,0:T(8,128)(2,1)}, u32[]{:S(2)}, u32[]{:S(2)}) collective-permute-start(bf16[1,1,1024,128]{3,2,1,0:T(8,128)(2,1)} %collective-permute-done.6.refs_1_), channel_id=1, source_target_pairs={{0,1},{2,0},{4,2},{6,4},{7,6},{5,7},{3,5},{1,3},{8,9},{10,8},{12,1... | collective-permute-start | bytes 786440 | tf_op jit(solution)/shard_map/ppermute | solution.py:449
  24.5 4.0 %copy-start = (f32[128,1024]{1,0:T(8,128)S(1)}, f32[128,1024]{1,0:T(8,128)}, u32[]{:S(2)}) copy-start(f32[128,1024]{1,0:T(8,128)} %conv.1) | copy-start | bytes 1572868
  32.8 16.9 %collective-permute-start.10 = (bf16[1,2,1024,128]{3,2,1,0:T(8,128)(2,1)S(1)}, bf16[1,2,1024,128]{3,2,1,0:T(8,128)(2,1)S(1)}, u32[]{:S(2)}, u32[]{:S(2)}) collective-permute-start(bf16[1,2,1024,128]{3,2,1,0:T(8,128)(2,1)S(1)} %collective-permute-done.4.refs_1_.refs_0_), channel_id=1, source_target_pairs={{0,1},{2,0},{4,2},{6,4},{7,6},{5,7},{3,5},{1,3},{8,9},{10,8},{12,1... | collective-permute-start | bytes 1572872 | tf_op jit(solution)/shard_map/ppermute | solution.py:449
  32.8 16.9 %collective-permute-start.9 = (bf16[1,2,1024,128]{3,2,1,0:T(8,128)(2,1)S(1)}, bf16[1,2,1024,128]{3,2,1,0:T(8,128)(2,1)S(1)}, u32[]{:S(2)}, u32[]{:S(2)}) collective-permute-start(bf16[1,2,1024,128]{3,2,1,0:T(8,128)(2,1)S(1)} %collective-permute-done.3.refs_0_), channel_id=1, source_target_pairs={{0,2},{2,4},{4,6},{6,7},{7,5},{5,3},{3,1},{1,0},{8,10},{10,12},{12... | collective-permute-start | bytes 1572872 | tf_op jit(solution)/shard_map/ppermute | solution.py:446
  39.2 6.5 %collective-permute-start.11 = (f32[17,1024]{1,0:T(8,128)S(1)}, f32[17,1024]{1,0:T(8,128)S(1)}, u32[]{:S(2)}, u32[]{:S(2)}) collective-permute-start(f32[17,1024]{1,0:T(8,128)S(1)} %get-tuple-element.93), channel_id=1, source_target_pairs={{0,8},{8,0},{16,24},{24,16},{1,9},{9,1},{17,25},{25,17},{2,10},{10... | collective-permute-start | bytes 208904 | tf_op jit(solution)/shard_map/ppermute | solution.py:461
  39.3 16.8 %collective-permute-start.12 = (bf16[1,1,1024,128]{3,2,1,0:T(8,128)(2,1)}, bf16[1,1,1024,128]{3,2,1,0:T(8,128)(2,1)S(1)}, u32[]{:S(2)}, u32[]{:S(2)}) collective-permute-start(bf16[1,1,1024,128]{3,2,1,0:T(8,128)(2,1)} %collective-permute-done.7.refs_1_), channel_id=1, source_target_pairs={{0,2},{2,4},{4,6},{6,7},{7,5},{5,3},{3,1},{1,0},{8,10},{10,12},{12... | collective-permute-start | bytes 786440 | tf_op jit(solution)/shard_map/ppermute | solution.py:446
  40.9 15.1 %collective-permute-start.13 = (bf16[1,1,1024,128]{3,2,1,0:T(8,128)(2,1)}, bf16[1,1,1024,128]{3,2,1,0:T(8,128)(2,1)S(1)}, u32[]{:S(2)}, u32[]{:S(2)}) collective-permute-start(bf16[1,1,1024,128]{3,2,1,0:T(8,128)(2,1)} %collective-permute-done.8.refs_2_), channel_id=1, source_target_pairs={{0,1},{2,0},{4,2},{6,4},{7,6},{5,7},{3,5},{1,3},{8,9},{10,8},{12,1... | collective-permute-start | bytes 786440 | tf_op jit(solution)/shard_map/ppermute | solution.py:449
  49.6 15.1 %collective-permute-start.14 = (bf16[1,2,1024,128]{3,2,1,0:T(8,128)(2,1)S(1)}, bf16[1,2,1024,128]{3,2,1,0:T(8,128)(2,1)S(1)}, u32[]{:S(2)}, u32[]{:S(2)}) collective-permute-start(bf16[1,2,1024,128]{3,2,1,0:T(8,128)(2,1)S(1)} %collective-permute-done.9.refs_0_), channel_id=1, source_target_pairs={{0,2},{2,4},{4,6},{6,7},{7,5},{5,3},{3,1},{1,0},{8,10},{10,12},{12... | collective-permute-start | bytes 1572872 | tf_op jit(solution)/shard_map/ppermute | solution.py:446
  51.2 14.8 %collective-permute-start.15 = (bf16[1,2,1024,128]{3,2,1,0:T(8,128)(2,1)S(1)}, bf16[1,2,1024,128]{3,2,1,0:T(8,128)(2,1)S(1)}, u32[]{:S(2)}, u32[]{:S(2)}) collective-permute-start(bf16[1,2,1024,128]{3,2,1,0:T(8,128)(2,1)S(1)} %collective-permute-done.10.refs_1_.refs_0_), channel_id=1, source_target_pairs={{0,1},{2,0},{4,2},{6,4},{7,6},{5,7},{3,5},{1,3},{8,9},{10,8},{12,1... | collective-permute-start | bytes 1572872 | tf_op jit(solution)/shard_map/ppermute | solution.py:449
  56.0 7.4 %collective-permute-start.16 = (f32[17,1024]{1,0:T(8,128)S(1)}, f32[17,1024]{1,0:T(8,128)S(1)}, u32[]{:S(2)}, u32[]{:S(2)}) collective-permute-start(f32[17,1024]{1,0:T(8,128)S(1)} %add.6), channel_id=1, source_target_pairs={{0,16},{8,24},{16,0},{24,8},{1,17},{9,25},{17,1},{25,9},{2,18},{10... | collective-permute-start | bytes 208904 | tf_op jit(solution)/shard_map/ppermute | solution.py:461
  56.1 16.0 %collective-permute-start.19 = (bf16[1,1,512,128]{3,2,1,0:T(8,128)(2,1)S(1)}, bf16[1,1,512,128]{3,2,1,0:T(8,128)(2,1)S(1)}, u32[]{:S(2)}, u32[]{:S(2)}) collective-permute-start(bf16[1,1,512,128]{3,2,1,0:T(8,128)(2,1)S(1)} %slice.22), channel_id=1, source_target_pairs={{0,2},{2,4},{4,6},{6,7},{7,5},{5,3},{3,1},{1,0},{8,10},{10,12},{12... | collective-permute-start | bytes 393224 | tf_op jit(solution)/shard_map/ppermute | solution.py:446
  57.8 14.4 %collective-permute-start.20 = (bf16[1,1,512,128]{3,2,1,0:T(8,128)(2,1)S(1)}, bf16[1,1,512,128]{3,2,1,0:T(8,128)(2,1)S(1)}, u32[]{:S(2)}, u32[]{:S(2)}) collective-permute-start(bf16[1,1,512,128]{3,2,1,0:T(8,128)(2,1)S(1)} %slice.23), channel_id=1, source_target_pairs={{0,1},{2,0},{4,2},{6,4},{7,6},{5,7},{3,5},{1,3},{8,9},{10,8},{12,1... | collective-permute-start | bytes 393224 | tf_op jit(solution)/shard_map/ppermute | solution.py:449
  66.0 6.9 %collective-permute-start.18 = (bf16[1,1,1024,128]{3,2,1,0:T(8,128)(2,1)S(1)}, bf16[1,1,1024,128]{3,2,1,0:T(8,128)(2,1)S(1)}, u32[]{:S(2)}, u32[]{:S(2)}) collective-permute-start(bf16[1,1,1024,128]{3,2,1,0:T(8,128)(2,1)S(1)} %slice.21), channel_id=1, source_target_pairs={{0,2},{2,4},{4,6},{6,7},{7,5},{5,3},{3,1},{1,0},{8,10},{10,12},{12... | collective-permute-start | bytes 786440 | tf_op jit(solution)/shard_map/ppermute | solution.py:446
  67.7 6.6 %collective-permute-start.17 = (bf16[1,1,1024,128]{3,2,1,0:T(8,128)(2,1)S(1)}, bf16[1,1,1024,128]{3,2,1,0:T(8,128)(2,1)S(1)}, u32[]{:S(2)}, u32[]{:S(2)}) collective-permute-start(bf16[1,1,1024,128]{3,2,1,0:T(8,128)(2,1)S(1)} %slice.20), channel_id=1, source_target_pairs={{0,1},{2,0},{4,2},{6,4},{7,6},{5,7},{3,5},{1,3},{8,9},{10,8},{12,1... | collective-permute-start | bytes 786440 | tf_op jit(solution)/shard_map/ppermute | solution.py:449

commit v9 on v8

--- a/solution.py
+++ b/solution.py
@@ -11,8 +11,6 @@
 RING = 8
 LONG = 1 << 36, 1 << 28
 SHORT = 1 << 16, 1 << 8
-MIDDLE = 1 << 30, 9 << 20
-TAIL = 7 << 28, 13 << 20
 VMEM = 8 * 1024 * 1024
 F32 = jnp.float32
 BF16 = jnp.bfloat16
@@ -491,12 +489,11 @@
         [("y1", (1,), 1, 1), ("a2", a, 0, ring - 2), ("z2", a, 0, 2)],
         [("b2", b, 1, ring - 2), ("y2", (0,), 1, 2)],
         [("y2", (1,), 1, 2), ("a3", a, 0, ring - 3), ("z3", a, 0, 3)],
-        [("b3", b, 1, ring - 3), ("y3", b, 1, 3)],
+        [("b3", a, 1, ring - 3), ("y3", a, 2, 3), ("c3", a, 2, ring - 3), ("x3", a, 1, 3)],
+        [("b4", a, 1, back), ("y4", a, 2, back)],
         [("a4", a, 0, back)],
-        [("b4", a, 1, back)],
-        [("y4", a, 2, back)],
     ]
-    costs = [LONG, LONG, SHORT, LONG, SHORT, LONG, MIDDLE, TAIL, SHORT, SHORT]
+    costs = [LONG, LONG, SHORT, LONG, SHORT, SHORT, SHORT, SHORT, SHORT]
     hollow = jax.ShapeDtypeStruct((heights, 2, channels, tokens), BF16)
 
     def plan_of(n):
@@ -516,43 +513,44 @@
     b0 = stacked(rounds)
 
     b1, y1 = up(b0), down(b0)
-    a1, z1, b0 = lax.optimization_barrier((a1, z1, b0))
+    a1, z1, b0, sums = lax.optimization_barrier((a1, z1, b0, sums))
     a2, z2 = up(a1), down(z1)
+    distances = [1 << n for n in range((blocks - 1).bit_length())]
+    for by in distances[:1]:
+        sums = exchanged(sums, by)
     total, ready = times(0, None, ready, a0=a0, b0=b0)
     total, ready = times(1, total, ready, a1=a1, z1=z1)
-    grads = gradients(feat, saved_conv, og, filt, bias_row, payloads[0], after(gp, total))
-
-    b1, y1, total, grads = lax.optimization_barrier((b1, y1, total, grads))
+
+    b1, y1, total, sums = lax.optimization_barrier((b1, y1, total, sums))
     b2, y2 = up(b1), down(y1)
     total, ready = times(2, total, ready, b1=b1, y1=y1)
 
     a2, z2, total, sums = lax.optimization_barrier((a2, z2, total, sums))
     a3, z3 = up(a2), down(z2)
-    distances = [1 << n for n in range((blocks - 1).bit_length())]
-    for by in distances[:-1]:
+    for by in distances[1:]:
         sums = exchanged(sums, by)
     total, ready = times(3, total, ready, y1=y1, a2=a2, z2=z2)
-
-    b2, y2, total, sums = lax.optimization_barrier((b2, y2, total, sums))
-    b3, y3 = up(b2), down(y2)
+    grads = gradients(features, saved_conv, out_grad, short_filter, bias[None], payloads[0], after(gp, total))
+
+    b2, y2, total, sums, grads = lax.optimization_barrier((b2, y2, total, sums, grads))
+    b3, y3 = up(b2[:, :1]), down(y2[:, 1:])
+    c3 = up(b2[:, 1:])
     total, ready = times(4, total, ready, b2=b2, y2=y2)
-
-    a3, z3, total, sums = lax.optimization_barrier((a3, z3, total, sums))
-    for by in distances[-1:]:
-        sums = exchanged(sums, by)
+    x3 = down(after(y2[:, :1], total))
+    a3, z3, total = lax.optimization_barrier((a3, z3, total))
+    total, ready = times(5, total, ready, y2=y2, a3=a3, z3=z3)
+
+    b3, y3, total, sums = lax.optimization_barrier((b3, y3, total, sums))
+    b4, y4 = up(b3), down(y3)
+    a4 = up(a3[:, :, :half]), down(z3[:, :, half:])
     sums = sums * (tokens * blocks) ** (-0.5)
-    a4 = up(a3[:, :, :half]), down(z3[:, :, half:])
-    total, ready = times(5, total, ready, y2=y2, a3=a3, z3=z3)
-
+    total, ready = times(6, total, ready, b3=b3, y3=y3, c3=c3, x3=x3)
+
+    b4, y4, total, sums = lax.optimization_barrier((b4, y4, total, sums))
+    (total,) = times(7, total, ready, b4=b4, y4=y4)
     grad_residue, grad_bias = sums[:modes].T, sums[modes]
-    b3, y3, total, grad_residue, grad_bias = lax.optimization_barrier((b3, y3, total, grad_residue, grad_bias))
-    b4, y4 = up(b3[:, :1]), down(y3[:, 1:])
-    total, ready = times(6, total, ready, b3=b3, y3=y3)
-
-    a4, total = lax.optimization_barrier((a4, total))
-    (total,) = times(7, total, ready, a4=a4)
-    (total,) = times(8, total, ready, b4=b4)
-    (grad_x,) = times(9, total, ready, y4=y4)
+    a4, total, grad_residue, grad_bias = lax.optimization_barrier((a4, total, grad_residue, grad_bias))
+    (grad_x,) = times(8, total, ready, a4=a4)
     return (grads, grad_x, grad_residue, grad_bias)
 
 

time: 76.3 us -> 77.3 us (1.013)
  waiting for transfers between devices: 11.6 us -> 8.77 us
  starting transfers between devices: 21.9 us -> 24.4 us
  Pallas kernels: 40.2 us -> 41.4 us
    ppermute x8 -> x9, waiting for transfers between devices: 8.61 us -> 4.59 us  [down(): return lax.ppermute(x, 'chan', pairs[-1])]
    ppermute x8 -> x9, waiting for transfers between devices: 0.26 us -> 1.53 us  [up(): return lax.ppermute(x, 'chan', pairs[1])]
    pallas_call x10 -> x9, Pallas kernels: 32.9 us -> 34.1 us  [add_product(): pl.pallas_call(functools.partial(product_kernel, plan, base, later, first...]
    ppermute x8 -> x9, starting transfers between devices: 15.3 us -> 16.5 us  [up(): return lax.ppermute(x, 'chan', pairs[1])]
    ppermute x8 -> x9, starting transfers between devices: 2.55 us -> 3.25 us  [down(): return lax.ppermute(x, 'chan', pairs[-1])]
  transfers between devices with their start and end apart: 21 -> 23, of which waited for: 8 -> 6; matrix products, arithmetic and copies ran while one was open for 2% -> 2% of each run, Pallas kernels for 48% -> 49%
where the time goes in v9:
time: 77.3 us; the launch traced here: 77.1 us
  Pallas kernels  41.4 us (54%)
  starting transfers between devices  24.4 us (32%)
  waiting for transfers between devices  8.77 us (11%)
  local copies, waits for them, and re-layouts  1.36 us (2%)
  between operations  1.13 us (1%)
    pallas_call x9, Pallas kernels, add_product(): pl.pallas_call(functools.partial(product_kernel, plan, base, later, first...  34.1 us
    ppermute x9, starting transfers between devices, up(): return lax.ppermute(x, 'chan', pairs[1])  16.5 us
    ppermute x9, waiting for transfers between devices, down(): return lax.ppermute(x, 'chan', pairs[-1])  4.59 us
    ppermute x3, starting transfers between devices, from_later(): return lax.ppermute(array, 'ctx', [(i, i - by) for i in range(by, blocks)])  3.88 us
    ppermute x9, starting transfers between devices, down(): return lax.ppermute(x, 'chan', pairs[-1])  3.25 us
    pallas_call x1, Pallas kernels, state_streams(): pl.pallas_call(functools.partial(state_kernel, spans, plan, ring), in_spe...  2.95 us
    ppermute x3, waiting for transfers between devices, from_later(): return lax.ppermute(array, 'ctx', [(i, i - by) for i in range(by, blocks)])  2.65 us
    pallas_call x1, Pallas kernels, front(): pl.pallas_call(front_kernel, in_specs=[in_hbm()] * 7, out_specs=[whole()]...  2.11 us
  transfers between devices with their start and end apart: 23, of which 6 were waited for; matrix products, arithmetic and copies ran while one was open for 2% of the time, Pallas kernels for 49%

profile of v9, /device:TPU:0, one launch (start us, length us, event | category | flops | bytes accessed | tf_op | source)
XLA Modules:
  0.0 77.1 jit_solution(4006706288332584749)
XLA Ops:
  0.6 2.1 %front.1 = (f32[3,128,1024]{2,1,0:T(8,128)S(1)}, f32[128,1024]{1,0:T(8,128)S(1)}, f32[128,1024]{1,0:T(8,128)S(1)}, f32[3,3,1024]{2,1,0:T(4,128)S(1)}, f32[1,1024...) custom-call(f32[3,128,1024]{2,1,0:T(8,128)} %feat.1, ...), custom_call_target="tpu_custom_call" | custom-call | flops 8388608 | bytes 2621440 | tf_op jit(solution)/shard_map/front/pallas_call | solution.py:94
  7.0 3.1 %collective-permute-start.5 = (bf16[1,1,1024,128]{3,2,1,0:T(8,128)(2,1)S(1)}, bf16[1,1,1024,128]{3,2,1,0:T(8,128)(2,1)}, u32[]{:S(2)}, u32[]{:S(2)}) collective-permute-start(bf16[1,1,1024,128]{3,2,1,0:T(8,128)(2,1)S(1)} %bitcast.15), channel_id=1, source_target_pairs={{0,2},{2,4},{4,6},{6,7},{7,5},{5,3},{3,1},{1,0},{8,10},{10,12},{12... | collective-permute-start | bytes 786440 | tf_op jit(solution)/shard_map/ppermute | solution.py:444
  10.1 2.0 %collective-permute-done.1.refs_1_ = f32[144,128]{1,0:T(8,128)S(1)} collective-permute-done((f32[144,128]{1,0:T(8,128)S(1)}, f32[144,128]{1,0:T(8,128)S(1)}, u32[]{:S(2)}, u32[]{:S(2)}) %collective-permute-start.1) | collective-permute-done | bytes 73760 | tf_op jit(solution)/shard_map/ppermute | solution.py:456
  12.8 3.0 %state_streams.1 = (bf16[2,1024,128]{2,1,0:T(8,128)(2,1)S(1)}, f32[17,1024]{1,0:T(8,128)S(1)}, f32[1040,128]{1,0:T(8,128)S(1)}, bf16[1024,3072]{1,0:T(8,128)(2,1)S(1)}) custom-call(f32[3,128,1024]{2,1,0:T(8,128)S(1)} %get-tuple-element.67.feat, f32[128,1024]{1,0:T(8,128)S(1)} %get-tuple-element.68.og, f32[3,3,1024]{2,1,0:T(4,128)S(1)} %get-tuple-element.69.filt, ...), custom_call_target="tpu_custom_call" | custom-call | flops 4294967296 | bytes 16777216 | tf_op jit(solution)/shard_map/state_streams/pallas_call | solution.py:324
  15.7 2.2 %collective-permute-start.3 = (bf16[1,2,1024,128]{3,2,1,0:T(8,128)(2,1)S(1)}, bf16[1,2,1024,128]{3,2,1,0:T(8,128)(2,1)S(1)}, u32[]{:S(2)}, u32[]{:S(2)}) collective-permute-start(bf16[1,2,1024,128]{3,2,1,0:T(8,128)(2,1)S(1)} %bitcast.12), channel_id=1, source_target_pairs={{0,2},{2,4},{4,6},{6,7},{7,5},{5,3},{3,1},{1,0},{8,10},{10,12},{12... | collective-permute-start | bytes 1572872 | tf_op jit(solution)/shard_map/ppermute | solution.py:444
  19.2 1.6 %collective-permute-start.10 = (bf16[1,1,1024,128]{3,2,1,0:T(8,128)(2,1)}, bf16[1,1,1024,128]{3,2,1,0:T(8,128)(2,1)}, u32[]{:S(2)}, u32[]{:S(2)}) collective-permute-start(bf16[1,1,1024,128]{3,2,1,0:T(8,128)(2,1)} %collective-permute-done.5.refs_0_), channel_id=1, source_target_pairs={{0,2},{2,4},{4,6},{6,7},{7,5},{5,3},{3,1},{1,0},{8,10},{10,12},{12... | collective-permute-start | bytes 786440 | tf_op jit(solution)/shard_map/ppermute | solution.py:444
  21.2 3.9 %add_product.9 = (f32[1024,128]{1,0:T(8,128)S(1)}, bf16[1024,2048]{1,0:T(8,128)(2,1)S(1)}) custom-call(bf16[3,1024,8192]{2,1,0:T(8,128)(2,1)} %w_proj.17, bf16[1024,3072]{1,0:T(8,128)(2,1)S(1)} %get-tuple-element.77.w, bf16[1,1,1024,128]{3,2,1,0:T(8,128)(2,1)S(1)} %bitcast.17, bf16[1,2,1024,128]{3,2,1,0:T(8,128)(2,1)S(1)} %bitcast.14), custom_call_target="tpu_custom_call" | custom-call | flops 68719476736 | bytes 268435456 | tf_op jit(solution)/shard_map/add_product/pallas_call | solution.py:404
  25.1 4.0 %add_product.10 = (f32[1024,128]{1,0:T(8,128)S(1)}, bf16[1024,3072]{1,0:T(8,128)(2,1)S(1)}) custom-call(bf16[3,1024,8192]{2,1,0:T(8,128)(2,1)} %w_proj.17, bf16[1024,2048]{1,0:T(8,128)(2,1)S(1)} %get-tuple-element.81.w, bf16[1,1,1024,128]{3,2,1,0:T(8,128)(2,1)} %collective-permute-done.5.refs_0_, bf16[1,1,1024,128]{3,2,1,0:T(8,128)(2,1)} %collective-permute-done.6.refs_1_, ...), custom_call_target="tpu_custom_call" | custom-call | flops 68719476736 | bytes 268435456 | tf_op jit(solution)/shard_map/add_product/pallas_call | solution.py:404
  29.1 1.5 %collective-permute-done.3.refs_0_ = bf16[1,2,1024,128]{3,2,1,0:T(8,128)(2,1)S(1)} collective-permute-done((bf16[1,2,1024,128]{3,2,1,0:T(8,128)(2,1)S(1)}, bf16[1,2,1024,128]{3,2,1,0:T(8,128)(2,1)S(1)}, u32[]{:S(2)}, u32[]{:S(2)}) %collective-permute-start.3) | collective-permute-done | bytes 524320 | tf_op jit(solution)/shard_map/ppermute | solution.py:444
  30.6 2.1 %collective-permute-done.4.refs_1_.refs_0_ = bf16[1,2,1024,128]{3,2,1,0:T(8,128)(2,1)S(1)} collective-permute-done((bf16[1,2,1024,128]{3,2,1,0:T(8,128)(2,1)S(1)}, bf16[1,2,1024,128]{3,2,1,0:T(8,128)(2,1)S(1)}, u32[]{:S(2)}, u32[]{:S(2)}) %collective-permute-start.4) | collective-permute-done | bytes 524320 | tf_op jit(solution)/shard_map/ppermute | solution.py:447
  32.8 1.6 %collective-permute-start.8 = (bf16[1,2,1024,128]{3,2,1,0:T(8,128)(2,1)S(1)}, bf16[1,2,1024,128]{3,2,1,0:T(8,128)(2,1)S(1)}, u32[]{:S(2)}, u32[]{:S(2)}) collective-permute-start(bf16[1,2,1024,128]{3,2,1,0:T(8,128)(2,1)S(1)} %collective-permute-done.3.refs_0_), channel_id=1, source_target_pairs={{0,2},{2,4},{4,6},{6,7},{7,5},{5,3},{3,1},{1,0},{8,10},{10,12},{12... | collective-permute-start | bytes 1572872 | tf_op jit(solution)/shard_map/ppermute | solution.py:444
  34.8 4.4 %add_product.11 = (f32[1024,128]{1,0:T(8,128)S(1)}, bf16[1024,3072]{1,0:T(8,128)(2,1)S(1)}) custom-call(bf16[3,1024,8192]{2,1,0:T(8,128)(2,1)} %w_proj.17, bf16[1024,3072]{1,0:T(8,128)(2,1)S(1)} %get-tuple-element.89.w, bf16[1,2,1024,128]{3,2,1,0:T(8,128)(2,1)S(1)} %collective-permute-done.3.refs_0_, ...), custom_call_target="tpu_custom_call" | custom-call | flops 65536 | bytes 256 | tf_op jit(solution)/shard_map/add_product/pallas_call | solution.py:404
  39.3 1.6 %collective-permute-start.13 = (bf16[1,1,1024,128]{3,2,1,0:T(8,128)(2,1)}, bf16[1,1,1024,128]{3,2,1,0:T(8,128)(2,1)S(1)}, u32[]{:S(2)}, u32[]{:S(2)}) collective-permute-start(bf16[1,1,1024,128]{3,2,1,0:T(8,128)(2,1)} %collective-permute-done.10.refs_1_), channel_id=1, source_target_pairs={{0,2},{2,4},{4,6},{6,7},{7,5},{5,3},{3,1},{1,0},{8,10},{10,12},{12... | collective-permute-start | bytes 786440 | tf_op jit(solution)/shard_map/ppermute | solution.py:444
  41.4 4.5 %add_product.12 = (f32[1024,128]{1,0:T(8,128)S(1)}, bf16[1024,3072]{1,0:T(8,128)(2,1)S(1)}) custom-call(bf16[3,1024,8192]{2,1,0:T(8,128)(2,1)} %w_proj.17, bf16[1024,3072]{1,0:T(8,128)(2,1)S(1)} %get-tuple-element.91.w, bf16[1,2,1024,128]{3,2,1,0:T(8,128)(2,1)S(1)} %collective-permute-done.4.refs_1_.refs_0_, ...), custom_call_target="tpu_custom_call" | custom-call | flops 68719476736 | bytes 268435456 | tf_op jit(solution)/shard_map/add_product/pallas_call | solution.py:404
  45.9 1.9 %gradients.1 = f32[3,128,1024]{2,1,0:T(8,128)} custom-call(f32[3,128,1024]{2,1,0:T(8,128)S(1)} %copy-done, f32[128,1024]{1,0:T(8,128)S(1)} %copy-done.1, f32[128,1024]{1,0:T(8,128)S(1)} %copy-done.2, f32[3,3,1024]{2,1,0:T(4,128)S(1)} %copy-done.5, f32[1,1024]{1,0:T(1,128)S(1)} %bitcast.10, f32[224,128]{1,0:T(8,128)S(1)} %copy-done.4, ...), custom_call_target="tpu_custom_call" | custom-call | flops 3932160 | bytes 5242880 | tf_op jit(solution)/shard_map/gradients/pallas_call | solution.py:215
  47.8 1.8 %collective-permute-done.9.refs_1_.refs_0_ = bf16[1,2,1024,128]{3,2,1,0:T(8,128)(2,1)S(1)} collective-permute-done((bf16[1,2,1024,128]{3,2,1,0:T(8,128)(2,1)S(1)}, bf16[1,2,1024,128]{3,2,1,0:T(8,128)(2,1)S(1)}, u32[]{:S(2)}, u32[]{:S(2)}) %collective-permute-start.9) | collective-permute-done | bytes 524320 | tf_op jit(solution)/shard_map/ppermute | solution.py:447
  49.7 1.6 %collective-permute-start.15 = (bf16[1,1,1024,128]{3,2,1,0:T(8,128)(2,1)S(1)}, bf16[1,1,1024,128]{3,2,1,0:T(8,128)(2,1)S(1)}, u32[]{:S(2)}, u32[]{:S(2)}) collective-permute-start(bf16[1,1,1024,128]{3,2,1,0:T(8,128)(2,1)S(1)} %get-tuple-element.133), channel_id=1, source_target_pairs={{0,2},{2,4},{4,6},{6,7},{7,5},{5,3},{3,1},{1,0},{8,10},{10,12},{12... | collective-permute-start | bytes 786440 | tf_op jit(solution)/shard_map/ppermute | solution.py:444
  51.8 1.6 %collective-permute-start.17 = (bf16[1,1,1024,128]{3,2,1,0:T(8,128)(2,1)S(1)}, bf16[1,1,1024,128]{3,2,1,0:T(8,128)(2,1)S(1)}, u32[]{:S(2)}, u32[]{:S(2)}) collective-permute-start(bf16[1,1,1024,128]{3,2,1,0:T(8,128)(2,1)S(1)} %get-tuple-element.132), channel_id=1, source_target_pairs={{0,2},{2,4},{4,6},{6,7},{7,5},{5,3},{3,1},{1,0},{8,10},{10,12},{12... | collective-permute-start | bytes 786440 | tf_op jit(solution)/shard_map/ppermute | solution.py:444
  53.4 4.4 %add_product.13 = (f32[1024,128]{1,0:T(8,128)S(1)}, bf16[1024,3072]{1,0:T(8,128)(2,1)S(1)}) custom-call(bf16[3,1024,8192]{2,1,0:T(8,128)(2,1)} %w_proj.17, bf16[1024,3072]{1,0:T(8,128)(2,1)S(1)} %get-tuple-element.102.w, bf16[1,2,1024,128]{3,2,1,0:T(8,128)(2,1)S(1)} %collective-permute-done.8.refs_0_, ...), custom_call_target="tpu_custom_call" | custom-call | flops 65536 | bytes 256 | tf_op jit(solution)/shard_map/add_product/pallas_call | solution.py:404
  58.3 5.2 %add_product.14 = (f32[1024,128]{1,0:T(8,128)S(1)}, bf16[1024,4096]{1,0:T(8,128)(2,1)S(1)}) custom-call(bf16[3,1024,8192]{2,1,0:T(8,128)(2,1)} %w_proj.17, bf16[1024,3072]{1,0:T(8,128)(2,1)S(1)} %get-tuple-element.106.w, bf16[1,2,1024,128]{3,2,1,0:T(8,128)(2,1)S(1)} %collective-permute-done.9.refs_1_.refs_0_, ...), custom_call_target="tpu_custom_call" | custom-call | flops 65536 | bytes 256 | tf_op jit(solution)/shard_map/add_product/pallas_call | solution.py:404
  63.5 1.6 %collective-permute-start.21 = (bf16[1,1,1024,128]{3,2,1,0:T(8,128)(2,1)S(1)}, bf16[1,1,1024,128]{3,2,1,0:T(8,128)(2,1)S(1)}, u32[]{:S(2)}, u32[]{:S(2)}) collective-permute-start(bf16[1,1,1024,128]{3,2,1,0:T(8,128)(2,1)S(1)} %collective-permute-done.15.refs_0_), channel_id=1, source_target_pairs={{0,2},{2,4},{4,6},{6,7},{7,5},{5,3},{3,1},{1,0},{8,10},{10,12},{12... | collective-permute-start | bytes 786440 | tf_op jit(solution)/shard_map/ppermute | solution.py:444
  65.6 1.6 %collective-permute-start.19 = (bf16[1,1,512,128]{3,2,1,0:T(8,128)(2,1)S(1)}, bf16[1,1,512,128]{3,2,1,0:T(8,128)(2,1)S(1)}, u32[]{:S(2)}, u32[]{:S(2)}) collective-permute-start(bf16[1,1,512,128]{3,2,1,0:T(8,128)(2,1)S(1)} %slice.28), channel_id=1, source_target_pairs={{0,2},{2,4},{4,6},{6,7},{7,5},{5,3},{3,1},{1,0},{8,10},{10,12},{12... | collective-permute-start | bytes 393224 | tf_op jit(solution)/shard_map/ppermute | solution.py:444
  67.7 5.1 %add_product.15 = (f32[1024,128]{1,0:T(8,128)S(1)}, bf16[1024,3072]{1,0:T(8,128)(2,1)S(1)}) custom-call(bf16[3,1024,8192]{2,1,0:T(8,128)(2,1)} %w_proj.17, bf16[1024,4096]{1,0:T(8,128)(2,1)S(1)} %get-tuple-element.111.w, bf16[1,1,1024,128]{3,2,1,0:T(8,128)(2,1)S(1)} %collective-permute-done.15.refs_0_, ...), custom_call_target="tpu_custom_call" | custom-call | flops 65536 | bytes 256 | tf_op jit(solution)/shard_map/add_product/pallas_call | solution.py:404
  75.4 1.6 %add_product.17 = f32[128,1024]{1,0:T(8,128)} custom-call(bf16[3,1024,8192]{2,1,0:T(8,128)(2,1)} %w_proj.17, bf16[1024,3072]{1,0:T(8,128)(2,1)S(1)} %get-tuple-element.118.w, bf16[1,1,512,128]{3,2,1,0:T(8,128)(2,1)S(1)} %collective-permute-done.19.refs_0_, bf16[1,1,512,128]{3,2,1,0:T(8,128)(2,1)S(1)} %collective-permute-done.20.refs_1_, ...), custom_call_target="tpu_custom_call" | custom-call | flops 65536 | bytes 256 | tf_op jit(solution)/shard_map/add_product/pallas_call | solution.py:404
  (58 shorter events, 12.2 us)
Async XLA Ops:
  2.8 3.9 %collective-permute-start = (f32[224,128]{1,0:T(8,128)S(1)}, f32[224,128]{1,0:T(8,128)S(1)}, u32[]{:S(2)}, u32[]{:S(2)}) collective-permute-start(f32[224,128]{1,0:T(8,128)S(1)} %get-tuple-element.72), channel_id=1, source_target_pairs={{8,0},{16,8},{24,16},{9,1},{17,9},{25,17},{10,2},{18,10},{26,18},{... | collective-permute-start | bytes 344072 | tf_op jit(solution)/shard_map/ppermute | solution.py:456
  4.1 8.0 %collective-permute-start.1 = (f32[144,128]{1,0:T(8,128)S(1)}, f32[144,128]{1,0:T(8,128)S(1)}, u32[]{:S(2)}, u32[]{:S(2)}) collective-permute-start(f32[144,128]{1,0:T(8,128)S(1)} %get-tuple-element.75), channel_id=1, source_target_pairs={{16,0},{24,8},{17,1},{25,9},{18,2},{26,10},{19,3},{27,11},{20,4},{... | collective-permute-start | bytes 221192 | tf_op jit(solution)/shard_map/ppermute | solution.py:456
  5.4 7.4 %collective-permute-start.2 = (f32[144,128]{1,0:T(8,128)S(1)}, f32[144,128]{1,0:T(8,128)S(1)}, u32[]{:S(2)}, u32[]{:S(2)}) collective-permute-start(f32[144,128]{1,0:T(8,128)S(1)} %get-tuple-element.75), channel_id=1, source_target_pairs={{24,0},{25,1},{26,2},{27,3},{28,4},{29,5},{30,6},{31,7}} | collective-permute-start | bytes 221192 | tf_op jit(solution)/shard_map/ppermute | solution.py:456
  6.7 6.1 %copy-start.3 = (f32[224,128]{1,0:T(8,128)}, f32[224,128]{1,0:T(8,128)S(1)}, u32[]{:S(2)}) copy-start(f32[224,128]{1,0:T(8,128)S(1)} %collective-permute-done.later.refs_0_) | copy-start | bytes 344068
  7.0 10.9 %collective-permute-start.5 = (bf16[1,1,1024,128]{3,2,1,0:T(8,128)(2,1)S(1)}, bf16[1,1,1024,128]{3,2,1,0:T(8,128)(2,1)}, u32[]{:S(2)}, u32[]{:S(2)}) collective-permute-start(bf16[1,1,1024,128]{3,2,1,0:T(8,128)(2,1)S(1)} %bitcast.15), channel_id=1, source_target_pairs={{0,2},{2,4},{4,6},{6,7},{7,5},{5,3},{3,1},{1,0},{8,10},{10,12},{12... | collective-permute-start | bytes 786440 | tf_op jit(solution)/shard_map/ppermute | solution.py:444
  10.1 8.5 %collective-permute-start.6 = (bf16[1,1,1024,128]{3,2,1,0:T(8,128)(2,1)S(1)}, bf16[1,1,1024,128]{3,2,1,0:T(8,128)(2,1)}, u32[]{:S(2)}, u32[]{:S(2)}) collective-permute-start(bf16[1,1,1024,128]{3,2,1,0:T(8,128)(2,1)S(1)} %bitcast.16), channel_id=1, source_target_pairs={{0,1},{2,0},{4,2},{6,4},{7,6},{5,7},{3,5},{1,3},{8,9},{10,8},{12,1... | collective-permute-start | bytes 786440 | tf_op jit(solution)/shard_map/ppermute | solution.py:447
  15.7 14.9 %collective-permute-start.3 = (bf16[1,2,1024,128]{3,2,1,0:T(8,128)(2,1)S(1)}, bf16[1,2,1024,128]{3,2,1,0:T(8,128)(2,1)S(1)}, u32[]{:S(2)}, u32[]{:S(2)}) collective-permute-start(bf16[1,2,1024,128]{3,2,1,0:T(8,128)(2,1)S(1)} %bitcast.12), channel_id=1, source_target_pairs={{0,2},{2,4},{4,6},{6,7},{7,5},{5,3},{3,1},{1,0},{8,10},{10,12},{12... | collective-permute-start | bytes 1572872 | tf_op jit(solution)/shard_map/ppermute | solution.py:444
  17.9 14.9 %collective-permute-start.4 = (bf16[1,2,1024,128]{3,2,1,0:T(8,128)(2,1)S(1)}, bf16[1,2,1024,128]{3,2,1,0:T(8,128)(2,1)S(1)}, u32[]{:S(2)}, u32[]{:S(2)}) collective-permute-start(bf16[1,2,1024,128]{3,2,1,0:T(8,128)(2,1)S(1)} %bitcast.13), channel_id=1, source_target_pairs={{0,1},{2,0},{4,2},{6,4},{7,6},{5,7},{3,5},{1,3},{8,9},{10,8},{12,1... | collective-permute-start | bytes 1572872 | tf_op jit(solution)/shard_map/ppermute | solution.py:447
  18.6 10.5 %collective-permute-start.7 = (f32[17,1024]{1,0:T(8,128)S(1)}, f32[17,1024]{1,0:T(8,128)S(1)}, u32[]{:S(2)}, u32[]{:S(2)}) collective-permute-start(f32[17,1024]{1,0:T(8,128)S(1)} %get-tuple-element.86), channel_id=1, source_target_pairs={{0,8},{8,0},{16,24},{24,16},{1,9},{9,1},{17,25},{25,17},{2,10},{10... | collective-permute-start | bytes 208904 | tf_op jit(solution)/shard_map/ppermute | solution.py:459
  19.2 20.0 %collective-permute-start.10 = (bf16[1,1,1024,128]{3,2,1,0:T(8,128)(2,1)}, bf16[1,1,1024,128]{3,2,1,0:T(8,128)(2,1)}, u32[]{:S(2)}, u32[]{:S(2)}) collective-permute-start(bf16[1,1,1024,128]{3,2,1,0:T(8,128)(2,1)} %collective-permute-done.5.refs_0_), channel_id=1, source_target_pairs={{0,2},{2,4},{4,6},{6,7},{7,5},{5,3},{3,1},{1,0},{8,10},{10,12},{12... | collective-permute-start | bytes 786440 | tf_op jit(solution)/shard_map/ppermute | solution.py:444
  20.8 18.4 %collective-permute-start.11 = (bf16[1,1,1024,128]{3,2,1,0:T(8,128)(2,1)}, bf16[1,1,1024,128]{3,2,1,0:T(8,128)(2,1)}, u32[]{:S(2)}, u32[]{:S(2)}) collective-permute-start(bf16[1,1,1024,128]{3,2,1,0:T(8,128)(2,1)} %collective-permute-done.6.refs_1_), channel_id=1, source_target_pairs={{0,1},{2,0},{4,2},{6,4},{7,6},{5,7},{3,5},{1,3},{8,9},{10,8},{12,1... | collective-permute-start | bytes 786440 | tf_op jit(solution)/shard_map/ppermute | solution.py:447
  32.8 15.1 %collective-permute-start.8 = (bf16[1,2,1024,128]{3,2,1,0:T(8,128)(2,1)S(1)}, bf16[1,2,1024,128]{3,2,1,0:T(8,128)(2,1)S(1)}, u32[]{:S(2)}, u32[]{:S(2)}) collective-permute-start(bf16[1,2,1024,128]{3,2,1,0:T(8,128)(2,1)S(1)} %collective-permute-done.3.refs_0_), channel_id=1, source_target_pairs={{0,2},{2,4},{4,6},{6,7},{7,5},{5,3},{3,1},{1,0},{8,10},{10,12},{12... | collective-permute-start | bytes 1572872 | tf_op jit(solution)/shard_map/ppermute | solution.py:444
  34.4 15.3 %collective-permute-start.9 = (bf16[1,2,1024,128]{3,2,1,0:T(8,128)(2,1)S(1)}, bf16[1,2,1024,128]{3,2,1,0:T(8,128)(2,1)S(1)}, u32[]{:S(2)}, u32[]{:S(2)}) collective-permute-start(bf16[1,2,1024,128]{3,2,1,0:T(8,128)(2,1)S(1)} %collective-permute-done.4.refs_1_.refs_0_), channel_id=1, source_target_pairs={{0,1},{2,0},{4,2},{6,4},{7,6},{5,7},{3,5},{1,3},{8,9},{10,8},{12,1... | collective-permute-start | bytes 1572872 | tf_op jit(solution)/shard_map/ppermute | solution.py:447
  39.2 8.6 %collective-permute-start.12 = (f32[17,1024]{1,0:T(8,128)S(1)}, f32[17,1024]{1,0:T(8,128)S(1)}, u32[]{:S(2)}, u32[]{:S(2)}) collective-permute-start(f32[17,1024]{1,0:T(8,128)S(1)} %add.6), channel_id=1, source_target_pairs={{0,16},{8,24},{16,0},{24,8},{1,17},{9,25},{17,1},{25,9},{2,18},{10... | collective-permute-start | bytes 208904 | tf_op jit(solution)/shard_map/ppermute | solution.py:459
  39.3 18.5 %collective-permute-start.13 = (bf16[1,1,1024,128]{3,2,1,0:T(8,128)(2,1)}, bf16[1,1,1024,128]{3,2,1,0:T(8,128)(2,1)S(1)}, u32[]{:S(2)}, u32[]{:S(2)}) collective-permute-start(bf16[1,1,1024,128]{3,2,1,0:T(8,128)(2,1)} %collective-permute-done.10.refs_1_), channel_id=1, source_target_pairs={{0,2},{2,4},{4,6},{6,7},{7,5},{5,3},{3,1},{1,0},{8,10},{10,12},{12... | collective-permute-start | bytes 786440 | tf_op jit(solution)/shard_map/ppermute | solution.py:444
  40.9 17.4 %collective-permute-start.14 = (bf16[1,1,1024,128]{3,2,1,0:T(8,128)(2,1)}, bf16[1,1,1024,128]{3,2,1,0:T(8,128)(2,1)S(1)}, u32[]{:S(2)}, u32[]{:S(2)}) collective-permute-start(bf16[1,1,1024,128]{3,2,1,0:T(8,128)(2,1)} %collective-permute-done.11.refs_2_), channel_id=1, source_target_pairs={{0,1},{2,0},{4,2},{6,4},{7,6},{5,7},{3,5},{1,3},{8,9},{10,8},{12,1... | collective-permute-start | bytes 786440 | tf_op jit(solution)/shard_map/ppermute | solution.py:447
  49.7 13.8 %collective-permute-start.15 = (bf16[1,1,1024,128]{3,2,1,0:T(8,128)(2,1)S(1)}, bf16[1,1,1024,128]{3,2,1,0:T(8,128)(2,1)S(1)}, u32[]{:S(2)}, u32[]{:S(2)}) collective-permute-start(bf16[1,1,1024,128]{3,2,1,0:T(8,128)(2,1)S(1)} %get-tuple-element.133), channel_id=1, source_target_pairs={{0,2},{2,4},{4,6},{6,7},{7,5},{5,3},{3,1},{1,0},{8,10},{10,12},{12... | collective-permute-start | bytes 786440 | tf_op jit(solution)/shard_map/ppermute | solution.py:444
  51.3 12.2 %collective-permute-start.16 = (bf16[1,1,1024,128]{3,2,1,0:T(8,128)(2,1)S(1)}, bf16[1,1,1024,128]{3,2,1,0:T(8,128)(2,1)S(1)}, u32[]{:S(2)}, u32[]{:S(2)}) collective-permute-start(bf16[1,1,1024,128]{3,2,1,0:T(8,128)(2,1)S(1)} %get-tuple-element.131), channel_id=1, source_target_pairs={{0,1},{2,0},{4,2},{6,4},{7,6},{5,7},{3,5},{1,3},{8,9},{10,8},{12,1... | collective-permute-start | bytes 786440 | tf_op jit(solution)/shard_map/ppermute | solution.py:447
  51.8 15.4 %collective-permute-start.17 = (bf16[1,1,1024,128]{3,2,1,0:T(8,128)(2,1)S(1)}, bf16[1,1,1024,128]{3,2,1,0:T(8,128)(2,1)S(1)}, u32[]{:S(2)}, u32[]{:S(2)}) collective-permute-start(bf16[1,1,1024,128]{3,2,1,0:T(8,128)(2,1)S(1)} %get-tuple-element.132), channel_id=1, source_target_pairs={{0,2},{2,4},{4,6},{6,7},{7,5},{5,3},{3,1},{1,0},{8,10},{10,12},{12... | collective-permute-start | bytes 786440 | tf_op jit(solution)/shard_map/ppermute | solution.py:444
  57.8 9.9 %collective-permute-start.18 = (bf16[1,1,1024,128]{3,2,1,0:T(8,128)(2,1)S(1)}, bf16[1,1,1024,128]{3,2,1,0:T(8,128)(2,1)S(1)}, u32[]{:S(2)}, u32[]{:S(2)}) collective-permute-start(bf16[1,1,1024,128]{3,2,1,0:T(8,128)(2,1)S(1)} %get-tuple-element.116), channel_id=1, source_target_pairs={{0,1},{2,0},{4,2},{6,4},{7,6},{5,7},{3,5},{1,3},{8,9},{10,8},{12,1... | collective-permute-start | bytes 786440 | tf_op jit(solution)/shard_map/ppermute | solution.py:447
  63.5 9.3 %collective-permute-start.21 = (bf16[1,1,1024,128]{3,2,1,0:T(8,128)(2,1)S(1)}, bf16[1,1,1024,128]{3,2,1,0:T(8,128)(2,1)S(1)}, u32[]{:S(2)}, u32[]{:S(2)}) collective-permute-start(bf16[1,1,1024,128]{3,2,1,0:T(8,128)(2,1)S(1)} %collective-permute-done.15.refs_0_), channel_id=1, source_target_pairs={{0,2},{2,4},{4,6},{6,7},{7,5},{5,3},{3,1},{1,0},{8,10},{10,12},{12... | collective-permute-start | bytes 786440 | tf_op jit(solution)/shard_map/ppermute | solution.py:444
  65.1 7.7 %collective-permute-start.22 = (bf16[1,1,1024,128]{3,2,1,0:T(8,128)(2,1)S(1)}, bf16[1,1,1024,128]{3,2,1,0:T(8,128)(2,1)S(1)}, u32[]{:S(2)}, u32[]{:S(2)}) collective-permute-start(bf16[1,1,1024,128]{3,2,1,0:T(8,128)(2,1)S(1)} %collective-permute-done.16.refs_1_), channel_id=1, source_target_pairs={{0,1},{2,0},{4,2},{6,4},{7,6},{5,7},{3,5},{1,3},{8,9},{10,8},{12,1... | collective-permute-start | bytes 786440 | tf_op jit(solution)/shard_map/ppermute | solution.py:447
  65.6 9.7 %collective-permute-start.19 = (bf16[1,1,512,128]{3,2,1,0:T(8,128)(2,1)S(1)}, bf16[1,1,512,128]{3,2,1,0:T(8,128)(2,1)S(1)}, u32[]{:S(2)}, u32[]{:S(2)}) collective-permute-start(bf16[1,1,512,128]{3,2,1,0:T(8,128)(2,1)S(1)} %slice.28), channel_id=1, source_target_pairs={{0,2},{2,4},{4,6},{6,7},{7,5},{5,3},{3,1},{1,0},{8,10},{10,12},{12... | collective-permute-start | bytes 393224 | tf_op jit(solution)/shard_map/ppermute | solution.py:444
  67.3 8.1 %collective-permute-start.20 = (bf16[1,1,512,128]{3,2,1,0:T(8,128)(2,1)S(1)}, bf16[1,1,512,128]{3,2,1,0:T(8,128)(2,1)S(1)}, u32[]{:S(2)}, u32[]{:S(2)}) collective-permute-start(bf16[1,1,512,128]{3,2,1,0:T(8,128)(2,1)S(1)} %slice.29), channel_id=1, source_target_pairs={{0,1},{2,0},{4,2},{6,4},{7,6},{5,7},{3,5},{1,3},{8,9},{10,8},{12,1... | collective-permute-start | bytes 393224 | tf_op jit(solution)/shard_map/ppermute | solution.py:447
  (6 other events, 27.1 us)

commit v10 on v8

--- a/solution.py
+++ b/solution.py
@@ -358,7 +358,7 @@
     x = jnp.concatenate([refs[n][h, p] for *_, parts in plan for n, h, p in parts], axis=0)
     columns = slice(base * (x.shape[0] // len(plan)), (base + len(plan)) * (x.shape[0] // len(plan)))
     features = w.shape[0]
-    wide = min(512, features)
+    wide = min(256, features)
     for d in range(0, features, wide):
         rows = slice(d, d + wide)
         y = jnp.dot(w[rows, columns], x, preferred_element_type=F32)
@@ -398,7 +398,7 @@
     if last:
         out_specs = [in_hbm()]
         out_shape = [jax.ShapeDtypeStruct((tokens, features), F32)]
-        scratch = [pltpu.VMEM((tokens, features), F32), pltpu.SemaphoreType.DMA((max(1, features // 512),))]
+        scratch = [pltpu.VMEM((tokens, features), F32), pltpu.SemaphoreType.DMA((max(1, features // 256),))]
     elif later:
         out_specs += [whole()]
         out_shape += [pltpu.VMEM((features, len(later) * channels), BF16)]
@@ -516,41 +516,41 @@
     b0 = stacked(rounds)
 
     b1, y1 = up(b0), down(b0)
-    a1, z1, b0 = lax.optimization_barrier((a1, z1, b0))
+    a1, z1, b0, sums = lax.optimization_barrier((a1, z1, b0, sums))
     a2, z2 = up(a1), down(z1)
+    distances = [1 << n for n in range((blocks - 1).bit_length())]
+    for by in distances[:1]:
+        sums = exchanged(sums, by)
     total, ready = times(0, None, ready, a0=a0, b0=b0)
     total, ready = times(1, total, ready, a1=a1, z1=z1)
-    grads = gradients(feat, saved_conv, og, filt, bias_row, payloads[0], after(gp, total))
-
-    b1, y1, total, grads = lax.optimization_barrier((b1, y1, total, grads))
+    b1, y1, total, sums = lax.optimization_barrier((b1, y1, total, sums))
     b2, y2 = up(b1), down(y1)
     total, ready = times(2, total, ready, b1=b1, y1=y1)
 
     a2, z2, total, sums = lax.optimization_barrier((a2, z2, total, sums))
     a3, z3 = up(a2), down(z2)
-    distances = [1 << n for n in range((blocks - 1).bit_length())]
-    for by in distances[:-1]:
+    for by in distances[1:]:
         sums = exchanged(sums, by)
     total, ready = times(3, total, ready, y1=y1, a2=a2, z2=z2)
-
-    b2, y2, total, sums = lax.optimization_barrier((b2, y2, total, sums))
+    grads = gradients(features, saved_conv, out_grad, short_filter, bias[None], payloads[0], after(gp, total))
+
+    b2, y2, total, sums, grads = lax.optimization_barrier((b2, y2, total, sums, grads))
     b3, y3 = up(b2), down(y2)
     total, ready = times(4, total, ready, b2=b2, y2=y2)
 
-    a3, z3, total, sums = lax.optimization_barrier((a3, z3, total, sums))
-    for by in distances[-1:]:
-        sums = exchanged(sums, by)
-    sums = sums * (tokens * blocks) ** (-0.5)
+    a3, z3, total = lax.optimization_barrier((a3, z3, total))
     a4 = up(a3[:, :, :half]), down(z3[:, :, half:])
     total, ready = times(5, total, ready, y2=y2, a3=a3, z3=z3)
 
-    grad_residue, grad_bias = sums[:modes].T, sums[modes]
-    b3, y3, total, grad_residue, grad_bias = lax.optimization_barrier((b3, y3, total, grad_residue, grad_bias))
+    b3, y3, total, sums = lax.optimization_barrier((b3, y3, total, sums))
     b4, y4 = up(b3[:, :1]), down(y3[:, 1:])
     total, ready = times(6, total, ready, b3=b3, y3=y3)
 
-    a4, total = lax.optimization_barrier((a4, total))
+    a4, total, sums = lax.optimization_barrier((a4, total, sums))
     (total,) = times(7, total, ready, a4=a4)
+    sums = sums * (tokens * blocks) ** (-0.5)
+    grad_residue, grad_bias = sums[:modes].T, sums[modes]
+    b4, total, grad_residue, grad_bias = lax.optimization_barrier((b4, total, grad_residue, grad_bias))
     (total,) = times(8, total, ready, b4=b4)
     (grad_x,) = times(9, total, ready, y4=y4)
     return (grads, grad_x, grad_residue, grad_bias)

time: 76.3 us -> 77.9 us (1.021)
  Pallas kernels: 40.2 us -> 44.5 us
  waiting for transfers between devices: 11.6 us -> 8.41 us
    pallas_call x10, Pallas kernels: 32.9 us -> 37.2 us  [add_product(): pl.pallas_call(functools.partial(product_kernel, plan, base, later, first...]
    ppermute x8, waiting for transfers between devices: 8.61 us -> 4.62 us  [down(): return lax.ppermute(x, 'chan', pairs[-1])]
    ppermute x8, waiting for transfers between devices: 0.26 us -> 1.13 us  [up(): return lax.ppermute(x, 'chan', pairs[1])]
  transfers between devices with their start and end apart: 21 -> 21, of which waited for: 8 -> 8; matrix products, arithmetic and copies ran while one was open for 2% -> 2% of each run, Pallas kernels for 48% -> 53%
where the time goes in v10:
time: 77.9 us; the launch traced here: 77.7 us
  Pallas kernels  44.5 us (57%)
  starting transfers between devices  22.3 us (29%)
  waiting for transfers between devices  8.41 us (11%)
  local copies, waits for them, and re-layouts  1.32 us (2%)
  between operations  1.13 us (1%)
    pallas_call x10, Pallas kernels, add_product(): pl.pallas_call(functools.partial(product_kernel, plan, base, later, first...  37.2 us
    ppermute x8, starting transfers between devices, up(): return lax.ppermute(x, 'chan', pairs[1])  15.1 us
    ppermute x8, waiting for transfers between devices, down(): return lax.ppermute(x, 'chan', pairs[-1])  4.62 us
    ppermute x3, starting transfers between devices, from_later(): return lax.ppermute(array, 'ctx', [(i, i - by) for i in range(by, blocks)])  3.88 us
    pallas_call x1, Pallas kernels, state_streams(): pl.pallas_call(functools.partial(state_kernel, spans, plan, ring), in_spe...  2.95 us
    ppermute x3, waiting for transfers between devices, from_later(): return lax.ppermute(array, 'ctx', [(i, i - by) for i in range(by, blocks)])  2.65 us
    ppermute x8, starting transfers between devices, down(): return lax.ppermute(x, 'chan', pairs[-1])  2.6 us
    pallas_call x1, Pallas kernels, front(): pl.pallas_call(front_kernel, in_specs=[in_hbm()] * 7, out_specs=[whole()]...  2.11 us
  transfers between devices with their start and end apart: 21, of which 8 were waited for; matrix products, arithmetic and copies ran while one was open for 2% of the time, Pallas kernels for 53%

profile of v10, /device:TPU:0, one launch (start us, length us, event | category | flops | bytes accessed | tf_op | source)
XLA Modules:
  0.0 77.7 jit_solution(17737302695299610319)
XLA Ops:
  0.6 2.1 %front.1 = (f32[3,128,1024]{2,1,0:T(8,128)S(1)}, f32[128,1024]{1,0:T(8,128)S(1)}, f32[128,1024]{1,0:T(8,128)S(1)}, f32[3,3,1024]{2,1,0:T(4,128)S(1)}, f32[1,1024...) custom-call(f32[3,128,1024]{2,1,0:T(8,128)} %feat.1, ...), custom_call_target="tpu_custom_call" | custom-call | flops 8388608 | bytes 2621440 | tf_op jit(solution)/shard_map/front/pallas_call | solution.py:96
  2.8 1.3 %collective-permute-start = (f32[224,128]{1,0:T(8,128)S(1)}, f32[224,128]{1,0:T(8,128)S(1)}, u32[]{:S(2)}, u32[]{:S(2)}) collective-permute-start(f32[224,128]{1,0:T(8,128)S(1)} %get-tuple-element.70), channel_id=1, source_target_pairs={{8,0},{16,8},{24,16},{9,1},{17,9},{25,17},{10,2},{18,10},{26,18},{... | collective-permute-start | bytes 344072 | tf_op jit(solution)/shard_map/ppermute | solution.py:458
  4.1 1.3 %collective-permute-start.1 = (f32[144,128]{1,0:T(8,128)S(1)}, f32[144,128]{1,0:T(8,128)S(1)}, u32[]{:S(2)}, u32[]{:S(2)}) collective-permute-start(f32[144,128]{1,0:T(8,128)S(1)} %get-tuple-element.73), channel_id=1, source_target_pairs={{16,0},{24,8},{17,1},{25,9},{18,2},{26,10},{19,3},{27,11},{20,4},{... | collective-permute-start | bytes 221192 | tf_op jit(solution)/shard_map/ppermute | solution.py:458
  7.0 3.1 %collective-permute-start.5 = (bf16[1,1,1024,128]{3,2,1,0:T(8,128)(2,1)S(1)}, bf16[1,1,1024,128]{3,2,1,0:T(8,128)(2,1)}, u32[]{:S(2)}, u32[]{:S(2)}) collective-permute-start(bf16[1,1,1024,128]{3,2,1,0:T(8,128)(2,1)S(1)} %bitcast.15), channel_id=1, source_target_pairs={{0,2},{2,4},{4,6},{6,7},{7,5},{5,3},{3,1},{1,0},{8,10},{10,12},{12... | collective-permute-start | bytes 786440 | tf_op jit(solution)/shard_map/ppermute | solution.py:446
  10.1 2.0 %collective-permute-done.1.refs_1_ = f32[144,128]{1,0:T(8,128)S(1)} collective-permute-done((f32[144,128]{1,0:T(8,128)S(1)}, f32[144,128]{1,0:T(8,128)S(1)}, u32[]{:S(2)}, u32[]{:S(2)}) %collective-permute-start.1) | collective-permute-done | bytes 73760 | tf_op jit(solution)/shard_map/ppermute | solution.py:458
  12.8 3.0 %state_streams.1 = (bf16[2,1024,128]{2,1,0:T(8,128)(2,1)S(1)}, f32[17,1024]{1,0:T(8,128)S(1)}, f32[1040,128]{1,0:T(8,128)S(1)}, bf16[1024,3072]{1,0:T(8,128)(2,1)S(1)}) custom-call(f32[3,128,1024]{2,1,0:T(8,128)S(1)} %get-tuple-element.65.feat, f32[128,1024]{1,0:T(8,128)S(1)} %get-tuple-element.66.og, f32[3,3,1024]{2,1,0:T(4,128)S(1)} %get-tuple-element.67.filt, ...), custom_call_target="tpu_custom_call" | custom-call | flops 4294967296 | bytes 16777216 | tf_op jit(solution)/shard_map/state_streams/pallas_call | solution.py:326
  15.7 2.2 %collective-permute-start.3 = (bf16[1,2,1024,128]{3,2,1,0:T(8,128)(2,1)S(1)}, bf16[1,2,1024,128]{3,2,1,0:T(8,128)(2,1)S(1)}, u32[]{:S(2)}, u32[]{:S(2)}) collective-permute-start(bf16[1,2,1024,128]{3,2,1,0:T(8,128)(2,1)S(1)} %bitcast.12), channel_id=1, source_target_pairs={{0,2},{2,4},{4,6},{6,7},{7,5},{5,3},{3,1},{1,0},{8,10},{10,12},{12... | collective-permute-start | bytes 1572872 | tf_op jit(solution)/shard_map/ppermute | solution.py:446
  19.2 1.6 %collective-permute-start.10 = (bf16[1,1,1024,128]{3,2,1,0:T(8,128)(2,1)}, bf16[1,1,1024,128]{3,2,1,0:T(8,128)(2,1)}, u32[]{:S(2)}, u32[]{:S(2)}) collective-permute-start(bf16[1,1,1024,128]{3,2,1,0:T(8,128)(2,1)} %collective-permute-done.5.refs_0_), channel_id=1, source_target_pairs={{0,2},{2,4},{4,6},{6,7},{7,5},{5,3},{3,1},{1,0},{8,10},{10,12},{12... | collective-permute-start | bytes 786440 | tf_op jit(solution)/shard_map/ppermute | solution.py:446
  21.2 4.0 %add_product.10 = (f32[1024,128]{1,0:T(8,128)S(1)}, bf16[1024,2048]{1,0:T(8,128)(2,1)S(1)}) custom-call(bf16[3,1024,8192]{2,1,0:T(8,128)(2,1)} %w_proj.19, bf16[1024,3072]{1,0:T(8,128)(2,1)S(1)} %get-tuple-element.75.w, bf16[1,1,1024,128]{3,2,1,0:T(8,128)(2,1)S(1)} %bitcast.17, bf16[1,2,1024,128]{3,2,1,0:T(8,128)(2,1)S(1)} %bitcast.14), custom_call_target="tpu_custom_call" | custom-call | flops 68719476736 | bytes 268435456 | tf_op jit(solution)/shard_map/add_product/pallas_call | solution.py:406
  25.2 5.1 %add_product.11 = (f32[1024,128]{1,0:T(8,128)S(1)}, bf16[1024,3072]{1,0:T(8,128)(2,1)S(1)}) custom-call(bf16[3,1024,8192]{2,1,0:T(8,128)(2,1)} %w_proj.19, bf16[1024,2048]{1,0:T(8,128)(2,1)S(1)} %get-tuple-element.79.w, bf16[1,1,1024,128]{3,2,1,0:T(8,128)(2,1)} %collective-permute-done.5.refs_0_, bf16[1,1,1024,128]{3,2,1,0:T(8,128)(2,1)} %collective-permute-done.6.refs_1_, ...), custom_call_target="tpu_custom_call" | custom-call | flops 68719476736 | bytes 268435456 | tf_op jit(solution)/shard_map/add_product/pallas_call | solution.py:406
  30.6 2.1 %collective-permute-done.4.refs_1_.refs_0_ = bf16[1,2,1024,128]{3,2,1,0:T(8,128)(2,1)S(1)} collective-permute-done((bf16[1,2,1024,128]{3,2,1,0:T(8,128)(2,1)S(1)}, bf16[1,2,1024,128]{3,2,1,0:T(8,128)(2,1)S(1)}, u32[]{:S(2)}, u32[]{:S(2)}) %collective-permute-start.4) | collective-permute-done | bytes 524320 | tf_op jit(solution)/shard_map/ppermute | solution.py:449
  32.8 1.6 %collective-permute-start.8 = (bf16[1,2,1024,128]{3,2,1,0:T(8,128)(2,1)S(1)}, bf16[1,2,1024,128]{3,2,1,0:T(8,128)(2,1)S(1)}, u32[]{:S(2)}, u32[]{:S(2)}) collective-permute-start(bf16[1,2,1024,128]{3,2,1,0:T(8,128)(2,1)S(1)} %collective-permute-done.3.refs_0_), channel_id=1, source_target_pairs={{0,2},{2,4},{4,6},{6,7},{7,5},{5,3},{3,1},{1,0},{8,10},{10,12},{12... | collective-permute-start | bytes 1572872 | tf_op jit(solution)/shard_map/ppermute | solution.py:446
  34.8 4.6 %add_product.12 = (f32[1024,128]{1,0:T(8,128)S(1)}, bf16[1024,3072]{1,0:T(8,128)(2,1)S(1)}) custom-call(bf16[3,1024,8192]{2,1,0:T(8,128)(2,1)} %w_proj.19, bf16[1024,3072]{1,0:T(8,128)(2,1)S(1)} %get-tuple-element.87.w, bf16[1,2,1024,128]{3,2,1,0:T(8,128)(2,1)S(1)} %collective-permute-done.3.refs_0_, ...), custom_call_target="tpu_custom_call" | custom-call | flops 65536 | bytes 256 | tf_op jit(solution)/shard_map/add_product/pallas_call | solution.py:406
  39.5 1.6 %collective-permute-start.13 = (bf16[1,1,1024,128]{3,2,1,0:T(8,128)(2,1)}, bf16[1,1,1024,128]{3,2,1,0:T(8,128)(2,1)S(1)}, u32[]{:S(2)}, u32[]{:S(2)}) collective-permute-start(bf16[1,1,1024,128]{3,2,1,0:T(8,128)(2,1)} %collective-permute-done.10.refs_1_), channel_id=1, source_target_pairs={{0,2},{2,4},{4,6},{6,7},{7,5},{5,3},{3,1},{1,0},{8,10},{10,12},{12... | collective-permute-start | bytes 786440 | tf_op jit(solution)/shard_map/ppermute | solution.py:446
  41.6 5.8 %add_product.13 = (f32[1024,128]{1,0:T(8,128)S(1)}, bf16[1024,3072]{1,0:T(8,128)(2,1)S(1)}) custom-call(bf16[3,1024,8192]{2,1,0:T(8,128)(2,1)} %w_proj.19, bf16[1024,3072]{1,0:T(8,128)(2,1)S(1)} %get-tuple-element.89.w, bf16[1,2,1024,128]{3,2,1,0:T(8,128)(2,1)S(1)} %collective-permute-done.4.refs_1_.refs_0_, ...), custom_call_target="tpu_custom_call" | custom-call | flops 68719476736 | bytes 268435456 | tf_op jit(solution)/shard_map/add_product/pallas_call | solution.py:406
  47.5 1.9 %gradients.1 = f32[3,128,1024]{2,1,0:T(8,128)} custom-call(f32[3,128,1024]{2,1,0:T(8,128)S(1)} %copy-done, f32[128,1024]{1,0:T(8,128)S(1)} %copy-done.1, f32[128,1024]{1,0:T(8,128)S(1)} %copy-done.2, f32[3,3,1024]{2,1,0:T(4,128)S(1)} %copy-done.5, f32[1,1024]{1,0:T(1,128)S(1)} %bitcast.10, f32[224,128]{1,0:T(8,128)S(1)} %copy-done.4, ...), custom_call_target="tpu_custom_call" | custom-call | flops 3932160 | bytes 5242880 | tf_op jit(solution)/shard_map/gradients/pallas_call | solution.py:217
  49.6 1.6 %collective-permute-start.15 = (bf16[1,2,1024,128]{3,2,1,0:T(8,128)(2,1)S(1)}, bf16[1,2,1024,128]{3,2,1,0:T(8,128)(2,1)S(1)}, u32[]{:S(2)}, u32[]{:S(2)}) collective-permute-start(bf16[1,2,1024,128]{3,2,1,0:T(8,128)(2,1)S(1)} %collective-permute-done.8.refs_0_), channel_id=1, source_target_pairs={{0,2},{2,4},{4,6},{6,7},{7,5},{5,3},{3,1},{1,0},{8,10},{10,12},{12... | collective-permute-start | bytes 1572872 | tf_op jit(solution)/shard_map/ppermute | solution.py:446
  51.7 4.6 %add_product.14 = (f32[1024,128]{1,0:T(8,128)S(1)}, bf16[1024,3072]{1,0:T(8,128)(2,1)S(1)}) custom-call(bf16[3,1024,8192]{2,1,0:T(8,128)(2,1)} %w_proj.19, bf16[1024,3072]{1,0:T(8,128)(2,1)S(1)} %get-tuple-element.100.w, bf16[1,2,1024,128]{3,2,1,0:T(8,128)(2,1)S(1)} %collective-permute-done.8.refs_0_, ...), custom_call_target="tpu_custom_call" | custom-call | flops 65536 | bytes 256 | tf_op jit(solution)/shard_map/add_product/pallas_call | solution.py:406
  56.3 1.6 %collective-permute-start.19 = (bf16[1,1,512,128]{3,2,1,0:T(8,128)(2,1)S(1)}, bf16[1,1,512,128]{3,2,1,0:T(8,128)(2,1)S(1)}, u32[]{:S(2)}, u32[]{:S(2)}) collective-permute-start(bf16[1,1,512,128]{3,2,1,0:T(8,128)(2,1)S(1)} %slice.20), channel_id=1, source_target_pairs={{0,2},{2,4},{4,6},{6,7},{7,5},{5,3},{3,1},{1,0},{8,10},{10,12},{12... | collective-permute-start | bytes 393224 | tf_op jit(solution)/shard_map/ppermute | solution.py:446
  58.4 5.2 %add_product.15 = (f32[1024,128]{1,0:T(8,128)S(1)}, bf16[1024,4096]{1,0:T(8,128)(2,1)S(1)}) custom-call(bf16[3,1024,8192]{2,1,0:T(8,128)(2,1)} %w_proj.19, bf16[1024,3072]{1,0:T(8,128)(2,1)S(1)} %get-tuple-element.104.w, bf16[1,2,1024,128]{3,2,1,0:T(8,128)(2,1)S(1)} %collective-permute-done.9.refs_1_.refs_0_, ...), custom_call_target="tpu_custom_call" | custom-call | flops 68719476736 | bytes 268435456 | tf_op jit(solution)/shard_map/add_product/pallas_call | solution.py:406
  64.5 1.6 %collective-permute-done.16.refs_1_ = bf16[1,2,1024,128]{3,2,1,0:T(8,128)(2,1)S(1)} collective-permute-done((bf16[1,2,1024,128]{3,2,1,0:T(8,128)(2,1)S(1)}, bf16[1,2,1024,128]{3,2,1,0:T(8,128)(2,1)S(1)}, u32[]{:S(2)}, u32[]{:S(2)}) %collective-permute-start.16) | collective-permute-done | bytes 524320 | tf_op jit(solution)/shard_map/ppermute | solution.py:449
  66.4 1.8 %collective-permute-start.18 = (bf16[1,1,1024,128]{3,2,1,0:T(8,128)(2,1)S(1)}, bf16[1,1,1024,128]{3,2,1,0:T(8,128)(2,1)S(1)}, u32[]{:S(2)}, u32[]{:S(2)}) collective-permute-start(bf16[1,1,1024,128]{3,2,1,0:T(8,128)(2,1)S(1)} %slice.19), channel_id=1, source_target_pairs={{0,2},{2,4},{4,6},{6,7},{7,5},{5,3},{3,1},{1,0},{8,10},{10,12},{12... | collective-permute-start | bytes 786440 | tf_op jit(solution)/shard_map/ppermute | solution.py:446
  68.2 5.1 %add_product.16 = (f32[1024,128]{1,0:T(8,128)S(1)}, bf16[1024,3072]{1,0:T(8,128)(2,1)S(1)}) custom-call(bf16[3,1024,8192]{2,1,0:T(8,128)(2,1)} %w_proj.19, bf16[1024,4096]{1,0:T(8,128)(2,1)S(1)} %get-tuple-element.109.w, bf16[1,2,1024,128]{3,2,1,0:T(8,128)(2,1)S(1)} %collective-permute-done.15.refs_0_, ...), custom_call_target="tpu_custom_call" | custom-call | flops 1073741824 | bytes 9437184 | tf_op jit(solution)/shard_map/add_product/pallas_call | solution.py:406
  76.1 1.5 %add_product.19 = f32[128,1024]{1,0:T(8,128)} custom-call(bf16[3,1024,8192]{2,1,0:T(8,128)(2,1)} %w_proj.19, bf16[1024,3072]{1,0:T(8,128)(2,1)S(1)} %get-tuple-element.115.w, bf16[1,1,1024,128]{3,2,1,0:T(8,128)(2,1)S(1)} %collective-permute-done.17.refs_0_, f32[1024,128]{1,0:T(8,128)S(1)} %add_product.18.refs_1_), custom_call_target="tpu_custom_call" | custom-call | flops 65536 | bytes 256 | tf_op jit(solution)/shard_map/add_product/pallas_call | solution.py:406
  (55 shorter events, 10.4 us)
Async XLA Ops:
  2.8 3.9 %collective-permute-start = (f32[224,128]{1,0:T(8,128)S(1)}, f32[224,128]{1,0:T(8,128)S(1)}, u32[]{:S(2)}, u32[]{:S(2)}) collective-permute-start(f32[224,128]{1,0:T(8,128)S(1)} %get-tuple-element.70), channel_id=1, source_target_pairs={{8,0},{16,8},{24,16},{9,1},{17,9},{25,17},{10,2},{18,10},{26,18},{... | collective-permute-start | bytes 344072 | tf_op jit(solution)/shard_map/ppermute | solution.py:458
  4.1 8.0 %collective-permute-start.1 = (f32[144,128]{1,0:T(8,128)S(1)}, f32[144,128]{1,0:T(8,128)S(1)}, u32[]{:S(2)}, u32[]{:S(2)}) collective-permute-start(f32[144,128]{1,0:T(8,128)S(1)} %get-tuple-element.73), channel_id=1, source_target_pairs={{16,0},{24,8},{17,1},{25,9},{18,2},{26,10},{19,3},{27,11},{20,4},{... | collective-permute-start | bytes 221192 | tf_op jit(solution)/shard_map/ppermute | solution.py:458
  5.4 7.4 %collective-permute-start.2 = (f32[144,128]{1,0:T(8,128)S(1)}, f32[144,128]{1,0:T(8,128)S(1)}, u32[]{:S(2)}, u32[]{:S(2)}) collective-permute-start(f32[144,128]{1,0:T(8,128)S(1)} %get-tuple-element.73), channel_id=1, source_target_pairs={{24,0},{25,1},{26,2},{27,3},{28,4},{29,5},{30,6},{31,7}} | collective-permute-start | bytes 221192 | tf_op jit(solution)/shard_map/ppermute | solution.py:458
  6.7 6.1 %copy-start.3 = (f32[224,128]{1,0:T(8,128)}, f32[224,128]{1,0:T(8,128)S(1)}, u32[]{:S(2)}) copy-start(f32[224,128]{1,0:T(8,128)S(1)} %collective-permute-done.later.refs_0_) | copy-start | bytes 344068
  7.0 10.9 %collective-permute-start.5 = (bf16[1,1,1024,128]{3,2,1,0:T(8,128)(2,1)S(1)}, bf16[1,1,1024,128]{3,2,1,0:T(8,128)(2,1)}, u32[]{:S(2)}, u32[]{:S(2)}) collective-permute-start(bf16[1,1,1024,128]{3,2,1,0:T(8,128)(2,1)S(1)} %bitcast.15), channel_id=1, source_target_pairs={{0,2},{2,4},{4,6},{6,7},{7,5},{5,3},{3,1},{1,0},{8,10},{10,12},{12... | collective-permute-start | bytes 786440 | tf_op jit(solution)/shard_map/ppermute | solution.py:446
  10.1 8.5 %collective-permute-start.6 = (bf16[1,1,1024,128]{3,2,1,0:T(8,128)(2,1)S(1)}, bf16[1,1,1024,128]{3,2,1,0:T(8,128)(2,1)}, u32[]{:S(2)}, u32[]{:S(2)}) collective-permute-start(bf16[1,1,1024,128]{3,2,1,0:T(8,128)(2,1)S(1)} %bitcast.16), channel_id=1, source_target_pairs={{0,1},{2,0},{4,2},{6,4},{7,6},{5,7},{3,5},{1,3},{8,9},{10,8},{12,1... | collective-permute-start | bytes 786440 | tf_op jit(solution)/shard_map/ppermute | solution.py:449
  15.7 14.9 %collective-permute-start.3 = (bf16[1,2,1024,128]{3,2,1,0:T(8,128)(2,1)S(1)}, bf16[1,2,1024,128]{3,2,1,0:T(8,128)(2,1)S(1)}, u32[]{:S(2)}, u32[]{:S(2)}) collective-permute-start(bf16[1,2,1024,128]{3,2,1,0:T(8,128)(2,1)S(1)} %bitcast.12), channel_id=1, source_target_pairs={{0,2},{2,4},{4,6},{6,7},{7,5},{5,3},{3,1},{1,0},{8,10},{10,12},{12... | collective-permute-start | bytes 1572872 | tf_op jit(solution)/shard_map/ppermute | solution.py:446
  17.9 14.9 %collective-permute-start.4 = (bf16[1,2,1024,128]{3,2,1,0:T(8,128)(2,1)S(1)}, bf16[1,2,1024,128]{3,2,1,0:T(8,128)(2,1)S(1)}, u32[]{:S(2)}, u32[]{:S(2)}) collective-permute-start(bf16[1,2,1024,128]{3,2,1,0:T(8,128)(2,1)S(1)} %bitcast.13), channel_id=1, source_target_pairs={{0,1},{2,0},{4,2},{6,4},{7,6},{5,7},{3,5},{1,3},{8,9},{10,8},{12,1... | collective-permute-start | bytes 1572872 | tf_op jit(solution)/shard_map/ppermute | solution.py:449
  18.6 11.7 %collective-permute-start.7 = (f32[17,1024]{1,0:T(8,128)S(1)}, f32[17,1024]{1,0:T(8,128)S(1)}, u32[]{:S(2)}, u32[]{:S(2)}) collective-permute-start(f32[17,1024]{1,0:T(8,128)S(1)} %get-tuple-element.84), channel_id=1, source_target_pairs={{0,8},{8,0},{16,24},{24,16},{1,9},{9,1},{17,25},{25,17},{2,10},{10... | collective-permute-start | bytes 208904 | tf_op jit(solution)/shard_map/ppermute | solution.py:461
  19.2 20.2 %collective-permute-start.10 = (bf16[1,1,1024,128]{3,2,1,0:T(8,128)(2,1)}, bf16[1,1,1024,128]{3,2,1,0:T(8,128)(2,1)}, u32[]{:S(2)}, u32[]{:S(2)}) collective-permute-start(bf16[1,1,1024,128]{3,2,1,0:T(8,128)(2,1)} %collective-permute-done.5.refs_0_), channel_id=1, source_target_pairs={{0,2},{2,4},{4,6},{6,7},{7,5},{5,3},{3,1},{1,0},{8,10},{10,12},{12... | collective-permute-start | bytes 786440 | tf_op jit(solution)/shard_map/ppermute | solution.py:446
  20.8 18.6 %collective-permute-start.11 = (bf16[1,1,1024,128]{3,2,1,0:T(8,128)(2,1)}, bf16[1,1,1024,128]{3,2,1,0:T(8,128)(2,1)}, u32[]{:S(2)}, u32[]{:S(2)}) collective-permute-start(bf16[1,1,1024,128]{3,2,1,0:T(8,128)(2,1)} %collective-permute-done.6.refs_1_), channel_id=1, source_target_pairs={{0,1},{2,0},{4,2},{6,4},{7,6},{5,7},{3,5},{1,3},{8,9},{10,8},{12,1... | collective-permute-start | bytes 786440 | tf_op jit(solution)/shard_map/ppermute | solution.py:449
  32.8 16.6 %collective-permute-start.8 = (bf16[1,2,1024,128]{3,2,1,0:T(8,128)(2,1)S(1)}, bf16[1,2,1024,128]{3,2,1,0:T(8,128)(2,1)S(1)}, u32[]{:S(2)}, u32[]{:S(2)}) collective-permute-start(bf16[1,2,1024,128]{3,2,1,0:T(8,128)(2,1)S(1)} %collective-permute-done.3.refs_0_), channel_id=1, source_target_pairs={{0,2},{2,4},{4,6},{6,7},{7,5},{5,3},{3,1},{1,0},{8,10},{10,12},{12... | collective-permute-start | bytes 1572872 | tf_op jit(solution)/shard_map/ppermute | solution.py:446
  34.4 15.3 %collective-permute-start.9 = (bf16[1,2,1024,128]{3,2,1,0:T(8,128)(2,1)S(1)}, bf16[1,2,1024,128]{3,2,1,0:T(8,128)(2,1)S(1)}, u32[]{:S(2)}, u32[]{:S(2)}) collective-permute-start(bf16[1,2,1024,128]{3,2,1,0:T(8,128)(2,1)S(1)} %collective-permute-done.4.refs_1_.refs_0_), channel_id=1, source_target_pairs={{0,1},{2,0},{4,2},{6,4},{7,6},{5,7},{3,5},{1,3},{8,9},{10,8},{12,1... | collective-permute-start | bytes 1572872 | tf_op jit(solution)/shard_map/ppermute | solution.py:449
  39.4 9.9 %collective-permute-start.12 = (f32[17,1024]{1,0:T(8,128)S(1)}, f32[17,1024]{1,0:T(8,128)S(1)}, u32[]{:S(2)}, u32[]{:S(2)}) collective-permute-start(f32[17,1024]{1,0:T(8,128)S(1)} %add.6), channel_id=1, source_target_pairs={{0,16},{8,24},{16,0},{24,8},{1,17},{9,25},{17,1},{25,9},{2,18},{10... | collective-permute-start | bytes 208904 | tf_op jit(solution)/shard_map/ppermute | solution.py:461
  39.5 16.7 %collective-permute-start.13 = (bf16[1,1,1024,128]{3,2,1,0:T(8,128)(2,1)}, bf16[1,1,1024,128]{3,2,1,0:T(8,128)(2,1)S(1)}, u32[]{:S(2)}, u32[]{:S(2)}) collective-permute-start(bf16[1,1,1024,128]{3,2,1,0:T(8,128)(2,1)} %collective-permute-done.10.refs_1_), channel_id=1, source_target_pairs={{0,2},{2,4},{4,6},{6,7},{7,5},{5,3},{3,1},{1,0},{8,10},{10,12},{12... | collective-permute-start | bytes 786440 | tf_op jit(solution)/shard_map/ppermute | solution.py:446
  41.1 15.1 %collective-permute-start.14 = (bf16[1,1,1024,128]{3,2,1,0:T(8,128)(2,1)}, bf16[1,1,1024,128]{3,2,1,0:T(8,128)(2,1)S(1)}, u32[]{:S(2)}, u32[]{:S(2)}) collective-permute-start(bf16[1,1,1024,128]{3,2,1,0:T(8,128)(2,1)} %collective-permute-done.11.refs_2_), channel_id=1, source_target_pairs={{0,1},{2,0},{4,2},{6,4},{7,6},{5,7},{3,5},{1,3},{8,9},{10,8},{12,1... | collective-permute-start | bytes 786440 | tf_op jit(solution)/shard_map/ppermute | solution.py:449
  41.6 5.8 %copy-start.5 = (f32[3,3,1024]{2,1,0:T(4,128)S(1)}, f32[3,3,1024]{2,1,0:T(4,128)}, u32[]{:S(2)}) copy-start(f32[3,3,1024]{2,1,0:T(4,128)} %filt.1) | copy-start | bytes 110596
  41.6 5.8 %copy-start.6 = (f32[1024]{0:T(1024)S(1)}, f32[1024]{0:T(1024)}, u32[]{:S(2)}) copy-start(f32[1024]{0:T(1024)} %param.14) | copy-start | bytes 12292
  49.6 14.8 %collective-permute-start.15 = (bf16[1,2,1024,128]{3,2,1,0:T(8,128)(2,1)S(1)}, bf16[1,2,1024,128]{3,2,1,0:T(8,128)(2,1)S(1)}, u32[]{:S(2)}, u32[]{:S(2)}) collective-permute-start(bf16[1,2,1024,128]{3,2,1,0:T(8,128)(2,1)S(1)} %collective-permute-done.8.refs_0_), channel_id=1, source_target_pairs={{0,2},{2,4},{4,6},{6,7},{7,5},{5,3},{3,1},{1,0},{8,10},{10,12},{12... | collective-permute-start | bytes 1572872 | tf_op jit(solution)/shard_map/ppermute | solution.py:446
  51.2 14.9 %collective-permute-start.16 = (bf16[1,2,1024,128]{3,2,1,0:T(8,128)(2,1)S(1)}, bf16[1,2,1024,128]{3,2,1,0:T(8,128)(2,1)S(1)}, u32[]{:S(2)}, u32[]{:S(2)}) collective-permute-start(bf16[1,2,1024,128]{3,2,1,0:T(8,128)(2,1)S(1)} %collective-permute-done.9.refs_1_.refs_0_), channel_id=1, source_target_pairs={{0,1},{2,0},{4,2},{6,4},{7,6},{5,7},{3,5},{1,3},{8,9},{10,8},{12,1... | collective-permute-start | bytes 1572872 | tf_op jit(solution)/shard_map/ppermute | solution.py:449
  56.3 17.1 %collective-permute-start.19 = (bf16[1,1,512,128]{3,2,1,0:T(8,128)(2,1)S(1)}, bf16[1,1,512,128]{3,2,1,0:T(8,128)(2,1)S(1)}, u32[]{:S(2)}, u32[]{:S(2)}) collective-permute-start(bf16[1,1,512,128]{3,2,1,0:T(8,128)(2,1)S(1)} %slice.20), channel_id=1, source_target_pairs={{0,2},{2,4},{4,6},{6,7},{7,5},{5,3},{3,1},{1,0},{8,10},{10,12},{12... | collective-permute-start | bytes 393224 | tf_op jit(solution)/shard_map/ppermute | solution.py:446
  57.9 15.5 %collective-permute-start.20 = (bf16[1,1,512,128]{3,2,1,0:T(8,128)(2,1)S(1)}, bf16[1,1,512,128]{3,2,1,0:T(8,128)(2,1)S(1)}, u32[]{:S(2)}, u32[]{:S(2)}) collective-permute-start(bf16[1,1,512,128]{3,2,1,0:T(8,128)(2,1)S(1)} %slice.21), channel_id=1, source_target_pairs={{0,1},{2,0},{4,2},{6,4},{7,6},{5,7},{3,5},{1,3},{8,9},{10,8},{12,1... | collective-permute-start | bytes 393224 | tf_op jit(solution)/shard_map/ppermute | solution.py:449
  66.1 10.0 %collective-permute-start.17 = (bf16[1,1,1024,128]{3,2,1,0:T(8,128)(2,1)S(1)}, bf16[1,1,1024,128]{3,2,1,0:T(8,128)(2,1)S(1)}, u32[]{:S(2)}, u32[]{:S(2)}) collective-permute-start(bf16[1,1,1024,128]{3,2,1,0:T(8,128)(2,1)S(1)} %slice.18), channel_id=1, source_target_pairs={{0,1},{2,0},{4,2},{6,4},{7,6},{5,7},{3,5},{1,3},{8,9},{10,8},{12,1... | collective-permute-start | bytes 786440 | tf_op jit(solution)/shard_map/ppermute | solution.py:449
  66.4 8.9 %collective-permute-start.18 = (bf16[1,1,1024,128]{3,2,1,0:T(8,128)(2,1)S(1)}, bf16[1,1,1024,128]{3,2,1,0:T(8,128)(2,1)S(1)}, u32[]{:S(2)}, u32[]{:S(2)}) collective-permute-start(bf16[1,1,1024,128]{3,2,1,0:T(8,128)(2,1)S(1)} %slice.19), channel_id=1, source_target_pairs={{0,2},{2,4},{4,6},{6,7},{7,5},{5,3},{3,1},{1,0},{8,10},{10,12},{12... | collective-permute-start | bytes 786440 | tf_op jit(solution)/shard_map/ppermute | solution.py:446
  (4 other events, 23.3 us)

commit v11 on v10

--- a/solution.py
+++ b/solution.py
@@ -358,7 +358,7 @@
     x = jnp.concatenate([refs[n][h, p] for *_, parts in plan for n, h, p in parts], axis=0)
     columns = slice(base * (x.shape[0] // len(plan)), (base + len(plan)) * (x.shape[0] // len(plan)))
     features = w.shape[0]
-    wide = min(256, features)
+    wide = min(512, features)
     for d in range(0, features, wide):
         rows = slice(d, d + wide)
         y = jnp.dot(w[rows, columns], x, preferred_element_type=F32)
@@ -398,7 +398,7 @@
     if last:
         out_specs = [in_hbm()]
         out_shape = [jax.ShapeDtypeStruct((tokens, features), F32)]
-        scratch = [pltpu.VMEM((tokens, features), F32), pltpu.SemaphoreType.DMA((max(1, features // 256),))]
+        scratch = [pltpu.VMEM((tokens, features), F32), pltpu.SemaphoreType.DMA((max(1, features // 512),))]
     elif later:
         out_specs += [whole()]
         out_shape += [pltpu.VMEM((features, len(later) * channels), BF16)]
@@ -485,10 +485,10 @@
 
     a, b = (0,), (0, 1)
     sets = [
-        [("a0", a, 0, 0), ("b0", b, 1, 0)],
-        [("a1", a, 0, ring - 1), ("z1", a, 0, 1)],
-        [("b1", b, 1, ring - 1), ("y1", (0,), 1, 1)],
-        [("y1", (1,), 1, 1), ("a2", a, 0, ring - 2), ("z2", a, 0, 2)],
+        [("a0", a, 0, 0), ("a1", a, 0, ring - 1), ("z1", a, 0, 1)],
+        [("b0", b, 1, 0)],
+        [("b1", b, 1, ring - 1), ("y1", b, 1, 1)],
+        [("a2", a, 0, ring - 2), ("z2", a, 0, 2)],
         [("b2", b, 1, ring - 2), ("y2", (0,), 1, 2)],
         [("y2", (1,), 1, 2), ("a3", a, 0, ring - 3), ("z3", a, 0, 3)],
         [("b3", b, 1, ring - 3), ("y3", b, 1, 3)],
@@ -521,8 +521,8 @@
     distances = [1 << n for n in range((blocks - 1).bit_length())]
     for by in distances[:1]:
         sums = exchanged(sums, by)
-    total, ready = times(0, None, ready, a0=a0, b0=b0)
-    total, ready = times(1, total, ready, a1=a1, z1=z1)
+    total, ready = times(0, None, ready, a0=a0, a1=a1, z1=z1)
+    total, ready = times(1, total, ready, b0=b0)
     b1, y1, total, sums = lax.optimization_barrier((b1, y1, total, sums))
     b2, y2 = up(b1), down(y1)
     total, ready = times(2, total, ready, b1=b1, y1=y1)
@@ -531,7 +531,7 @@
     a3, z3 = up(a2), down(z2)
     for by in distances[1:]:
         sums = exchanged(sums, by)
-    total, ready = times(3, total, ready, y1=y1, a2=a2, z2=z2)
+    total, ready = times(3, total, ready, a2=a2, z2=z2)
     grads = gradients(features, saved_conv, out_grad, short_filter, bias[None], payloads[0], after(gp, total))
 
     b2, y2, total, sums, grads = lax.optimization_barrier((b2, y2, total, sums, grads))

time: 77.9 us -> 77.3 us (level)
  Pallas kernels: 44.5 us -> 41.6 us
  waiting for transfers between devices: 8.41 us -> 10.1 us
    pallas_call x10, Pallas kernels: 37.2 us -> 34.3 us  [add_product(): pl.pallas_call(functools.partial(product_kernel, plan, base, later, first...]
    ppermute x8, waiting for transfers between devices: 4.62 us -> 6.33 us  [down(): return lax.ppermute(x, 'chan', pairs[-1])]
  transfers between devices with their start and end apart: 21 -> 21, of which waited for: 8 -> 7; matrix products, arithmetic and copies ran while one was open for 2% -> 2% of each run, Pallas kernels for 53% -> 49%
where the time goes in v11:
time: 77.3 us; the launch traced here: 77.1 us
  Pallas kernels  41.6 us (54%)
  starting transfers between devices  23 us (30%)
  waiting for transfers between devices  10.1 us (13%)
  local copies, waits for them, and re-layouts  1.32 us (2%)
  between operations  1.14 us (1%)
    pallas_call x10, Pallas kernels, add_product(): pl.pallas_call(functools.partial(product_kernel, plan, base, later, first...  34.3 us
    ppermute x8, starting transfers between devices, up(): return lax.ppermute(x, 'chan', pairs[1])  15.4 us
    ppermute x8, waiting for transfers between devices, down(): return lax.ppermute(x, 'chan', pairs[-1])  6.33 us
    ppermute x3, starting transfers between devices, from_later(): return lax.ppermute(array, 'ctx', [(i, i - by) for i in range(by, blocks)])  3.88 us
    pallas_call x1, Pallas kernels, state_streams(): pl.pallas_call(functools.partial(state_kernel, spans, plan, ring), in_spe...  2.96 us
    ppermute x3, waiting for transfers between devices, from_later(): return lax.ppermute(array, 'ctx', [(i, i - by) for i in range(by, blocks)])  2.65 us
    ppermute x8, starting transfers between devices, down(): return lax.ppermute(x, 'chan', pairs[-1])  2.36 us
    pallas_call x1, Pallas kernels, front(): pl.pallas_call(front_kernel, in_specs=[in_hbm()] * 7, out_specs=[whole()]...  2.11 us
  transfers between devices with their start and end apart: 21, of which 7 were waited for; matrix products, arithmetic and copies ran while one was open for 2% of the time, Pallas kernels for 49%

profile of v11, /device:TPU:0, one launch (start us, length us, event | category | flops | bytes accessed | tf_op | source)
XLA Modules:
  0.0 77.1 jit_solution(13159580326400547043)
XLA Ops:
  0.6 2.1 %front.1 = (f32[3,128,1024]{2,1,0:T(8,128)S(1)}, f32[128,1024]{1,0:T(8,128)S(1)}, f32[128,1024]{1,0:T(8,128)S(1)}, f32[3,3,1024]{2,1,0:T(4,128)S(1)}, f32[1,1024...) custom-call(f32[3,128,1024]{2,1,0:T(8,128)} %feat.1, ...), custom_call_target="tpu_custom_call" | custom-call | flops 8388608 | bytes 2621440 | tf_op jit(solution)/shard_map/front/pallas_call | solution.py:96
  2.8 1.3 %collective-permute-start = (f32[224,128]{1,0:T(8,128)S(1)}, f32[224,128]{1,0:T(8,128)S(1)}, u32[]{:S(2)}, u32[]{:S(2)}) collective-permute-start(f32[224,128]{1,0:T(8,128)S(1)} %get-tuple-element.70), channel_id=1, source_target_pairs={{8,0},{16,8},{24,16},{9,1},{17,9},{25,17},{10,2},{18,10},{26,18},{... | collective-permute-start | bytes 344072 | tf_op jit(solution)/shard_map/ppermute | solution.py:458
  7.0 3.1 %collective-permute-start.5 = (bf16[1,1,1024,128]{3,2,1,0:T(8,128)(2,1)S(1)}, bf16[1,1,1024,128]{3,2,1,0:T(8,128)(2,1)}, u32[]{:S(2)}, u32[]{:S(2)}) collective-permute-start(bf16[1,1,1024,128]{3,2,1,0:T(8,128)(2,1)S(1)} %bitcast.15), channel_id=1, source_target_pairs={{0,2},{2,4},{4,6},{6,7},{7,5},{5,3},{3,1},{1,0},{8,10},{10,12},{12... | collective-permute-start | bytes 786440 | tf_op jit(solution)/shard_map/ppermute | solution.py:446
  10.1 2.0 %collective-permute-done.1.refs_1_ = f32[144,128]{1,0:T(8,128)S(1)} collective-permute-done((f32[144,128]{1,0:T(8,128)S(1)}, f32[144,128]{1,0:T(8,128)S(1)}, u32[]{:S(2)}, u32[]{:S(2)}) %collective-permute-start.1) | collective-permute-done | bytes 73760 | tf_op jit(solution)/shard_map/ppermute | solution.py:458
  12.8 3.0 %state_streams.1 = (bf16[2,1024,128]{2,1,0:T(8,128)(2,1)S(1)}, f32[17,1024]{1,0:T(8,128)S(1)}, f32[1040,128]{1,0:T(8,128)S(1)}, bf16[1024,3072]{1,0:T(8,128)(2,1)S(1)}) custom-call(f32[3,128,1024]{2,1,0:T(8,128)S(1)} %get-tuple-element.65.feat, f32[128,1024]{1,0:T(8,128)S(1)} %get-tuple-element.66.og, f32[3,3,1024]{2,1,0:T(4,128)S(1)} %get-tuple-element.67.filt, ...), custom_call_target="tpu_custom_call" | custom-call | flops 4294967296 | bytes 16777216 | tf_op jit(solution)/shard_map/state_streams/pallas_call | solution.py:326
  15.7 2.2 %collective-permute-start.3 = (bf16[1,2,1024,128]{3,2,1,0:T(8,128)(2,1)S(1)}, bf16[1,2,1024,128]{3,2,1,0:T(8,128)(2,1)S(1)}, u32[]{:S(2)}, u32[]{:S(2)}) collective-permute-start(bf16[1,2,1024,128]{3,2,1,0:T(8,128)(2,1)S(1)} %bitcast.12), channel_id=1, source_target_pairs={{0,2},{2,4},{4,6},{6,7},{7,5},{5,3},{3,1},{1,0},{8,10},{10,12},{12... | collective-permute-start | bytes 1572872 | tf_op jit(solution)/shard_map/ppermute | solution.py:446
  19.2 1.6 %collective-permute-start.10 = (bf16[1,1,1024,128]{3,2,1,0:T(8,128)(2,1)}, bf16[1,1,1024,128]{3,2,1,0:T(8,128)(2,1)}, u32[]{:S(2)}, u32[]{:S(2)}) collective-permute-start(bf16[1,1,1024,128]{3,2,1,0:T(8,128)(2,1)} %collective-permute-done.5.refs_1_), channel_id=1, source_target_pairs={{0,2},{2,4},{4,6},{6,7},{7,5},{5,3},{3,1},{1,0},{8,10},{10,12},{12... | collective-permute-start | bytes 786440 | tf_op jit(solution)/shard_map/ppermute | solution.py:446
  21.2 4.9 %add_product.10 = (f32[1024,128]{1,0:T(8,128)S(1)}, bf16[1024,2048]{1,0:T(8,128)(2,1)S(1)}) custom-call(bf16[3,1024,8192]{2,1,0:T(8,128)(2,1)} %w_proj.19, bf16[1024,3072]{1,0:T(8,128)(2,1)S(1)} %get-tuple-element.75.w, bf16[1,1,1024,128]{3,2,1,0:T(8,128)(2,1)S(1)} %bitcast.17, bf16[1,1,1024,128]{3,2,1,0:T(8,128)(2,1)} %collective-permute-done.5.refs_1_, ...), custom_call_target="tpu_custom_call" | custom-call | flops 68719476736 | bytes 268435456 | tf_op jit(solution)/shard_map/add_product/pallas_call | solution.py:406
  26.2 4.7 %add_product.11 = (f32[1024,128]{1,0:T(8,128)S(1)}, bf16[1024,4096]{1,0:T(8,128)(2,1)S(1)}) custom-call(bf16[3,1024,8192]{2,1,0:T(8,128)(2,1)} %w_proj.19, bf16[1024,2048]{1,0:T(8,128)(2,1)S(1)} %get-tuple-element.80.w, bf16[1,2,1024,128]{3,2,1,0:T(8,128)(2,1)S(1)} %bitcast.14, f32[1024,128]{1,0:T(8,128)S(1)} %get-tuple-element.82.refs_1_), custom_call_target="tpu_custom_call" | custom-call | flops 68719476736 | bytes 268435456 | tf_op jit(solution)/shard_map/add_product/pallas_call | solution.py:406
  30.9 1.9 %collective-permute-done.4.refs_1_ = bf16[1,2,1024,128]{3,2,1,0:T(8,128)(2,1)S(1)} collective-permute-done((bf16[1,2,1024,128]{3,2,1,0:T(8,128)(2,1)S(1)}, bf16[1,2,1024,128]{3,2,1,0:T(8,128)(2,1)S(1)}, u32[]{:S(2)}, u32[]{:S(2)}) %collective-permute-start.4) | collective-permute-done | bytes 524320 | tf_op jit(solution)/shard_map/ppermute | solution.py:449
  32.8 1.6 %collective-permute-start.8 = (bf16[1,2,1024,128]{3,2,1,0:T(8,128)(2,1)S(1)}, bf16[1,2,1024,128]{3,2,1,0:T(8,128)(2,1)S(1)}, u32[]{:S(2)}, u32[]{:S(2)}) collective-permute-start(bf16[1,2,1024,128]{3,2,1,0:T(8,128)(2,1)S(1)} %collective-permute-done.3.refs_0_), channel_id=1, source_target_pairs={{0,2},{2,4},{4,6},{6,7},{7,5},{5,3},{3,1},{1,0},{8,10},{10,12},{12... | collective-permute-start | bytes 1572872 | tf_op jit(solution)/shard_map/ppermute | solution.py:446
  34.8 4.2 %add_product.12 = (f32[1024,128]{1,0:T(8,128)S(1)}, bf16[1024,2048]{1,0:T(8,128)(2,1)S(1)}) custom-call(bf16[3,1024,8192]{2,1,0:T(8,128)(2,1)} %w_proj.19, bf16[1024,4096]{1,0:T(8,128)(2,1)S(1)} %get-tuple-element.87.w, bf16[1,2,1024,128]{3,2,1,0:T(8,128)(2,1)S(1)} %collective-permute-done.3.refs_0_, ...), custom_call_target="tpu_custom_call" | custom-call | flops 65536 | bytes 256 | tf_op jit(solution)/shard_map/add_product/pallas_call | solution.py:406
  39.7 1.6 %collective-permute-start.13 = (bf16[1,1,1024,128]{3,2,1,0:T(8,128)(2,1)}, bf16[1,1,1024,128]{3,2,1,0:T(8,128)(2,1)S(1)}, u32[]{:S(2)}, u32[]{:S(2)}) collective-permute-start(bf16[1,1,1024,128]{3,2,1,0:T(8,128)(2,1)} %collective-permute-done.10.refs_0_), channel_id=1, source_target_pairs={{0,2},{2,4},{4,6},{6,7},{7,5},{5,3},{3,1},{1,0},{8,10},{10,12},{12... | collective-permute-start | bytes 786440 | tf_op jit(solution)/shard_map/ppermute | solution.py:446
  41.8 4.1 %add_product.13 = (f32[1024,128]{1,0:T(8,128)S(1)}, bf16[1024,3072]{1,0:T(8,128)(2,1)S(1)}) custom-call(bf16[3,1024,8192]{2,1,0:T(8,128)(2,1)} %w_proj.19, bf16[1024,2048]{1,0:T(8,128)(2,1)S(1)} %get-tuple-element.89.w, bf16[1,1,1024,128]{3,2,1,0:T(8,128)(2,1)} %collective-permute-done.10.refs_0_, bf16[1,1,1024,128]{3,2,1,0:T(8,128)(2,1)} %collective-permute-done.11.refs_1_, ...), custom_call_target="tpu_custom_call" | custom-call | flops 68719476736 | bytes 268435456 | tf_op jit(solution)/shard_map/add_product/pallas_call | solution.py:406
  45.9 1.9 %gradients.1 = f32[3,128,1024]{2,1,0:T(8,128)} custom-call(f32[3,128,1024]{2,1,0:T(8,128)S(1)} %copy-done, f32[128,1024]{1,0:T(8,128)S(1)} %copy-done.1, f32[128,1024]{1,0:T(8,128)S(1)} %copy-done.2, f32[3,3,1024]{2,1,0:T(4,128)S(1)} %copy-done.5, f32[1,1024]{1,0:T(1,128)S(1)} %bitcast.10, f32[224,128]{1,0:T(8,128)S(1)} %copy-done.4, ...), custom_call_target="tpu_custom_call" | custom-call | flops 3932160 | bytes 5242880 | tf_op jit(solution)/shard_map/gradients/pallas_call | solution.py:217
  47.9 1.8 %collective-permute-done.9.refs_1_.refs_0_ = bf16[1,2,1024,128]{3,2,1,0:T(8,128)(2,1)S(1)} collective-permute-done((bf16[1,2,1024,128]{3,2,1,0:T(8,128)(2,1)S(1)}, bf16[1,2,1024,128]{3,2,1,0:T(8,128)(2,1)S(1)}, u32[]{:S(2)}, u32[]{:S(2)}) %collective-permute-start.9) | collective-permute-done | bytes 524320 | tf_op jit(solution)/shard_map/ppermute | solution.py:449
  49.6 1.6 %collective-permute-start.15 = (bf16[1,2,1024,128]{3,2,1,0:T(8,128)(2,1)S(1)}, bf16[1,2,1024,128]{3,2,1,0:T(8,128)(2,1)S(1)}, u32[]{:S(2)}, u32[]{:S(2)}) collective-permute-start(bf16[1,2,1024,128]{3,2,1,0:T(8,128)(2,1)S(1)} %collective-permute-done.8.refs_0_), channel_id=1, source_target_pairs={{0,2},{2,4},{4,6},{6,7},{7,5},{5,3},{3,1},{1,0},{8,10},{10,12},{12... | collective-permute-start | bytes 1572872 | tf_op jit(solution)/shard_map/ppermute | solution.py:446
  51.7 4.4 %add_product.14 = (f32[1024,128]{1,0:T(8,128)S(1)}, bf16[1024,3072]{1,0:T(8,128)(2,1)S(1)}) custom-call(bf16[3,1024,8192]{2,1,0:T(8,128)(2,1)} %w_proj.19, bf16[1024,3072]{1,0:T(8,128)(2,1)S(1)} %get-tuple-element.100.w, bf16[1,2,1024,128]{3,2,1,0:T(8,128)(2,1)S(1)} %collective-permute-done.8.refs_0_, ...), custom_call_target="tpu_custom_call" | custom-call | flops 65536 | bytes 256 | tf_op jit(solution)/shard_map/add_product/pallas_call | solution.py:406
  56.1 1.6 %collective-permute-start.19 = (bf16[1,1,512,128]{3,2,1,0:T(8,128)(2,1)S(1)}, bf16[1,1,512,128]{3,2,1,0:T(8,128)(2,1)S(1)}, u32[]{:S(2)}, u32[]{:S(2)}) collective-permute-start(bf16[1,1,512,128]{3,2,1,0:T(8,128)(2,1)S(1)} %slice.20), channel_id=1, source_target_pairs={{0,2},{2,4},{4,6},{6,7},{7,5},{5,3},{3,1},{1,0},{8,10},{10,12},{12... | collective-permute-start | bytes 393224 | tf_op jit(solution)/shard_map/ppermute | solution.py:446
  58.2 5.2 %add_product.15 = (f32[1024,128]{1,0:T(8,128)S(1)}, bf16[1024,4096]{1,0:T(8,128)(2,1)S(1)}) custom-call(bf16[3,1024,8192]{2,1,0:T(8,128)(2,1)} %w_proj.19, bf16[1024,3072]{1,0:T(8,128)(2,1)S(1)} %get-tuple-element.104.w, bf16[1,2,1024,128]{3,2,1,0:T(8,128)(2,1)S(1)} %collective-permute-done.9.refs_1_.refs_0_, ...), custom_call_target="tpu_custom_call" | custom-call | flops 68719476736 | bytes 268435456 | tf_op jit(solution)/shard_map/add_product/pallas_call | solution.py:406
  64.5 2.0 %collective-permute-done.16.refs_1_ = bf16[1,2,1024,128]{3,2,1,0:T(8,128)(2,1)S(1)} collective-permute-done((bf16[1,2,1024,128]{3,2,1,0:T(8,128)(2,1)S(1)}, bf16[1,2,1024,128]{3,2,1,0:T(8,128)(2,1)S(1)}, u32[]{:S(2)}, u32[]{:S(2)}) %collective-permute-start.16) | collective-permute-done | bytes 524320 | tf_op jit(solution)/shard_map/ppermute | solution.py:449
  66.6 2.2 %collective-permute-start.18 = (bf16[1,1,1024,128]{3,2,1,0:T(8,128)(2,1)S(1)}, bf16[1,1,1024,128]{3,2,1,0:T(8,128)(2,1)S(1)}, u32[]{:S(2)}, u32[]{:S(2)}) collective-permute-start(bf16[1,1,1024,128]{3,2,1,0:T(8,128)(2,1)S(1)} %slice.19), channel_id=1, source_target_pairs={{0,2},{2,4},{4,6},{6,7},{7,5},{5,3},{3,1},{1,0},{8,10},{10,12},{12... | collective-permute-start | bytes 786440 | tf_op jit(solution)/shard_map/ppermute | solution.py:446
  68.8 3.8 %add_product.16 = (f32[1024,128]{1,0:T(8,128)S(1)}, bf16[1024,3072]{1,0:T(8,128)(2,1)S(1)}) custom-call(bf16[3,1024,8192]{2,1,0:T(8,128)(2,1)} %w_proj.19, bf16[1024,4096]{1,0:T(8,128)(2,1)S(1)} %get-tuple-element.109.w, bf16[1,2,1024,128]{3,2,1,0:T(8,128)(2,1)S(1)} %collective-permute-done.15.refs_0_, ...), custom_call_target="tpu_custom_call" | custom-call | flops 1073741824 | bytes 9437184 | tf_op jit(solution)/shard_map/add_product/pallas_call | solution.py:406
  75.4 1.6 %add_product.19 = f32[128,1024]{1,0:T(8,128)} custom-call(bf16[3,1024,8192]{2,1,0:T(8,128)(2,1)} %w_proj.19, bf16[1024,3072]{1,0:T(8,128)(2,1)S(1)} %get-tuple-element.115.w, bf16[1,1,1024,128]{3,2,1,0:T(8,128)(2,1)S(1)} %collective-permute-done.17.refs_0_, f32[1024,128]{1,0:T(8,128)S(1)} %add_product.18.refs_1_), custom_call_target="tpu_custom_call" | custom-call | flops 65536 | bytes 256 | tf_op jit(solution)/shard_map/add_product/pallas_call | solution.py:406
  (55 shorter events, 11.8 us)
Async XLA Ops:
  2.8 3.9 %collective-permute-start = (f32[224,128]{1,0:T(8,128)S(1)}, f32[224,128]{1,0:T(8,128)S(1)}, u32[]{:S(2)}, u32[]{:S(2)}) collective-permute-start(f32[224,128]{1,0:T(8,128)S(1)} %get-tuple-element.70), channel_id=1, source_target_pairs={{8,0},{16,8},{24,16},{9,1},{17,9},{25,17},{10,2},{18,10},{26,18},{... | collective-permute-start | bytes 344072 | tf_op jit(solution)/shard_map/ppermute | solution.py:458
  4.1 8.0 %collective-permute-start.1 = (f32[144,128]{1,0:T(8,128)S(1)}, f32[144,128]{1,0:T(8,128)S(1)}, u32[]{:S(2)}, u32[]{:S(2)}) collective-permute-start(f32[144,128]{1,0:T(8,128)S(1)} %get-tuple-element.73), channel_id=1, source_target_pairs={{16,0},{24,8},{17,1},{25,9},{18,2},{26,10},{19,3},{27,11},{20,4},{... | collective-permute-start | bytes 221192 | tf_op jit(solution)/shard_map/ppermute | solution.py:458
  5.4 7.4 %collective-permute-start.2 = (f32[144,128]{1,0:T(8,128)S(1)}, f32[144,128]{1,0:T(8,128)S(1)}, u32[]{:S(2)}, u32[]{:S(2)}) collective-permute-start(f32[144,128]{1,0:T(8,128)S(1)} %get-tuple-element.73), channel_id=1, source_target_pairs={{24,0},{25,1},{26,2},{27,3},{28,4},{29,5},{30,6},{31,7}} | collective-permute-start | bytes 221192 | tf_op jit(solution)/shard_map/ppermute | solution.py:458
  6.7 6.1 %copy-start.3 = (f32[224,128]{1,0:T(8,128)}, f32[224,128]{1,0:T(8,128)S(1)}, u32[]{:S(2)}) copy-start(f32[224,128]{1,0:T(8,128)S(1)} %collective-permute-done.later.refs_0_) | copy-start | bytes 344068
  7.0 10.9 %collective-permute-start.5 = (bf16[1,1,1024,128]{3,2,1,0:T(8,128)(2,1)S(1)}, bf16[1,1,1024,128]{3,2,1,0:T(8,128)(2,1)}, u32[]{:S(2)}, u32[]{:S(2)}) collective-permute-start(bf16[1,1,1024,128]{3,2,1,0:T(8,128)(2,1)S(1)} %bitcast.15), channel_id=1, source_target_pairs={{0,2},{2,4},{4,6},{6,7},{7,5},{5,3},{3,1},{1,0},{8,10},{10,12},{12... | collective-permute-start | bytes 786440 | tf_op jit(solution)/shard_map/ppermute | solution.py:446
  10.1 8.5 %collective-permute-start.6 = (bf16[1,1,1024,128]{3,2,1,0:T(8,128)(2,1)S(1)}, bf16[1,1,1024,128]{3,2,1,0:T(8,128)(2,1)}, u32[]{:S(2)}, u32[]{:S(2)}) collective-permute-start(bf16[1,1,1024,128]{3,2,1,0:T(8,128)(2,1)S(1)} %bitcast.16), channel_id=1, source_target_pairs={{0,1},{2,0},{4,2},{6,4},{7,6},{5,7},{3,5},{1,3},{8,9},{10,8},{12,1... | collective-permute-start | bytes 786440 | tf_op jit(solution)/shard_map/ppermute | solution.py:449
  15.7 15.1 %collective-permute-start.3 = (bf16[1,2,1024,128]{3,2,1,0:T(8,128)(2,1)S(1)}, bf16[1,2,1024,128]{3,2,1,0:T(8,128)(2,1)S(1)}, u32[]{:S(2)}, u32[]{:S(2)}) collective-permute-start(bf16[1,2,1024,128]{3,2,1,0:T(8,128)(2,1)S(1)} %bitcast.12), channel_id=1, source_target_pairs={{0,2},{2,4},{4,6},{6,7},{7,5},{5,3},{3,1},{1,0},{8,10},{10,12},{12... | collective-permute-start | bytes 1572872 | tf_op jit(solution)/shard_map/ppermute | solution.py:446
  17.9 14.9 %collective-permute-start.4 = (bf16[1,2,1024,128]{3,2,1,0:T(8,128)(2,1)S(1)}, bf16[1,2,1024,128]{3,2,1,0:T(8,128)(2,1)S(1)}, u32[]{:S(2)}, u32[]{:S(2)}) collective-permute-start(bf16[1,2,1024,128]{3,2,1,0:T(8,128)(2,1)S(1)} %bitcast.13), channel_id=1, source_target_pairs={{0,1},{2,0},{4,2},{6,4},{7,6},{5,7},{3,5},{1,3},{8,9},{10,8},{12,1... | collective-permute-start | bytes 1572872 | tf_op jit(solution)/shard_map/ppermute | solution.py:449
  18.6 12.3 %collective-permute-start.7 = (f32[17,1024]{1,0:T(8,128)S(1)}, f32[17,1024]{1,0:T(8,128)S(1)}, u32[]{:S(2)}, u32[]{:S(2)}) collective-permute-start(f32[17,1024]{1,0:T(8,128)S(1)} %get-tuple-element.84), channel_id=1, source_target_pairs={{0,8},{8,0},{16,24},{24,16},{1,9},{9,1},{17,25},{25,17},{2,10},{10... | collective-permute-start | bytes 208904 | tf_op jit(solution)/shard_map/ppermute | solution.py:461
  19.2 19.8 %collective-permute-start.10 = (bf16[1,1,1024,128]{3,2,1,0:T(8,128)(2,1)}, bf16[1,1,1024,128]{3,2,1,0:T(8,128)(2,1)}, u32[]{:S(2)}, u32[]{:S(2)}) collective-permute-start(bf16[1,1,1024,128]{3,2,1,0:T(8,128)(2,1)} %collective-permute-done.5.refs_1_), channel_id=1, source_target_pairs={{0,2},{2,4},{4,6},{6,7},{7,5},{5,3},{3,1},{1,0},{8,10},{10,12},{12... | collective-permute-start | bytes 786440 | tf_op jit(solution)/shard_map/ppermute | solution.py:446
  20.8 18.3 %collective-permute-start.11 = (bf16[1,1,1024,128]{3,2,1,0:T(8,128)(2,1)}, bf16[1,1,1024,128]{3,2,1,0:T(8,128)(2,1)}, u32[]{:S(2)}, u32[]{:S(2)}) collective-permute-start(bf16[1,1,1024,128]{3,2,1,0:T(8,128)(2,1)} %collective-permute-done.6.refs_2_), channel_id=1, source_target_pairs={{0,1},{2,0},{4,2},{6,4},{7,6},{5,7},{3,5},{1,3},{8,9},{10,8},{12,1... | collective-permute-start | bytes 786440 | tf_op jit(solution)/shard_map/ppermute | solution.py:449
  32.8 15.1 %collective-permute-start.8 = (bf16[1,2,1024,128]{3,2,1,0:T(8,128)(2,1)S(1)}, bf16[1,2,1024,128]{3,2,1,0:T(8,128)(2,1)S(1)}, u32[]{:S(2)}, u32[]{:S(2)}) collective-permute-start(bf16[1,2,1024,128]{3,2,1,0:T(8,128)(2,1)S(1)} %collective-permute-done.3.refs_0_), channel_id=1, source_target_pairs={{0,2},{2,4},{4,6},{6,7},{7,5},{5,3},{3,1},{1,0},{8,10},{10,12},{12... | collective-permute-start | bytes 1572872 | tf_op jit(solution)/shard_map/ppermute | solution.py:446
  34.4 15.3 %collective-permute-start.9 = (bf16[1,2,1024,128]{3,2,1,0:T(8,128)(2,1)S(1)}, bf16[1,2,1024,128]{3,2,1,0:T(8,128)(2,1)S(1)}, u32[]{:S(2)}, u32[]{:S(2)}) collective-permute-start(bf16[1,2,1024,128]{3,2,1,0:T(8,128)(2,1)S(1)} %collective-permute-done.4.refs_1_), channel_id=1, source_target_pairs={{0,1},{2,0},{4,2},{6,4},{7,6},{5,7},{3,5},{1,3},{8,9},{10,8},{12,1... | collective-permute-start | bytes 1572872 | tf_op jit(solution)/shard_map/ppermute | solution.py:449
  39.1 8.8 %collective-permute-start.12 = (f32[17,1024]{1,0:T(8,128)S(1)}, f32[17,1024]{1,0:T(8,128)S(1)}, u32[]{:S(2)}, u32[]{:S(2)}) collective-permute-start(f32[17,1024]{1,0:T(8,128)S(1)} %add.6), channel_id=1, source_target_pairs={{0,16},{8,24},{16,0},{24,8},{1,17},{9,25},{17,1},{25,9},{2,18},{10... | collective-permute-start | bytes 208904 | tf_op jit(solution)/shard_map/ppermute | solution.py:461
  39.7 16.3 %collective-permute-start.13 = (bf16[1,1,1024,128]{3,2,1,0:T(8,128)(2,1)}, bf16[1,1,1024,128]{3,2,1,0:T(8,128)(2,1)S(1)}, u32[]{:S(2)}, u32[]{:S(2)}) collective-permute-start(bf16[1,1,1024,128]{3,2,1,0:T(8,128)(2,1)} %collective-permute-done.10.refs_0_), channel_id=1, source_target_pairs={{0,2},{2,4},{4,6},{6,7},{7,5},{5,3},{3,1},{1,0},{8,10},{10,12},{12... | collective-permute-start | bytes 786440 | tf_op jit(solution)/shard_map/ppermute | solution.py:446
  41.3 14.8 %collective-permute-start.14 = (bf16[1,1,1024,128]{3,2,1,0:T(8,128)(2,1)}, bf16[1,1,1024,128]{3,2,1,0:T(8,128)(2,1)S(1)}, u32[]{:S(2)}, u32[]{:S(2)}) collective-permute-start(bf16[1,1,1024,128]{3,2,1,0:T(8,128)(2,1)} %collective-permute-done.11.refs_1_), channel_id=1, source_target_pairs={{0,1},{2,0},{4,2},{6,4},{7,6},{5,7},{3,5},{1,3},{8,9},{10,8},{12,1... | collective-permute-start | bytes 786440 | tf_op jit(solution)/shard_map/ppermute | solution.py:449
  41.7 4.2 %copy-start.5 = (f32[3,3,1024]{2,1,0:T(4,128)S(1)}, f32[3,3,1024]{2,1,0:T(4,128)}, u32[]{:S(2)}) copy-start(f32[3,3,1024]{2,1,0:T(4,128)} %filt.1) | copy-start | bytes 110596
  41.8 4.2 %copy-start.6 = (f32[1024]{0:T(1024)S(1)}, f32[1024]{0:T(1024)}, u32[]{:S(2)}) copy-start(f32[1024]{0:T(1024)} %param.14) | copy-start | bytes 12292
  49.6 14.8 %collective-permute-start.15 = (bf16[1,2,1024,128]{3,2,1,0:T(8,128)(2,1)S(1)}, bf16[1,2,1024,128]{3,2,1,0:T(8,128)(2,1)S(1)}, u32[]{:S(2)}, u32[]{:S(2)}) collective-permute-start(bf16[1,2,1024,128]{3,2,1,0:T(8,128)(2,1)S(1)} %collective-permute-done.8.refs_0_), channel_id=1, source_target_pairs={{0,2},{2,4},{4,6},{6,7},{7,5},{5,3},{3,1},{1,0},{8,10},{10,12},{12... | collective-permute-start | bytes 1572872 | tf_op jit(solution)/shard_map/ppermute | solution.py:446
  51.2 15.3 %collective-permute-start.16 = (bf16[1,2,1024,128]{3,2,1,0:T(8,128)(2,1)S(1)}, bf16[1,2,1024,128]{3,2,1,0:T(8,128)(2,1)S(1)}, u32[]{:S(2)}, u32[]{:S(2)}) collective-permute-start(bf16[1,2,1024,128]{3,2,1,0:T(8,128)(2,1)S(1)} %collective-permute-done.9.refs_1_.refs_0_), channel_id=1, source_target_pairs={{0,1},{2,0},{4,2},{6,4},{7,6},{5,7},{3,5},{1,3},{8,9},{10,8},{12,1... | collective-permute-start | bytes 1572872 | tf_op jit(solution)/shard_map/ppermute | solution.py:449
  56.1 16.6 %collective-permute-start.19 = (bf16[1,1,512,128]{3,2,1,0:T(8,128)(2,1)S(1)}, bf16[1,1,512,128]{3,2,1,0:T(8,128)(2,1)S(1)}, u32[]{:S(2)}, u32[]{:S(2)}) collective-permute-start(bf16[1,1,512,128]{3,2,1,0:T(8,128)(2,1)S(1)} %slice.20), channel_id=1, source_target_pairs={{0,2},{2,4},{4,6},{6,7},{7,5},{5,3},{3,1},{1,0},{8,10},{10,12},{12... | collective-permute-start | bytes 393224 | tf_op jit(solution)/shard_map/ppermute | solution.py:446
  57.7 15.0 %collective-permute-start.20 = (bf16[1,1,512,128]{3,2,1,0:T(8,128)(2,1)S(1)}, bf16[1,1,512,128]{3,2,1,0:T(8,128)(2,1)S(1)}, u32[]{:S(2)}, u32[]{:S(2)}) collective-permute-start(bf16[1,1,512,128]{3,2,1,0:T(8,128)(2,1)S(1)} %slice.21), channel_id=1, source_target_pairs={{0,1},{2,0},{4,2},{6,4},{7,6},{5,7},{3,5},{1,3},{8,9},{10,8},{12,1... | collective-permute-start | bytes 393224 | tf_op jit(solution)/shard_map/ppermute | solution.py:449
  66.5 8.8 %collective-permute-start.17 = (bf16[1,1,1024,128]{3,2,1,0:T(8,128)(2,1)S(1)}, bf16[1,1,1024,128]{3,2,1,0:T(8,128)(2,1)S(1)}, u32[]{:S(2)}, u32[]{:S(2)}) collective-permute-start(bf16[1,1,1024,128]{3,2,1,0:T(8,128)(2,1)S(1)} %slice.18), channel_id=1, source_target_pairs={{0,1},{2,0},{4,2},{6,4},{7,6},{5,7},{3,5},{1,3},{8,9},{10,8},{12,1... | collective-permute-start | bytes 786440 | tf_op jit(solution)/shard_map/ppermute | solution.py:449
  66.6 8.0 %collective-permute-start.18 = (bf16[1,1,1024,128]{3,2,1,0:T(8,128)(2,1)S(1)}, bf16[1,1,1024,128]{3,2,1,0:T(8,128)(2,1)S(1)}, u32[]{:S(2)}, u32[]{:S(2)}) collective-permute-start(bf16[1,1,1024,128]{3,2,1,0:T(8,128)(2,1)S(1)} %slice.19), channel_id=1, source_target_pairs={{0,2},{2,4},{4,6},{6,7},{7,5},{5,3},{3,1},{1,0},{8,10},{10,12},{12... | collective-permute-start | bytes 786440 | tf_op jit(solution)/shard_map/ppermute | solution.py:446
  (4 other events, 16.7 us)

commit v12 on v11

--- a/solution.py
+++ b/solution.py
@@ -246,7 +246,7 @@
 
 def state_kernel(spans, plan, ring, feat, og, filt, bias, tables, *refs):
     later = len(spans)
-    payloads = refs[:later]
+    payloads = refs[:later][::-1]
     w_proj, rounded, sums, gp, ready, acc, prod, first_ext, second_ext, sems = refs[later:]
     exts = first_ext, second_ext
     moves = fetches(plan, ring, w_proj, ready, sems)
@@ -339,7 +339,7 @@
         compiler_params=params(),
         cost_estimate=cost(4 << 30, 16 << 20),
         name="state_streams",
-    )(feat, og, filt, bias, tables, *payloads, w_proj)
+    )(feat, og, filt, bias, tables, *reversed(payloads), w_proj)
 
 
 def product_kernel(plan, base, later, first, last, ring, w_proj, w, *refs):
@@ -523,8 +523,10 @@
         sums = exchanged(sums, by)
     total, ready = times(0, None, ready, a0=a0, a1=a1, z1=z1)
     total, ready = times(1, total, ready, b0=b0)
-    b1, y1, total, sums = lax.optimization_barrier((b1, y1, total, sums))
-    b2, y2 = up(b1), down(y1)
+    b1, total, sums = lax.optimization_barrier((b1, total, sums))
+    b2 = up(b1)
+    y1, total = lax.optimization_barrier((y1, total))
+    y2 = down(y1)
     total, ready = times(2, total, ready, b1=b1, y1=y1)
 
     a2, z2, total, sums = lax.optimization_barrier((a2, z2, total, sums))
@@ -534,23 +536,27 @@
     total, ready = times(3, total, ready, a2=a2, z2=z2)
     grads = gradients(features, saved_conv, out_grad, short_filter, bias[None], payloads[0], after(gp, total))
 
-    b2, y2, total, sums, grads = lax.optimization_barrier((b2, y2, total, sums, grads))
-    b3, y3 = up(b2), down(y2)
+    b2, total, sums, grads = lax.optimization_barrier((b2, total, sums, grads))
+    b3 = up(b2)
+    y2, total = lax.optimization_barrier((y2, total))
+    y3 = down(y2)
     total, ready = times(4, total, ready, b2=b2, y2=y2)
 
     a3, z3, total = lax.optimization_barrier((a3, z3, total))
     a4 = up(a3[:, :, :half]), down(z3[:, :, half:])
     total, ready = times(5, total, ready, y2=y2, a3=a3, z3=z3)
 
-    b3, y3, total, sums = lax.optimization_barrier((b3, y3, total, sums))
-    b4, y4 = up(b3[:, :1]), down(y3[:, 1:])
-    total, ready = times(6, total, ready, b3=b3, y3=y3)
-
-    a4, total, sums = lax.optimization_barrier((a4, total, sums))
-    (total,) = times(7, total, ready, a4=a4)
     sums = sums * (tokens * blocks) ** (-0.5)
     grad_residue, grad_bias = sums[:modes].T, sums[modes]
-    b4, total, grad_residue, grad_bias = lax.optimization_barrier((b4, total, grad_residue, grad_bias))
+    b3, total, grad_residue, grad_bias = lax.optimization_barrier((b3, total, grad_residue, grad_bias))
+    b4 = up(b3[:, :1])
+    y3, total = lax.optimization_barrier((y3, total))
+    y4 = down(y3[:, 1:])
+    total, ready = times(6, total, ready, b3=b3, y3=y3)
+
+    a4, total = lax.optimization_barrier((a4, total))
+    (total,) = times(7, total, ready, a4=a4)
+    b4, total = lax.optimization_barrier((b4, total))
     (total,) = times(8, total, ready, b4=b4)
     (grad_x,) = times(9, total, ready, y4=y4)
     return (grads, grad_x, grad_residue, grad_bias)

time: 77.3 us -> 76.7 us (level)
  waiting for transfers between devices: 10.1 us -> 8.72 us
    ppermute x8, waiting for transfers between devices: 1.08 us -> 0.02 us  [up(): return lax.ppermute(x, 'chan', pairs[1])]
    ppermute x8, starting transfers between devices: 2.36 us -> 3.29 us  [down(): return lax.ppermute(x, 'chan', pairs[-1])]
where the time goes in v12:
time: 76.7 us; the launch traced here: 76.5 us
  Pallas kernels  41.6 us (54%)
  starting transfers between devices  23.7 us (31%)
  waiting for transfers between devices  8.72 us (11%)
  local copies, waits for them, and re-layouts  1.32 us (2%)
  between operations  1.12 us (1%)
    pallas_call x10, Pallas kernels, add_product(): pl.pallas_call(functools.partial(product_kernel, plan, base, later, first...  34.2 us
    ppermute x8, starting transfers between devices, up(): return lax.ppermute(x, 'chan', pairs[1])  14.9 us
    ppermute x8, waiting for transfers between devices, down(): return lax.ppermute(x, 'chan', pairs[-1])  6.35 us
    ppermute x3, starting transfers between devices, from_later(): return lax.ppermute(array, 'ctx', [(i, i - by) for i in range(by, blocks)])  3.88 us
    ppermute x8, starting transfers between devices, down(): return lax.ppermute(x, 'chan', pairs[-1])  3.29 us
    pallas_call x1, Pallas kernels, state_streams(): pl.pallas_call(functools.partial(state_kernel, spans, plan, ring), in_spe...  2.96 us
    ppermute x3, waiting for transfers between devices, from_later(): return lax.ppermute(array, 'ctx', [(i, i - by) for i in range(by, blocks)])  2.34 us
    pallas_call x1, Pallas kernels, front(): pl.pallas_call(front_kernel, in_specs=[in_hbm()] * 7, out_specs=[whole()]...  2.11 us
  transfers between devices with their start and end apart: 21, of which 7 were waited for; matrix products, arithmetic and copies ran while one was open for 2% of the time, Pallas kernels for 49%

profile of v12, /device:TPU:0, one launch (start us, length us, event | category | flops | bytes accessed | tf_op | source)
XLA Modules:
  0.0 76.5 jit_solution(2300081931069726405)
XLA Ops:
  0.6 2.1 %front.1 = (f32[3,128,1024]{2,1,0:T(8,128)S(1)}, f32[128,1024]{1,0:T(8,128)S(1)}, f32[128,1024]{1,0:T(8,128)S(1)}, f32[3,3,1024]{2,1,0:T(4,128)S(1)}, f32[1,1024...) custom-call(f32[3,128,1024]{2,1,0:T(8,128)} %feat.1, ...), custom_call_target="tpu_custom_call" | custom-call | flops 8388608 | bytes 2621440 | tf_op jit(solution)/shard_map/front/pallas_call | solution.py:96
  2.8 1.3 %collective-permute-start.2 = (f32[224,128]{1,0:T(8,128)S(1)}, f32[224,128]{1,0:T(8,128)S(1)}, u32[]{:S(2)}, u32[]{:S(2)}) collective-permute-start(f32[224,128]{1,0:T(8,128)S(1)} %get-tuple-element.72), channel_id=1, source_target_pairs={{8,0},{16,8},{24,16},{9,1},{17,9},{25,17},{10,2},{18,10},{26,18},{... | collective-permute-start | bytes 344072 | tf_op jit(solution)/shard_map/ppermute | solution.py:458
  4.1 1.3 %collective-permute-start = (f32[144,128]{1,0:T(8,128)S(1)}, f32[144,128]{1,0:T(8,128)S(1)}, u32[]{:S(2)}, u32[]{:S(2)}) collective-permute-start(f32[144,128]{1,0:T(8,128)S(1)} %get-tuple-element.71), channel_id=1, source_target_pairs={{24,0},{25,1},{26,2},{27,3},{28,4},{29,5},{30,6},{31,7}} | collective-permute-start | bytes 221192 | tf_op jit(solution)/shard_map/ppermute | solution.py:458
  5.4 1.3 %collective-permute-start.1 = (f32[144,128]{1,0:T(8,128)S(1)}, f32[144,128]{1,0:T(8,128)S(1)}, u32[]{:S(2)}, u32[]{:S(2)}) collective-permute-start(f32[144,128]{1,0:T(8,128)S(1)} %get-tuple-element.71), channel_id=1, source_target_pairs={{16,0},{24,8},{17,1},{25,9},{18,2},{26,10},{19,3},{27,11},{20,4},{... | collective-permute-start | bytes 221192 | tf_op jit(solution)/shard_map/ppermute | solution.py:458
  7.0 3.1 %collective-permute-start.4 = (bf16[1,1,1024,128]{3,2,1,0:T(8,128)(2,1)S(1)}, bf16[1,1,1024,128]{3,2,1,0:T(8,128)(2,1)}, u32[]{:S(2)}, u32[]{:S(2)}) collective-permute-start(bf16[1,1,1024,128]{3,2,1,0:T(8,128)(2,1)S(1)} %bitcast.15), channel_id=1, source_target_pairs={{0,2},{2,4},{4,6},{6,7},{7,5},{5,3},{3,1},{1,0},{8,10},{10,12},{12... | collective-permute-start | bytes 786440 | tf_op jit(solution)/shard_map/ppermute | solution.py:446
  12.5 3.0 %state_streams.1 = (bf16[2,1024,128]{2,1,0:T(8,128)(2,1)S(1)}, f32[17,1024]{1,0:T(8,128)S(1)}, f32[1040,128]{1,0:T(8,128)S(1)}, bf16[1024,3072]{1,0:T(8,128)(2,1)S(1)}) custom-call(f32[3,128,1024]{2,1,0:T(8,128)S(1)} %get-tuple-element.66.feat, f32[128,1024]{1,0:T(8,128)S(1)} %get-tuple-element.67.og, f32[3,3,1024]{2,1,0:T(4,128)S(1)} %get-tuple-element.68.filt, ...), custom_call_target="tpu_custom_call" | custom-call | flops 4294967296 | bytes 16777216 | tf_op jit(solution)/shard_map/state_streams/pallas_call | solution.py:326
  15.4 2.5 %collective-permute-start.3 = (bf16[1,2,1024,128]{3,2,1,0:T(8,128)(2,1)S(1)}, bf16[1,2,1024,128]{3,2,1,0:T(8,128)(2,1)S(1)}, u32[]{:S(2)}, u32[]{:S(2)}) collective-permute-start(bf16[1,2,1024,128]{3,2,1,0:T(8,128)(2,1)S(1)} %bitcast.12), channel_id=1, source_target_pairs={{0,2},{2,4},{4,6},{6,7},{7,5},{5,3},{3,1},{1,0},{8,10},{10,12},{12... | collective-permute-start | bytes 1572872 | tf_op jit(solution)/shard_map/ppermute | solution.py:446
  21.2 4.9 %add_product.10 = (f32[1024,128]{1,0:T(8,128)S(1)}, bf16[1024,2048]{1,0:T(8,128)(2,1)S(1)}) custom-call(bf16[3,1024,8192]{2,1,0:T(8,128)(2,1)} %w_proj.19, bf16[1024,3072]{1,0:T(8,128)(2,1)S(1)} %get-tuple-element.76.w, bf16[1,1,1024,128]{3,2,1,0:T(8,128)(2,1)S(1)} %bitcast.17, bf16[1,1,1024,128]{3,2,1,0:T(8,128)(2,1)} %collective-permute-done.4.refs_1_, ...), custom_call_target="tpu_custom_call" | custom-call | flops 68719476736 | bytes 268435456 | tf_op jit(solution)/shard_map/add_product/pallas_call | solution.py:406
  26.2 4.7 %add_product.11 = (f32[1024,128]{1,0:T(8,128)S(1)}, bf16[1024,4096]{1,0:T(8,128)(2,1)S(1)}) custom-call(bf16[3,1024,8192]{2,1,0:T(8,128)(2,1)} %w_proj.19, bf16[1024,2048]{1,0:T(8,128)(2,1)S(1)} %get-tuple-element.81.w, bf16[1,2,1024,128]{3,2,1,0:T(8,128)(2,1)S(1)} %bitcast.14, f32[1024,128]{1,0:T(8,128)S(1)} %get-tuple-element.83.refs_1_), custom_call_target="tpu_custom_call" | custom-call | flops 68719476736 | bytes 268435456 | tf_op jit(solution)/shard_map/add_product/pallas_call | solution.py:406
  30.9 1.9 %collective-permute-done.8.refs_1_ = bf16[1,2,1024,128]{3,2,1,0:T(8,128)(2,1)S(1)} collective-permute-done((bf16[1,2,1024,128]{3,2,1,0:T(8,128)(2,1)S(1)}, bf16[1,2,1024,128]{3,2,1,0:T(8,128)(2,1)S(1)}, u32[]{:S(2)}, u32[]{:S(2)}) %collective-permute-start.8) | collective-permute-done | bytes 524320 | tf_op jit(solution)/shard_map/ppermute | solution.py:449
  32.8 1.6 %collective-permute-start.7 = (bf16[1,2,1024,128]{3,2,1,0:T(8,128)(2,1)S(1)}, bf16[1,2,1024,128]{3,2,1,0:T(8,128)(2,1)S(1)}, u32[]{:S(2)}, u32[]{:S(2)}) collective-permute-start(bf16[1,2,1024,128]{3,2,1,0:T(8,128)(2,1)S(1)} %collective-permute-done.3.refs_0_), channel_id=1, source_target_pairs={{0,2},{2,4},{4,6},{6,7},{7,5},{5,3},{3,1},{1,0},{8,10},{10,12},{12... | collective-permute-start | bytes 1572872 | tf_op jit(solution)/shard_map/ppermute | solution.py:446
  34.8 4.2 %add_product.12 = (f32[1024,128]{1,0:T(8,128)S(1)}, bf16[1024,2048]{1,0:T(8,128)(2,1)S(1)}) custom-call(bf16[3,1024,8192]{2,1,0:T(8,128)(2,1)} %w_proj.19, bf16[1024,4096]{1,0:T(8,128)(2,1)S(1)} %get-tuple-element.87.w, bf16[1,2,1024,128]{3,2,1,0:T(8,128)(2,1)S(1)} %collective-permute-done.3.refs_0_, ...), custom_call_target="tpu_custom_call" | custom-call | flops 65536 | bytes 256 | tf_op jit(solution)/shard_map/add_product/pallas_call | solution.py:406
  40.1 1.6 %collective-permute-start.13 = (bf16[1,1,1024,128]{3,2,1,0:T(8,128)(2,1)}, bf16[1,1,1024,128]{3,2,1,0:T(8,128)(2,1)S(1)}, u32[]{:S(2)}, u32[]{:S(2)}) collective-permute-start(bf16[1,1,1024,128]{3,2,1,0:T(8,128)(2,1)} %collective-permute-done.9.refs_0_), channel_id=1, source_target_pairs={{0,2},{2,4},{4,6},{6,7},{7,5},{5,3},{3,1},{1,0},{8,10},{10,12},{12... | collective-permute-start | bytes 786440 | tf_op jit(solution)/shard_map/ppermute | solution.py:446
  42.2 4.1 %add_product.13 = (f32[1024,128]{1,0:T(8,128)S(1)}, bf16[1024,3072]{1,0:T(8,128)(2,1)S(1)}) custom-call(bf16[3,1024,8192]{2,1,0:T(8,128)(2,1)} %w_proj.19, bf16[1024,2048]{1,0:T(8,128)(2,1)S(1)} %get-tuple-element.91.w, bf16[1,1,1024,128]{3,2,1,0:T(8,128)(2,1)} %collective-permute-done.9.refs_0_, bf16[1,1,1024,128]{3,2,1,0:T(8,128)(2,1)} %collective-permute-done.10.refs_1_, ...), custom_call_target="tpu_custom_call" | custom-call | flops 68719476736 | bytes 268435456 | tf_op jit(solution)/shard_map/add_product/pallas_call | solution.py:406
  46.3 1.9 %gradients.1 = f32[3,128,1024]{2,1,0:T(8,128)} custom-call(f32[3,128,1024]{2,1,0:T(8,128)S(1)} %copy-done, f32[128,1024]{1,0:T(8,128)S(1)} %copy-done.1, f32[128,1024]{1,0:T(8,128)S(1)} %copy-done.2, f32[3,3,1024]{2,1,0:T(4,128)S(1)} %copy-done.5, f32[1,1024]{1,0:T(1,128)S(1)} %bitcast.10, f32[224,128]{1,0:T(8,128)S(1)} %copy-done.4, ...), custom_call_target="tpu_custom_call" | custom-call | flops 3932160 | bytes 5242880 | tf_op jit(solution)/shard_map/gradients/pallas_call | solution.py:217
  48.3 1.4 %collective-permute-done.12.refs_1_.refs_0_ = bf16[1,2,1024,128]{3,2,1,0:T(8,128)(2,1)S(1)} collective-permute-done((bf16[1,2,1024,128]{3,2,1,0:T(8,128)(2,1)S(1)}, bf16[1,2,1024,128]{3,2,1,0:T(8,128)(2,1)S(1)}, u32[]{:S(2)}, u32[]{:S(2)}) %collective-permute-start.12) | collective-permute-done | bytes 524320 | tf_op jit(solution)/shard_map/ppermute | solution.py:449
  49.7 1.6 %collective-permute-start.15 = (bf16[1,2,1024,128]{3,2,1,0:T(8,128)(2,1)S(1)}, bf16[1,2,1024,128]{3,2,1,0:T(8,128)(2,1)S(1)}, u32[]{:S(2)}, u32[]{:S(2)}) collective-permute-start(bf16[1,2,1024,128]{3,2,1,0:T(8,128)(2,1)S(1)} %collective-permute-done.7.refs_0_), channel_id=1, source_target_pairs={{0,2},{2,4},{4,6},{6,7},{7,5},{5,3},{3,1},{1,0},{8,10},{10,12},{12... | collective-permute-start | bytes 1572872 | tf_op jit(solution)/shard_map/ppermute | solution.py:446
  51.7 4.3 %add_product.14 = (f32[1024,128]{1,0:T(8,128)S(1)}, bf16[1024,3072]{1,0:T(8,128)(2,1)S(1)}) custom-call(bf16[3,1024,8192]{2,1,0:T(8,128)(2,1)} %w_proj.19, bf16[1024,3072]{1,0:T(8,128)(2,1)S(1)} %get-tuple-element.102.w, bf16[1,2,1024,128]{3,2,1,0:T(8,128)(2,1)S(1)} %collective-permute-done.7.refs_0_, ...), custom_call_target="tpu_custom_call" | custom-call | flops 65536 | bytes 256 | tf_op jit(solution)/shard_map/add_product/pallas_call | solution.py:406
  56.1 1.6 %collective-permute-start.19 = (bf16[1,1,512,128]{3,2,1,0:T(8,128)(2,1)S(1)}, bf16[1,1,512,128]{3,2,1,0:T(8,128)(2,1)S(1)}, u32[]{:S(2)}, u32[]{:S(2)}) collective-permute-start(bf16[1,1,512,128]{3,2,1,0:T(8,128)(2,1)S(1)} %slice.22), channel_id=1, source_target_pairs={{0,2},{2,4},{4,6},{6,7},{7,5},{5,3},{3,1},{1,0},{8,10},{10,12},{12... | collective-permute-start | bytes 393224 | tf_op jit(solution)/shard_map/ppermute | solution.py:446
  58.2 5.2 %add_product.15 = (f32[1024,128]{1,0:T(8,128)S(1)}, bf16[1024,4096]{1,0:T(8,128)(2,1)S(1)}) custom-call(bf16[3,1024,8192]{2,1,0:T(8,128)(2,1)} %w_proj.19, bf16[1024,3072]{1,0:T(8,128)(2,1)S(1)} %get-tuple-element.107.w, bf16[1,2,1024,128]{3,2,1,0:T(8,128)(2,1)S(1)} %collective-permute-done.12.refs_1_.refs_0_, ...), custom_call_target="tpu_custom_call" | custom-call | flops 68719476736 | bytes 268435456 | tf_op jit(solution)/shard_map/add_product/pallas_call | solution.py:406
  64.7 1.8 %collective-permute-done.16.refs_1_ = bf16[1,2,1024,128]{3,2,1,0:T(8,128)(2,1)S(1)} collective-permute-done((bf16[1,2,1024,128]{3,2,1,0:T(8,128)(2,1)S(1)}, bf16[1,2,1024,128]{3,2,1,0:T(8,128)(2,1)S(1)}, u32[]{:S(2)}, u32[]{:S(2)}) %collective-permute-start.16) | collective-permute-done | bytes 524320 | tf_op jit(solution)/shard_map/ppermute | solution.py:449
  66.5 1.6 %collective-permute-start.18 = (bf16[1,1,1024,128]{3,2,1,0:T(8,128)(2,1)S(1)}, bf16[1,1,1024,128]{3,2,1,0:T(8,128)(2,1)S(1)}, u32[]{:S(2)}, u32[]{:S(2)}) collective-permute-start(bf16[1,1,1024,128]{3,2,1,0:T(8,128)(2,1)S(1)} %slice.21), channel_id=1, source_target_pairs={{0,2},{2,4},{4,6},{6,7},{7,5},{5,3},{3,1},{1,0},{8,10},{10,12},{12... | collective-permute-start | bytes 786440 | tf_op jit(solution)/shard_map/ppermute | solution.py:446
  68.8 3.8 %add_product.16 = (f32[1024,128]{1,0:T(8,128)S(1)}, bf16[1024,3072]{1,0:T(8,128)(2,1)S(1)}) custom-call(bf16[3,1024,8192]{2,1,0:T(8,128)(2,1)} %w_proj.19, bf16[1024,4096]{1,0:T(8,128)(2,1)S(1)} %get-tuple-element.112.w, bf16[1,2,1024,128]{3,2,1,0:T(8,128)(2,1)S(1)} %collective-permute-done.15.refs_0_, ...), custom_call_target="tpu_custom_call" | custom-call | flops 1073741824 | bytes 9437184 | tf_op jit(solution)/shard_map/add_product/pallas_call | solution.py:406
  74.7 1.6 %add_product.19 = f32[128,1024]{1,0:T(8,128)} custom-call(bf16[3,1024,8192]{2,1,0:T(8,128)(2,1)} %w_proj.19, bf16[1024,3072]{1,0:T(8,128)(2,1)S(1)} %get-tuple-element.119.w, bf16[1,1,1024,128]{3,2,1,0:T(8,128)(2,1)S(1)} %collective-permute-done.17.refs_0_, f32[1024,128]{1,0:T(8,128)S(1)} %add_product.18.refs_1_), custom_call_target="tpu_custom_call" | custom-call | flops 65536 | bytes 256 | tf_op jit(solution)/shard_map/add_product/pallas_call | solution.py:406
  (55 shorter events, 13.0 us)
Async XLA Ops:
  2.8 3.9 %collective-permute-start.2 = (f32[224,128]{1,0:T(8,128)S(1)}, f32[224,128]{1,0:T(8,128)S(1)}, u32[]{:S(2)}, u32[]{:S(2)}) collective-permute-start(f32[224,128]{1,0:T(8,128)S(1)} %get-tuple-element.72), channel_id=1, source_target_pairs={{8,0},{16,8},{24,16},{9,1},{17,9},{25,17},{10,2},{18,10},{26,18},{... | collective-permute-start | bytes 344072 | tf_op jit(solution)/shard_map/ppermute | solution.py:458
  4.1 7.2 %collective-permute-start = (f32[144,128]{1,0:T(8,128)S(1)}, f32[144,128]{1,0:T(8,128)S(1)}, u32[]{:S(2)}, u32[]{:S(2)}) collective-permute-start(f32[144,128]{1,0:T(8,128)S(1)} %get-tuple-element.71), channel_id=1, source_target_pairs={{24,0},{25,1},{26,2},{27,3},{28,4},{29,5},{30,6},{31,7}} | collective-permute-start | bytes 221192 | tf_op jit(solution)/shard_map/ppermute | solution.py:458
  5.4 7.1 %collective-permute-start.1 = (f32[144,128]{1,0:T(8,128)S(1)}, f32[144,128]{1,0:T(8,128)S(1)}, u32[]{:S(2)}, u32[]{:S(2)}) collective-permute-start(f32[144,128]{1,0:T(8,128)S(1)} %get-tuple-element.71), channel_id=1, source_target_pairs={{16,0},{24,8},{17,1},{25,9},{18,2},{26,10},{19,3},{27,11},{20,4},{... | collective-permute-start | bytes 221192 | tf_op jit(solution)/shard_map/ppermute | solution.py:458
  6.7 5.8 %copy-start.3 = (f32[224,128]{1,0:T(8,128)}, f32[224,128]{1,0:T(8,128)S(1)}, u32[]{:S(2)}) copy-start(f32[224,128]{1,0:T(8,128)S(1)} %collective-permute-done.2.later.refs_2_) | copy-start | bytes 344068
  7.0 10.9 %collective-permute-start.4 = (bf16[1,1,1024,128]{3,2,1,0:T(8,128)(2,1)S(1)}, bf16[1,1,1024,128]{3,2,1,0:T(8,128)(2,1)}, u32[]{:S(2)}, u32[]{:S(2)}) collective-permute-start(bf16[1,1,1024,128]{3,2,1,0:T(8,128)(2,1)S(1)} %bitcast.15), channel_id=1, source_target_pairs={{0,2},{2,4},{4,6},{6,7},{7,5},{5,3},{3,1},{1,0},{8,10},{10,12},{12... | collective-permute-start | bytes 786440 | tf_op jit(solution)/shard_map/ppermute | solution.py:446
  10.1 8.5 %collective-permute-start.5 = (bf16[1,1,1024,128]{3,2,1,0:T(8,128)(2,1)S(1)}, bf16[1,1,1024,128]{3,2,1,0:T(8,128)(2,1)}, u32[]{:S(2)}, u32[]{:S(2)}) collective-permute-start(bf16[1,1,1024,128]{3,2,1,0:T(8,128)(2,1)S(1)} %bitcast.16), channel_id=1, source_target_pairs={{0,1},{2,0},{4,2},{6,4},{7,6},{5,7},{3,5},{1,3},{8,9},{10,8},{12,1... | collective-permute-start | bytes 786440 | tf_op jit(solution)/shard_map/ppermute | solution.py:449
  15.4 15.5 %collective-permute-start.3 = (bf16[1,2,1024,128]{3,2,1,0:T(8,128)(2,1)S(1)}, bf16[1,2,1024,128]{3,2,1,0:T(8,128)(2,1)S(1)}, u32[]{:S(2)}, u32[]{:S(2)}) collective-permute-start(bf16[1,2,1024,128]{3,2,1,0:T(8,128)(2,1)S(1)} %bitcast.12), channel_id=1, source_target_pairs={{0,2},{2,4},{4,6},{6,7},{7,5},{5,3},{3,1},{1,0},{8,10},{10,12},{12... | collective-permute-start | bytes 1572872 | tf_op jit(solution)/shard_map/ppermute | solution.py:446
  18.0 14.9 %collective-permute-start.8 = (bf16[1,2,1024,128]{3,2,1,0:T(8,128)(2,1)S(1)}, bf16[1,2,1024,128]{3,2,1,0:T(8,128)(2,1)S(1)}, u32[]{:S(2)}, u32[]{:S(2)}) collective-permute-start(bf16[1,2,1024,128]{3,2,1,0:T(8,128)(2,1)S(1)} %bitcast.13), channel_id=1, source_target_pairs={{0,1},{2,0},{4,2},{6,4},{7,6},{5,7},{3,5},{1,3},{8,9},{10,8},{12,1... | collective-permute-start | bytes 1572872 | tf_op jit(solution)/shard_map/ppermute | solution.py:449
  18.6 12.3 %collective-permute-start.6 = (f32[17,1024]{1,0:T(8,128)S(1)}, f32[17,1024]{1,0:T(8,128)S(1)}, u32[]{:S(2)}, u32[]{:S(2)}) collective-permute-start(f32[17,1024]{1,0:T(8,128)S(1)} %get-tuple-element.85), channel_id=1, source_target_pairs={{0,8},{8,0},{16,24},{24,16},{1,9},{9,1},{17,25},{25,17},{2,10},{10... | collective-permute-start | bytes 208904 | tf_op jit(solution)/shard_map/ppermute | solution.py:461
  19.2 19.9 %collective-permute-start.10 = (bf16[1,1,1024,128]{3,2,1,0:T(8,128)(2,1)}, bf16[1,1,1024,128]{3,2,1,0:T(8,128)(2,1)}, u32[]{:S(2)}, u32[]{:S(2)}) collective-permute-start(bf16[1,1,1024,128]{3,2,1,0:T(8,128)(2,1)} %collective-permute-done.5.refs_2_), channel_id=1, source_target_pairs={{0,1},{2,0},{4,2},{6,4},{7,6},{5,7},{3,5},{1,3},{8,9},{10,8},{12,1... | collective-permute-start | bytes 786440 | tf_op jit(solution)/shard_map/ppermute | solution.py:449
  20.0 19.1 %collective-permute-start.9 = (bf16[1,1,1024,128]{3,2,1,0:T(8,128)(2,1)}, bf16[1,1,1024,128]{3,2,1,0:T(8,128)(2,1)}, u32[]{:S(2)}, u32[]{:S(2)}) collective-permute-start(bf16[1,1,1024,128]{3,2,1,0:T(8,128)(2,1)} %collective-permute-done.4.refs_1_), channel_id=1, source_target_pairs={{0,2},{2,4},{4,6},{6,7},{7,5},{5,3},{3,1},{1,0},{8,10},{10,12},{12... | collective-permute-start | bytes 786440 | tf_op jit(solution)/shard_map/ppermute | solution.py:446
  32.8 15.5 %collective-permute-start.7 = (bf16[1,2,1024,128]{3,2,1,0:T(8,128)(2,1)S(1)}, bf16[1,2,1024,128]{3,2,1,0:T(8,128)(2,1)S(1)}, u32[]{:S(2)}, u32[]{:S(2)}) collective-permute-start(bf16[1,2,1024,128]{3,2,1,0:T(8,128)(2,1)S(1)} %collective-permute-done.3.refs_0_), channel_id=1, source_target_pairs={{0,2},{2,4},{4,6},{6,7},{7,5},{5,3},{3,1},{1,0},{8,10},{10,12},{12... | collective-permute-start | bytes 1572872 | tf_op jit(solution)/shard_map/ppermute | solution.py:446
  34.4 15.3 %collective-permute-start.12 = (bf16[1,2,1024,128]{3,2,1,0:T(8,128)(2,1)S(1)}, bf16[1,2,1024,128]{3,2,1,0:T(8,128)(2,1)S(1)}, u32[]{:S(2)}, u32[]{:S(2)}) collective-permute-start(bf16[1,2,1024,128]{3,2,1,0:T(8,128)(2,1)S(1)} %collective-permute-done.8.refs_1_), channel_id=1, source_target_pairs={{0,1},{2,0},{4,2},{6,4},{7,6},{5,7},{3,5},{1,3},{8,9},{10,8},{12,1... | collective-permute-start | bytes 1572872 | tf_op jit(solution)/shard_map/ppermute | solution.py:449
  39.1 9.2 %collective-permute-start.11 = (f32[17,1024]{1,0:T(8,128)S(1)}, f32[17,1024]{1,0:T(8,128)S(1)}, u32[]{:S(2)}, u32[]{:S(2)}) collective-permute-start(f32[17,1024]{1,0:T(8,128)S(1)} %add.6), channel_id=1, source_target_pairs={{0,16},{8,24},{16,0},{24,8},{1,17},{9,25},{17,1},{25,9},{2,18},{10... | collective-permute-start | bytes 208904 | tf_op jit(solution)/shard_map/ppermute | solution.py:461
  40.1 16.0 %collective-permute-start.13 = (bf16[1,1,1024,128]{3,2,1,0:T(8,128)(2,1)}, bf16[1,1,1024,128]{3,2,1,0:T(8,128)(2,1)S(1)}, u32[]{:S(2)}, u32[]{:S(2)}) collective-permute-start(bf16[1,1,1024,128]{3,2,1,0:T(8,128)(2,1)} %collective-permute-done.9.refs_0_), channel_id=1, source_target_pairs={{0,2},{2,4},{4,6},{6,7},{7,5},{5,3},{3,1},{1,0},{8,10},{10,12},{12... | collective-permute-start | bytes 786440 | tf_op jit(solution)/shard_map/ppermute | solution.py:446
  41.7 14.4 %collective-permute-start.14 = (bf16[1,1,1024,128]{3,2,1,0:T(8,128)(2,1)}, bf16[1,1,1024,128]{3,2,1,0:T(8,128)(2,1)S(1)}, u32[]{:S(2)}, u32[]{:S(2)}) collective-permute-start(bf16[1,1,1024,128]{3,2,1,0:T(8,128)(2,1)} %collective-permute-done.10.refs_1_), channel_id=1, source_target_pairs={{0,1},{2,0},{4,2},{6,4},{7,6},{5,7},{3,5},{1,3},{8,9},{10,8},{12,1... | collective-permute-start | bytes 786440 | tf_op jit(solution)/shard_map/ppermute | solution.py:449
  42.1 4.2 %copy-start.5 = (f32[3,3,1024]{2,1,0:T(4,128)S(1)}, f32[3,3,1024]{2,1,0:T(4,128)}, u32[]{:S(2)}) copy-start(f32[3,3,1024]{2,1,0:T(4,128)} %filt.1) | copy-start | bytes 110596
  42.1 4.2 %copy-start.6 = (f32[1024]{0:T(1024)S(1)}, f32[1024]{0:T(1024)}, u32[]{:S(2)}) copy-start(f32[1024]{0:T(1024)} %param.14) | copy-start | bytes 12292
  49.7 15.0 %collective-permute-start.15 = (bf16[1,2,1024,128]{3,2,1,0:T(8,128)(2,1)S(1)}, bf16[1,2,1024,128]{3,2,1,0:T(8,128)(2,1)S(1)}, u32[]{:S(2)}, u32[]{:S(2)}) collective-permute-start(bf16[1,2,1024,128]{3,2,1,0:T(8,128)(2,1)S(1)} %collective-permute-done.7.refs_0_), channel_id=1, source_target_pairs={{0,2},{2,4},{4,6},{6,7},{7,5},{5,3},{3,1},{1,0},{8,10},{10,12},{12... | collective-permute-start | bytes 1572872 | tf_op jit(solution)/shard_map/ppermute | solution.py:446
  51.2 15.2 %collective-permute-start.16 = (bf16[1,2,1024,128]{3,2,1,0:T(8,128)(2,1)S(1)}, bf16[1,2,1024,128]{3,2,1,0:T(8,128)(2,1)S(1)}, u32[]{:S(2)}, u32[]{:S(2)}) collective-permute-start(bf16[1,2,1024,128]{3,2,1,0:T(8,128)(2,1)S(1)} %collective-permute-done.12.refs_1_.refs_0_), channel_id=1, source_target_pairs={{0,1},{2,0},{4,2},{6,4},{7,6},{5,7},{3,5},{1,3},{8,9},{10,8},{12,1... | collective-permute-start | bytes 1572872 | tf_op jit(solution)/shard_map/ppermute | solution.py:449
  56.1 16.5 %collective-permute-start.19 = (bf16[1,1,512,128]{3,2,1,0:T(8,128)(2,1)S(1)}, bf16[1,1,512,128]{3,2,1,0:T(8,128)(2,1)S(1)}, u32[]{:S(2)}, u32[]{:S(2)}) collective-permute-start(bf16[1,1,512,128]{3,2,1,0:T(8,128)(2,1)S(1)} %slice.22), channel_id=1, source_target_pairs={{0,2},{2,4},{4,6},{6,7},{7,5},{5,3},{3,1},{1,0},{8,10},{10,12},{12... | collective-permute-start | bytes 393224 | tf_op jit(solution)/shard_map/ppermute | solution.py:446
  57.7 14.9 %collective-permute-start.20 = (bf16[1,1,512,128]{3,2,1,0:T(8,128)(2,1)S(1)}, bf16[1,1,512,128]{3,2,1,0:T(8,128)(2,1)S(1)}, u32[]{:S(2)}, u32[]{:S(2)}) collective-permute-start(bf16[1,1,512,128]{3,2,1,0:T(8,128)(2,1)S(1)} %slice.23), channel_id=1, source_target_pairs={{0,1},{2,0},{4,2},{6,4},{7,6},{5,7},{3,5},{1,3},{8,9},{10,8},{12,1... | collective-permute-start | bytes 393224 | tf_op jit(solution)/shard_map/ppermute | solution.py:449
  66.5 6.9 %collective-permute-start.18 = (bf16[1,1,1024,128]{3,2,1,0:T(8,128)(2,1)S(1)}, bf16[1,1,1024,128]{3,2,1,0:T(8,128)(2,1)S(1)}, u32[]{:S(2)}, u32[]{:S(2)}) collective-permute-start(bf16[1,1,1024,128]{3,2,1,0:T(8,128)(2,1)S(1)} %slice.21), channel_id=1, source_target_pairs={{0,2},{2,4},{4,6},{6,7},{7,5},{5,3},{3,1},{1,0},{8,10},{10,12},{12... | collective-permute-start | bytes 786440 | tf_op jit(solution)/shard_map/ppermute | solution.py:446
  68.1 6.6 %collective-permute-start.17 = (bf16[1,1,1024,128]{3,2,1,0:T(8,128)(2,1)S(1)}, bf16[1,1,1024,128]{3,2,1,0:T(8,128)(2,1)S(1)}, u32[]{:S(2)}, u32[]{:S(2)}) collective-permute-start(bf16[1,1,1024,128]{3,2,1,0:T(8,128)(2,1)S(1)} %slice.20), channel_id=1, source_target_pairs={{0,1},{2,0},{4,2},{6,4},{7,6},{5,7},{3,5},{1,3},{8,9},{10,8},{12,1... | collective-permute-start | bytes 786440 | tf_op jit(solution)/shard_map/ppermute | solution.py:449
  (4 other events, 16.7 us)

commit v13 on v9

--- a/solution.py
+++ b/solution.py
@@ -340,12 +340,16 @@
     )(feat, og, filt, bias, tables, *payloads, w_proj)
 
 
-def product_kernel(plan, base, later, first, last, ring, w_proj, w, *refs):
+def product_kernel(plan, parts, laters, first, last, ring, w_proj, *refs):
     refs = list(refs)
     moves = []
-    if later:
+    if laters:
         sems = refs.pop()
-        moves = fetches(later, ring, w_proj, refs.pop(), sems)
+        at = 0
+        for later, target in zip(laters, refs[-len(laters) :]):
+            moves += fetches(later, ring, w_proj, target, sems.at[pl.ds(at, len(later))])
+            at += len(later)
+        del refs[-len(laters) :]
     elif last:
         sems = refs.pop()
         turned = refs.pop()
@@ -353,15 +357,22 @@
     before = None if first else refs.pop()
     for move in moves:
         move.start()
-    x = jnp.concatenate([refs[n][h, p] for *_, parts in plan for n, h, p in parts], axis=0)
-    columns = slice(base * (x.shape[0] // len(plan)), (base + len(plan)) * (x.shape[0] // len(plan)))
-    features = w.shape[0]
+    weights, xs = refs[: len(parts)], refs[len(parts) :]
+    blocks = [[xs[n][h, p] for n, h, p in pieces] for *_, pieces in plan]
+    channels = sum(x.shape[0] for x in blocks[0])
+    features = weights[0].shape[0]
     wide = min(512, features)
     for d in range(0, features, wide):
         rows = slice(d, d + wide)
-        y = jnp.dot(w[rows, columns], x, preferred_element_type=F32)
-        if not first:
-            y = y + before[rows]
+        y = None if first else before[rows]
+        done = 0
+        for w, (begin, count) in zip(weights, parts):
+            x = jnp.concatenate(sum(blocks[done : done + count], []), axis=0)
+            done += count
+            z = jnp.dot(
+                w[rows, begin * channels : (begin + count) * channels], x, preferred_element_type=F32
+            )
+            y = z if y is None else y + z
         if last:
             turned[:, rows] = y.T
             moves.append(pltpu.make_async_copy(
@@ -385,7 +396,7 @@
     return arrays, plan
 
 
-def add_product(total, ready, base, pieces, later, last, ring, w_proj, span):
+def add_product(total, weights, pieces, laters, last, ring, w_proj, span):
     features = w_proj.shape[1]
     arrays, plan = steps_of(pieces)
     channels, tokens = w_proj.shape[2] // lax.axis_size("chan"), arrays[0].shape[3]
@@ -397,21 +408,21 @@
         out_specs = [in_hbm()]
         out_shape = [jax.ShapeDtypeStruct((tokens, features), F32)]
         scratch = [pltpu.VMEM((tokens, features), F32), pltpu.SemaphoreType.DMA((max(1, features // 512),))]
-    elif later:
-        out_specs += [whole()]
-        out_shape += [pltpu.VMEM((features, len(later) * channels), BF16)]
-        scratch = [pltpu.SemaphoreType.DMA((len(later),))]
+    elif laters:
+        out_specs += [whole()] * len(laters)
+        out_shape += [pltpu.VMEM((features, len(later) * channels), BF16) for later in laters]
+        scratch = [pltpu.SemaphoreType.DMA((sum(map(len, laters)),))]
+    parts = [(begin, count) for _, begin, count in weights]
     return pl.pallas_call(
-        functools.partial(product_kernel, plan, base, later, first, last, ring),
-        in_specs=[in_hbm()]
-        + [whole()] * (1 + len(arrays) + (not first)),
+        functools.partial(product_kernel, plan, parts, laters, first, last, ring),
+        in_specs=[in_hbm()] + [whole()] * (len(weights) + len(arrays) + (not first)),
         out_specs=out_specs,
         out_shape=out_shape,
         scratch_shapes=scratch,
         compiler_params=params(),
         cost_estimate=cost(*span),
         name="add_product",
-    )(w_proj, ready, *arrays, *([] if first else [total]))
+    )(w_proj, *(w for w, _, _ in weights), *arrays, *([] if first else [total]))
 
 
 def ring_order(size):
@@ -483,10 +494,10 @@
 
     a, b = (0,), (0, 1)
     sets = [
-        [("a0", a, 0, 0), ("b0", b, 1, 0)],
-        [("a1", a, 0, ring - 1), ("z1", a, 0, 1)],
-        [("b1", b, 1, ring - 1), ("y1", (0,), 1, 1)],
-        [("y1", (1,), 1, 1), ("a2", a, 0, ring - 2), ("z2", a, 0, 2)],
+        [("a0", a, 0, 0), ("a1", a, 0, ring - 1), ("z1", a, 0, 1)],
+        [("b0", b, 1, 0)],
+        [("b1", b, 1, ring - 1), ("y1", b, 1, 1)],
+        [("a2", a, 0, ring - 2), ("z2", a, 0, 2)],
         [("b2", b, 1, ring - 2), ("y2", (0,), 1, 2)],
         [("y2", (1,), 1, 2), ("a3", a, 0, ring - 3), ("z3", a, 0, 3)],
         [("b3", a, 1, ring - 3), ("y3", a, 2, 3), ("c3", a, 2, ring - 3), ("x3", a, 1, 3)],
@@ -499,16 +510,21 @@
     def plan_of(n):
         return steps_of([(hollow, *piece[1:]) for piece in sets[n]])[1]
 
-    def times(n, total, ready, **arrays):
+    plans = [plan_of(n) for n in range(len(sets))]
+    early, late = plans[6][: len(plans[6]) // 2], plans[6][len(plans[6]) // 2 :]
+    laters = [[plan] for plan in plans[1:6]] + [[late], [plans[7] + plans[8]], [], []]
+    laters[1].append(early)
+
+    def times(n, total, weights, **arrays):
         pieces = [(arrays[name], *rest) for name, *rest in sets[n]]
-        after_next = [plan_of(k) for k in range(7, len(sets))]
-        later = plan_of(n + 1) if n < 6 else sum(after_next, []) if n == 6 else None
-        base = sum(len(plan) for plan in after_next[: max(0, n - 7)])
-        return add_product(total, ready, base, pieces, later, n == len(sets) - 1, ring, w_proj, costs[n])
+        return add_product(total, weights, pieces, laters[n], n == len(sets) - 1, ring, w_proj, costs[n])
+
+    def all_of(weights, n):
+        return [(weights, 0, len(plans[n]))]
 
     payloads[0], a0 = lax.optimization_barrier((payloads[0], a0))
     rounds, sums, gp, ready = state_streams(
-        feat, og, filt, bias_row.reshape(fold, LANES), tables, payloads, spans, plan_of(0), ring, w_proj
+        feat, og, filt, bias_row.reshape(fold, LANES), tables, payloads, spans, plans[0], ring, w_proj
     )
     b0 = stacked(rounds)
 
@@ -518,39 +534,41 @@
     distances = [1 << n for n in range((blocks - 1).bit_length())]
     for by in distances[:1]:
         sums = exchanged(sums, by)
-    total, ready = times(0, None, ready, a0=a0, b0=b0)
-    total, ready = times(1, total, ready, a1=a1, z1=z1)
+    total, ready = times(0, None, all_of(ready, 0), a0=a0, a1=a1, z1=z1)
+    total, ready, soon = times(1, total, all_of(ready, 1), b0=b0)
 
     b1, y1, total, sums = lax.optimization_barrier((b1, y1, total, sums))
     b2, y2 = up(b1), down(y1)
-    total, ready = times(2, total, ready, b1=b1, y1=y1)
+    total, ready = times(2, total, all_of(ready, 2), b1=b1, y1=y1)
 
     a2, z2, total, sums = lax.optimization_barrier((a2, z2, total, sums))
     a3, z3 = up(a2), down(z2)
     for by in distances[1:]:
         sums = exchanged(sums, by)
-    total, ready = times(3, total, ready, y1=y1, a2=a2, z2=z2)
+    total, ready = times(3, total, all_of(ready, 3), a2=a2, z2=z2)
     grads = gradients(features, saved_conv, out_grad, short_filter, bias[None], payloads[0], after(gp, total))
 
-    b2, y2, total, sums, grads = lax.optimization_barrier((b2, y2, total, sums, grads))
+    sums = sums * (tokens * blocks) ** (-0.5)
+    outputs = grads, sums[:modes].T, sums[modes]
+    b2, y2, total, outputs = lax.optimization_barrier((b2, y2, total, outputs))
     b3, y3 = up(b2[:, :1]), down(y2[:, 1:])
     c3 = up(b2[:, 1:])
-    total, ready = times(4, total, ready, b2=b2, y2=y2)
+    total, ready = times(4, total, all_of(ready, 4), b2=b2, y2=y2)
     x3 = down(after(y2[:, :1], total))
     a3, z3, total = lax.optimization_barrier((a3, z3, total))
-    total, ready = times(5, total, ready, y2=y2, a3=a3, z3=z3)
-
-    b3, y3, total, sums = lax.optimization_barrier((b3, y3, total, sums))
+    total, ready = times(5, total, all_of(ready, 5), y2=y2, a3=a3, z3=z3)
+
+    b3, y3, total = lax.optimization_barrier((b3, y3, total))
     b4, y4 = up(b3), down(y3)
     a4 = up(a3[:, :, :half]), down(z3[:, :, half:])
-    sums = sums * (tokens * blocks) ** (-0.5)
-    total, ready = times(6, total, ready, b3=b3, y3=y3, c3=c3, x3=x3)
-
-    b4, y4, total, sums = lax.optimization_barrier((b4, y4, total, sums))
-    (total,) = times(7, total, ready, b4=b4, y4=y4)
-    grad_residue, grad_bias = sums[:modes].T, sums[modes]
-    a4, total, grad_residue, grad_bias = lax.optimization_barrier((a4, total, grad_residue, grad_bias))
-    (grad_x,) = times(8, total, ready, a4=a4)
+    weights = [(soon, 0, len(early)), (ready, 0, len(late))]
+    total, ready = times(6, total, weights, b3=b3, y3=y3, c3=c3, x3=x3)
+
+    b4, y4, total = lax.optimization_barrier((b4, y4, total))
+    (total,) = times(7, total, [(ready, 0, len(plans[7]))], b4=b4, y4=y4)
+    a4, total = lax.optimization_barrier((a4, total))
+    (grad_x,) = times(8, total, [(ready, len(plans[7]), len(plans[8]))], a4=a4)
+    grads, grad_residue, grad_bias = outputs
     return (grads, grad_x, grad_residue, grad_bias)
 
 

time: 77.3 us -> 76.5 us (0.990)
  waiting for transfers between devices: 8.77 us -> 3.47 us
  starting transfers between devices: 24.4 us -> 26.9 us
  Pallas kernels: 41.4 us -> 43.4 us
    ppermute x9, starting transfers between devices: 3.25 us -> 16.8 us  [down(): return lax.ppermute(x, 'chan', pairs[-1])]
    ppermute x9, starting transfers between devices: 16.5 us -> 3.3 us  [up(): return lax.ppermute(x, 'chan', pairs[1])]
    ppermute x9, waiting for transfers between devices: 4.59 us -> 0.02 us  [down(): return lax.ppermute(x, 'chan', pairs[-1])]
    ppermute x2, starting transfers between devices: 0.71 us -> 2.9 us  [exchanged(): lax.ppermute(sums, 'ctx', [(i, i ^ by) for i in range(blocks)])]
    pallas_call x9, Pallas kernels: 34.1 us -> 36 us  [add_product(): pl.pallas_call(functools.partial(product_kernel, plan, parts, laters, fir...]
  transfers between devices with their start and end apart: 23 -> 23, of which waited for: 6 -> 4; matrix products, arithmetic and copies ran while one was open for 2% -> 2% of each run, Pallas kernels for 49% -> 52%
where the time goes in v13:
time: 76.5 us; the launch traced here: 76.3 us
  Pallas kernels  43.4 us (57%)
  starting transfers between devices  26.9 us (35%)
  waiting for transfers between devices  3.47 us (5%)
  local copies, waits for them, and re-layouts  1.35 us (2%)
  between operations  1.13 us (1%)
    pallas_call x9, Pallas kernels, add_product(): pl.pallas_call(functools.partial(product_kernel, plan, parts, laters, fir...  36 us
    ppermute x9, starting transfers between devices, down(): return lax.ppermute(x, 'chan', pairs[-1])  16.8 us
    ppermute x3, starting transfers between devices, from_later(): return lax.ppermute(array, 'ctx', [(i, i - by) for i in range(by, blocks)])  3.88 us
    ppermute x9, starting transfers between devices, up(): return lax.ppermute(x, 'chan', pairs[1])  3.3 us
    pallas_call x1, Pallas kernels, state_streams(): pl.pallas_call(functools.partial(state_kernel, spans, plan, ring), in_spe...  2.96 us
    ppermute x2, starting transfers between devices, exchanged(): lax.ppermute(sums, 'ctx', [(i, i ^ by) for i in range(blocks)])  2.9 us
    ppermute x3, waiting for transfers between devices, from_later(): return lax.ppermute(array, 'ctx', [(i, i - by) for i in range(by, blocks)])  2.28 us
    pallas_call x1, Pallas kernels, front(): pl.pallas_call(front_kernel, in_specs=[in_hbm()] * 7, out_specs=[whole()]...  2.11 us
  transfers between devices with their start and end apart: 23, of which 4 were waited for; matrix products, arithmetic and copies ran while one was open for 2% of the time, Pallas kernels for 52%

profile of v13, /device:TPU:0, one launch (start us, length us, event | category | flops | bytes accessed | tf_op | source)
XLA Modules:
  0.0 76.3 jit_solution(3995886954390465595)
XLA Ops:
  0.6 2.1 %front.1 = (f32[3,128,1024]{2,1,0:T(8,128)S(1)}, f32[128,1024]{1,0:T(8,128)S(1)}, f32[128,1024]{1,0:T(8,128)S(1)}, f32[3,3,1024]{2,1,0:T(4,128)S(1)}, f32[1,1024...) custom-call(f32[3,128,1024]{2,1,0:T(8,128)} %feat.1, ...), custom_call_target="tpu_custom_call" | custom-call | flops 8388608 | bytes 2621440 | tf_op jit(solution)/shard_map/front/pallas_call | solution.py:94
  2.8 1.3 %collective-permute-start = (f32[224,128]{1,0:T(8,128)S(1)}, f32[224,128]{1,0:T(8,128)S(1)}, u32[]{:S(2)}, u32[]{:S(2)}) collective-permute-start(f32[224,128]{1,0:T(8,128)S(1)} %get-tuple-element.70), channel_id=1, source_target_pairs={{8,0},{16,8},{24,16},{9,1},{17,9},{25,17},{10,2},{18,10},{26,18},{... | collective-permute-start | bytes 344072 | tf_op jit(solution)/shard_map/ppermute | solution.py:467
  4.1 1.3 %collective-permute-start.2 = (f32[144,128]{1,0:T(8,128)S(1)}, f32[144,128]{1,0:T(8,128)S(1)}, u32[]{:S(2)}, u32[]{:S(2)}) collective-permute-start(f32[144,128]{1,0:T(8,128)S(1)} %get-tuple-element.73), channel_id=1, source_target_pairs={{24,0},{25,1},{26,2},{27,3},{28,4},{29,5},{30,6},{31,7}} | collective-permute-start | bytes 221192 | tf_op jit(solution)/shard_map/ppermute | solution.py:467
  5.4 1.3 %collective-permute-start.1 = (f32[144,128]{1,0:T(8,128)S(1)}, f32[144,128]{1,0:T(8,128)S(1)}, u32[]{:S(2)}, u32[]{:S(2)}) collective-permute-start(f32[144,128]{1,0:T(8,128)S(1)} %get-tuple-element.73), channel_id=1, source_target_pairs={{16,0},{24,8},{17,1},{25,9},{18,2},{26,10},{19,3},{27,11},{20,4},{... | collective-permute-start | bytes 221192 | tf_op jit(solution)/shard_map/ppermute | solution.py:467
  7.0 3.0 %collective-permute-start.6 = (bf16[1,1,1024,128]{3,2,1,0:T(8,128)(2,1)S(1)}, bf16[1,1,1024,128]{3,2,1,0:T(8,128)(2,1)}, u32[]{:S(2)}, u32[]{:S(2)}) collective-permute-start(bf16[1,1,1024,128]{3,2,1,0:T(8,128)(2,1)S(1)} %bitcast.15), channel_id=1, source_target_pairs={{0,1},{2,0},{4,2},{6,4},{7,6},{5,7},{3,5},{1,3},{8,9},{10,8},{12,1... | collective-permute-start | bytes 786440 | tf_op jit(solution)/shard_map/ppermute | solution.py:458
  12.5 3.0 %state_streams.1 = (bf16[2,1024,128]{2,1,0:T(8,128)(2,1)S(1)}, f32[17,1024]{1,0:T(8,128)S(1)}, f32[1040,128]{1,0:T(8,128)S(1)}, bf16[1024,3072]{1,0:T(8,128)(2,1)S(1)}) custom-call(f32[3,128,1024]{2,1,0:T(8,128)S(1)} %get-tuple-element.65.feat, f32[128,1024]{1,0:T(8,128)S(1)} %get-tuple-element.66.og, f32[3,3,1024]{2,1,0:T(4,128)S(1)} %get-tuple-element.67.filt, ...), custom_call_target="tpu_custom_call" | custom-call | flops 4294967296 | bytes 16777216 | tf_op jit(solution)/shard_map/state_streams/pallas_call | solution.py:324
  15.4 2.5 %collective-permute-start.4 = (bf16[1,2,1024,128]{3,2,1,0:T(8,128)(2,1)S(1)}, bf16[1,2,1024,128]{3,2,1,0:T(8,128)(2,1)S(1)}, u32[]{:S(2)}, u32[]{:S(2)}) collective-permute-start(bf16[1,2,1024,128]{3,2,1,0:T(8,128)(2,1)S(1)} %bitcast.12), channel_id=1, source_target_pairs={{0,1},{2,0},{4,2},{6,4},{7,6},{5,7},{3,5},{1,3},{8,9},{10,8},{12,1... | collective-permute-start | bytes 1572872 | tf_op jit(solution)/shard_map/ppermute | solution.py:458
  21.2 4.9 %add_product.9 = (f32[1024,128]{1,0:T(8,128)S(1)}, bf16[1024,2048]{1,0:T(8,128)(2,1)S(1)}) custom-call(bf16[3,1024,8192]{2,1,0:T(8,128)(2,1)} %w_proj.17, bf16[1024,3072]{1,0:T(8,128)(2,1)S(1)} %get-tuple-element.75.refs_0_, bf16[1,1,1024,128]{3,2,1,0:T(8,128)(2,1)S(1)} %bitcast.17, bf16[1,1,1024,128]{3,2,1,0:T(8,128)(2,1)} %collective-permute-done.5.refs_2_, ...), custom_call_target="tpu_custom_call" | custom-call | flops 68719476736 | bytes 268435456 | tf_op jit(solution)/shard_map/add_product/pallas_call | solution.py:416
  26.1 5.9 %add_product.10 = (f32[1024,128]{1,0:T(8,128)S(1)}, bf16[1024,4096]{1,0:T(8,128)(2,1)S(1)}, bf16[1024,2048]{1,0:T(8,128)(2,1)S(1)}) custom-call(bf16[3,1024,8192]{2,1,0:T(8,128)(2,1)} %w_proj.17, bf16[1024,2048]{1,0:T(8,128)(2,1)S(1)} %get-tuple-element.80.refs_0_, bf16[1,2,1024,128]{3,2,1,0:T(8,128)(2,1)S(1)} %bitcast.14, ...), custom_call_target="tpu_custom_call" | custom-call | flops 68719476736 | bytes 268435456 | tf_op jit(solution)/shard_map/add_product/pallas_call | solution.py:416
  33.0 1.7 %collective-permute-start.9 = (bf16[1,2,1024,128]{3,2,1,0:T(8,128)(2,1)S(1)}, bf16[1,2,1024,128]{3,2,1,0:T(8,128)(2,1)S(1)}, u32[]{:S(2)}, u32[]{:S(2)}) collective-permute-start(bf16[1,2,1024,128]{3,2,1,0:T(8,128)(2,1)S(1)} %collective-permute-done.4.refs_2_), channel_id=1, source_target_pairs={{0,1},{2,0},{4,2},{6,4},{7,6},{5,7},{3,5},{1,3},{8,9},{10,8},{12,1... | collective-permute-start | bytes 1572872 | tf_op jit(solution)/shard_map/ppermute | solution.py:458
  34.8 4.5 %add_product.11 = (f32[1024,128]{1,0:T(8,128)S(1)}, bf16[1024,2048]{1,0:T(8,128)(2,1)S(1)}) custom-call(bf16[3,1024,8192]{2,1,0:T(8,128)(2,1)} %w_proj.17, bf16[1024,4096]{1,0:T(8,128)(2,1)S(1)} %get-tuple-element.87.refs_0_, bf16[1,2,1024,128]{3,2,1,0:T(8,128)(2,1)S(1)} %collective-permute-done.3.refs_1_, ...), custom_call_target="tpu_custom_call" | custom-call | flops 65536 | bytes 256 | tf_op jit(solution)/shard_map/add_product/pallas_call | solution.py:416
  39.3 2.3 %collective-permute-start.12 = (f32[17,1024]{1,0:T(8,128)S(1)}, f32[17,1024]{1,0:T(8,128)S(1)}, u32[]{:S(2)}, u32[]{:S(2)}) collective-permute-start(f32[17,1024]{1,0:T(8,128)S(1)} %add.6), channel_id=1, source_target_pairs={{0,16},{8,24},{16,0},{24,8},{1,17},{9,25},{17,1},{25,9},{2,18},{10... | collective-permute-start | bytes 208904 | tf_op jit(solution)/shard_map/ppermute | solution.py:470
  41.6 1.9 %collective-permute-start.14 = (bf16[1,1,1024,128]{3,2,1,0:T(8,128)(2,1)}, bf16[1,1,1024,128]{3,2,1,0:T(8,128)(2,1)S(1)}, u32[]{:S(2)}, u32[]{:S(2)}) collective-permute-start(bf16[1,1,1024,128]{3,2,1,0:T(8,128)(2,1)} %collective-permute-done.11.refs_2_), channel_id=1, source_target_pairs={{0,1},{2,0},{4,2},{6,4},{7,6},{5,7},{3,5},{1,3},{8,9},{10,8},{12,1... | collective-permute-start | bytes 786440 | tf_op jit(solution)/shard_map/ppermute | solution.py:458
  43.6 4.3 %add_product.12 = (f32[1024,128]{1,0:T(8,128)S(1)}, bf16[1024,3072]{1,0:T(8,128)(2,1)S(1)}) custom-call(bf16[3,1024,8192]{2,1,0:T(8,128)(2,1)} %w_proj.17, bf16[1024,2048]{1,0:T(8,128)(2,1)S(1)} %get-tuple-element.89.refs_0_, bf16[1,1,1024,128]{3,2,1,0:T(8,128)(2,1)} %collective-permute-done.10.refs_1_, ...), custom_call_target="tpu_custom_call" | custom-call | flops 68719476736 | bytes 268435456 | tf_op jit(solution)/shard_map/add_product/pallas_call | solution.py:416
  48.0 1.9 %gradients.1 = f32[3,128,1024]{2,1,0:T(8,128)} custom-call(f32[3,128,1024]{2,1,0:T(8,128)S(1)} %copy-done, f32[128,1024]{1,0:T(8,128)S(1)} %copy-done.1, f32[128,1024]{1,0:T(8,128)S(1)} %copy-done.2, f32[3,3,1024]{2,1,0:T(4,128)S(1)} %copy-done.5, f32[1,1024]{1,0:T(1,128)S(1)} %bitcast.10, f32[224,128]{1,0:T(8,128)S(1)} %copy-done.4, ...), custom_call_target="tpu_custom_call" | custom-call | flops 3932160 | bytes 5242880 | tf_op jit(solution)/shard_map/gradients/pallas_call | solution.py:215
  51.3 1.6 %collective-permute-start.16 = (bf16[1,1,1024,128]{3,2,1,0:T(8,128)(2,1)S(1)}, bf16[1,1,1024,128]{3,2,1,0:T(8,128)(2,1)S(1)}, u32[]{:S(2)}, u32[]{:S(2)}) collective-permute-start(bf16[1,1,1024,128]{3,2,1,0:T(8,128)(2,1)S(1)} %get-tuple-element.127), channel_id=1, source_target_pairs={{0,1},{2,0},{4,2},{6,4},{7,6},{5,7},{3,5},{1,3},{8,9},{10,8},{12,1... | collective-permute-start | bytes 786440 | tf_op jit(solution)/shard_map/ppermute | solution.py:458
  53.3 4.6 %add_product.13 = (f32[1024,128]{1,0:T(8,128)S(1)}, bf16[1024,3072]{1,0:T(8,128)(2,1)S(1)}) custom-call(bf16[3,1024,8192]{2,1,0:T(8,128)(2,1)} %w_proj.17, bf16[1024,3072]{1,0:T(8,128)(2,1)S(1)} %get-tuple-element.101.refs_0_, bf16[1,2,1024,128]{3,2,1,0:T(8,128)(2,1)S(1)} %collective-permute-done.8.refs_1_, ...), custom_call_target="tpu_custom_call" | custom-call | flops 65536 | bytes 256 | tf_op jit(solution)/shard_map/add_product/pallas_call | solution.py:416
  57.9 1.6 %collective-permute-start.18 = (bf16[1,1,1024,128]{3,2,1,0:T(8,128)(2,1)S(1)}, bf16[1,1,1024,128]{3,2,1,0:T(8,128)(2,1)S(1)}, u32[]{:S(2)}, u32[]{:S(2)}) collective-permute-start(bf16[1,1,1024,128]{3,2,1,0:T(8,128)(2,1)S(1)} %get-tuple-element.114), channel_id=1, source_target_pairs={{0,1},{2,0},{4,2},{6,4},{7,6},{5,7},{3,5},{1,3},{8,9},{10,8},{12,1... | collective-permute-start | bytes 786440 | tf_op jit(solution)/shard_map/ppermute | solution.py:458
  60.0 3.9 %add_product.14 = (f32[1024,128]{1,0:T(8,128)S(1)}, bf16[1024,2048]{1,0:T(8,128)(2,1)S(1)}) custom-call(bf16[3,1024,8192]{2,1,0:T(8,128)(2,1)} %w_proj.17, bf16[1024,3072]{1,0:T(8,128)(2,1)S(1)} %get-tuple-element.105.refs_0_, bf16[1,2,1024,128]{3,2,1,0:T(8,128)(2,1)S(1)} %collective-permute-done.9.refs_2_.refs_1_, ...), custom_call_target="tpu_custom_call" | custom-call | flops 65536 | bytes 256 | tf_op jit(solution)/shard_map/add_product/pallas_call | solution.py:416
  64.4 1.7 %collective-permute-start.22 = (bf16[1,1,1024,128]{3,2,1,0:T(8,128)(2,1)S(1)}, bf16[1,1,1024,128]{3,2,1,0:T(8,128)(2,1)S(1)}, u32[]{:S(2)}, u32[]{:S(2)}) collective-permute-start(bf16[1,1,1024,128]{3,2,1,0:T(8,128)(2,1)S(1)} %collective-permute-done.16.refs_3_), channel_id=1, source_target_pairs={{0,1},{2,0},{4,2},{6,4},{7,6},{5,7},{3,5},{1,3},{8,9},{10,8},{12,1... | collective-permute-start | bytes 786440 | tf_op jit(solution)/shard_map/ppermute | solution.py:458
  66.5 1.7 %collective-permute-start.20 = (bf16[1,1,512,128]{3,2,1,0:T(8,128)(2,1)S(1)}, bf16[1,1,512,128]{3,2,1,0:T(8,128)(2,1)S(1)}, u32[]{:S(2)}, u32[]{:S(2)}) collective-permute-start(bf16[1,1,512,128]{3,2,1,0:T(8,128)(2,1)S(1)} %slice.31), channel_id=1, source_target_pairs={{0,1},{2,0},{4,2},{6,4},{7,6},{5,7},{3,5},{1,3},{8,9},{10,8},{12,1... | collective-permute-start | bytes 393224 | tf_op jit(solution)/shard_map/ppermute | solution.py:458
  68.2 5.1 %add_product.15 = (f32[1024,128]{1,0:T(8,128)S(1)}, bf16[1024,3072]{1,0:T(8,128)(2,1)S(1)}) custom-call(bf16[3,1024,8192]{2,1,0:T(8,128)(2,1)} %w_proj.17, bf16[1024,2048]{1,0:T(8,128)(2,1)S(1)} %get-tuple-element.100.refs_0_, bf16[1024,2048]{1,0:T(8,128)(2,1)S(1)} %get-tuple-element.110.refs_1_, ...), custom_call_target="tpu_custom_call" | custom-call | flops 65536 | bytes 256 | tf_op jit(solution)/shard_map/add_product/pallas_call | solution.py:416
  73.3 1.3 %add_product.16.refs_3_ = f32[1024,128]{1,0:T(8,128)S(1)} custom-call(bf16[3,1024,8192]{2,1,0:T(8,128)(2,1)} %w_proj.17, bf16[1024,3072]{1,0:T(8,128)(2,1)S(1)} %get-tuple-element.116.refs_0_, bf16[1,1,1024,128]{3,2,1,0:T(8,128)(2,1)S(1)} %collective-permute-done.21.refs_1_, bf16[1,1,1024,128]{3,2,1,0:T(8,128)(2,1)S(1)} %collective-permute-done.22.refs_2_, ...), custom_call_target="tpu_custom_call" | custom-call | flops 65536 | bytes 256 | tf_op jit(solution)/shard_map/add_product/pallas_call | solution.py:416
  74.6 1.5 %add_product.17 = f32[128,1024]{1,0:T(8,128)} custom-call(bf16[3,1024,8192]{2,1,0:T(8,128)(2,1)} %w_proj.17, bf16[1024,3072]{1,0:T(8,128)(2,1)S(1)} %get-tuple-element.116.refs_0_, bf16[1,1,512,128]{3,2,1,0:T(8,128)(2,1)S(1)} %collective-permute-done.19.refs_1_, bf16[1,1,512,128]{3,2,1,0:T(8,128)(2,1)S(1)} %collective-permute-done.20.refs_2_, ...), custom_call_target="tpu_custom_call" | custom-call | flops 65536 | bytes 256 | tf_op jit(solution)/shard_map/add_product/pallas_call | solution.py:416
  (57 shorter events, 10.3 us)
Async XLA Ops:
  2.8 3.9 %collective-permute-start = (f32[224,128]{1,0:T(8,128)S(1)}, f32[224,128]{1,0:T(8,128)S(1)}, u32[]{:S(2)}, u32[]{:S(2)}) collective-permute-start(f32[224,128]{1,0:T(8,128)S(1)} %get-tuple-element.70), channel_id=1, source_target_pairs={{8,0},{16,8},{24,16},{9,1},{17,9},{25,17},{10,2},{18,10},{26,18},{... | collective-permute-start | bytes 344072 | tf_op jit(solution)/shard_map/ppermute | solution.py:467
  4.1 7.2 %collective-permute-start.2 = (f32[144,128]{1,0:T(8,128)S(1)}, f32[144,128]{1,0:T(8,128)S(1)}, u32[]{:S(2)}, u32[]{:S(2)}) collective-permute-start(f32[144,128]{1,0:T(8,128)S(1)} %get-tuple-element.73), channel_id=1, source_target_pairs={{24,0},{25,1},{26,2},{27,3},{28,4},{29,5},{30,6},{31,7}} | collective-permute-start | bytes 221192 | tf_op jit(solution)/shard_map/ppermute | solution.py:467
  5.4 7.1 %collective-permute-start.1 = (f32[144,128]{1,0:T(8,128)S(1)}, f32[144,128]{1,0:T(8,128)S(1)}, u32[]{:S(2)}, u32[]{:S(2)}) collective-permute-start(f32[144,128]{1,0:T(8,128)S(1)} %get-tuple-element.73), channel_id=1, source_target_pairs={{16,0},{24,8},{17,1},{25,9},{18,2},{26,10},{19,3},{27,11},{20,4},{... | collective-permute-start | bytes 221192 | tf_op jit(solution)/shard_map/ppermute | solution.py:467
  6.7 5.8 %copy-start.3 = (f32[224,128]{1,0:T(8,128)}, f32[224,128]{1,0:T(8,128)S(1)}, u32[]{:S(2)}) copy-start(f32[224,128]{1,0:T(8,128)S(1)} %collective-permute-done.later.refs_0_) | copy-start | bytes 344068
  7.0 11.0 %collective-permute-start.6 = (bf16[1,1,1024,128]{3,2,1,0:T(8,128)(2,1)S(1)}, bf16[1,1,1024,128]{3,2,1,0:T(8,128)(2,1)}, u32[]{:S(2)}, u32[]{:S(2)}) collective-permute-start(bf16[1,1,1024,128]{3,2,1,0:T(8,128)(2,1)S(1)} %bitcast.15), channel_id=1, source_target_pairs={{0,1},{2,0},{4,2},{6,4},{7,6},{5,7},{3,5},{1,3},{8,9},{10,8},{12,1... | collective-permute-start | bytes 786440 | tf_op jit(solution)/shard_map/ppermute | solution.py:458
  10.0 8.5 %collective-permute-start.5 = (bf16[1,1,1024,128]{3,2,1,0:T(8,128)(2,1)S(1)}, bf16[1,1,1024,128]{3,2,1,0:T(8,128)(2,1)}, u32[]{:S(2)}, u32[]{:S(2)}) collective-permute-start(bf16[1,1,1024,128]{3,2,1,0:T(8,128)(2,1)S(1)} %bitcast.16), channel_id=1, source_target_pairs={{0,2},{2,4},{4,6},{6,7},{7,5},{5,3},{3,1},{1,0},{8,10},{10,12},{12... | collective-permute-start | bytes 786440 | tf_op jit(solution)/shard_map/ppermute | solution.py:455
  15.4 16.6 %collective-permute-start.4 = (bf16[1,2,1024,128]{3,2,1,0:T(8,128)(2,1)S(1)}, bf16[1,2,1024,128]{3,2,1,0:T(8,128)(2,1)S(1)}, u32[]{:S(2)}, u32[]{:S(2)}) collective-permute-start(bf16[1,2,1024,128]{3,2,1,0:T(8,128)(2,1)S(1)} %bitcast.12), channel_id=1, source_target_pairs={{0,1},{2,0},{4,2},{6,4},{7,6},{5,7},{3,5},{1,3},{8,9},{10,8},{12,1... | collective-permute-start | bytes 1572872 | tf_op jit(solution)/shard_map/ppermute | solution.py:458
  17.9 14.9 %collective-permute-start.3 = (bf16[1,2,1024,128]{3,2,1,0:T(8,128)(2,1)S(1)}, bf16[1,2,1024,128]{3,2,1,0:T(8,128)(2,1)S(1)}, u32[]{:S(2)}, u32[]{:S(2)}) collective-permute-start(bf16[1,2,1024,128]{3,2,1,0:T(8,128)(2,1)S(1)} %bitcast.13), channel_id=1, source_target_pairs={{0,2},{2,4},{4,6},{6,7},{7,5},{5,3},{3,1},{1,0},{8,10},{10,12},{12... | collective-permute-start | bytes 1572872 | tf_op jit(solution)/shard_map/ppermute | solution.py:455
  18.5 13.5 %collective-permute-start.7 = (f32[17,1024]{1,0:T(8,128)S(1)}, f32[17,1024]{1,0:T(8,128)S(1)}, u32[]{:S(2)}, u32[]{:S(2)}) collective-permute-start(f32[17,1024]{1,0:T(8,128)S(1)} %get-tuple-element.84), channel_id=1, source_target_pairs={{0,8},{8,0},{16,24},{24,16},{1,9},{9,1},{17,25},{25,17},{2,10},{10... | collective-permute-start | bytes 208904 | tf_op jit(solution)/shard_map/ppermute | solution.py:470
  19.1 20.1 %collective-permute-start.10 = (bf16[1,1,1024,128]{3,2,1,0:T(8,128)(2,1)}, bf16[1,1,1024,128]{3,2,1,0:T(8,128)(2,1)}, u32[]{:S(2)}, u32[]{:S(2)}) collective-permute-start(bf16[1,1,1024,128]{3,2,1,0:T(8,128)(2,1)} %collective-permute-done.5.refs_2_), channel_id=1, source_target_pairs={{0,2},{2,4},{4,6},{6,7},{7,5},{5,3},{3,1},{1,0},{8,10},{10,12},{12... | collective-permute-start | bytes 786440 | tf_op jit(solution)/shard_map/ppermute | solution.py:455
  20.1 19.2 %collective-permute-start.11 = (bf16[1,1,1024,128]{3,2,1,0:T(8,128)(2,1)}, bf16[1,1,1024,128]{3,2,1,0:T(8,128)(2,1)}, u32[]{:S(2)}, u32[]{:S(2)}) collective-permute-start(bf16[1,1,1024,128]{3,2,1,0:T(8,128)(2,1)} %collective-permute-done.6.refs_3_), channel_id=1, source_target_pairs={{0,1},{2,0},{4,2},{6,4},{7,6},{5,7},{3,5},{1,3},{8,9},{10,8},{12,1... | collective-permute-start | bytes 786440 | tf_op jit(solution)/shard_map/ppermute | solution.py:458
  32.7 18.4 %collective-permute-start.8 = (bf16[1,2,1024,128]{3,2,1,0:T(8,128)(2,1)S(1)}, bf16[1,2,1024,128]{3,2,1,0:T(8,128)(2,1)S(1)}, u32[]{:S(2)}, u32[]{:S(2)}) collective-permute-start(bf16[1,2,1024,128]{3,2,1,0:T(8,128)(2,1)S(1)} %collective-permute-done.3.refs_1_), channel_id=1, source_target_pairs={{0,2},{2,4},{4,6},{6,7},{7,5},{5,3},{3,1},{1,0},{8,10},{10,12},{12... | collective-permute-start | bytes 1572872 | tf_op jit(solution)/shard_map/ppermute | solution.py:455
  33.0 18.1 %collective-permute-start.9 = (bf16[1,2,1024,128]{3,2,1,0:T(8,128)(2,1)S(1)}, bf16[1,2,1024,128]{3,2,1,0:T(8,128)(2,1)S(1)}, u32[]{:S(2)}, u32[]{:S(2)}) collective-permute-start(bf16[1,2,1024,128]{3,2,1,0:T(8,128)(2,1)S(1)} %collective-permute-done.4.refs_2_), channel_id=1, source_target_pairs={{0,1},{2,0},{4,2},{6,4},{7,6},{5,7},{3,5},{1,3},{8,9},{10,8},{12,1... | collective-permute-start | bytes 1572872 | tf_op jit(solution)/shard_map/ppermute | solution.py:458
  39.3 10.6 %collective-permute-start.12 = (f32[17,1024]{1,0:T(8,128)S(1)}, f32[17,1024]{1,0:T(8,128)S(1)}, u32[]{:S(2)}, u32[]{:S(2)}) collective-permute-start(f32[17,1024]{1,0:T(8,128)S(1)} %add.6), channel_id=1, source_target_pairs={{0,16},{8,24},{16,0},{24,8},{1,17},{9,25},{17,1},{25,9},{2,18},{10... | collective-permute-start | bytes 208904 | tf_op jit(solution)/shard_map/ppermute | solution.py:470
  41.5 18.0 %collective-permute-start.13 = (bf16[1,1,1024,128]{3,2,1,0:T(8,128)(2,1)}, bf16[1,1,1024,128]{3,2,1,0:T(8,128)(2,1)S(1)}, u32[]{:S(2)}, u32[]{:S(2)}) collective-permute-start(bf16[1,1,1024,128]{3,2,1,0:T(8,128)(2,1)} %collective-permute-done.10.refs_1_), channel_id=1, source_target_pairs={{0,2},{2,4},{4,6},{6,7},{7,5},{5,3},{3,1},{1,0},{8,10},{10,12},{12... | collective-permute-start | bytes 786440 | tf_op jit(solution)/shard_map/ppermute | solution.py:455
  41.6 17.9 %collective-permute-start.14 = (bf16[1,1,1024,128]{3,2,1,0:T(8,128)(2,1)}, bf16[1,1,1024,128]{3,2,1,0:T(8,128)(2,1)S(1)}, u32[]{:S(2)}, u32[]{:S(2)}) collective-permute-start(bf16[1,1,1024,128]{3,2,1,0:T(8,128)(2,1)} %collective-permute-done.11.refs_2_), channel_id=1, source_target_pairs={{0,1},{2,0},{4,2},{6,4},{7,6},{5,7},{3,5},{1,3},{8,9},{10,8},{12,1... | collective-permute-start | bytes 786440 | tf_op jit(solution)/shard_map/ppermute | solution.py:458
  51.3 12.7 %collective-permute-start.16 = (bf16[1,1,1024,128]{3,2,1,0:T(8,128)(2,1)S(1)}, bf16[1,1,1024,128]{3,2,1,0:T(8,128)(2,1)S(1)}, u32[]{:S(2)}, u32[]{:S(2)}) collective-permute-start(bf16[1,1,1024,128]{3,2,1,0:T(8,128)(2,1)S(1)} %get-tuple-element.127), channel_id=1, source_target_pairs={{0,1},{2,0},{4,2},{6,4},{7,6},{5,7},{3,5},{1,3},{8,9},{10,8},{12,1... | collective-permute-start | bytes 786440 | tf_op jit(solution)/shard_map/ppermute | solution.py:458
  52.9 11.1 %collective-permute-start.15 = (bf16[1,1,1024,128]{3,2,1,0:T(8,128)(2,1)S(1)}, bf16[1,1,1024,128]{3,2,1,0:T(8,128)(2,1)S(1)}, u32[]{:S(2)}, u32[]{:S(2)}) collective-permute-start(bf16[1,1,1024,128]{3,2,1,0:T(8,128)(2,1)S(1)} %get-tuple-element.129), channel_id=1, source_target_pairs={{0,2},{2,4},{4,6},{6,7},{7,5},{5,3},{3,1},{1,0},{8,10},{10,12},{12... | collective-permute-start | bytes 786440 | tf_op jit(solution)/shard_map/ppermute | solution.py:455
  57.9 8.5 %collective-permute-start.18 = (bf16[1,1,1024,128]{3,2,1,0:T(8,128)(2,1)S(1)}, bf16[1,1,1024,128]{3,2,1,0:T(8,128)(2,1)S(1)}, u32[]{:S(2)}, u32[]{:S(2)}) collective-permute-start(bf16[1,1,1024,128]{3,2,1,0:T(8,128)(2,1)S(1)} %get-tuple-element.114), channel_id=1, source_target_pairs={{0,1},{2,0},{4,2},{6,4},{7,6},{5,7},{3,5},{1,3},{8,9},{10,8},{12,1... | collective-permute-start | bytes 786440 | tf_op jit(solution)/shard_map/ppermute | solution.py:458
  59.6 8.6 %collective-permute-start.17 = (bf16[1,1,1024,128]{3,2,1,0:T(8,128)(2,1)S(1)}, bf16[1,1,1024,128]{3,2,1,0:T(8,128)(2,1)S(1)}, u32[]{:S(2)}, u32[]{:S(2)}) collective-permute-start(bf16[1,1,1024,128]{3,2,1,0:T(8,128)(2,1)S(1)} %get-tuple-element.128), channel_id=1, source_target_pairs={{0,2},{2,4},{4,6},{6,7},{7,5},{5,3},{3,1},{1,0},{8,10},{10,12},{12... | collective-permute-start | bytes 786440 | tf_op jit(solution)/shard_map/ppermute | solution.py:455
  64.0 9.3 %collective-permute-start.21 = (bf16[1,1,1024,128]{3,2,1,0:T(8,128)(2,1)S(1)}, bf16[1,1,1024,128]{3,2,1,0:T(8,128)(2,1)S(1)}, u32[]{:S(2)}, u32[]{:S(2)}) collective-permute-start(bf16[1,1,1024,128]{3,2,1,0:T(8,128)(2,1)S(1)} %collective-permute-done.15.refs_2_), channel_id=1, source_target_pairs={{0,2},{2,4},{4,6},{6,7},{7,5},{5,3},{3,1},{1,0},{8,10},{10,12},{12... | collective-permute-start | bytes 786440 | tf_op jit(solution)/shard_map/ppermute | solution.py:455
  64.4 8.9 %collective-permute-start.22 = (bf16[1,1,1024,128]{3,2,1,0:T(8,128)(2,1)S(1)}, bf16[1,1,1024,128]{3,2,1,0:T(8,128)(2,1)S(1)}, u32[]{:S(2)}, u32[]{:S(2)}) collective-permute-start(bf16[1,1,1024,128]{3,2,1,0:T(8,128)(2,1)S(1)} %collective-permute-done.16.refs_3_), channel_id=1, source_target_pairs={{0,1},{2,0},{4,2},{6,4},{7,6},{5,7},{3,5},{1,3},{8,9},{10,8},{12,1... | collective-permute-start | bytes 786440 | tf_op jit(solution)/shard_map/ppermute | solution.py:458
  66.1 8.5 %collective-permute-start.19 = (bf16[1,1,512,128]{3,2,1,0:T(8,128)(2,1)S(1)}, bf16[1,1,512,128]{3,2,1,0:T(8,128)(2,1)S(1)}, u32[]{:S(2)}, u32[]{:S(2)}) collective-permute-start(bf16[1,1,512,128]{3,2,1,0:T(8,128)(2,1)S(1)} %slice.30), channel_id=1, source_target_pairs={{0,2},{2,4},{4,6},{6,7},{7,5},{5,3},{3,1},{1,0},{8,10},{10,12},{12... | collective-permute-start | bytes 393224 | tf_op jit(solution)/shard_map/ppermute | solution.py:455
  66.5 8.1 %collective-permute-start.20 = (bf16[1,1,512,128]{3,2,1,0:T(8,128)(2,1)S(1)}, bf16[1,1,512,128]{3,2,1,0:T(8,128)(2,1)S(1)}, u32[]{:S(2)}, u32[]{:S(2)}) collective-permute-start(bf16[1,1,512,128]{3,2,1,0:T(8,128)(2,1)S(1)} %slice.31), channel_id=1, source_target_pairs={{0,1},{2,0},{4,2},{6,4},{7,6},{5,7},{3,5},{1,3},{8,9},{10,8},{12,1... | collective-permute-start | bytes 393224 | tf_op jit(solution)/shard_map/ppermute | solution.py:458
  (6 other events, 26.4 us)

commit v14 on v13

--- a/solution.py
+++ b/solution.py
@@ -194,11 +194,15 @@
             ext[tokens : tokens + 2, lanes] = rim * rim_rows(later, n, j, fold)
 
 
-def gradients_kernel(feat, conv, og, filt, bias, later, gp, out, first, second, third, ready, sems):
-    tokens, channels = og.shape
+def gradients_kernel(
+    plan, ring, feat, conv, og, filt, bias, later, gp, w_proj, out, columns, first, second, third, ready, sems
+):
+    tokens, channels = og.shape
+    moves = fetches(plan, ring, w_proj, columns, sems.at[pl.ds(3, len(plan))])
+    for move in moves:
+        move.start()
     gate_gradient(feat, conv, og, bias, later, first)
     product_gradients(feat, gp, later, (second, third))
-    moves = []
     for p, ext in enumerate((first, second, third)):
         taps = [filt[p, j : j + 1, :] for j in range(3)]
         for j in range(channels // LANES):
@@ -210,19 +214,22 @@
         move.wait()
 
 
-def gradients(feat, conv, og, filt, bias, later, gp):
+def gradients(feat, conv, og, filt, bias, later, gp, plan, ring, w_proj):
     tokens, channels = og.shape
     return pl.pallas_call(
-        gradients_kernel,
-        in_specs=[whole()] * 7,
-        out_specs=in_hbm(),
-        out_shape=jax.ShapeDtypeStruct((3, tokens, channels), F32),
+        functools.partial(gradients_kernel, plan, ring),
+        in_specs=[whole()] * 7 + [in_hbm()],
+        out_specs=[in_hbm(), whole()],
+        out_shape=[
+            jax.ShapeDtypeStruct((3, tokens, channels), F32),
+            pltpu.VMEM((w_proj.shape[1], len(plan) * channels), BF16),
+        ],
         scratch_shapes=[pltpu.VMEM((tokens + 8, channels), F32)] * 3
-        + [pltpu.VMEM((3, tokens, channels), F32), pltpu.SemaphoreType.DMA((3,))],
+        + [pltpu.VMEM((3, tokens, channels), F32), pltpu.SemaphoreType.DMA((3 + len(plan),))],
         compiler_params=params(),
         cost_estimate=cost(30 * tokens * channels, 40 * tokens * channels),
         name="gradients",
-    )(feat, conv, og, filt, bias, later, gp)
+    )(feat, conv, og, filt, bias, later, gp, w_proj)
 
 
 def on_ring(offset, ring):
@@ -512,7 +519,7 @@
 
     plans = [plan_of(n) for n in range(len(sets))]
     early, late = plans[6][: len(plans[6]) // 2], plans[6][len(plans[6]) // 2 :]
-    laters = [[plan] for plan in plans[1:6]] + [[late], [plans[7] + plans[8]], [], []]
+    laters = [[plan] for plan in plans[1:6]] + [[late], [], [], []]
     laters[1].append(early)
 
     def times(n, total, weights, **arrays):
@@ -546,7 +553,10 @@
     for by in distances[1:]:
         sums = exchanged(sums, by)
     total, ready = times(3, total, all_of(ready, 3), a2=a2, z2=z2)
-    grads = gradients(features, saved_conv, out_grad, short_filter, bias[None], payloads[0], after(gp, total))
+    final_plan = plans[7] + plans[8]
+    grads, final = gradients(
+        features, saved_conv, out_grad, short_filter, bias[None], payloads[0], after(gp, total), final_plan, ring, w_proj
+    )
 
     sums = sums * (tokens * blocks) ** (-0.5)
     outputs = grads, sums[:modes].T, sums[modes]
@@ -562,12 +572,12 @@
     b4, y4 = up(b3), down(y3)
     a4 = up(a3[:, :, :half]), down(z3[:, :, half:])
     weights = [(soon, 0, len(early)), (ready, 0, len(late))]
-    total, ready = times(6, total, weights, b3=b3, y3=y3, c3=c3, x3=x3)
+    (total,) = times(6, total, weights, b3=b3, y3=y3, c3=c3, x3=x3)
 
     b4, y4, total = lax.optimization_barrier((b4, y4, total))
-    (total,) = times(7, total, [(ready, 0, len(plans[7]))], b4=b4, y4=y4)
+    (total,) = times(7, total, [(final, 0, len(plans[7]))], b4=b4, y4=y4)
     a4, total = lax.optimization_barrier((a4, total))
-    (grad_x,) = times(8, total, [(ready, len(plans[7]), len(plans[8]))], a4=a4)
+    (grad_x,) = times(8, total, [(final, len(plans[7]), len(plans[8]))], a4=a4)
     grads, grad_residue, grad_bias = outputs
     return (grads, grad_x, grad_residue, grad_bias)
 

time: 76.5 us -> 78 us (1.020)
  waiting for transfers between devices: 3.47 us -> 6.06 us
  Pallas kernels: 43.4 us -> 42.3 us
    pallas_call x9, Pallas kernels: 36 us -> 33.3 us  [add_product(): pl.pallas_call(functools.partial(product_kernel, plan, parts, laters, fir...]
    ppermute x9, waiting for transfers between devices: 1.16 us -> 3.76 us  [up(): return lax.ppermute(x, 'chan', pairs[1])]
    pallas_call x1, Pallas kernels: 1.89 us -> 3.56 us  [gradients(): pl.pallas_call(functools.partial(gradients_kernel, plan, ring), in_specs=...]
  transfers between devices with their start and end apart: 23 -> 23, of which waited for: 4 -> 6; matrix products, arithmetic and copies ran while one was open for 2% -> 2% of each run, Pallas kernels for 52% -> 50%
where the time goes in v14:
time: 78 us; the launch traced here: 77.7 us
  Pallas kernels  42.3 us (54%)
  starting transfers between devices  26.9 us (34%)
  waiting for transfers between devices  6.06 us (8%)
  local copies, waits for them, and re-layouts  1.35 us (2%)
  between operations  1.1 us (1%)
    pallas_call x9, Pallas kernels, add_product(): pl.pallas_call(functools.partial(product_kernel, plan, parts, laters, fir...  33.3 us
    ppermute x9, starting transfers between devices, down(): return lax.ppermute(x, 'chan', pairs[-1])  16.8 us
    ppermute x3, starting transfers between devices, from_later(): return lax.ppermute(array, 'ctx', [(i, i - by) for i in range(by, blocks)])  3.88 us
    ppermute x9, waiting for transfers between devices, up(): return lax.ppermute(x, 'chan', pairs[1])  3.76 us
    pallas_call x1, Pallas kernels, gradients(): pl.pallas_call(functools.partial(gradients_kernel, plan, ring), in_specs=...  3.56 us
    ppermute x9, starting transfers between devices, up(): return lax.ppermute(x, 'chan', pairs[1])  3.3 us
    pallas_call x1, Pallas kernels, state_streams(): pl.pallas_call(functools.partial(state_kernel, spans, plan, ring), in_spe...  2.96 us
    ppermute x2, starting transfers between devices, exchanged(): lax.ppermute(sums, 'ctx', [(i, i ^ by) for i in range(blocks)])  2.9 us
  transfers between devices with their start and end apart: 23, of which 6 were waited for; matrix products, arithmetic and copies ran while one was open for 2% of the time, Pallas kernels for 50%

profile of v14, /device:TPU:0, one launch (start us, length us, event | category | flops | bytes accessed | tf_op | source)
XLA Modules:
  0.0 77.7 jit_solution(15810930014751773451)
XLA Ops:
  0.6 2.1 %front.1 = (f32[3,128,1024]{2,1,0:T(8,128)S(1)}, f32[128,1024]{1,0:T(8,128)S(1)}, f32[128,1024]{1,0:T(8,128)S(1)}, f32[3,3,1024]{2,1,0:T(4,128)S(1)}, f32[1,1024...) custom-call(f32[3,128,1024]{2,1,0:T(8,128)} %feat.1, ...), custom_call_target="tpu_custom_call" | custom-call | flops 8388608 | bytes 2621440 | tf_op jit(solution)/shard_map/front/pallas_call | solution.py:94
  2.8 1.3 %collective-permute-start = (f32[224,128]{1,0:T(8,128)S(1)}, f32[224,128]{1,0:T(8,128)S(1)}, u32[]{:S(2)}, u32[]{:S(2)}) collective-permute-start(f32[224,128]{1,0:T(8,128)S(1)} %get-tuple-element.70), channel_id=1, source_target_pairs={{8,0},{16,8},{24,16},{9,1},{17,9},{25,17},{10,2},{18,10},{26,18},{... | collective-permute-start | bytes 344072 | tf_op jit(solution)/shard_map/ppermute | solution.py:474
  4.1 1.3 %collective-permute-start.2 = (f32[144,128]{1,0:T(8,128)S(1)}, f32[144,128]{1,0:T(8,128)S(1)}, u32[]{:S(2)}, u32[]{:S(2)}) collective-permute-start(f32[144,128]{1,0:T(8,128)S(1)} %get-tuple-element.73), channel_id=1, source_target_pairs={{24,0},{25,1},{26,2},{27,3},{28,4},{29,5},{30,6},{31,7}} | collective-permute-start | bytes 221192 | tf_op jit(solution)/shard_map/ppermute | solution.py:474
  5.4 1.3 %collective-permute-start.1 = (f32[144,128]{1,0:T(8,128)S(1)}, f32[144,128]{1,0:T(8,128)S(1)}, u32[]{:S(2)}, u32[]{:S(2)}) collective-permute-start(f32[144,128]{1,0:T(8,128)S(1)} %get-tuple-element.73), channel_id=1, source_target_pairs={{16,0},{24,8},{17,1},{25,9},{18,2},{26,10},{19,3},{27,11},{20,4},{... | collective-permute-start | bytes 221192 | tf_op jit(solution)/shard_map/ppermute | solution.py:474
  7.0 3.0 %collective-permute-start.6 = (bf16[1,1,1024,128]{3,2,1,0:T(8,128)(2,1)S(1)}, bf16[1,1,1024,128]{3,2,1,0:T(8,128)(2,1)}, u32[]{:S(2)}, u32[]{:S(2)}) collective-permute-start(bf16[1,1,1024,128]{3,2,1,0:T(8,128)(2,1)S(1)} %bitcast.15), channel_id=1, source_target_pairs={{0,1},{2,0},{4,2},{6,4},{7,6},{5,7},{3,5},{1,3},{8,9},{10,8},{12,1... | collective-permute-start | bytes 786440 | tf_op jit(solution)/shard_map/ppermute | solution.py:465
  12.5 3.0 %state_streams.1 = (bf16[2,1024,128]{2,1,0:T(8,128)(2,1)S(1)}, f32[17,1024]{1,0:T(8,128)S(1)}, f32[1040,128]{1,0:T(8,128)S(1)}, bf16[1024,3072]{1,0:T(8,128)(2,1)S(1)}) custom-call(f32[3,128,1024]{2,1,0:T(8,128)S(1)} %get-tuple-element.65.feat, f32[128,1024]{1,0:T(8,128)S(1)} %get-tuple-element.66.og, f32[3,3,1024]{2,1,0:T(4,128)S(1)} %get-tuple-element.67.filt, ...), custom_call_target="tpu_custom_call" | custom-call | flops 4294967296 | bytes 16777216 | tf_op jit(solution)/shard_map/state_streams/pallas_call | solution.py:331
  15.4 2.5 %collective-permute-start.4 = (bf16[1,2,1024,128]{3,2,1,0:T(8,128)(2,1)S(1)}, bf16[1,2,1024,128]{3,2,1,0:T(8,128)(2,1)S(1)}, u32[]{:S(2)}, u32[]{:S(2)}) collective-permute-start(bf16[1,2,1024,128]{3,2,1,0:T(8,128)(2,1)S(1)} %bitcast.12), channel_id=1, source_target_pairs={{0,1},{2,0},{4,2},{6,4},{7,6},{5,7},{3,5},{1,3},{8,9},{10,8},{12,1... | collective-permute-start | bytes 1572872 | tf_op jit(solution)/shard_map/ppermute | solution.py:465
  21.2 4.9 %add_product.9 = (f32[1024,128]{1,0:T(8,128)S(1)}, bf16[1024,2048]{1,0:T(8,128)(2,1)S(1)}) custom-call(bf16[3,1024,8192]{2,1,0:T(8,128)(2,1)} %w_proj.19, bf16[1024,3072]{1,0:T(8,128)(2,1)S(1)} %get-tuple-element.75.refs_0_, bf16[1,1,1024,128]{3,2,1,0:T(8,128)(2,1)S(1)} %bitcast.17, bf16[1,1,1024,128]{3,2,1,0:T(8,128)(2,1)} %collective-permute-done.5.refs_2_, ...), custom_call_target="tpu_custom_call" | custom-call | flops 68719476736 | bytes 268435456 | tf_op jit(solution)/shard_map/add_product/pallas_call | solution.py:423
  26.1 5.9 %add_product.10 = (f32[1024,128]{1,0:T(8,128)S(1)}, bf16[1024,4096]{1,0:T(8,128)(2,1)S(1)}, bf16[1024,2048]{1,0:T(8,128)(2,1)S(1)}) custom-call(bf16[3,1024,8192]{2,1,0:T(8,128)(2,1)} %w_proj.19, bf16[1024,2048]{1,0:T(8,128)(2,1)S(1)} %get-tuple-element.80.refs_0_, bf16[1,2,1024,128]{3,2,1,0:T(8,128)(2,1)S(1)} %bitcast.14, ...), custom_call_target="tpu_custom_call" | custom-call | flops 68719476736 | bytes 268435456 | tf_op jit(solution)/shard_map/add_product/pallas_call | solution.py:423
  33.0 1.7 %collective-permute-start.9 = (bf16[1,2,1024,128]{3,2,1,0:T(8,128)(2,1)S(1)}, bf16[1,2,1024,128]{3,2,1,0:T(8,128)(2,1)S(1)}, u32[]{:S(2)}, u32[]{:S(2)}) collective-permute-start(bf16[1,2,1024,128]{3,2,1,0:T(8,128)(2,1)S(1)} %collective-permute-done.4.refs_2_), channel_id=1, source_target_pairs={{0,1},{2,0},{4,2},{6,4},{7,6},{5,7},{3,5},{1,3},{8,9},{10,8},{12,1... | collective-permute-start | bytes 1572872 | tf_op jit(solution)/shard_map/ppermute | solution.py:465
  34.8 4.5 %add_product.11 = (f32[1024,128]{1,0:T(8,128)S(1)}, bf16[1024,2048]{1,0:T(8,128)(2,1)S(1)}) custom-call(bf16[3,1024,8192]{2,1,0:T(8,128)(2,1)} %w_proj.19, bf16[1024,4096]{1,0:T(8,128)(2,1)S(1)} %get-tuple-element.87.refs_0_, bf16[1,2,1024,128]{3,2,1,0:T(8,128)(2,1)S(1)} %collective-permute-done.3.refs_1_, ...), custom_call_target="tpu_custom_call" | custom-call | flops 65536 | bytes 256 | tf_op jit(solution)/shard_map/add_product/pallas_call | solution.py:423
  39.3 2.3 %collective-permute-start.12 = (f32[17,1024]{1,0:T(8,128)S(1)}, f32[17,1024]{1,0:T(8,128)S(1)}, u32[]{:S(2)}, u32[]{:S(2)}) collective-permute-start(f32[17,1024]{1,0:T(8,128)S(1)} %add.6), channel_id=1, source_target_pairs={{0,16},{8,24},{16,0},{24,8},{1,17},{9,25},{17,1},{25,9},{2,18},{10... | collective-permute-start | bytes 208904 | tf_op jit(solution)/shard_map/ppermute | solution.py:477
  41.7 1.9 %collective-permute-start.14 = (bf16[1,1,1024,128]{3,2,1,0:T(8,128)(2,1)}, bf16[1,1,1024,128]{3,2,1,0:T(8,128)(2,1)S(1)}, u32[]{:S(2)}, u32[]{:S(2)}) collective-permute-start(bf16[1,1,1024,128]{3,2,1,0:T(8,128)(2,1)} %collective-permute-done.11.refs_2_), channel_id=1, source_target_pairs={{0,1},{2,0},{4,2},{6,4},{7,6},{5,7},{3,5},{1,3},{8,9},{10,8},{12,1... | collective-permute-start | bytes 786440 | tf_op jit(solution)/shard_map/ppermute | solution.py:465
  43.6 4.3 %add_product.12 = (f32[1024,128]{1,0:T(8,128)S(1)}, bf16[1024,3072]{1,0:T(8,128)(2,1)S(1)}) custom-call(bf16[3,1024,8192]{2,1,0:T(8,128)(2,1)} %w_proj.19, bf16[1024,2048]{1,0:T(8,128)(2,1)S(1)} %get-tuple-element.89.refs_0_, bf16[1,1,1024,128]{3,2,1,0:T(8,128)(2,1)} %collective-permute-done.10.refs_1_, ...), custom_call_target="tpu_custom_call" | custom-call | flops 68719476736 | bytes 268435456 | tf_op jit(solution)/shard_map/add_product/pallas_call | solution.py:423
  48.0 3.6 %gradients.1 = (f32[3,128,1024]{2,1,0:T(8,128)}, bf16[1024,3072]{1,0:T(8,128)(2,1)S(1)}) custom-call(f32[3,128,1024]{2,1,0:T(8,128)S(1)} %copy-done, f32[128,1024]{1,0:T(8,128)S(1)} %copy-done.1, f32[128,1024]{1,0:T(8,128)S(1)} %copy-done.2, f32[3,3,1024]{2,1,0:T(4,128)S(1)} %copy-done.5, f32[1,1024]{1,0:T(1,128)S(1)} %bitcast.10, f32[224,128]{1,0:T(8,128)S(1)} %copy-done.4, ...), custom_call_target="tpu_custom_call" | custom-call | flops 3932160 | bytes 5242880 | tf_op jit(solution)/shard_map/gradients/pallas_call | solution.py:219
  53.0 1.6 %collective-permute-start.18 = (bf16[1,1,1024,128]{3,2,1,0:T(8,128)(2,1)S(1)}, bf16[1,1,1024,128]{3,2,1,0:T(8,128)(2,1)S(1)}, u32[]{:S(2)}, u32[]{:S(2)}) collective-permute-start(bf16[1,1,1024,128]{3,2,1,0:T(8,128)(2,1)S(1)} %get-tuple-element.127), channel_id=1, source_target_pairs={{0,1},{2,0},{4,2},{6,4},{7,6},{5,7},{3,5},{1,3},{8,9},{10,8},{12,1... | collective-permute-start | bytes 786440 | tf_op jit(solution)/shard_map/ppermute | solution.py:465
  55.0 4.6 %add_product.13 = (f32[1024,128]{1,0:T(8,128)S(1)}, bf16[1024,3072]{1,0:T(8,128)(2,1)S(1)}) custom-call(bf16[3,1024,8192]{2,1,0:T(8,128)(2,1)} %w_proj.19, bf16[1024,3072]{1,0:T(8,128)(2,1)S(1)} %get-tuple-element.102.refs_0_, bf16[1,2,1024,128]{3,2,1,0:T(8,128)(2,1)S(1)} %collective-permute-done.8.refs_1_, ...), custom_call_target="tpu_custom_call" | custom-call | flops 65536 | bytes 256 | tf_op jit(solution)/shard_map/add_product/pallas_call | solution.py:423
  59.6 1.6 %collective-permute-start.22 = (bf16[1,1,1024,128]{3,2,1,0:T(8,128)(2,1)S(1)}, bf16[1,1,1024,128]{3,2,1,0:T(8,128)(2,1)S(1)}, u32[]{:S(2)}, u32[]{:S(2)}) collective-permute-start(bf16[1,1,1024,128]{3,2,1,0:T(8,128)(2,1)S(1)} %get-tuple-element.116), channel_id=1, source_target_pairs={{0,1},{2,0},{4,2},{6,4},{7,6},{5,7},{3,5},{1,3},{8,9},{10,8},{12,1... | collective-permute-start | bytes 786440 | tf_op jit(solution)/shard_map/ppermute | solution.py:465
  61.7 3.9 %add_product.14 = (f32[1024,128]{1,0:T(8,128)S(1)}, bf16[1024,2048]{1,0:T(8,128)(2,1)S(1)}) custom-call(bf16[3,1024,8192]{2,1,0:T(8,128)(2,1)} %w_proj.19, bf16[1024,3072]{1,0:T(8,128)(2,1)S(1)} %get-tuple-element.109.refs_0_, bf16[1,2,1024,128]{3,2,1,0:T(8,128)(2,1)S(1)} %collective-permute-done.9.refs_2_.refs_1_, ...), custom_call_target="tpu_custom_call" | custom-call | flops 65536 | bytes 256 | tf_op jit(solution)/shard_map/add_product/pallas_call | solution.py:423
  66.1 1.7 %collective-permute-start.20 = (bf16[1,1,1024,128]{3,2,1,0:T(8,128)(2,1)S(1)}, bf16[1,1,1024,128]{3,2,1,0:T(8,128)(2,1)S(1)}, u32[]{:S(2)}, u32[]{:S(2)}) collective-permute-start(bf16[1,1,1024,128]{3,2,1,0:T(8,128)(2,1)S(1)} %collective-permute-done.18.refs_3_), channel_id=1, source_target_pairs={{0,1},{2,0},{4,2},{6,4},{7,6},{5,7},{3,5},{1,3},{8,9},{10,8},{12,1... | collective-permute-start | bytes 786440 | tf_op jit(solution)/shard_map/ppermute | solution.py:465
  68.2 1.7 %collective-permute-start.16 = (bf16[1,1,512,128]{3,2,1,0:T(8,128)(2,1)S(1)}, bf16[1,1,512,128]{3,2,1,0:T(8,128)(2,1)S(1)}, u32[]{:S(2)}, u32[]{:S(2)}) collective-permute-start(bf16[1,1,512,128]{3,2,1,0:T(8,128)(2,1)S(1)} %slice.27), channel_id=1, source_target_pairs={{0,1},{2,0},{4,2},{6,4},{7,6},{5,7},{3,5},{1,3},{8,9},{10,8},{12,1... | collective-permute-start | bytes 393224 | tf_op jit(solution)/shard_map/ppermute | solution.py:465
  69.9 2.3 %add_product.15.refs_3_ = f32[1024,128]{1,0:T(8,128)S(1)} custom-call(bf16[3,1024,8192]{2,1,0:T(8,128)(2,1)} %w_proj.19, bf16[1024,2048]{1,0:T(8,128)(2,1)S(1)} %get-tuple-element.114.refs_0_, bf16[1024,2048]{1,0:T(8,128)(2,1)S(1)} %get-tuple-element.115.refs_1_, bf16[1,1,1024,128]{3,2,1,0:T(8,128)(2,1)S(1)} %collective-permute-done.17.refs_2_, ...), custom_call_target="tpu_custom_call" | custom-call | flops 65536 | bytes 256 | tf_op jit(solution)/shard_map/add_product/pallas_call | solution.py:423
  72.2 2.5 %collective-permute-done.19.refs_1_ = bf16[1,1,1024,128]{3,2,1,0:T(8,128)(2,1)S(1)} collective-permute-done((bf16[1,1,1024,128]{3,2,1,0:T(8,128)(2,1)S(1)}, bf16[1,1,1024,128]{3,2,1,0:T(8,128)(2,1)S(1)}, u32[]{:S(2)}, u32[]{:S(2)}) %collective-permute-start.19) | collective-permute-done | bytes 262176 | tf_op jit(solution)/shard_map/ppermute | solution.py:462
  76.1 1.5 %add_product.17 = f32[128,1024]{1,0:T(8,128)} custom-call(bf16[3,1024,8192]{2,1,0:T(8,128)(2,1)} %w_proj.19, bf16[1024,3072]{1,0:T(8,128)(2,1)S(1)} %get-tuple-element.101.refs_0_, bf16[1,1,512,128]{3,2,1,0:T(8,128)(2,1)S(1)} %collective-permute-done.15.refs_1_, bf16[1,1,512,128]{3,2,1,0:T(8,128)(2,1)S(1)} %collective-permute-done.16.refs_2_, ...), custom_call_target="tpu_custom_call" | custom-call | flops 65536 | bytes 256 | tf_op jit(solution)/shard_map/add_product/pallas_call | solution.py:423
  (57 shorter events, 11.6 us)
Async XLA Ops:
  2.8 3.9 %collective-permute-start = (f32[224,128]{1,0:T(8,128)S(1)}, f32[224,128]{1,0:T(8,128)S(1)}, u32[]{:S(2)}, u32[]{:S(2)}) collective-permute-start(f32[224,128]{1,0:T(8,128)S(1)} %get-tuple-element.70), channel_id=1, source_target_pairs={{8,0},{16,8},{24,16},{9,1},{17,9},{25,17},{10,2},{18,10},{26,18},{... | collective-permute-start | bytes 344072 | tf_op jit(solution)/shard_map/ppermute | solution.py:474
  4.1 7.2 %collective-permute-start.2 = (f32[144,128]{1,0:T(8,128)S(1)}, f32[144,128]{1,0:T(8,128)S(1)}, u32[]{:S(2)}, u32[]{:S(2)}) collective-permute-start(f32[144,128]{1,0:T(8,128)S(1)} %get-tuple-element.73), channel_id=1, source_target_pairs={{24,0},{25,1},{26,2},{27,3},{28,4},{29,5},{30,6},{31,7}} | collective-permute-start | bytes 221192 | tf_op jit(solution)/shard_map/ppermute | solution.py:474
  5.4 7.1 %collective-permute-start.1 = (f32[144,128]{1,0:T(8,128)S(1)}, f32[144,128]{1,0:T(8,128)S(1)}, u32[]{:S(2)}, u32[]{:S(2)}) collective-permute-start(f32[144,128]{1,0:T(8,128)S(1)} %get-tuple-element.73), channel_id=1, source_target_pairs={{16,0},{24,8},{17,1},{25,9},{18,2},{26,10},{19,3},{27,11},{20,4},{... | collective-permute-start | bytes 221192 | tf_op jit(solution)/shard_map/ppermute | solution.py:474
  6.7 5.8 %copy-start.3 = (f32[224,128]{1,0:T(8,128)}, f32[224,128]{1,0:T(8,128)S(1)}, u32[]{:S(2)}) copy-start(f32[224,128]{1,0:T(8,128)S(1)} %collective-permute-done.later.refs_0_) | copy-start | bytes 344068
  7.0 11.0 %collective-permute-start.6 = (bf16[1,1,1024,128]{3,2,1,0:T(8,128)(2,1)S(1)}, bf16[1,1,1024,128]{3,2,1,0:T(8,128)(2,1)}, u32[]{:S(2)}, u32[]{:S(2)}) collective-permute-start(bf16[1,1,1024,128]{3,2,1,0:T(8,128)(2,1)S(1)} %bitcast.15), channel_id=1, source_target_pairs={{0,1},{2,0},{4,2},{6,4},{7,6},{5,7},{3,5},{1,3},{8,9},{10,8},{12,1... | collective-permute-start | bytes 786440 | tf_op jit(solution)/shard_map/ppermute | solution.py:465
  10.0 8.5 %collective-permute-start.5 = (bf16[1,1,1024,128]{3,2,1,0:T(8,128)(2,1)S(1)}, bf16[1,1,1024,128]{3,2,1,0:T(8,128)(2,1)}, u32[]{:S(2)}, u32[]{:S(2)}) collective-permute-start(bf16[1,1,1024,128]{3,2,1,0:T(8,128)(2,1)S(1)} %bitcast.16), channel_id=1, source_target_pairs={{0,2},{2,4},{4,6},{6,7},{7,5},{5,3},{3,1},{1,0},{8,10},{10,12},{12... | collective-permute-start | bytes 786440 | tf_op jit(solution)/shard_map/ppermute | solution.py:462
  15.4 16.6 %collective-permute-start.4 = (bf16[1,2,1024,128]{3,2,1,0:T(8,128)(2,1)S(1)}, bf16[1,2,1024,128]{3,2,1,0:T(8,128)(2,1)S(1)}, u32[]{:S(2)}, u32[]{:S(2)}) collective-permute-start(bf16[1,2,1024,128]{3,2,1,0:T(8,128)(2,1)S(1)} %bitcast.12), channel_id=1, source_target_pairs={{0,1},{2,0},{4,2},{6,4},{7,6},{5,7},{3,5},{1,3},{8,9},{10,8},{12,1... | collective-permute-start | bytes 1572872 | tf_op jit(solution)/shard_map/ppermute | solution.py:465
  17.9 14.9 %collective-permute-start.3 = (bf16[1,2,1024,128]{3,2,1,0:T(8,128)(2,1)S(1)}, bf16[1,2,1024,128]{3,2,1,0:T(8,128)(2,1)S(1)}, u32[]{:S(2)}, u32[]{:S(2)}) collective-permute-start(bf16[1,2,1024,128]{3,2,1,0:T(8,128)(2,1)S(1)} %bitcast.13), channel_id=1, source_target_pairs={{0,2},{2,4},{4,6},{6,7},{7,5},{5,3},{3,1},{1,0},{8,10},{10,12},{12... | collective-permute-start | bytes 1572872 | tf_op jit(solution)/shard_map/ppermute | solution.py:462
  18.5 13.5 %collective-permute-start.7 = (f32[17,1024]{1,0:T(8,128)S(1)}, f32[17,1024]{1,0:T(8,128)S(1)}, u32[]{:S(2)}, u32[]{:S(2)}) collective-permute-start(f32[17,1024]{1,0:T(8,128)S(1)} %get-tuple-element.84), channel_id=1, source_target_pairs={{0,8},{8,0},{16,24},{24,16},{1,9},{9,1},{17,25},{25,17},{2,10},{10... | collective-permute-start | bytes 208904 | tf_op jit(solution)/shard_map/ppermute | solution.py:477
  19.1 20.1 %collective-permute-start.10 = (bf16[1,1,1024,128]{3,2,1,0:T(8,128)(2,1)}, bf16[1,1,1024,128]{3,2,1,0:T(8,128)(2,1)}, u32[]{:S(2)}, u32[]{:S(2)}) collective-permute-start(bf16[1,1,1024,128]{3,2,1,0:T(8,128)(2,1)} %collective-permute-done.5.refs_2_), channel_id=1, source_target_pairs={{0,2},{2,4},{4,6},{6,7},{7,5},{5,3},{3,1},{1,0},{8,10},{10,12},{12... | collective-permute-start | bytes 786440 | tf_op jit(solution)/shard_map/ppermute | solution.py:462
  20.1 19.2 %collective-permute-start.11 = (bf16[1,1,1024,128]{3,2,1,0:T(8,128)(2,1)}, bf16[1,1,1024,128]{3,2,1,0:T(8,128)(2,1)}, u32[]{:S(2)}, u32[]{:S(2)}) collective-permute-start(bf16[1,1,1024,128]{3,2,1,0:T(8,128)(2,1)} %collective-permute-done.6.refs_3_), channel_id=1, source_target_pairs={{0,1},{2,0},{4,2},{6,4},{7,6},{5,7},{3,5},{1,3},{8,9},{10,8},{12,1... | collective-permute-start | bytes 786440 | tf_op jit(solution)/shard_map/ppermute | solution.py:465
  32.7 20.1 %collective-permute-start.8 = (bf16[1,2,1024,128]{3,2,1,0:T(8,128)(2,1)S(1)}, bf16[1,2,1024,128]{3,2,1,0:T(8,128)(2,1)S(1)}, u32[]{:S(2)}, u32[]{:S(2)}) collective-permute-start(bf16[1,2,1024,128]{3,2,1,0:T(8,128)(2,1)S(1)} %collective-permute-done.3.refs_1_), channel_id=1, source_target_pairs={{0,2},{2,4},{4,6},{6,7},{7,5},{5,3},{3,1},{1,0},{8,10},{10,12},{12... | collective-permute-start | bytes 1572872 | tf_op jit(solution)/shard_map/ppermute | solution.py:462
  33.0 19.8 %collective-permute-start.9 = (bf16[1,2,1024,128]{3,2,1,0:T(8,128)(2,1)S(1)}, bf16[1,2,1024,128]{3,2,1,0:T(8,128)(2,1)S(1)}, u32[]{:S(2)}, u32[]{:S(2)}) collective-permute-start(bf16[1,2,1024,128]{3,2,1,0:T(8,128)(2,1)S(1)} %collective-permute-done.4.refs_2_), channel_id=1, source_target_pairs={{0,1},{2,0},{4,2},{6,4},{7,6},{5,7},{3,5},{1,3},{8,9},{10,8},{12,1... | collective-permute-start | bytes 1572872 | tf_op jit(solution)/shard_map/ppermute | solution.py:465
  39.3 12.3 %collective-permute-start.12 = (f32[17,1024]{1,0:T(8,128)S(1)}, f32[17,1024]{1,0:T(8,128)S(1)}, u32[]{:S(2)}, u32[]{:S(2)}) collective-permute-start(f32[17,1024]{1,0:T(8,128)S(1)} %add.6), channel_id=1, source_target_pairs={{0,16},{8,24},{16,0},{24,8},{1,17},{9,25},{17,1},{25,9},{2,18},{10... | collective-permute-start | bytes 208904 | tf_op jit(solution)/shard_map/ppermute | solution.py:477
  41.6 19.7 %collective-permute-start.13 = (bf16[1,1,1024,128]{3,2,1,0:T(8,128)(2,1)}, bf16[1,1,1024,128]{3,2,1,0:T(8,128)(2,1)S(1)}, u32[]{:S(2)}, u32[]{:S(2)}) collective-permute-start(bf16[1,1,1024,128]{3,2,1,0:T(8,128)(2,1)} %collective-permute-done.10.refs_1_), channel_id=1, source_target_pairs={{0,2},{2,4},{4,6},{6,7},{7,5},{5,3},{3,1},{1,0},{8,10},{10,12},{12... | collective-permute-start | bytes 786440 | tf_op jit(solution)/shard_map/ppermute | solution.py:462
  41.7 19.6 %collective-permute-start.14 = (bf16[1,1,1024,128]{3,2,1,0:T(8,128)(2,1)}, bf16[1,1,1024,128]{3,2,1,0:T(8,128)(2,1)S(1)}, u32[]{:S(2)}, u32[]{:S(2)}) collective-permute-start(bf16[1,1,1024,128]{3,2,1,0:T(8,128)(2,1)} %collective-permute-done.11.refs_2_), channel_id=1, source_target_pairs={{0,1},{2,0},{4,2},{6,4},{7,6},{5,7},{3,5},{1,3},{8,9},{10,8},{12,1... | collective-permute-start | bytes 786440 | tf_op jit(solution)/shard_map/ppermute | solution.py:465
  53.0 12.7 %collective-permute-start.18 = (bf16[1,1,1024,128]{3,2,1,0:T(8,128)(2,1)S(1)}, bf16[1,1,1024,128]{3,2,1,0:T(8,128)(2,1)S(1)}, u32[]{:S(2)}, u32[]{:S(2)}) collective-permute-start(bf16[1,1,1024,128]{3,2,1,0:T(8,128)(2,1)S(1)} %get-tuple-element.127), channel_id=1, source_target_pairs={{0,1},{2,0},{4,2},{6,4},{7,6},{5,7},{3,5},{1,3},{8,9},{10,8},{12,1... | collective-permute-start | bytes 786440 | tf_op jit(solution)/shard_map/ppermute | solution.py:465
  54.6 11.1 %collective-permute-start.17 = (bf16[1,1,1024,128]{3,2,1,0:T(8,128)(2,1)S(1)}, bf16[1,1,1024,128]{3,2,1,0:T(8,128)(2,1)S(1)}, u32[]{:S(2)}, u32[]{:S(2)}) collective-permute-start(bf16[1,1,1024,128]{3,2,1,0:T(8,128)(2,1)S(1)} %get-tuple-element.129), channel_id=1, source_target_pairs={{0,2},{2,4},{4,6},{6,7},{7,5},{5,3},{3,1},{1,0},{8,10},{10,12},{12... | collective-permute-start | bytes 786440 | tf_op jit(solution)/shard_map/ppermute | solution.py:462
  59.6 8.5 %collective-permute-start.22 = (bf16[1,1,1024,128]{3,2,1,0:T(8,128)(2,1)S(1)}, bf16[1,1,1024,128]{3,2,1,0:T(8,128)(2,1)S(1)}, u32[]{:S(2)}, u32[]{:S(2)}) collective-permute-start(bf16[1,1,1024,128]{3,2,1,0:T(8,128)(2,1)S(1)} %get-tuple-element.116), channel_id=1, source_target_pairs={{0,1},{2,0},{4,2},{6,4},{7,6},{5,7},{3,5},{1,3},{8,9},{10,8},{12,1... | collective-permute-start | bytes 786440 | tf_op jit(solution)/shard_map/ppermute | solution.py:465
  61.3 8.6 %collective-permute-start.21 = (bf16[1,1,1024,128]{3,2,1,0:T(8,128)(2,1)S(1)}, bf16[1,1,1024,128]{3,2,1,0:T(8,128)(2,1)S(1)}, u32[]{:S(2)}, u32[]{:S(2)}) collective-permute-start(bf16[1,1,1024,128]{3,2,1,0:T(8,128)(2,1)S(1)} %get-tuple-element.128), channel_id=1, source_target_pairs={{0,2},{2,4},{4,6},{6,7},{7,5},{5,3},{3,1},{1,0},{8,10},{10,12},{12... | collective-permute-start | bytes 786440 | tf_op jit(solution)/shard_map/ppermute | solution.py:462
  65.7 9.0 %collective-permute-start.19 = (bf16[1,1,1024,128]{3,2,1,0:T(8,128)(2,1)S(1)}, bf16[1,1,1024,128]{3,2,1,0:T(8,128)(2,1)S(1)}, u32[]{:S(2)}, u32[]{:S(2)}) collective-permute-start(bf16[1,1,1024,128]{3,2,1,0:T(8,128)(2,1)S(1)} %collective-permute-done.17.refs_2_), channel_id=1, source_target_pairs={{0,2},{2,4},{4,6},{6,7},{7,5},{5,3},{3,1},{1,0},{8,10},{10,12},{12... | collective-permute-start | bytes 786440 | tf_op jit(solution)/shard_map/ppermute | solution.py:462
  66.1 8.6 %collective-permute-start.20 = (bf16[1,1,1024,128]{3,2,1,0:T(8,128)(2,1)S(1)}, bf16[1,1,1024,128]{3,2,1,0:T(8,128)(2,1)S(1)}, u32[]{:S(2)}, u32[]{:S(2)}) collective-permute-start(bf16[1,1,1024,128]{3,2,1,0:T(8,128)(2,1)S(1)} %collective-permute-done.18.refs_3_), channel_id=1, source_target_pairs={{0,1},{2,0},{4,2},{6,4},{7,6},{5,7},{3,5},{1,3},{8,9},{10,8},{12,1... | collective-permute-start | bytes 786440 | tf_op jit(solution)/shard_map/ppermute | solution.py:465
  67.8 8.3 %collective-permute-start.15 = (bf16[1,1,512,128]{3,2,1,0:T(8,128)(2,1)S(1)}, bf16[1,1,512,128]{3,2,1,0:T(8,128)(2,1)S(1)}, u32[]{:S(2)}, u32[]{:S(2)}) collective-permute-start(bf16[1,1,512,128]{3,2,1,0:T(8,128)(2,1)S(1)} %slice.26), channel_id=1, source_target_pairs={{0,2},{2,4},{4,6},{6,7},{7,5},{5,3},{3,1},{1,0},{8,10},{10,12},{12... | collective-permute-start | bytes 393224 | tf_op jit(solution)/shard_map/ppermute | solution.py:462
  68.2 7.9 %collective-permute-start.16 = (bf16[1,1,512,128]{3,2,1,0:T(8,128)(2,1)S(1)}, bf16[1,1,512,128]{3,2,1,0:T(8,128)(2,1)S(1)}, u32[]{:S(2)}, u32[]{:S(2)}) collective-permute-start(bf16[1,1,512,128]{3,2,1,0:T(8,128)(2,1)S(1)} %slice.27), channel_id=1, source_target_pairs={{0,1},{2,0},{4,2},{6,4},{7,6},{5,7},{3,5},{1,3},{8,9},{10,8},{12,1... | collective-permute-start | bytes 393224 | tf_op jit(solution)/shard_map/ppermute | solution.py:465
  (6 other events, 26.4 us)
